TPU v7x, 512 devices: a whole 4x8x8 slice. The times are simulated.
512 devices in a mesh: dp: 2 (over y_hi), row: 16 (over z, core), col: 16 (over y_lo, x).
Axes of the slice: x: 4, y: 8 (y_hi: 2, y_lo: 4; y = y_hi * 4 + y_lo), z: 8, core: 2. Of those that a mesh axis runs over, the one named last changes fastest.
Arguments:
- features: bfloat16 [4096, 3072], P(('dp', 'row'), 'col'), may hold values from -6 to 6
- up_weight: bfloat16 [3072, 24576], P('row', 'col'), may hold values from -0.109375 to 0.109375
- out_grad: bfloat16 [4096, 24576], P(('dp', 'row'), 'col'), may hold values from -6 to 6
Outputs:
- gelu_out: bfloat16 [4096, 24576], P(('dp', 'row'), 'col')
- feature_grad: bfloat16 [4096, 3072], P(('dp', 'row'), 'col')
- weight_grad: float32 [3072, 24576], P('row', 'col')
All inputs are finite; a program needn't handle non-finite values.
Results may differ from a plain program's by a relative error of at most 0.022.
Values may be sent and summed in bfloat16 or wider, within the bound.
No kernel may reach another device: no remote copies, remote signals or barrier semaphores. Data moves between devices by JAX's collectives and lax.ppermute only.
A program may use at most 64 MiB of HBM per device.

v0:
```python
import math

import jax
import jax.numpy as jnp
from jax import lax
from jax.sharding import PartitionSpec as P


def from_root(value, axis, source):
    kept = jnp.where(lax.axis_index(axis) == source, value, 0).astype(value.dtype)
    return lax.psum(kept, axis)


def per_device(features, up_weight, out_grad):
    token_rows = lax.all_gather(features, "col", axis=1, tiled=True)
    hidden = jnp.dot(
        token_rows,
        lax.all_gather(up_weight, "row", axis=0, tiled=True),
        preferred_element_type=jnp.float32,
    )
    normal_cdf = 0.5 * (1.0 + jax.scipy.special.erf(hidden / math.sqrt(2.0)))
    density = jnp.exp(-0.5 * hidden * hidden) / math.sqrt(2.0 * math.pi)
    gelu_out = (hidden * normal_cdf).astype(jnp.bfloat16)
    hidden_grad = (out_grad.astype(jnp.float32) * (normal_cdf + hidden * density)).astype(
        jnp.bfloat16
    )
    contract_last = (((1,), (1,)), ((), ()))
    partial_value = lax.dot_general(
        hidden_grad,
        lax.all_gather(up_weight, "row", axis=0, tiled=True),
        contract_last,
        preferred_element_type=jnp.float32,
    )
    feature_grad = lax.psum_scatter(
        partial_value.astype(jnp.bfloat16), "col", scatter_dimension=1, tiled=True
    )
    grad_cols = lax.all_gather(hidden_grad, "row", axis=0, tiled=True)
    column = lax.all_gather(features, "row", axis=0, tiled=True)
    column = from_root(column, "col", lax.axis_index("row"))
    own_grad = lax.dot_general(
        column, grad_cols, (((0,), (0,)), ((), ())), preferred_element_type=jnp.float32
    )
    weight_grad = lax.psum(own_grad.astype(jnp.bfloat16), "dp").astype(jnp.float32)
    return (gelu_out, feature_grad, weight_grad)


def solution(mesh):
    placed = (P(("dp", "row"), "col"), P("row", "col"), P(("dp", "row"), "col"))
    return jax.shard_map(
        per_device,
        mesh=mesh,
        in_specs=placed,
        out_specs=(P(("dp", "row"), "col"), P(("dp", "row"), "col"), P("row", "col")),
        check_vma=False,
    )
```

profile of v0, /device:TPU:64, one launch (start us, length us, event | category | flops | bytes accessed | tf_op | source)
XLA Modules:
  0.0 361.5 jit_solution(11489043769685606549)
XLA Ops:
  8.0 0.0 all-gather.3.cloned.1.call-start
  8.0 0.7 all-gather.3.cloned.1.call-update
  8.7 0.0 all-reduce.3.cloned.1.call-start
  8.8 22.8 %all_gather.15 = bf16[2048,192]{0,1:T(8,128)(2,1)S(1)} all-gather(bf16[128,192]{0,1:T(8,128)(2,1)} %param.3), channel_id=1, replica_groups=mesh['dp'=2,'row'=16,'col'=16] {'row'}, dimensions={0}, use_global_device_ids=true | all-gather | bytes 835584 | tf_op jit(solution)/shard_map/all_gather | solution.py:38
  31.6 0.9 broadcast_select_fusion
  32.6 0.0 all-reduce.3.cloned.1.call-update
  32.6 0.0 all-gather.5.cloned.1.call-start
  32.6 47.8 %all_gather.13 = bf16[128,3072]{0,1:T(8,128)(2,1)S(1)} all-gather(bf16[128,192]{0,1:T(8,128)(2,1)} %param.3), channel_id=1, replica_groups=mesh['dp'=2,'row'=16,'col'=16] {'col'}, dimensions={1}, use_global_device_ids=true | all-gather | bytes 835584 | tf_op jit(solution)/shard_map/all_gather | solution.py:15
  80.5 0.0 all-gather.3.cloned.1.call-done
  80.5 6.3 %fusion.5 = (bf16[128,1536]{1,0:T(8,128)(2,1)}, bf16[128,1536]{1,0:T(8,128)(2,1)}) fusion(bf16[128,1536]{1,0:T(8,128)(2,1)} %param.5, bf16[128,3072]{0,1:T(8,128)(2,1)S(1)} %all_gather.13, bf16[3072,1536]{1,0:T(8,128)(2,1)} %all-gather.3.cloned.1.call-done), kind=kOutput, calls=%fused_computation.8 | convolution fusion | flops 1210515456 | bytes 11403264 | tf_op jit(solution)/shard_map/dot_general | solution.py:16
  86.8 0.0 copy-start
  86.8 0.0 all-gather.5.cloned.1.call-update
  86.8 0.0 all-reduce.5.cloned.1.call-start
  86.9 112.8 %all-reduce.3.cloned.1.call-done = bf16[2048,192]{0,1:T(8,128)(2,1)} async-done(((bf16[2048,192]{0,1:T(8,128)(2,1)}), bf16[2048,192]{0,1:T(8,128)(2,1)}) %all-reduce.3.cloned.1.call-update) | async-done | bytes 786448 | tf_op jit(solution)/shard_map/psum | solution.py:11
  199.6 0.0 all-gather.5.cloned.1.call-done
  199.6 5.2 %convolution_convert_fusion.1 = bf16[192,1536]{1,0:T(8,128)(2,1)} fusion(bf16[2048,192]{0,1:T(8,128)(2,1)} %all-reduce.3.cloned.1.call-done, bf16[2048,1536]{1,0:T(8,128)(2,1)} %all-gather.5.cloned.1.call-done), kind=kOutput, calls=%fused_computation.1 | convolution fusion | flops 1208254464 | bytes 7667712 | tf_op jit(solution)/shard_map/dot_general | solution.py:40
  204.9 0.0 all-reduce.5.cloned.1.call-update
  204.9 0.0 reduce-scatter.2.cloned.1.call-start
  205.0 0.0 copy-done
  205.0 7.2 %convolution_convert_fusion = bf16[128,3072]{0,1:T(8,128)(2,1)} fusion(bf16[128,1536]{1,0:T(8,128)(2,1)S(1)} %copy-done, bf16[3072,1536]{1,0:T(8,128)(2,1)} %all-gather.3.cloned.1.call-done), kind=kOutput, calls=%fused_computation | convolution fusion | flops 1208352768 | bytes 10616832 | tf_op jit(solution)/shard_map/dot_general | solution.py:28
  212.1 0.0 reduce-scatter.2.cloned.1.call-update
  212.2 50.4 %all-reduce.5.cloned.1.call-done = bf16[192,1536]{1,0:T(8,128)(2,1)} async-done(((bf16[192,1536]{1,0:T(8,128)(2,1)}), bf16[192,1536]{1,0:T(8,128)(2,1)}) %all-reduce.5.cloned.1.call-update) | async-done | bytes 589840 | tf_op jit(solution)/shard_map/psum | solution.py:43
  262.5 2.2 convert_element_type.25
  264.7 89.2 %reduce-scatter.2.cloned.1.call-done = bf16[128,192]{0,1:T(8,128)(2,1)} async-done(((bf16[128,3072]{0,1:T(8,128)(2,1)}), bf16[128,192]{0,1:T(8,128)(2,1)}) %reduce-scatter.2.cloned.1.call-update) | async-done | bytes 49168 | tf_op jit(solution)/shard_map/reduce_scatter | solution.py:34
Async XLA Ops:
  8.0 72.5 %all-gather.3.cloned.1.call-start = ((), (), s32[]{:S(2)}) async-start(), calls=%async_computation.1 | async-start | bytes 10027008 | tf_op jit(solution)/shard_map/all_gather | solution.py:18
  8.7 190.9 %all-reduce.3.cloned.1.call-start = ((), (), s32[]{:S(2)}) async-start(), calls=%async_computation.3 | async-start | bytes 1572864 | tf_op jit(solution)/shard_map/psum | solution.py:11
  32.6 167.0 %all-gather.5.cloned.1.call-start = ((), (), s32[]{:S(2)}) async-start(), calls=%async_computation.4 | async-start | bytes 6684672 | tf_op jit(solution)/shard_map/all_gather | solution.py:37
  86.8 118.2 %copy-start = (bf16[128,1536]{1,0:T(8,128)(2,1)S(1)}, bf16[128,1536]{1,0:T(8,128)(2,1)}, u32[]{:S(2)}) copy-start(bf16[128,1536]{1,0:T(8,128)(2,1)} %get-tuple-element.3) | copy-start | bytes 1179652
  86.8 175.7 %all-reduce.5.cloned.1.call-start = ((), (), s32[]{:S(2)}) async-start(), calls=%async_computation.5 | async-start | bytes 1179648 | tf_op jit(solution)/shard_map/psum | solution.py:43
  204.9 149.0 %reduce-scatter.2.cloned.1.call-start = ((), (), s32[]{:S(2)}) async-start(), calls=%async_computation.2 | async-start | bytes 835584 | tf_op jit(solution)/shard_map/reduce_scatter | solution.py:34
Sparse Core Ops, SparseCore 0:
  11.0 65.8 all-gather.2
  86.9 45.4 all-gather.4
Sparse Core Ops, SparseCore 1:
  32.7 166.9 all-reduce.2
  205.0 57.5 all-reduce.4
  265.8 88.1 reduce-scatter.1
where the time goes:
time: 362 us; the launch traced here: 361 us
  waiting for transfers between devices  253 us (70%)
  blocking collectives  70.7 us (20%)
  matrix products  18.8 us (5%)
  between operations  15.7 us (4%)
    psum x1, waiting for transfers between devices, from_root(): return lax.psum(kept, axis)  113 us
    reduce_scatter x1, waiting for transfers between devices, per_device(): lax.psum_scatter(partial_value.astype(jnp.bfloat16), 'col', scatter_dimen...  89.2 us
    psum x1, waiting for transfers between devices, per_device(): lax.psum(own_grad.astype(jnp.bfloat16), 'dp').astype(jnp.float32)  50.4 us
    all_gather x1, blocking collectives, per_device(): token_rows = lax.all_gather(features, 'col', axis=1, tiled=True)  47.8 us
    all_gather x1, blocking collectives, per_device(): column = lax.all_gather(features, 'row', axis=0, tiled=True)  22.8 us
  transfers between devices with their start and end apart: 5, of which 3 were waited for; matrix products, arithmetic and copies ran while one was open for 5% of the time, Pallas kernels for 0%

commit v1 on v0

v1 whole, which is shorter than its diff:
```python
import math

import jax
import jax.numpy as jnp
from jax import lax
from jax.sharding import PartitionSpec as P

ROWS = 16


def per_device(features, up_weight, out_grad):
    tokens, depth = features.shape
    weight = lax.all_gather(up_weight, "row", axis=0, tiled=True)
    token_rows = lax.all_gather(features, "col", axis=1, tiled=True)
    swap = [(r * ROWS + c, c * ROWS + r) for r in range(ROWS) for c in range(ROWS)]
    turned = lax.ppermute(features, ("row", "col"), swap)
    column = lax.all_gather(turned, "col", axis=0, tiled=True)

    hidden = jnp.dot(token_rows, weight, preferred_element_type=jnp.float32)
    normal_cdf = 0.5 * (1.0 + jax.scipy.special.erf(hidden / math.sqrt(2.0)))
    density = jnp.exp(-0.5 * hidden * hidden) / math.sqrt(2.0 * math.pi)
    gelu_out = (hidden * normal_cdf).astype(jnp.bfloat16)
    hidden_grad = (out_grad.astype(jnp.float32) * (normal_cdf + hidden * density)).astype(
        jnp.bfloat16
    )
    grad_cols = lax.all_gather(hidden_grad, "row", axis=0, tiled=True)

    contract_last = (((1,), (1,)), ((), ()))
    partial_value = lax.dot_general(
        weight, hidden_grad, contract_last, preferred_element_type=jnp.float32
    ).astype(jnp.bfloat16)
    pieces = lax.all_to_all(
        partial_value.reshape(ROWS, depth, tokens), "col", 0, 0, tiled=True
    )
    feature_grad = jnp.sum(pieces.astype(jnp.float32), axis=0).astype(jnp.bfloat16).T

    grad_cols, feature_grad = lax.optimization_barrier((grad_cols, feature_grad))
    own_grad = lax.dot_general(
        column, grad_cols, (((0,), (0,)), ((), ())), preferred_element_type=jnp.float32
    ).astype(jnp.bfloat16)
    other_grad = lax.ppermute(own_grad, "dp", [(0, 1), (1, 0)])
    weight_grad = own_grad.astype(jnp.float32) + other_grad.astype(jnp.float32)
    return (gelu_out, feature_grad, weight_grad)


def solution(mesh):
    placed = (P(("dp", "row"), "col"), P("row", "col"), P(("dp", "row"), "col"))
    return jax.shard_map(
        per_device,
        mesh=mesh,
        in_specs=placed,
        out_specs=(P(("dp", "row"), "col"), P(("dp", "row"), "col"), P("row", "col")),
        check_vma=False,
    )
```

time: 362 us -> 202 us (0.56)
  the two profiles are of different devices: /device:TPU:64 before, /device:TPU:128 now
where the time goes in v1:
time: 202 us
  blocking collectives  108 us (53%)
  waiting for transfers between devices  41.7 us (21%)
  starting transfers between devices  18.2 us (9%)
  matrix products  17.5 us (9%)
  between operations  14.1 us (7%)
    all_gather x1, blocking collectives, per_device(): column = lax.all_gather(turned, 'col', axis=0, tiled=True)  60.2 us
    all_gather x1, blocking collectives, per_device(): token_rows = lax.all_gather(features, 'col', axis=1, tiled=True)  47.4 us
    all_gather x1, waiting for transfers between devices, per_device(): weight = lax.all_gather(up_weight, 'row', axis=0, tiled=True)  19.9 us
    ppermute x1, waiting for transfers between devices, per_device(): other_grad = lax.ppermute(own_grad, 'dp', [(0, 1), (1, 0)])  10.6 us
    ppermute x1, waiting for transfers between devices, per_device(): turned = lax.ppermute(features, ('row', 'col'), swap)  10.5 us
    all_to_all x1, starting transfers between devices, per_device(): lax.all_to_all(partial_value.reshape(ROWS, depth, tokens), 'col', 0, 0, t...  7.1 us
    dot_general x1, matrix products, per_device(): lax.dot_general(weight, hidden_grad, contract_last, preferred_element_typ...  7 us
    dot_general x1, matrix products, per_device(): hidden = jnp.dot(token_rows, weight, preferred_element_type=jnp.float32)  6.32 us
  transfers between devices with their start and end apart: 5, of which 3 were waited for; matrix products, arithmetic and copies ran while one was open for 4% of the time, Pallas kernels for 0%

profile of v1, /device:TPU:128, one launch (start us, length us, event | category | flops | bytes accessed | tf_op | source)
XLA Modules:
  0.0 202.2 jit_solution(15706445418760913772)
XLA Ops:
  7.2 0.0 all-gather.3.cloned.1.call-start
  7.2 0.7 all-gather.3.cloned.1.call-update
  7.9 0.0 all-gather.5.cloned.1.call-start
  7.9 47.4 %all_gather.12 = bf16[128,3072]{0,1:T(8,128)(2,1)S(1)} all-gather(bf16[128,192]{0,1:T(8,128)(2,1)} %param.3), channel_id=1, replica_groups=mesh['dp'=2,'row'=16,'col'=16] {'col'}, dimensions={1}, use_global_device_ids=true | all-gather | bytes 835584 | tf_op jit(solution)/shard_map/all_gather | solution.py:14
  55.4 19.9 %all-gather.3.cloned.1.call-done = bf16[3072,1536]{1,0:T(8,128)(2,1)} async-done(((bf16[192,1536]{1,0:T(8,128)(2,1)}), bf16[3072,1536]{1,0:T(8,128)(2,1)}) %all-gather.3.cloned.1.call-update) | async-done | bytes 9437200 | tf_op jit(solution)/shard_map/all_gather | solution.py:13
  75.2 6.3 %fusion.7 = (bf16[128,1536]{1,0:T(8,128)(2,1)}, bf16[128,1536]{1,0:T(8,128)(2,1)}) fusion(bf16[128,1536]{1,0:T(8,128)(2,1)} %param.5, bf16[128,3072]{0,1:T(8,128)(2,1)S(1)} %all_gather.12, bf16[3072,1536]{1,0:T(8,128)(2,1)} %all-gather.3.cloned.1.call-done), kind=kOutput, calls=%fused_computation.11 | convolution fusion | flops 1210515456 | bytes 11403264 | tf_op jit(solution)/shard_map/dot_general | solution.py:19
  81.6 0.0 all-gather.5.cloned.1.call-update
  81.6 0.0 copy-start
  81.6 7.0 %fusion = bf16[3072,128]{0,1:T(8,128)(2,1)S(1)} fusion(bf16[128,1536]{1,0:T(8,128)(2,1)} %get-tuple-element.7, bf16[3072,1536]{1,0:T(8,128)(2,1)} %all-gather.3.cloned.1.call-done), kind=kOutput, calls=%fused_computation.1 | convolution fusion | flops 1208352768 | bytes 10616832 | tf_op jit(solution)/shard_map/dot_general | solution.py:29
  88.6 1.2 copy.6
  89.8 7.1 %all-to-all-start = ((bf16[16,192,128]{2,1,0:T(8,128)(2,1)}), bf16[16,192,128]{2,1,0:T(8,128)(2,1)S(1)}, u32[]{:S(2)}, u32[]{:S(2)}) async-start(bf16[16,192,128]{2,1,0:T(8,128)(2,1)} %bitcast.1), calls=%async_computation | async-start | bytes 1572864 | tf_op jit(solution)/shard_map/all_to_all | solution.py:32
  96.9 0.0 copy-done
  96.9 5.9 %collective-permute-start = (bf16[128,192]{0,1:T(8,128)(2,1)S(1)}, bf16[128,192]{0,1:T(8,128)(2,1)S(1)}, u32[]{:S(2)}, u32[]{:S(2)}) collective-permute-start(bf16[128,192]{0,1:T(8,128)(2,1)S(1)} %copy-done), channel_id=1, source_target_pairs={{0,0},{1,16},{2,32},{3,48},{4,64},{5,80},{6,96},{7,112},{8,128},{9... | collective-permute-start | bytes 147464 | tf_op jit(solution)/shard_map/ppermute | solution.py:16
  102.8 10.5 %collective-permute-done = bf16[128,192]{0,1:T(8,128)(2,1)S(1)} collective-permute-done((bf16[128,192]{0,1:T(8,128)(2,1)S(1)}, bf16[128,192]{0,1:T(8,128)(2,1)S(1)}, u32[]{:S(2)}, u32[]{:S(2)}) %collective-permute-start) | collective-permute-done | bytes 49184 | tf_op jit(solution)/shard_map/ppermute | solution.py:16
  113.3 60.2 %all_gather.15 = bf16[2048,192]{0,1:T(8,128)(2,1)S(1)} all-gather(bf16[128,192]{0,1:T(8,128)(2,1)S(1)} %collective-permute-done), channel_id=1, replica_groups=mesh['dp'=2,'row'=16,'col'=16] {'col'}, dimensions={0}, use_global_device_ids=true | all-gather | bytes 835584 | tf_op jit(solution)/shard_map/all_gather | solution.py:17
  173.5 0.0 all-to-all-done
  173.5 0.7 reduce_sum.12
  174.3 0.0 all-gather.5.cloned.1.call-done
  174.3 4.2 %fusion.1 = bf16[192,1536]{1,0:T(8,128)(2,1)S(1)} fusion(bf16[2048,192]{0,1:T(8,128)(2,1)S(1)} %all_gather.15, bf16[2048,1536]{1,0:T(8,128)(2,1)} %all-gather.5.cloned.1.call-done), kind=kOutput, calls=%fused_computation.3 | convolution fusion | flops 1208254464 | bytes 7667712 | tf_op jit(solution)/shard_map/dot_general | solution.py:38
  178.5 5.1 %collective-permute-start.1 = (bf16[192,1536]{1,0:T(8,128)(2,1)S(1)}, bf16[192,1536]{1,0:T(8,128)(2,1)S(1)}, u32[]{:S(2)}, u32[]{:S(2)}) collective-permute-start(bf16[192,1536]{1,0:T(8,128)(2,1)S(1)} %fusion.1), channel_id=1, source_target_pairs={{0,256},{256,0},{1,257},{257,1},{2,258},{258,2},{3,259},{259,3},{4... | collective-permute-start | bytes 1769480 | tf_op jit(solution)/shard_map/ppermute | solution.py:41
  183.6 10.6 %collective-permute-done.1 = bf16[192,1536]{1,0:T(8,128)(2,1)S(1)} collective-permute-done((bf16[192,1536]{1,0:T(8,128)(2,1)S(1)}, bf16[192,1536]{1,0:T(8,128)(2,1)S(1)}, u32[]{:S(2)}, u32[]{:S(2)}) %collective-permute-start.1) | collective-permute-done | bytes 589856 | tf_op jit(solution)/shard_map/ppermute | solution.py:41
  194.1 1.2 convert_add_fusion
Async XLA Ops:
  7.2 68.1 %all-gather.3.cloned.1.call-start = ((), (), s32[]{:S(2)}) async-start(), calls=%async_computation.1 | async-start | bytes 10027008 | tf_op jit(solution)/shard_map/all_gather | solution.py:13
  7.9 166.4 %all-gather.5.cloned.1.call-start = ((), (), s32[]{:S(2)}) async-start(), calls=%async_computation.2 | async-start | bytes 6684672 | tf_op jit(solution)/shard_map/all_gather | solution.py:26
  81.6 15.3 %copy-start = (bf16[128,192]{0,1:T(8,128)(2,1)S(1)}, bf16[128,192]{0,1:T(8,128)(2,1)}, u32[]{:S(2)}) copy-start(bf16[128,192]{0,1:T(8,128)(2,1)} %param.3) | copy-start | bytes 147460
  89.8 83.8 %all-to-all-start = ((bf16[16,192,128]{2,1,0:T(8,128)(2,1)}), bf16[16,192,128]{2,1,0:T(8,128)(2,1)S(1)}, u32[]{:S(2)}, u32[]{:S(2)}) async-start(bf16[16,192,128]{2,1,0:T(8,128)(2,1)} %bitcast.1), calls=%async_computation | async-start | bytes 1572864 | tf_op jit(solution)/shard_map/all_to_all | solution.py:32
  96.9 16.4 %collective-permute-start = (bf16[128,192]{0,1:T(8,128)(2,1)S(1)}, bf16[128,192]{0,1:T(8,128)(2,1)S(1)}, u32[]{:S(2)}, u32[]{:S(2)}) collective-permute-start(bf16[128,192]{0,1:T(8,128)(2,1)S(1)} %copy-done), channel_id=1, source_target_pairs={{0,0},{1,16},{2,32},{3,48},{4,64},{5,80},{6,96},{7,112},{8,128},{9... | collective-permute-start | bytes 147464 | tf_op jit(solution)/shard_map/ppermute | solution.py:16
  178.5 15.7 %collective-permute-start.1 = (bf16[192,1536]{1,0:T(8,128)(2,1)S(1)}, bf16[192,1536]{1,0:T(8,128)(2,1)S(1)}, u32[]{:S(2)}, u32[]{:S(2)}) collective-permute-start(bf16[192,1536]{1,0:T(8,128)(2,1)S(1)} %fusion.1), channel_id=1, source_target_pairs={{0,256},{256,0},{1,257},{257,1},{2,258},{258,2},{3,259},{259,3},{4... | collective-permute-start | bytes 1769480 | tf_op jit(solution)/shard_map/ppermute | solution.py:41
Sparse Core Ops, SparseCore 0:
  10.1 65.0 all-gather.2
  81.7 51.2 all-gather.4

commit v2 on v1

v2 whole, which is shorter than its diff:
```python
import math

import jax
import jax.numpy as jnp
from jax import lax
from jax.sharding import PartitionSpec as P

ROWS = 16
COLS = 16
CHIPS = ROWS // 2
ROUNDS = CHIPS // 2
SLOTS = CHIPS
PARTS = 2


def held_from(chip, core, slot):
    steps = (slot + 1) // 2
    parity = core if slot % 2 or slot == 0 else 1 - core
    away = -steps if core == 0 else steps
    return 2 * ((chip + away) % CHIPS) + parity


def every_place():
    for chip in range(CHIPS):
        for core in range(2):
            for slot in range(SLOTS):
                for other in range(2):
                    yield chip, core, slot, other


def depth_moves():
    return [
        (
            (2 * chip + (core ^ other)) * COLS + held_from(chip, core, slot),
            (2 * chip + core) * COLS + 2 * slot + other,
        )
        for chip, core, slot, other in every_place()
    ]


def token_moves():
    return [
        (
            held_from(chip, core, slot) * COLS + 2 * chip + (core ^ other),
            (2 * chip + core) * COLS + 2 * slot + other,
        )
        for chip, core, slot, other in every_place()
    ]


def ring_moves(cross):
    moves = []
    for chip in range(CHIPS):
        moves.append((2 * chip + cross, 2 * ((chip + 1) % CHIPS)))
        moves.append((2 * chip + 1 - cross, 2 * ((chip - 1) % CHIPS) + 1))
    return moves


def ring(block):
    slots = [block]
    same = cross = block
    for step in range(1, ROUNDS + 1):
        same = lax.ppermute(same, "row", ring_moves(0))
        slots.append(same)
        if step < ROUNDS:
            cross = lax.ppermute(cross, "row", ring_moves(1 if step == 1 else 0))
            slots.append(cross)
    return slots


def to_other_core(value):
    return lax.ppermute(value, "row", [(row, row ^ 1) for row in range(ROWS)])


def to_all_cols(block):
    copies = jnp.broadcast_to(block[None], (COLS,) + block.shape)
    return lax.all_to_all(copies, "col", 0, 0, tiled=True)


def per_device(features, up_weight, out_grad):
    tokens, depth = features.shape
    hidden_units = up_weight.shape[1]
    features = features.T
    weights = ring(up_weight)
    by_depth = to_all_cols(lax.ppermute(features, ("row", "col"), depth_moves()))
    by_token = to_all_cols(lax.ppermute(features, ("row", "col"), token_moves()))

    both = 0.0
    for slot, weight in enumerate(weights):
        block = jnp.concatenate([by_depth[2 * slot], by_depth[2 * slot + 1]], axis=1)
        both += lax.dot_general(
            block, weight, (((0,), (0,)), ((), ())), preferred_element_type=jnp.float32
        )
    hidden = both[:tokens] + to_other_core(both[tokens:].astype(jnp.bfloat16)).astype(jnp.float32)
    normal_cdf = 0.5 * (1.0 + jax.scipy.special.erf(hidden / math.sqrt(2.0)))
    density = jnp.exp(-0.5 * hidden * hidden) / math.sqrt(2.0 * math.pi)
    gelu_out = (hidden * normal_cdf).astype(jnp.bfloat16)
    hidden_grad = (out_grad.astype(jnp.float32) * (normal_cdf + hidden * density)).astype(
        jnp.bfloat16
    )

    width = hidden_units // PARTS
    totals = []
    for part in range(PARTS):
        total = 0.0
        for slot, grad in enumerate(ring(hidden_grad[:, part * width : (part + 1) * width])):
            block = by_token[2 * slot : 2 * slot + 2].reshape(2 * depth, tokens)
            total += jnp.dot(block, grad, preferred_element_type=jnp.float32)
        totals.append(total)

    chip_grad = jnp.concatenate([hidden_grad, to_other_core(hidden_grad)], axis=0)
    pieces = []
    for weight in weights:
        piece = lax.dot_general(
            weight, chip_grad, (((1,), (1,)), ((), ())), preferred_element_type=jnp.float32
        ).astype(jnp.bfloat16)
        pieces += [piece[:, :tokens], piece[:, tokens:]]
    pieces = lax.all_to_all(jnp.stack(pieces), "col", 0, 0, tiled=True)
    feature_grad = jnp.sum(pieces.astype(jnp.float32), axis=0).astype(jnp.bfloat16)
    feature_grad = lax.ppermute(
        feature_grad, ("row", "col"), [(to, source) for source, to in depth_moves()]
    ).T

    weight_grad = []
    for total in totals:
        own = total[:depth] + to_other_core(total[depth:].astype(jnp.bfloat16)).astype(jnp.float32)
        own = own.astype(jnp.bfloat16)
        replica = lax.ppermute(own, "dp", [(0, 1), (1, 0)])
        weight_grad.append(own.astype(jnp.float32) + replica.astype(jnp.float32))
    return (gelu_out, feature_grad, jnp.concatenate(weight_grad, axis=1))


def solution(mesh):
    placed = (P(("dp", "row"), "col"), P("row", "col"), P(("dp", "row"), "col"))
    return jax.shard_map(
        per_device,
        mesh=mesh,
        in_specs=placed,
        out_specs=(P(("dp", "row"), "col"), P(("dp", "row"), "col"), P("row", "col")),
        check_vma=False,
    )
```

time: 202 us -> 231 us (1.14)
  the two profiles are of different devices: /device:TPU:128 before, /device:TPU:56 now
where the time goes in v2:
time: 231 us; the launch traced here: 230 us
  starting transfers between devices  121 us (52%)
  waiting for transfers between devices  66.6 us (29%)
  matrix products  23 us (10%)
  local copies, waits for them, and re-layouts  15.4 us (7%)
  other arithmetic  2.7 us (1%)
    ppermute x9, starting transfers between devices, ring(): cross = lax.ppermute(cross, 'row', ring_moves(1 if step == 1 else 0))  33.3 us
    ppermute x12, starting transfers between devices, ring(): same = lax.ppermute(same, 'row', ring_moves(0))  28 us
    ppermute x2, waiting for transfers between devices, per_device(): replica = lax.ppermute(own, 'dp', [(0, 1), (1, 0)])  24.1 us
    ppermute x12, waiting for transfers between devices, ring(): same = lax.ppermute(same, 'row', ring_moves(0))  22.4 us
    all_to_all x2, starting transfers between devices, to_all_cols(): return lax.all_to_all(copies, 'col', 0, 0, tiled=True)  14 us
    ppermute x9, waiting for transfers between devices, ring(): cross = lax.ppermute(cross, 'row', ring_moves(1 if step == 1 else 0))  13.1 us
    dot_general x16, matrix products, per_device(): total += jnp.dot(block, grad, preferred_element_type=jnp.float32)  12.3 us
    unnamed x50, local copies, waits for them, and re-layouts  11.8 us
  transfers between devices with their start and end apart: 33, of which 12 were waited for; matrix products, arithmetic and copies ran while one was open for 16% of the time, Pallas kernels for 0%

profile of v2, /device:TPU:56, one launch (start us, length us, event | category | flops | bytes accessed | tf_op | source)
XLA Modules:
  0.0 229.9 jit_solution(9854449749610540340)
XLA Ops:
  0.7 6.6 %collective-permute-start = (bf16[192,128]{1,0:T(8,128)(2,1)}, bf16[192,128]{1,0:T(8,128)(2,1)S(1)}, u32[]{:S(2)}, u32[]{:S(2)}) collective-permute-start(bf16[192,128]{1,0:T(8,128)(2,1)} %bitcast.189), channel_id=1, source_target_pairs={{0,0},{16,1},{14,2},{30,3},{15,4},{31,5},{12,6},{28,7},{13,8},{29,... | collective-permute-start | bytes 147464 | tf_op jit(solution)/shard_map/ppermute | solution.py:85
  7.3 2.3 %collective-permute-done = bf16[192,128]{1,0:T(8,128)(2,1)S(1)} collective-permute-done((bf16[192,128]{1,0:T(8,128)(2,1)}, bf16[192,128]{1,0:T(8,128)(2,1)S(1)}, u32[]{:S(2)}, u32[]{:S(2)}) %collective-permute-start) | collective-permute-done | bytes 49184 | tf_op jit(solution)/shard_map/ppermute | solution.py:85
  10.6 8.0 %all-to-all-start = ((bf16[16,192,128]{2,1,0:T(8,128)(2,1)}), bf16[16,192,128]{2,1,0:T(8,128)(2,1)S(1)}, u32[]{:S(2)}, u32[]{:S(2)}) async-start(bf16[16,192,128]{2,1,0:T(8,128)(2,1)} %broadcast_in_dim.4), calls=%async_computation | async-start | bytes 1572864 | tf_op jit(solution)/shard_map/all_to_all | solution.py:77
  18.7 8.6 %collective-permute-start.2 = (bf16[192,1536]{1,0:T(8,128)(2,1)S(1)}, bf16[192,1536]{1,0:T(8,128)(2,1)S(1)}, u32[]{:S(2)}, u32[]{:S(2)}) collective-permute-start(bf16[192,1536]{1,0:T(8,128)(2,1)S(1)} %copy-done.1), channel_id=1, source_target_pairs={{16,32},{0,240},{48,64},{32,16},{80,96},{64,48},{112,128},{96,80},... | collective-permute-start | bytes 1769480 | tf_op jit(solution)/shard_map/ppermute | solution.py:66
  29.2 10.4 %collective-permute-done.2 = bf16[192,1536]{1,0:T(8,128)(2,1)S(1)} collective-permute-done((bf16[192,1536]{1,0:T(8,128)(2,1)S(1)}, bf16[192,1536]{1,0:T(8,128)(2,1)S(1)}, u32[]{:S(2)}, u32[]{:S(2)}) %collective-permute-start.2) | collective-permute-done | bytes 589856 | tf_op jit(solution)/shard_map/ppermute | solution.py:66
  41.5 1.9 collective-permute-start.3
  43.5 7.0 %collective-permute-start.11 = (bf16[192,128]{1,0:T(8,128)(2,1)S(1)}, bf16[192,128]{1,0:T(8,128)(2,1)S(1)}, u32[]{:S(2)}, u32[]{:S(2)}) collective-permute-start(bf16[192,128]{1,0:T(8,128)(2,1)S(1)} %bitcast.190), channel_id=1, source_target_pairs={{0,0},{1,1},{224,2},{225,3},{240,4},{241,5},{192,6},{193,7},{208,8... | collective-permute-start | bytes 147464 | tf_op jit(solution)/shard_map/ppermute | solution.py:86
  50.5 2.7 %collective-permute-done.4 = bf16[192,1536]{1,0:T(8,128)(2,1)S(1)} collective-permute-done((bf16[192,1536]{1,0:T(8,128)(2,1)S(1)}, bf16[192,1536]{1,0:T(8,128)(2,1)S(1)}, u32[]{:S(2)}, u32[]{:S(2)}) %collective-permute-start.4) | collective-permute-done | bytes 589856 | tf_op jit(solution)/shard_map/ppermute | solution.py:66
  55.1 7.7 %collective-permute-done.3 = bf16[192,1536]{1,0:T(8,128)(2,1)} collective-permute-done((bf16[192,1536]{1,0:T(8,128)(2,1)S(1)}, bf16[192,1536]{1,0:T(8,128)(2,1)}, u32[]{:S(2)}, u32[]{:S(2)}) %collective-permute-start.3) | collective-permute-done | bytes 589856 | tf_op jit(solution)/shard_map/ppermute | solution.py:63
  65.8 6.0 %all-to-all-start.2 = ((bf16[16,192,128]{2,1,0:T(8,128)(2,1)}), bf16[16,192,128]{2,1,0:T(8,128)(2,1)S(1)}, u32[]{:S(2)}, u32[]{:S(2)}) async-start(bf16[16,192,128]{2,1,0:T(8,128)(2,1)} %broadcast_in_dim.5), calls=%async_computation.2 | async-start | bytes 1572864 | tf_op jit(solution)/shard_map/all_to_all | solution.py:77
  80.1 9.4 %collective-permute-done.7 = bf16[192,1536]{1,0:T(8,128)(2,1)S(1)} collective-permute-done((bf16[192,1536]{1,0:T(8,128)(2,1)}, bf16[192,1536]{1,0:T(8,128)(2,1)S(1)}, u32[]{:S(2)}, u32[]{:S(2)}) %collective-permute-start.7) | collective-permute-done | bytes 589856 | tf_op jit(solution)/shard_map/ppermute | solution.py:63
  90.3 2.2 collective-permute-start.8
  95.1 1.9 collective-permute-start.21
  97.8 3.7 %collective-permute-start.9 = (bf16[128,1536]{1,0:T(8,128)(2,1)S(1)}, bf16[128,1536]{1,0:T(8,128)(2,1)S(1)}, u32[]{:S(2)}, u32[]{:S(2)}) collective-permute-start(bf16[128,1536]{1,0:T(8,128)(2,1)S(1)} %get-tuple-element.3), channel_id=1, source_target_pairs={{0,16},{16,0},{32,48},{48,32},{64,80},{80,64},{96,112},{112,96},{1... | collective-permute-start | bytes 1179656 | tf_op jit(solution)/shard_map/ppermute | solution.py:72
  101.5 3.4 %collective-permute-start.22 = (bf16[128,768]{1,0:T(8,128)(2,1)S(1)}, bf16[128,768]{1,0:T(8,128)(2,1)}, u32[]{:S(2)}, u32[]{:S(2)}) collective-permute-start(bf16[128,768]{1,0:T(8,128)(2,1)S(1)} %get-tuple-element.30), channel_id=1, source_target_pairs={{16,32},{0,240},{48,64},{32,16},{80,96},{64,48},{112,128},{96,80},... | collective-permute-start | bytes 589832 | tf_op jit(solution)/shard_map/ppermute | solution.py:66
  104.9 3.4 %collective-permute-start.13 = (bf16[128,768]{1,0:T(8,128)(2,1)S(1)}, bf16[128,768]{1,0:T(8,128)(2,1)}, u32[]{:S(2)}, u32[]{:S(2)}) collective-permute-start(bf16[128,768]{1,0:T(8,128)(2,1)S(1)} %get-tuple-element.29), channel_id=1, source_target_pairs={{16,32},{0,240},{48,64},{32,16},{80,96},{64,48},{112,128},{96,80},... | collective-permute-start | bytes 589832 | tf_op jit(solution)/shard_map/ppermute | solution.py:66
  108.3 1.9 collective-permute-start.12
  110.3 4.0 %collective-permute-start.23 = (bf16[128,768]{1,0:T(8,128)(2,1)}, bf16[128,768]{1,0:T(8,128)(2,1)}, u32[]{:S(2)}, u32[]{:S(2)}) collective-permute-start(bf16[128,768]{1,0:T(8,128)(2,1)} %collective-permute-done.21), channel_id=1, source_target_pairs={{0,32},{16,240},{32,64},{48,16},{64,96},{80,48},{96,128},{112,80},... | collective-permute-start | bytes 589832 | tf_op jit(solution)/shard_map/ppermute | solution.py:63
  120.4 4.9 %collective-permute-start.24 = (bf16[128,768]{1,0:T(8,128)(2,1)}, bf16[128,768]{1,0:T(8,128)(2,1)}, u32[]{:S(2)}, u32[]{:S(2)}) collective-permute-start(bf16[128,768]{1,0:T(8,128)(2,1)} %collective-permute-done.22), channel_id=1, source_target_pairs={{0,32},{16,240},{32,64},{48,16},{64,96},{80,48},{96,128},{112,80},... | collective-permute-start | bytes 589832 | tf_op jit(solution)/shard_map/ppermute | solution.py:66
  125.5 1.9 collective-permute-start.15
  145.6 7.5 %all-to-all-start.1 = ((bf16[16,192,128]{2,1,0:T(8,128)(2,1)}), bf16[16,192,128]{2,1,0:T(8,128)(2,1)S(1)}, u32[]{:S(2)}, u32[]{:S(2)}) async-start(bf16[16,192,128]{2,1,0:T(8,128)(2,1)} %fusion.51), calls=%async_computation.1 | async-start | bytes 1572864 | tf_op jit(solution)/shard_map/all_to_all | solution.py:118
  153.1 5.4 %collective-permute-start.26 = (bf16[128,768]{1,0:T(8,128)(2,1)}, bf16[128,768]{1,0:T(8,128)(2,1)S(1)}, u32[]{:S(2)}, u32[]{:S(2)}) collective-permute-start(bf16[128,768]{1,0:T(8,128)(2,1)} %collective-permute-done.24), channel_id=1, source_target_pairs={{0,32},{16,240},{32,64},{48,16},{64,96},{80,48},{96,128},{112,80},... | collective-permute-start | bytes 589832 | tf_op jit(solution)/shard_map/ppermute | solution.py:66
  161.7 1.9 collective-permute-start.17
  164.9 1.9 collective-permute-start.16
  169.3 4.7 %collective-permute-start.27 = (bf16[128,768]{1,0:T(8,128)(2,1)S(1)}, bf16[128,768]{1,0:T(8,128)(2,1)S(1)}, u32[]{:S(2)}, u32[]{:S(2)}) collective-permute-start(bf16[128,768]{1,0:T(8,128)(2,1)S(1)} %collective-permute-done.25), channel_id=1, source_target_pairs={{0,32},{16,240},{32,64},{48,16},{64,96},{80,48},{96,128},{112,80},... | collective-permute-start | bytes 589832 | tf_op jit(solution)/shard_map/ppermute | solution.py:63
  180.4 3.1 %collective-permute-done.18 = bf16[128,768]{1,0:T(8,128)(2,1)S(1)} collective-permute-done((bf16[128,768]{1,0:T(8,128)(2,1)S(1)}, bf16[128,768]{1,0:T(8,128)(2,1)S(1)}, u32[]{:S(2)}, u32[]{:S(2)}) %collective-permute-start.18) | collective-permute-done | bytes 196640 | tf_op jit(solution)/shard_map/ppermute | solution.py:63
  185.8 3.9 %collective-permute-start.29 = (bf16[192,768]{1,0:T(8,128)(2,1)S(1)}, bf16[192,768]{1,0:T(8,128)(2,1)S(1)}, u32[]{:S(2)}, u32[]{:S(2)}) collective-permute-start(bf16[192,768]{1,0:T(8,128)(2,1)S(1)} %fusion.22), channel_id=1, source_target_pairs={{0,256},{256,0},{1,257},{257,1},{2,258},{258,2},{3,259},{259,3},{4... | collective-permute-start | bytes 884744 | tf_op jit(solution)/shard_map/ppermute | solution.py:128
  189.8 5.9 %collective-permute-start.20 = (bf16[192,768]{1,0:T(8,128)(2,1)S(1)}, bf16[192,768]{1,0:T(8,128)(2,1)S(1)}, u32[]{:S(2)}, u32[]{:S(2)}) collective-permute-start(bf16[192,768]{1,0:T(8,128)(2,1)S(1)} %fusion.23), channel_id=1, source_target_pairs={{0,256},{256,0},{1,257},{257,1},{2,258},{258,2},{3,259},{259,3},{4... | collective-permute-start | bytes 884744 | tf_op jit(solution)/shard_map/ppermute | solution.py:128
  195.6 17.4 %collective-permute-done.29 = bf16[192,768]{1,0:T(8,128)(2,1)S(1)} collective-permute-done((bf16[192,768]{1,0:T(8,128)(2,1)S(1)}, bf16[192,768]{1,0:T(8,128)(2,1)S(1)}, u32[]{:S(2)}, u32[]{:S(2)}) %collective-permute-start.29) | collective-permute-done | bytes 294944 | tf_op jit(solution)/shard_map/ppermute | solution.py:128
  213.1 6.7 %collective-permute-done.20 = bf16[192,768]{1,0:T(8,128)(2,1)S(1)} collective-permute-done((bf16[192,768]{1,0:T(8,128)(2,1)S(1)}, bf16[192,768]{1,0:T(8,128)(2,1)S(1)}, u32[]{:S(2)}, u32[]{:S(2)}) %collective-permute-start.20) | collective-permute-done | bytes 294944 | tf_op jit(solution)/shard_map/ppermute | solution.py:128
  220.0 4.8 %collective-permute-start.10 = (bf16[192,128]{1,0:T(8,128)(2,1)S(1)}, bf16[192,128]{1,0:T(8,128)(2,1)S(1)}, u32[]{:S(2)}, u32[]{:S(2)}) collective-permute-start(bf16[192,128]{1,0:T(8,128)(2,1)S(1)} %reduce_sum.12), channel_id=1, source_target_pairs={{0,0},{1,16},{2,14},{3,30},{4,15},{5,31},{6,12},{7,28},{8,13},{9,2... | collective-permute-start | bytes 147464 | tf_op jit(solution)/shard_map/ppermute | solution.py:120
  225.9 3.4 %collective-permute-done.10 = bf16[192,128]{1,0:T(8,128)(2,1)S(1)} collective-permute-done((bf16[192,128]{1,0:T(8,128)(2,1)S(1)}, bf16[192,128]{1,0:T(8,128)(2,1)S(1)}, u32[]{:S(2)}, u32[]{:S(2)}) %collective-permute-start.10) | collective-permute-done | bytes 49184 | tf_op jit(solution)/shard_map/ppermute | solution.py:120
  (132 shorter events, 63.8 us)
Async XLA Ops:
  0.7 9.0 %collective-permute-start = (bf16[192,128]{1,0:T(8,128)(2,1)}, bf16[192,128]{1,0:T(8,128)(2,1)S(1)}, u32[]{:S(2)}, u32[]{:S(2)}) collective-permute-start(bf16[192,128]{1,0:T(8,128)(2,1)} %bitcast.189), channel_id=1, source_target_pairs={{0,0},{16,1},{14,2},{30,3},{15,4},{31,5},{12,6},{28,7},{13,8},{29,... | collective-permute-start | bytes 147464 | tf_op jit(solution)/shard_map/ppermute | solution.py:85
  10.6 54.1 %all-to-all-start = ((bf16[16,192,128]{2,1,0:T(8,128)(2,1)}), bf16[16,192,128]{2,1,0:T(8,128)(2,1)S(1)}, u32[]{:S(2)}, u32[]{:S(2)}) async-start(bf16[16,192,128]{2,1,0:T(8,128)(2,1)} %broadcast_in_dim.4), calls=%async_computation | async-start | bytes 1572864 | tf_op jit(solution)/shard_map/all_to_all | solution.py:77
  18.7 20.9 %collective-permute-start.2 = (bf16[192,1536]{1,0:T(8,128)(2,1)S(1)}, bf16[192,1536]{1,0:T(8,128)(2,1)S(1)}, u32[]{:S(2)}, u32[]{:S(2)}) collective-permute-start(bf16[192,1536]{1,0:T(8,128)(2,1)S(1)} %copy-done.1), channel_id=1, source_target_pairs={{16,32},{0,240},{48,64},{32,16},{80,96},{64,48},{112,128},{96,80},... | collective-permute-start | bytes 1769480 | tf_op jit(solution)/shard_map/ppermute | solution.py:66
  27.3 14.2 %collective-permute-start.1 = (bf16[192,1536]{1,0:T(8,128)(2,1)S(1)}, bf16[192,1536]{1,0:T(8,128)(2,1)S(1)}, u32[]{:S(2)}, u32[]{:S(2)}) collective-permute-start(bf16[192,1536]{1,0:T(8,128)(2,1)S(1)} %copy-done.1), channel_id=1, source_target_pairs={{0,32},{16,240},{32,64},{48,16},{64,96},{80,48},{96,128},{112,80},... | collective-permute-start | bytes 1769480 | tf_op jit(solution)/shard_map/ppermute | solution.py:63
  39.6 13.6 %collective-permute-start.4 = (bf16[192,1536]{1,0:T(8,128)(2,1)S(1)}, bf16[192,1536]{1,0:T(8,128)(2,1)S(1)}, u32[]{:S(2)}, u32[]{:S(2)}) collective-permute-start(bf16[192,1536]{1,0:T(8,128)(2,1)S(1)} %collective-permute-done.2), channel_id=1, source_target_pairs={{0,32},{16,240},{32,64},{48,16},{64,96},{80,48},{96,128},{112,80},... | collective-permute-start | bytes 1769480 | tf_op jit(solution)/shard_map/ppermute | solution.py:66
  41.5 21.3 %collective-permute-start.3 = (bf16[192,1536]{1,0:T(8,128)(2,1)S(1)}, bf16[192,1536]{1,0:T(8,128)(2,1)}, u32[]{:S(2)}, u32[]{:S(2)}) collective-permute-start(bf16[192,1536]{1,0:T(8,128)(2,1)S(1)} %collective-permute-done.1), channel_id=1, source_target_pairs={{0,32},{16,240},{32,64},{48,16},{64,96},{80,48},{96,128},{112,80},... | collective-permute-start | bytes 1769480 | tf_op jit(solution)/shard_map/ppermute | solution.py:63
  43.5 21.3 %collective-permute-start.11 = (bf16[192,128]{1,0:T(8,128)(2,1)S(1)}, bf16[192,128]{1,0:T(8,128)(2,1)S(1)}, u32[]{:S(2)}, u32[]{:S(2)}) collective-permute-start(bf16[192,128]{1,0:T(8,128)(2,1)S(1)} %bitcast.190), channel_id=1, source_target_pairs={{0,0},{1,1},{224,2},{225,3},{240,4},{241,5},{192,6},{193,7},{208,8... | collective-permute-start | bytes 147464 | tf_op jit(solution)/shard_map/ppermute | solution.py:86
  53.2 25.0 %collective-permute-start.6 = (bf16[192,1536]{1,0:T(8,128)(2,1)S(1)}, bf16[192,1536]{1,0:T(8,128)(2,1)S(1)}, u32[]{:S(2)}, u32[]{:S(2)}) collective-permute-start(bf16[192,1536]{1,0:T(8,128)(2,1)S(1)} %collective-permute-done.4), channel_id=1, source_target_pairs={{0,32},{16,240},{32,64},{48,16},{64,96},{80,48},{96,128},{112,80},... | collective-permute-start | bytes 1769480 | tf_op jit(solution)/shard_map/ppermute | solution.py:66
  62.8 13.4 %collective-permute-start.5 = (bf16[192,1536]{1,0:T(8,128)(2,1)}, bf16[192,1536]{1,0:T(8,128)(2,1)}, u32[]{:S(2)}, u32[]{:S(2)}) collective-permute-start(bf16[192,1536]{1,0:T(8,128)(2,1)} %collective-permute-done.3), channel_id=1, source_target_pairs={{0,32},{16,240},{32,64},{48,16},{64,96},{80,48},{96,128},{112,80},... | collective-permute-start | bytes 1769480 | tf_op jit(solution)/shard_map/ppermute | solution.py:63
  65.8 31.3 %all-to-all-start.2 = ((bf16[16,192,128]{2,1,0:T(8,128)(2,1)}), bf16[16,192,128]{2,1,0:T(8,128)(2,1)S(1)}, u32[]{:S(2)}, u32[]{:S(2)}) async-start(bf16[16,192,128]{2,1,0:T(8,128)(2,1)} %broadcast_in_dim.5), calls=%async_computation.2 | async-start | bytes 1572864 | tf_op jit(solution)/shard_map/all_to_all | solution.py:77
  76.2 13.2 %collective-permute-start.7 = (bf16[192,1536]{1,0:T(8,128)(2,1)}, bf16[192,1536]{1,0:T(8,128)(2,1)S(1)}, u32[]{:S(2)}, u32[]{:S(2)}) collective-permute-start(bf16[192,1536]{1,0:T(8,128)(2,1)} %collective-permute-done.5), channel_id=1, source_target_pairs={{0,32},{16,240},{32,64},{48,16},{64,96},{80,48},{96,128},{112,80},... | collective-permute-start | bytes 1769480 | tf_op jit(solution)/shard_map/ppermute | solution.py:63
  95.1 15.1 %collective-permute-start.21 = (bf16[128,768]{1,0:T(8,128)(2,1)S(1)}, bf16[128,768]{1,0:T(8,128)(2,1)}, u32[]{:S(2)}, u32[]{:S(2)}) collective-permute-start(bf16[128,768]{1,0:T(8,128)(2,1)S(1)} %get-tuple-element.30), channel_id=1, source_target_pairs={{0,32},{16,240},{32,64},{48,16},{64,96},{80,48},{96,128},{112,80},... | collective-permute-start | bytes 589832 | tf_op jit(solution)/shard_map/ppermute | solution.py:63
  97.8 32.2 %collective-permute-start.9 = (bf16[128,1536]{1,0:T(8,128)(2,1)S(1)}, bf16[128,1536]{1,0:T(8,128)(2,1)S(1)}, u32[]{:S(2)}, u32[]{:S(2)}) collective-permute-start(bf16[128,1536]{1,0:T(8,128)(2,1)S(1)} %get-tuple-element.3), channel_id=1, source_target_pairs={{0,16},{16,0},{32,48},{48,32},{64,80},{80,64},{96,112},{112,96},{1... | collective-permute-start | bytes 1179656 | tf_op jit(solution)/shard_map/ppermute | solution.py:72
  101.5 18.8 %collective-permute-start.22 = (bf16[128,768]{1,0:T(8,128)(2,1)S(1)}, bf16[128,768]{1,0:T(8,128)(2,1)}, u32[]{:S(2)}, u32[]{:S(2)}) collective-permute-start(bf16[128,768]{1,0:T(8,128)(2,1)S(1)} %get-tuple-element.30), channel_id=1, source_target_pairs={{16,32},{0,240},{48,64},{32,16},{80,96},{64,48},{112,128},{96,80},... | collective-permute-start | bytes 589832 | tf_op jit(solution)/shard_map/ppermute | solution.py:66
  104.9 20.6 %collective-permute-start.13 = (bf16[128,768]{1,0:T(8,128)(2,1)S(1)}, bf16[128,768]{1,0:T(8,128)(2,1)}, u32[]{:S(2)}, u32[]{:S(2)}) collective-permute-start(bf16[128,768]{1,0:T(8,128)(2,1)S(1)} %get-tuple-element.29), channel_id=1, source_target_pairs={{16,32},{0,240},{48,64},{32,16},{80,96},{64,48},{112,128},{96,80},... | collective-permute-start | bytes 589832 | tf_op jit(solution)/shard_map/ppermute | solution.py:66
  108.3 8.9 %collective-permute-start.12 = (bf16[128,768]{1,0:T(8,128)(2,1)S(1)}, bf16[128,768]{1,0:T(8,128)(2,1)}, u32[]{:S(2)}, u32[]{:S(2)}) collective-permute-start(bf16[128,768]{1,0:T(8,128)(2,1)S(1)} %get-tuple-element.29), channel_id=1, source_target_pairs={{0,32},{16,240},{32,64},{48,16},{64,96},{80,48},{96,128},{112,80},... | collective-permute-start | bytes 589832 | tf_op jit(solution)/shard_map/ppermute | solution.py:63
  110.3 48.2 %collective-permute-start.23 = (bf16[128,768]{1,0:T(8,128)(2,1)}, bf16[128,768]{1,0:T(8,128)(2,1)}, u32[]{:S(2)}, u32[]{:S(2)}) collective-permute-start(bf16[128,768]{1,0:T(8,128)(2,1)} %collective-permute-done.21), channel_id=1, source_target_pairs={{0,32},{16,240},{32,64},{48,16},{64,96},{80,48},{96,128},{112,80},... | collective-permute-start | bytes 589832 | tf_op jit(solution)/shard_map/ppermute | solution.py:63
  117.2 47.7 %collective-permute-start.14 = (bf16[128,768]{1,0:T(8,128)(2,1)}, bf16[128,768]{1,0:T(8,128)(2,1)}, u32[]{:S(2)}, u32[]{:S(2)}) collective-permute-start(bf16[128,768]{1,0:T(8,128)(2,1)} %collective-permute-done.12), channel_id=1, source_target_pairs={{0,32},{16,240},{32,64},{48,16},{64,96},{80,48},{96,128},{112,80},... | collective-permute-start | bytes 589832 | tf_op jit(solution)/shard_map/ppermute | solution.py:63
  120.4 32.8 %collective-permute-start.24 = (bf16[128,768]{1,0:T(8,128)(2,1)}, bf16[128,768]{1,0:T(8,128)(2,1)}, u32[]{:S(2)}, u32[]{:S(2)}) collective-permute-start(bf16[128,768]{1,0:T(8,128)(2,1)} %collective-permute-done.22), channel_id=1, source_target_pairs={{0,32},{16,240},{32,64},{48,16},{64,96},{80,48},{96,128},{112,80},... | collective-permute-start | bytes 589832 | tf_op jit(solution)/shard_map/ppermute | solution.py:66
  125.5 36.2 %collective-permute-start.15 = (bf16[128,768]{1,0:T(8,128)(2,1)}, bf16[128,768]{1,0:T(8,128)(2,1)}, u32[]{:S(2)}, u32[]{:S(2)}) collective-permute-start(bf16[128,768]{1,0:T(8,128)(2,1)} %collective-permute-done.13), channel_id=1, source_target_pairs={{0,32},{16,240},{32,64},{48,16},{64,96},{80,48},{96,128},{112,80},... | collective-permute-start | bytes 589832 | tf_op jit(solution)/shard_map/ppermute | solution.py:66
  145.6 74.3 %all-to-all-start.1 = ((bf16[16,192,128]{2,1,0:T(8,128)(2,1)}), bf16[16,192,128]{2,1,0:T(8,128)(2,1)S(1)}, u32[]{:S(2)}, u32[]{:S(2)}) async-start(bf16[16,192,128]{2,1,0:T(8,128)(2,1)} %fusion.51), calls=%async_computation.1 | async-start | bytes 1572864 | tf_op jit(solution)/shard_map/all_to_all | solution.py:118
  153.1 21.0 %collective-permute-start.26 = (bf16[128,768]{1,0:T(8,128)(2,1)}, bf16[128,768]{1,0:T(8,128)(2,1)S(1)}, u32[]{:S(2)}, u32[]{:S(2)}) collective-permute-start(bf16[128,768]{1,0:T(8,128)(2,1)} %collective-permute-done.24), channel_id=1, source_target_pairs={{0,32},{16,240},{32,64},{48,16},{64,96},{80,48},{96,128},{112,80},... | collective-permute-start | bytes 589832 | tf_op jit(solution)/shard_map/ppermute | solution.py:66
  158.5 10.8 %collective-permute-start.25 = (bf16[128,768]{1,0:T(8,128)(2,1)}, bf16[128,768]{1,0:T(8,128)(2,1)S(1)}, u32[]{:S(2)}, u32[]{:S(2)}) collective-permute-start(bf16[128,768]{1,0:T(8,128)(2,1)} %collective-permute-done.23), channel_id=1, source_target_pairs={{0,32},{16,240},{32,64},{48,16},{64,96},{80,48},{96,128},{112,80},... | collective-permute-start | bytes 589832 | tf_op jit(solution)/shard_map/ppermute | solution.py:63
  161.7 12.7 %collective-permute-start.17 = (bf16[128,768]{1,0:T(8,128)(2,1)}, bf16[128,768]{1,0:T(8,128)(2,1)S(1)}, u32[]{:S(2)}, u32[]{:S(2)}) collective-permute-start(bf16[128,768]{1,0:T(8,128)(2,1)} %collective-permute-done.15), channel_id=1, source_target_pairs={{0,32},{16,240},{32,64},{48,16},{64,96},{80,48},{96,128},{112,80},... | collective-permute-start | bytes 589832 | tf_op jit(solution)/shard_map/ppermute | solution.py:66
  164.9 9.8 %collective-permute-start.16 = (bf16[128,768]{1,0:T(8,128)(2,1)}, bf16[128,768]{1,0:T(8,128)(2,1)S(1)}, u32[]{:S(2)}, u32[]{:S(2)}) collective-permute-start(bf16[128,768]{1,0:T(8,128)(2,1)} %collective-permute-done.14), channel_id=1, source_target_pairs={{0,32},{16,240},{32,64},{48,16},{64,96},{80,48},{96,128},{112,80},... | collective-permute-start | bytes 589832 | tf_op jit(solution)/shard_map/ppermute | solution.py:63
  169.3 8.8 %collective-permute-start.27 = (bf16[128,768]{1,0:T(8,128)(2,1)S(1)}, bf16[128,768]{1,0:T(8,128)(2,1)S(1)}, u32[]{:S(2)}, u32[]{:S(2)}) collective-permute-start(bf16[128,768]{1,0:T(8,128)(2,1)S(1)} %collective-permute-done.25), channel_id=1, source_target_pairs={{0,32},{16,240},{32,64},{48,16},{64,96},{80,48},{96,128},{112,80},... | collective-permute-start | bytes 589832 | tf_op jit(solution)/shard_map/ppermute | solution.py:63
  174.7 8.8 %collective-permute-start.18 = (bf16[128,768]{1,0:T(8,128)(2,1)S(1)}, bf16[128,768]{1,0:T(8,128)(2,1)S(1)}, u32[]{:S(2)}, u32[]{:S(2)}) collective-permute-start(bf16[128,768]{1,0:T(8,128)(2,1)S(1)} %collective-permute-done.16), channel_id=1, source_target_pairs={{0,32},{16,240},{32,64},{48,16},{64,96},{80,48},{96,128},{112,80},... | collective-permute-start | bytes 589832 | tf_op jit(solution)/shard_map/ppermute | solution.py:63
  178.4 7.3 %collective-permute-start.28 = (bf16[192,768]{1,0:T(8,128)(2,1)S(1)}, bf16[192,768]{1,0:T(8,128)(2,1)S(1)}, u32[]{:S(2)}, u32[]{:S(2)}) collective-permute-start(bf16[192,768]{1,0:T(8,128)(2,1)S(1)} %slice.340), channel_id=1, source_target_pairs={{0,16},{16,0},{32,48},{48,32},{64,80},{80,64},{96,112},{112,96},{1... | collective-permute-start | bytes 884744 | tf_op jit(solution)/shard_map/ppermute | solution.py:72
  183.8 5.9 %collective-permute-start.19 = (bf16[192,768]{1,0:T(8,128)(2,1)S(1)}, bf16[192,768]{1,0:T(8,128)(2,1)S(1)}, u32[]{:S(2)}, u32[]{:S(2)}) collective-permute-start(bf16[192,768]{1,0:T(8,128)(2,1)S(1)} %slice.341), channel_id=1, source_target_pairs={{0,16},{16,0},{32,48},{48,32},{64,80},{80,64},{96,112},{112,96},{1... | collective-permute-start | bytes 884744 | tf_op jit(solution)/shard_map/ppermute | solution.py:72
  185.8 27.2 %collective-permute-start.29 = (bf16[192,768]{1,0:T(8,128)(2,1)S(1)}, bf16[192,768]{1,0:T(8,128)(2,1)S(1)}, u32[]{:S(2)}, u32[]{:S(2)}) collective-permute-start(bf16[192,768]{1,0:T(8,128)(2,1)S(1)} %fusion.22), channel_id=1, source_target_pairs={{0,256},{256,0},{1,257},{257,1},{2,258},{258,2},{3,259},{259,3},{4... | collective-permute-start | bytes 884744 | tf_op jit(solution)/shard_map/ppermute | solution.py:128
  189.8 30.0 %collective-permute-start.20 = (bf16[192,768]{1,0:T(8,128)(2,1)S(1)}, bf16[192,768]{1,0:T(8,128)(2,1)S(1)}, u32[]{:S(2)}, u32[]{:S(2)}) collective-permute-start(bf16[192,768]{1,0:T(8,128)(2,1)S(1)} %fusion.23), channel_id=1, source_target_pairs={{0,256},{256,0},{1,257},{257,1},{2,258},{258,2},{3,259},{259,3},{4... | collective-permute-start | bytes 884744 | tf_op jit(solution)/shard_map/ppermute | solution.py:128
  220.0 9.3 %collective-permute-start.10 = (bf16[192,128]{1,0:T(8,128)(2,1)S(1)}, bf16[192,128]{1,0:T(8,128)(2,1)S(1)}, u32[]{:S(2)}, u32[]{:S(2)}) collective-permute-start(bf16[192,128]{1,0:T(8,128)(2,1)S(1)} %reduce_sum.12), channel_id=1, source_target_pairs={{0,0},{1,16},{2,14},{3,30},{4,15},{5,31},{6,12},{7,28},{8,13},{9,2... | collective-permute-start | bytes 147464 | tf_op jit(solution)/shard_map/ppermute | solution.py:120
  (18 other events, 161.6 us)

commit v3 on v2

--- a/solution.py
+++ b/solution.py
@@ -3,6 +3,8 @@
 import jax
 import jax.numpy as jnp
 from jax import lax
+from jax.experimental import pallas as pl
+from jax.experimental.pallas import tpu as pltpu
 from jax.sharding import PartitionSpec as P
 
 ROWS = 16
@@ -77,13 +79,51 @@
     return lax.all_to_all(copies, "col", 0, 0, tiled=True)
 
 
+def after(value, *others):
+    return lax.optimization_barrier((value,) + others)[0]
+
+
+def input_grad_kernel(grad_ref, *refs):
+    *weight_refs, pieces_ref = refs
+    tokens = pieces_ref.shape[2]
+    for slot, weight_ref in enumerate(weight_refs):
+        piece = lax.dot_general(
+            weight_ref[...],
+            grad_ref[...],
+            (((1,), (1,)), ((), ())),
+            preferred_element_type=jnp.float32,
+        ).astype(jnp.bfloat16)
+        pieces_ref[2 * slot] = piece[:, :tokens]
+        pieces_ref[2 * slot + 1] = piece[:, tokens:]
+
+
+def input_grad_pieces(chip_grad, weights):
+    depth, hidden_units = weights[0].shape
+    tokens = chip_grad.shape[0] // 2
+    moved = (SLOTS * depth * hidden_units + chip_grad.size + SLOTS * depth * 2 * tokens) * 2
+    return pl.pallas_call(
+        input_grad_kernel,
+        out_shape=jax.ShapeDtypeStruct((2 * SLOTS, depth, tokens), jnp.bfloat16),
+        in_specs=[pl.BlockSpec(memory_space=pltpu.VMEM)] * (1 + SLOTS),
+        out_specs=pl.BlockSpec(memory_space=pltpu.VMEM),
+        compiler_params=pltpu.CompilerParams(vmem_limit_bytes=16 * 2**20),
+        cost_estimate=pl.CostEstimate(
+            flops=4 * SLOTS * depth * hidden_units * tokens,
+            bytes_accessed=moved,
+            transcendentals=0,
+        ),
+    )(chip_grad, *weights)
+
+
 def per_device(features, up_weight, out_grad):
     tokens, depth = features.shape
     hidden_units = up_weight.shape[1]
     features = features.T
     weights = ring(up_weight)
-    by_depth = to_all_cols(lax.ppermute(features, ("row", "col"), depth_moves()))
-    by_token = to_all_cols(lax.ppermute(features, ("row", "col"), token_moves()))
+    by_depth = lax.ppermute(features, ("row", "col"), depth_moves())
+    by_token = lax.ppermute(features, ("row", "col"), token_moves())
+    by_depth = to_all_cols(after(by_depth, weights[1]))
+    by_token = to_all_cols(after(by_token, weights[3], by_depth))
 
     both = 0.0
     for slot, weight in enumerate(weights):
@@ -91,6 +131,7 @@
         both += lax.dot_general(
             block, weight, (((0,), (0,)), ((), ())), preferred_element_type=jnp.float32
         )
+    both = after(both, by_token)
     hidden = both[:tokens] + to_other_core(both[tokens:].astype(jnp.bfloat16)).astype(jnp.float32)
     normal_cdf = 0.5 * (1.0 + jax.scipy.special.erf(hidden / math.sqrt(2.0)))
     density = jnp.exp(-0.5 * hidden * hidden) / math.sqrt(2.0 * math.pi)
@@ -99,34 +140,28 @@
         jnp.bfloat16
     )
 
-    width = hidden_units // PARTS
-    totals = []
-    for part in range(PARTS):
-        total = 0.0
-        for slot, grad in enumerate(ring(hidden_grad[:, part * width : (part + 1) * width])):
-            block = by_token[2 * slot : 2 * slot + 2].reshape(2 * depth, tokens)
-            total += jnp.dot(block, grad, preferred_element_type=jnp.float32)
-        totals.append(total)
-
     chip_grad = jnp.concatenate([hidden_grad, to_other_core(hidden_grad)], axis=0)
-    pieces = []
-    for weight in weights:
-        piece = lax.dot_general(
-            weight, chip_grad, (((1,), (1,)), ((), ())), preferred_element_type=jnp.float32
-        ).astype(jnp.bfloat16)
-        pieces += [piece[:, :tokens], piece[:, tokens:]]
-    pieces = lax.all_to_all(jnp.stack(pieces), "col", 0, 0, tiled=True)
+    pieces = input_grad_pieces(chip_grad, weights)
+    pieces = lax.all_to_all(pieces, "col", 0, 0, tiled=True)
     feature_grad = jnp.sum(pieces.astype(jnp.float32), axis=0).astype(jnp.bfloat16)
     feature_grad = lax.ppermute(
         feature_grad, ("row", "col"), [(to, source) for source, to in depth_moves()]
-    ).T
+    )
 
+    total = 0.0
+    for slot, grad in enumerate(ring(hidden_grad)):
+        block = by_token[2 * slot : 2 * slot + 2].reshape(2 * depth, tokens)
+        total += jnp.dot(block, grad, preferred_element_type=jnp.float32)
+    total = after(total, pieces)
+    width = hidden_units // PARTS
     weight_grad = []
-    for total in totals:
-        own = total[:depth] + to_other_core(total[depth:].astype(jnp.bfloat16)).astype(jnp.float32)
-        own = own.astype(jnp.bfloat16)
+    for part in range(PARTS):
+        share = total[:, part * width : (part + 1) * width]
+        own = share[:depth] + to_other_core(share[depth:].astype(jnp.bfloat16)).astype(jnp.float32)
+        own = after(own.astype(jnp.bfloat16), feature_grad)
         replica = lax.ppermute(own, "dp", [(0, 1), (1, 0)])
         weight_grad.append(own.astype(jnp.float32) + replica.astype(jnp.float32))
+    feature_grad = feature_grad.T
     return (gelu_out, feature_grad, jnp.concatenate(weight_grad, axis=1))
 
 

time: 231 us -> 216 us (0.935); the launches traced: 230 us -> 213 us
  starting transfers between devices: 121 us -> 88.9 us
  waiting for transfers between devices: 66.6 us -> 88.4 us
  matrix products: 23 us -> 14.3 us
  local copies, waits for them, and re-layouts: 15.4 us -> 9.5 us
  Pallas kernels: 0 us -> 4.13 us
  other arithmetic: 2.7 us -> 6.2 us
    ppermute x9 -> x6, starting transfers between devices: 33.3 us -> 14.2 us  [ring(): cross = lax.ppermute(cross, 'row', ring_moves(1 if step == 1 else 0))]
    all_to_all x2, waiting for transfers between devices: 0.01 us -> 11.5 us  [to_all_cols(): return lax.all_to_all(copies, 'col', 0, 0, tiled=True)]
    unnamed x50 -> x23, local copies, waits for them, and re-layouts: 11.8 us -> 1.33 us
    ppermute x12 -> x8, waiting for transfers between devices: 22.4 us -> 32.9 us  [ring(): same = lax.ppermute(same, 'row', ring_moves(0))]
    ppermute x12 -> x8, starting transfers between devices: 28 us -> 19.1 us  [ring(): same = lax.ppermute(same, 'row', ring_moves(0))]
    dot_general x8 -> x0, matrix products: 5.48 us -> none  [per_device(): lax.dot_general(weight, chip_grad, (((1,), (1,)), ((), ())), preferred_el...]
    pallas_call x0 -> x1, Pallas kernels: none -> 4.13 us  [input_grad_pieces(): pl.pallas_call(input_grad_kernel, out_shape=jax.ShapeDtypeStruct((2 * SLO...]
    dot_general x16 -> x8, matrix products: 12.3 us -> 8.94 us  [per_device(): total += jnp.dot(block, grad, preferred_element_type=jnp.float32)]
  transfers between devices with their start and end apart: 33 -> 26, of which waited for: 12 -> 15; matrix products, arithmetic and copies ran while one was open for 16% -> 10% of each run, Pallas kernels for 0% -> 2%
where the time goes in v3:
time: 216 us; the launch traced here: 213 us
  starting transfers between devices  88.9 us (41%)
  waiting for transfers between devices  88.4 us (41%)
  matrix products  14.3 us (7%)
  local copies, waits for them, and re-layouts  9.5 us (4%)
  other arithmetic  6.2 us (3%)
  Pallas kernels  4.13 us (2%)
    ppermute x8, waiting for transfers between devices, ring(): same = lax.ppermute(same, 'row', ring_moves(0))  32.9 us
    ppermute x2, waiting for transfers between devices, per_device(): replica = lax.ppermute(own, 'dp', [(0, 1), (1, 0)])  20.8 us
    ppermute x8, starting transfers between devices, ring(): same = lax.ppermute(same, 'row', ring_moves(0))  19.1 us
    ppermute x6, waiting for transfers between devices, ring(): cross = lax.ppermute(cross, 'row', ring_moves(1 if step == 1 else 0))  16.2 us
    ppermute x6, starting transfers between devices, ring(): cross = lax.ppermute(cross, 'row', ring_moves(1 if step == 1 else 0))  14.2 us
    all_to_all x2, starting transfers between devices, to_all_cols(): return lax.all_to_all(copies, 'col', 0, 0, tiled=True)  13.6 us
    all_to_all x2, waiting for transfers between devices, to_all_cols(): return lax.all_to_all(copies, 'col', 0, 0, tiled=True)  11.5 us
    ppermute x2, starting transfers between devices, per_device(): replica = lax.ppermute(own, 'dp', [(0, 1), (1, 0)])  9.74 us
  transfers between devices with their start and end apart: 26, of which 15 were waited for; matrix products, arithmetic and copies ran while one was open for 10% of the time, Pallas kernels for 2%

profile of v3, /device:TPU:56, one launch (start us, length us, event | category | flops | bytes accessed | tf_op | source)
XLA Modules:
  0.0 212.5 jit_solution(4987576444177049177)
XLA Ops:
  0.6 4.4 %collective-permute-start.1 = (bf16[192,1536]{1,0:T(8,128)(2,1)}, bf16[192,1536]{1,0:T(8,128)(2,1)S(1)}, u32[]{:S(2)}, u32[]{:S(2)}) collective-permute-start(bf16[192,1536]{1,0:T(8,128)(2,1)} %refs_0_.1), channel_id=1, source_target_pairs={{0,32},{16,240},{32,64},{48,16},{64,96},{80,48},{96,128},{112,80},... | collective-permute-start | bytes 1769480 | tf_op jit(solution)/shard_map/ppermute | solution.py:65
  5.1 6.5 %collective-permute-start = (bf16[192,128]{1,0:T(8,128)(2,1)}, bf16[192,128]{1,0:T(8,128)(2,1)S(1)}, u32[]{:S(2)}, u32[]{:S(2)}) collective-permute-start(bf16[192,128]{1,0:T(8,128)(2,1)} %bitcast), channel_id=1, source_target_pairs={{0,0},{16,1},{14,2},{30,3},{15,4},{31,5},{12,6},{28,7},{13,8},{29,... | collective-permute-start | bytes 147464 | tf_op jit(solution)/shard_map/ppermute | solution.py:123
  13.6 6.2 %collective-permute-done.1.refs_1_ = bf16[192,1536]{1,0:T(8,128)(2,1)S(1)} collective-permute-done((bf16[192,1536]{1,0:T(8,128)(2,1)}, bf16[192,1536]{1,0:T(8,128)(2,1)S(1)}, u32[]{:S(2)}, u32[]{:S(2)}) %collective-permute-start.1) | collective-permute-done | bytes 589856 | tf_op jit(solution)/shard_map/ppermute | solution.py:65
  20.8 7.6 %all-to-all-start = ((bf16[16,192,128]{2,1,0:T(8,128)(2,1)}), bf16[16,192,128]{2,1,0:T(8,128)(2,1)}, u32[]{:S(2)}, u32[]{:S(2)}) async-start(bf16[16,192,128]{2,1,0:T(8,128)(2,1)} %broadcast_in_dim.4), calls=%async_computation | async-start | bytes 1572864 | tf_op jit(solution)/shard_map/all_to_all | solution.py:79
  28.4 2.9 %collective-permute-start.2 = (bf16[192,1536]{1,0:T(8,128)(2,1)S(1)}, bf16[192,1536]{1,0:T(8,128)(2,1)S(1)}, u32[]{:S(2)}, u32[]{:S(2)}) collective-permute-start(bf16[192,1536]{1,0:T(8,128)(2,1)S(1)} %copy-done), channel_id=1, source_target_pairs={{16,32},{0,240},{48,64},{32,16},{80,96},{64,48},{112,128},{96,80},... | collective-permute-start | bytes 1769480 | tf_op jit(solution)/shard_map/ppermute | solution.py:68
  33.2 10.4 %collective-permute-done.2.refs_2_ = bf16[192,1536]{1,0:T(8,128)(2,1)S(1)} collective-permute-done((bf16[192,1536]{1,0:T(8,128)(2,1)S(1)}, bf16[192,1536]{1,0:T(8,128)(2,1)S(1)}, u32[]{:S(2)}, u32[]{:S(2)}) %collective-permute-start.2) | collective-permute-done | bytes 589856 | tf_op jit(solution)/shard_map/ppermute | solution.py:68
  49.0 4.6 %collective-permute-start.8 = (bf16[192,128]{1,0:T(8,128)(2,1)}, bf16[192,128]{1,0:T(8,128)(2,1)}, u32[]{:S(2)}, u32[]{:S(2)}) collective-permute-start(bf16[192,128]{1,0:T(8,128)(2,1)} %bitcast), channel_id=1, source_target_pairs={{0,0},{1,1},{224,2},{225,3},{240,4},{241,5},{192,6},{193,7},{208,8... | collective-permute-start | bytes 147464 | tf_op jit(solution)/shard_map/ppermute | solution.py:124
  53.7 2.9 %collective-permute-done.4.refs_4_ = bf16[192,1536]{1,0:T(8,128)(2,1)S(1)} collective-permute-done((bf16[192,1536]{1,0:T(8,128)(2,1)S(1)}, bf16[192,1536]{1,0:T(8,128)(2,1)S(1)}, u32[]{:S(2)}, u32[]{:S(2)}) %collective-permute-start.4) | collective-permute-done | bytes 589856 | tf_op jit(solution)/shard_map/ppermute | solution.py:68
  58.5 7.6 %collective-permute-done.5.refs_5_ = bf16[192,1536]{1,0:T(8,128)(2,1)S(1)} collective-permute-done((bf16[192,1536]{1,0:T(8,128)(2,1)S(1)}, bf16[192,1536]{1,0:T(8,128)(2,1)S(1)}, u32[]{:S(2)}, u32[]{:S(2)}) %collective-permute-start.5) | collective-permute-done | bytes 589856 | tf_op jit(solution)/shard_map/ppermute | solution.py:65
  69.8 6.0 %all-to-all-start.1 = ((bf16[16,192,128]{2,1,0:T(8,128)(2,1)}), bf16[16,192,128]{2,1,0:T(8,128)(2,1)}, u32[]{:S(2)}, u32[]{:S(2)}) async-start(bf16[16,192,128]{2,1,0:T(8,128)(2,1)} %broadcast_in_dim.5), calls=%async_computation.1 | async-start | bytes 1572864 | tf_op jit(solution)/shard_map/all_to_all | solution.py:79
  80.5 2.6 %convolution_add_fusion.5 = f32[256,1536]{1,0:T(8,128)} fusion(f32[256,1536]{1,0:T(8,128)S(1)} %fusion.2, bf16[192,1536]{1,0:T(8,128)(2,1)} %collective-permute-done.7.refs_7_, bf16[192,128]{1,0:T(8,128)(2,1)S(1)} %get-tuple-element.30, bf16[192,128]{1,0:T(8,128)(2,1)S(1)} %get-tuple-element.29), kind=kOutput, calls=%fused_computation.7 | convolution fusion | flops 151584768 | bytes 3833856 | tf_op jit(solution)/shard_map/dot_general | solution.py:131
  83.1 11.5 %all-to-all-done.1 = bf16[16,192,128]{2,1,0:T(8,128)(2,1)} async-done(((bf16[16,192,128]{2,1,0:T(8,128)(2,1)}), bf16[16,192,128]{2,1,0:T(8,128)(2,1)}, u32[]{:S(2)}, u32[]{:S(2)}) %all-to-all-start.1) | async-done | bytes 786464 | tf_op jit(solution)/shard_map/all_to_all | solution.py:79
  95.8 2.8 %collective-permute-start.9 = (bf16[128,1536]{1,0:T(8,128)(2,1)S(1)}, bf16[128,1536]{1,0:T(8,128)(2,1)S(1)}, u32[]{:S(2)}, u32[]{:S(2)}) collective-permute-start(bf16[128,1536]{1,0:T(8,128)(2,1)S(1)} %slice.186), channel_id=1, source_target_pairs={{0,16},{16,0},{32,48},{48,32},{64,80},{80,64},{96,112},{112,96},{1... | collective-permute-start | bytes 1179656 | tf_op jit(solution)/shard_map/ppermute | solution.py:74
  99.9 2.6 %fusion.9 = (bf16[128,1536]{1,0:T(8,128)(2,1)}, bf16[128,1536]{1,0:T(8,128)(2,1)}) fusion(bf16[128,1536]{1,0:T(8,128)(2,1)} %param.5, bf16[128,1536]{1,0:T(8,128)(2,1)S(1)} %collective-permute-done.9, f32[256,1536]{1,0:T(8,128)} %convolution_add_fusion.5), kind=kLoop, calls=%fused_computation.21 | loop fusion | flops 2949120 | bytes 2359296 | tf_op jit(solution)/shard_map/convert_element_type | solution.py:139
  106.9 3.2 %collective-permute-start.13 = (bf16[128,1536]{1,0:T(8,128)(2,1)}, bf16[128,1536]{1,0:T(8,128)(2,1)}, u32[]{:S(2)}, u32[]{:S(2)}) collective-permute-start(bf16[128,1536]{1,0:T(8,128)(2,1)} %get-tuple-element.17), channel_id=1, source_target_pairs={{16,32},{0,240},{48,64},{32,16},{80,96},{64,48},{112,128},{96,80},... | collective-permute-start | bytes 1179656 | tf_op jit(solution)/shard_map/ppermute | solution.py:68
  110.1 2.3 %collective-permute-start.12 = (bf16[128,1536]{1,0:T(8,128)(2,1)}, bf16[128,1536]{1,0:T(8,128)(2,1)}, u32[]{:S(2)}, u32[]{:S(2)}) collective-permute-start(bf16[128,1536]{1,0:T(8,128)(2,1)} %get-tuple-element.17), channel_id=1, source_target_pairs={{0,32},{16,240},{32,64},{48,16},{64,96},{80,48},{96,128},{112,80},... | collective-permute-start | bytes 1179656 | tf_op jit(solution)/shard_map/ppermute | solution.py:65
  112.5 2.9 %fusion.47 = f32[384,1536]{1,0:T(8,128)} fusion(bf16[384,128]{1,0:T(8,128)(2,1)S(1)} %bitcast.68, bf16[128,1536]{1,0:T(8,128)(2,1)} %get-tuple-element.17), kind=kOutput, calls=%fused_computation.84 | convolution fusion | flops 150994944 | bytes 2850816 | tf_op jit(solution)/shard_map/dot_general | solution.py:154
  116.5 4.1 %shard_map.58 = bf16[16,192,128]{2,1,0:T(8,128)(2,1)} custom-call(bf16[256,1536]{1,0:T(8,128)(2,1)S(1)} %pad_maximum_fusion.1.grad_ref, bf16[192,1536]{1,0:T(8,128)(2,1)S(1)} %copy-done, bf16[192,1536]{1,0:T(8,128)(2,1)S(1)} %collective-permute-done.1.refs_1_, bf16[192,1536]{1,0:T(8,128)(2,1)S(1)} %copy-done.3, ...), custom_call_target="tpu_custom_call" | custom-call | flops 1207959552 | bytes 6291456 | tf_op jit(solution)/shard_map/pallas_call | solution.py:104
  120.6 7.2 %all-to-all-start.2 = ((bf16[16,192,128]{2,1,0:T(8,128)(2,1)}), bf16[16,192,128]{2,1,0:T(8,128)(2,1)S(1)}, u32[]{:S(2)}, u32[]{:S(2)}) async-start(bf16[16,192,128]{2,1,0:T(8,128)(2,1)} %shard_map.58), calls=%async_computation.2 | async-start | bytes 1572864 | tf_op jit(solution)/shard_map/all_to_all | solution.py:145
  129.7 2.4 %collective-permute-start.14 = (bf16[128,1536]{1,0:T(8,128)(2,1)}, bf16[128,1536]{1,0:T(8,128)(2,1)S(1)}, u32[]{:S(2)}, u32[]{:S(2)}) collective-permute-start(bf16[128,1536]{1,0:T(8,128)(2,1)} %collective-permute-done.12), channel_id=1, source_target_pairs={{0,32},{16,240},{32,64},{48,16},{64,96},{80,48},{96,128},{112,80},... | collective-permute-start | bytes 1179656 | tf_op jit(solution)/shard_map/ppermute | solution.py:65
  132.2 2.3 %convolution_add_fusion.4 = f32[384,1536]{1,0:T(8,128)S(1)} fusion(f32[384,1536]{1,0:T(8,128)} %fusion.47, bf16[384,128]{1,0:T(8,128)(2,1)S(1)} %bitcast.71, bf16[128,1536]{1,0:T(8,128)(2,1)} %collective-permute-done.12), kind=kOutput, calls=%fused_computation.6 | convolution fusion | flops 151584768 | bytes 5210112 | tf_op jit(solution)/shard_map/dot_general | solution.py:154
  136.0 2.9 %collective-permute-done.15 = bf16[128,1536]{1,0:T(8,128)(2,1)S(1)} collective-permute-done((bf16[128,1536]{1,0:T(8,128)(2,1)}, bf16[128,1536]{1,0:T(8,128)(2,1)S(1)}, u32[]{:S(2)}, u32[]{:S(2)}) %collective-permute-start.15) | collective-permute-done | bytes 393248 | tf_op jit(solution)/shard_map/ppermute | solution.py:68
  138.9 2.4 %collective-permute-start.17 = (bf16[128,1536]{1,0:T(8,128)(2,1)S(1)}, bf16[128,1536]{1,0:T(8,128)(2,1)S(1)}, u32[]{:S(2)}, u32[]{:S(2)}) collective-permute-start(bf16[128,1536]{1,0:T(8,128)(2,1)S(1)} %collective-permute-done.15), channel_id=1, source_target_pairs={{0,32},{16,240},{32,64},{48,16},{64,96},{80,48},{96,128},{112,80},... | collective-permute-start | bytes 1179656 | tf_op jit(solution)/shard_map/ppermute | solution.py:68
  145.8 8.1 %collective-permute-done.16 = bf16[128,1536]{1,0:T(8,128)(2,1)S(1)} collective-permute-done((bf16[128,1536]{1,0:T(8,128)(2,1)S(1)}, bf16[128,1536]{1,0:T(8,128)(2,1)S(1)}, u32[]{:S(2)}, u32[]{:S(2)}) %collective-permute-start.16) | collective-permute-done | bytes 393248 | tf_op jit(solution)/shard_map/ppermute | solution.py:65
  156.8 8.0 %collective-permute-done.18 = bf16[128,1536]{1,0:T(8,128)(2,1)S(1)} collective-permute-done((bf16[128,1536]{1,0:T(8,128)(2,1)S(1)}, bf16[128,1536]{1,0:T(8,128)(2,1)S(1)}, u32[]{:S(2)}, u32[]{:S(2)}) %collective-permute-start.18) | collective-permute-done | bytes 393248 | tf_op jit(solution)/shard_map/ppermute | solution.py:65
  168.2 2.4 %collective-permute-start.21 = (bf16[192,768]{1,0:T(8,128)(2,1)}, bf16[192,768]{1,0:T(8,128)(2,1)}, u32[]{:S(2)}, u32[]{:S(2)}) collective-permute-start(bf16[192,768]{1,0:T(8,128)(2,1)} %get-tuple-element.20), channel_id=1, source_target_pairs={{0,16},{16,0},{32,48},{48,32},{64,80},{80,64},{96,112},{112,96},{1... | collective-permute-start | bytes 884744 | tf_op jit(solution)/shard_map/ppermute | solution.py:74
  170.7 4.6 %collective-permute-start.11 = (bf16[192,128]{1,0:T(8,128)(2,1)S(1)}, bf16[192,128]{1,0:T(8,128)(2,1)S(1)}, u32[]{:S(2)}, u32[]{:S(2)}) collective-permute-start(bf16[192,128]{1,0:T(8,128)(2,1)S(1)} %reduce_sum.12), channel_id=1, source_target_pairs={{0,0},{1,16},{2,14},{3,30},{4,15},{5,31},{6,12},{7,28},{8,13},{9,2... | collective-permute-start | bytes 147464 | tf_op jit(solution)/shard_map/ppermute | solution.py:147
  176.4 3.6 %collective-permute-done.11 = bf16[192,128]{1,0:T(8,128)(2,1)S(1)} collective-permute-done((bf16[192,128]{1,0:T(8,128)(2,1)S(1)}, bf16[192,128]{1,0:T(8,128)(2,1)S(1)}, u32[]{:S(2)}, u32[]{:S(2)}) %collective-permute-start.11) | collective-permute-done | bytes 49184 | tf_op jit(solution)/shard_map/ppermute | solution.py:147
  180.0 4.8 %collective-permute-start.22 = (bf16[192,768]{1,0:T(8,128)(2,1)S(1)}, bf16[192,768]{1,0:T(8,128)(2,1)S(1)}, u32[]{:S(2)}, u32[]{:S(2)}) collective-permute-start(bf16[192,768]{1,0:T(8,128)(2,1)S(1)} %get-tuple-element.14), channel_id=1, source_target_pairs={{0,256},{256,0},{1,257},{257,1},{2,258},{258,2},{3,259},{259,3},{4... | collective-permute-start | bytes 884744 | tf_op jit(solution)/shard_map/ppermute | solution.py:162
  184.8 5.0 %collective-permute-start.20 = (bf16[192,768]{1,0:T(8,128)(2,1)S(1)}, bf16[192,768]{1,0:T(8,128)(2,1)S(1)}, u32[]{:S(2)}, u32[]{:S(2)}) collective-permute-start(bf16[192,768]{1,0:T(8,128)(2,1)S(1)} %get-tuple-element.13), channel_id=1, source_target_pairs={{0,256},{256,0},{1,257},{257,1},{2,258},{258,2},{3,259},{259,3},{4... | collective-permute-start | bytes 884744 | tf_op jit(solution)/shard_map/ppermute | solution.py:162
  189.8 14.7 %collective-permute-done.22 = bf16[192,768]{1,0:T(8,128)(2,1)S(1)} collective-permute-done((bf16[192,768]{1,0:T(8,128)(2,1)S(1)}, bf16[192,768]{1,0:T(8,128)(2,1)S(1)}, u32[]{:S(2)}, u32[]{:S(2)}) %collective-permute-start.22) | collective-permute-done | bytes 294944 | tf_op jit(solution)/shard_map/ppermute | solution.py:162
  204.6 6.1 %collective-permute-done.20 = bf16[192,768]{1,0:T(8,128)(2,1)S(1)} collective-permute-done((bf16[192,768]{1,0:T(8,128)(2,1)S(1)}, bf16[192,768]{1,0:T(8,128)(2,1)S(1)}, u32[]{:S(2)}, u32[]{:S(2)}) %collective-permute-start.20) | collective-permute-done | bytes 294944 | tf_op jit(solution)/shard_map/ppermute | solution.py:162
  (74 shorter events, 45.8 us)
Async XLA Ops:
  0.6 27.8 %copy-start = (bf16[192,1536]{1,0:T(8,128)(2,1)S(1)}, bf16[192,1536]{1,0:T(8,128)(2,1)}, u32[]{:S(2)}) copy-start(bf16[192,1536]{1,0:T(8,128)(2,1)} %refs_0_.1) | copy-start | bytes 1769476
  0.6 19.1 %collective-permute-start.1 = (bf16[192,1536]{1,0:T(8,128)(2,1)}, bf16[192,1536]{1,0:T(8,128)(2,1)S(1)}, u32[]{:S(2)}, u32[]{:S(2)}) collective-permute-start(bf16[192,1536]{1,0:T(8,128)(2,1)} %refs_0_.1), channel_id=1, source_target_pairs={{0,32},{16,240},{32,64},{48,16},{64,96},{80,48},{96,128},{112,80},... | collective-permute-start | bytes 1769480 | tf_op jit(solution)/shard_map/ppermute | solution.py:65
  5.1 8.6 %collective-permute-start = (bf16[192,128]{1,0:T(8,128)(2,1)}, bf16[192,128]{1,0:T(8,128)(2,1)S(1)}, u32[]{:S(2)}, u32[]{:S(2)}) collective-permute-start(bf16[192,128]{1,0:T(8,128)(2,1)} %bitcast), channel_id=1, source_target_pairs={{0,0},{16,1},{14,2},{30,3},{15,4},{31,5},{12,6},{28,7},{13,8},{29,... | collective-permute-start | bytes 147464 | tf_op jit(solution)/shard_map/ppermute | solution.py:123
  20.8 47.2 %all-to-all-start = ((bf16[16,192,128]{2,1,0:T(8,128)(2,1)}), bf16[16,192,128]{2,1,0:T(8,128)(2,1)}, u32[]{:S(2)}, u32[]{:S(2)}) async-start(bf16[16,192,128]{2,1,0:T(8,128)(2,1)} %broadcast_in_dim.4), calls=%async_computation | async-start | bytes 1572864 | tf_op jit(solution)/shard_map/all_to_all | solution.py:79
  28.4 15.2 %collective-permute-start.2 = (bf16[192,1536]{1,0:T(8,128)(2,1)S(1)}, bf16[192,1536]{1,0:T(8,128)(2,1)S(1)}, u32[]{:S(2)}, u32[]{:S(2)}) collective-permute-start(bf16[192,1536]{1,0:T(8,128)(2,1)S(1)} %copy-done), channel_id=1, source_target_pairs={{16,32},{0,240},{48,64},{32,16},{80,96},{64,48},{112,128},{96,80},... | collective-permute-start | bytes 1769480 | tf_op jit(solution)/shard_map/ppermute | solution.py:68
  31.3 15.8 %collective-permute-start.3 = (bf16[192,1536]{1,0:T(8,128)(2,1)S(1)}, bf16[192,1536]{1,0:T(8,128)(2,1)S(1)}, u32[]{:S(2)}, u32[]{:S(2)}) collective-permute-start(bf16[192,1536]{1,0:T(8,128)(2,1)S(1)} %collective-permute-done.1.refs_1_), channel_id=1, source_target_pairs={{0,32},{16,240},{32,64},{48,16},{64,96},{80,48},{96,128},{112,80},... | collective-permute-start | bytes 1769480 | tf_op jit(solution)/shard_map/ppermute | solution.py:65
  43.6 10.1 %copy-start.1 = (bf16[192,1536]{1,0:T(8,128)(2,1)}, bf16[192,1536]{1,0:T(8,128)(2,1)S(1)}, u32[]{:S(2)}) copy-start(bf16[192,1536]{1,0:T(8,128)(2,1)S(1)} %collective-permute-done.2.refs_2_) | copy-start | bytes 1769476
  43.6 13.0 %collective-permute-start.4 = (bf16[192,1536]{1,0:T(8,128)(2,1)S(1)}, bf16[192,1536]{1,0:T(8,128)(2,1)S(1)}, u32[]{:S(2)}, u32[]{:S(2)}) collective-permute-start(bf16[192,1536]{1,0:T(8,128)(2,1)S(1)} %collective-permute-done.2.refs_2_), channel_id=1, source_target_pairs={{0,32},{16,240},{32,64},{48,16},{64,96},{80,48},{96,128},{112,80},... | collective-permute-start | bytes 1769480 | tf_op jit(solution)/shard_map/ppermute | solution.py:68
  47.1 18.9 %collective-permute-start.5 = (bf16[192,1536]{1,0:T(8,128)(2,1)S(1)}, bf16[192,1536]{1,0:T(8,128)(2,1)S(1)}, u32[]{:S(2)}, u32[]{:S(2)}) collective-permute-start(bf16[192,1536]{1,0:T(8,128)(2,1)S(1)} %collective-permute-done.3.refs_3_), channel_id=1, source_target_pairs={{0,32},{16,240},{32,64},{48,16},{64,96},{80,48},{96,128},{112,80},... | collective-permute-start | bytes 1769480 | tf_op jit(solution)/shard_map/ppermute | solution.py:65
  49.0 18.9 %collective-permute-start.8 = (bf16[192,128]{1,0:T(8,128)(2,1)}, bf16[192,128]{1,0:T(8,128)(2,1)}, u32[]{:S(2)}, u32[]{:S(2)}) collective-permute-start(bf16[192,128]{1,0:T(8,128)(2,1)} %bitcast), channel_id=1, source_target_pairs={{0,0},{1,1},{224,2},{225,3},{240,4},{241,5},{192,6},{193,7},{208,8... | collective-permute-start | bytes 147464 | tf_op jit(solution)/shard_map/ppermute | solution.py:124
  56.6 23.1 %collective-permute-start.6 = (bf16[192,1536]{1,0:T(8,128)(2,1)S(1)}, bf16[192,1536]{1,0:T(8,128)(2,1)S(1)}, u32[]{:S(2)}, u32[]{:S(2)}) collective-permute-start(bf16[192,1536]{1,0:T(8,128)(2,1)S(1)} %collective-permute-done.4.refs_4_), channel_id=1, source_target_pairs={{0,32},{16,240},{32,64},{48,16},{64,96},{80,48},{96,128},{112,80},... | collective-permute-start | bytes 1769480 | tf_op jit(solution)/shard_map/ppermute | solution.py:68
  66.1 14.4 %collective-permute-start.7 = (bf16[192,1536]{1,0:T(8,128)(2,1)S(1)}, bf16[192,1536]{1,0:T(8,128)(2,1)}, u32[]{:S(2)}, u32[]{:S(2)}) collective-permute-start(bf16[192,1536]{1,0:T(8,128)(2,1)S(1)} %collective-permute-done.5.refs_5_), channel_id=1, source_target_pairs={{0,32},{16,240},{32,64},{48,16},{64,96},{80,48},{96,128},{112,80},... | collective-permute-start | bytes 1769480 | tf_op jit(solution)/shard_map/ppermute | solution.py:65
  69.8 24.8 %all-to-all-start.1 = ((bf16[16,192,128]{2,1,0:T(8,128)(2,1)}), bf16[16,192,128]{2,1,0:T(8,128)(2,1)}, u32[]{:S(2)}, u32[]{:S(2)}) async-start(bf16[16,192,128]{2,1,0:T(8,128)(2,1)} %broadcast_in_dim.5), calls=%async_computation.1 | async-start | bytes 1572864 | tf_op jit(solution)/shard_map/all_to_all | solution.py:79
  95.8 4.1 %collective-permute-start.9 = (bf16[128,1536]{1,0:T(8,128)(2,1)S(1)}, bf16[128,1536]{1,0:T(8,128)(2,1)S(1)}, u32[]{:S(2)}, u32[]{:S(2)}) collective-permute-start(bf16[128,1536]{1,0:T(8,128)(2,1)S(1)} %slice.186), channel_id=1, source_target_pairs={{0,16},{16,0},{32,48},{48,32},{64,80},{80,64},{96,112},{112,96},{1... | collective-permute-start | bytes 1179656 | tf_op jit(solution)/shard_map/ppermute | solution.py:74
  102.5 12.9 %collective-permute-start.10 = (bf16[128,1536]{1,0:T(8,128)(2,1)}, bf16[128,1536]{1,0:T(8,128)(2,1)S(1)}, u32[]{:S(2)}, u32[]{:S(2)}) collective-permute-start(bf16[128,1536]{1,0:T(8,128)(2,1)} %get-tuple-element.17), channel_id=1, source_target_pairs={{0,16},{16,0},{32,48},{48,32},{64,80},{80,64},{96,112},{112,96},{1... | collective-permute-start | bytes 1179656 | tf_op jit(solution)/shard_map/ppermute | solution.py:74
  106.9 20.9 %collective-permute-start.13 = (bf16[128,1536]{1,0:T(8,128)(2,1)}, bf16[128,1536]{1,0:T(8,128)(2,1)}, u32[]{:S(2)}, u32[]{:S(2)}) collective-permute-start(bf16[128,1536]{1,0:T(8,128)(2,1)} %get-tuple-element.17), channel_id=1, source_target_pairs={{16,32},{0,240},{48,64},{32,16},{80,96},{64,48},{112,128},{96,80},... | collective-permute-start | bytes 1179656 | tf_op jit(solution)/shard_map/ppermute | solution.py:68
  110.1 19.6 %collective-permute-start.12 = (bf16[128,1536]{1,0:T(8,128)(2,1)}, bf16[128,1536]{1,0:T(8,128)(2,1)}, u32[]{:S(2)}, u32[]{:S(2)}) collective-permute-start(bf16[128,1536]{1,0:T(8,128)(2,1)} %get-tuple-element.17), channel_id=1, source_target_pairs={{0,32},{16,240},{32,64},{48,16},{64,96},{80,48},{96,128},{112,80},... | collective-permute-start | bytes 1179656 | tf_op jit(solution)/shard_map/ppermute | solution.py:65
  120.6 11.6 %copy-start.8 = (bf16[2,192,128]{2,1,0:T(8,128)(2,1)S(1)}, bf16[2,192,128]{2,1,0:T(8,128)(2,1)}, u32[]{:S(2)}) copy-start(bf16[2,192,128]{2,1,0:T(8,128)(2,1)} %get-tuple-element.27) | copy-start | bytes 294916
  120.6 44.7 %all-to-all-start.2 = ((bf16[16,192,128]{2,1,0:T(8,128)(2,1)}), bf16[16,192,128]{2,1,0:T(8,128)(2,1)S(1)}, u32[]{:S(2)}, u32[]{:S(2)}) async-start(bf16[16,192,128]{2,1,0:T(8,128)(2,1)} %shard_map.58), calls=%async_computation.2 | async-start | bytes 1572864 | tf_op jit(solution)/shard_map/all_to_all | solution.py:145
  127.8 11.1 %collective-permute-start.15 = (bf16[128,1536]{1,0:T(8,128)(2,1)}, bf16[128,1536]{1,0:T(8,128)(2,1)S(1)}, u32[]{:S(2)}, u32[]{:S(2)}) collective-permute-start(bf16[128,1536]{1,0:T(8,128)(2,1)} %collective-permute-done.13), channel_id=1, source_target_pairs={{0,32},{16,240},{32,64},{48,16},{64,96},{80,48},{96,128},{112,80},... | collective-permute-start | bytes 1179656 | tf_op jit(solution)/shard_map/ppermute | solution.py:68
  129.7 13.4 %collective-permute-start.14 = (bf16[128,1536]{1,0:T(8,128)(2,1)}, bf16[128,1536]{1,0:T(8,128)(2,1)S(1)}, u32[]{:S(2)}, u32[]{:S(2)}) collective-permute-start(bf16[128,1536]{1,0:T(8,128)(2,1)} %collective-permute-done.12), channel_id=1, source_target_pairs={{0,32},{16,240},{32,64},{48,16},{64,96},{80,48},{96,128},{112,80},... | collective-permute-start | bytes 1179656 | tf_op jit(solution)/shard_map/ppermute | solution.py:65
  136.0 9.4 %copy-start.10 = (bf16[2,192,128]{2,1,0:T(8,128)(2,1)S(1)}, bf16[2,192,128]{2,1,0:T(8,128)(2,1)}, u32[]{:S(2)}) copy-start(bf16[2,192,128]{2,1,0:T(8,128)(2,1)} %get-tuple-element.25) | copy-start | bytes 294916
  138.9 17.0 %collective-permute-start.17 = (bf16[128,1536]{1,0:T(8,128)(2,1)S(1)}, bf16[128,1536]{1,0:T(8,128)(2,1)S(1)}, u32[]{:S(2)}, u32[]{:S(2)}) collective-permute-start(bf16[128,1536]{1,0:T(8,128)(2,1)S(1)} %collective-permute-done.15), channel_id=1, source_target_pairs={{0,32},{16,240},{32,64},{48,16},{64,96},{80,48},{96,128},{112,80},... | collective-permute-start | bytes 1179656 | tf_op jit(solution)/shard_map/ppermute | solution.py:68
  143.1 10.9 %collective-permute-start.16 = (bf16[128,1536]{1,0:T(8,128)(2,1)S(1)}, bf16[128,1536]{1,0:T(8,128)(2,1)S(1)}, u32[]{:S(2)}, u32[]{:S(2)}) collective-permute-start(bf16[128,1536]{1,0:T(8,128)(2,1)S(1)} %collective-permute-done.14), channel_id=1, source_target_pairs={{0,32},{16,240},{32,64},{48,16},{64,96},{80,48},{96,128},{112,80},... | collective-permute-start | bytes 1179656 | tf_op jit(solution)/shard_map/ppermute | solution.py:65
  145.3 10.5 %copy-start.4 = (bf16[2,192,128]{2,1,0:T(8,128)(2,1)S(1)}, bf16[2,192,128]{2,1,0:T(8,128)(2,1)}, u32[]{:S(2)}) copy-start(bf16[2,192,128]{2,1,0:T(8,128)(2,1)} %get-tuple-element.22) | copy-start | bytes 294916
  145.8 10.5 %copy-start.9 = (bf16[2,192,128]{2,1,0:T(8,128)(2,1)S(1)}, bf16[2,192,128]{2,1,0:T(8,128)(2,1)}, u32[]{:S(2)}) copy-start(bf16[2,192,128]{2,1,0:T(8,128)(2,1)} %get-tuple-element.23) | copy-start | bytes 294916
  154.0 10.9 %collective-permute-start.18 = (bf16[128,1536]{1,0:T(8,128)(2,1)S(1)}, bf16[128,1536]{1,0:T(8,128)(2,1)S(1)}, u32[]{:S(2)}, u32[]{:S(2)}) collective-permute-start(bf16[128,1536]{1,0:T(8,128)(2,1)S(1)} %collective-permute-done.16), channel_id=1, source_target_pairs={{0,32},{16,240},{32,64},{48,16},{64,96},{80,48},{96,128},{112,80},... | collective-permute-start | bytes 1179656 | tf_op jit(solution)/shard_map/ppermute | solution.py:65
  166.3 9.0 %collective-permute-start.19 = (bf16[192,768]{1,0:T(8,128)(2,1)}, bf16[192,768]{1,0:T(8,128)(2,1)S(1)}, u32[]{:S(2)}, u32[]{:S(2)}) collective-permute-start(bf16[192,768]{1,0:T(8,128)(2,1)} %get-tuple-element.19), channel_id=1, source_target_pairs={{0,16},{16,0},{32,48},{48,32},{64,80},{80,64},{96,112},{112,96},{1... | collective-permute-start | bytes 884744 | tf_op jit(solution)/shard_map/ppermute | solution.py:74
  168.2 7.1 %collective-permute-start.21 = (bf16[192,768]{1,0:T(8,128)(2,1)}, bf16[192,768]{1,0:T(8,128)(2,1)}, u32[]{:S(2)}, u32[]{:S(2)}) collective-permute-start(bf16[192,768]{1,0:T(8,128)(2,1)} %get-tuple-element.20), channel_id=1, source_target_pairs={{0,16},{16,0},{32,48},{48,32},{64,80},{80,64},{96,112},{112,96},{1... | collective-permute-start | bytes 884744 | tf_op jit(solution)/shard_map/ppermute | solution.py:74
  170.7 9.3 %collective-permute-start.11 = (bf16[192,128]{1,0:T(8,128)(2,1)S(1)}, bf16[192,128]{1,0:T(8,128)(2,1)S(1)}, u32[]{:S(2)}, u32[]{:S(2)}) collective-permute-start(bf16[192,128]{1,0:T(8,128)(2,1)S(1)} %reduce_sum.12), channel_id=1, source_target_pairs={{0,0},{1,16},{2,14},{3,30},{4,15},{5,31},{6,12},{7,28},{8,13},{9,2... | collective-permute-start | bytes 147464 | tf_op jit(solution)/shard_map/ppermute | solution.py:147
  180.0 24.5 %collective-permute-start.22 = (bf16[192,768]{1,0:T(8,128)(2,1)S(1)}, bf16[192,768]{1,0:T(8,128)(2,1)S(1)}, u32[]{:S(2)}, u32[]{:S(2)}) collective-permute-start(bf16[192,768]{1,0:T(8,128)(2,1)S(1)} %get-tuple-element.14), channel_id=1, source_target_pairs={{0,256},{256,0},{1,257},{257,1},{2,258},{258,2},{3,259},{259,3},{4... | collective-permute-start | bytes 884744 | tf_op jit(solution)/shard_map/ppermute | solution.py:162
  184.8 25.9 %collective-permute-start.20 = (bf16[192,768]{1,0:T(8,128)(2,1)S(1)}, bf16[192,768]{1,0:T(8,128)(2,1)S(1)}, u32[]{:S(2)}, u32[]{:S(2)}) collective-permute-start(bf16[192,768]{1,0:T(8,128)(2,1)S(1)} %get-tuple-element.13), channel_id=1, source_target_pairs={{0,256},{256,0},{1,257},{257,1},{2,258},{258,2},{3,259},{259,3},{4... | collective-permute-start | bytes 884744 | tf_op jit(solution)/shard_map/ppermute | solution.py:162
  (5 other events, 22.6 us)

commit v4 on v3

--- a/solution.py
+++ b/solution.py
@@ -12,7 +12,6 @@
 CHIPS = ROWS // 2
 ROUNDS = CHIPS // 2
 SLOTS = CHIPS
-PARTS = 2
 
 
 def held_from(chip, core, slot):
@@ -62,6 +61,8 @@
     slots = [block]
     same = cross = block
     for step in range(1, ROUNDS + 1):
+        if step == ROUNDS:
+            same = after(same, cross)
         same = lax.ppermute(same, "row", ring_moves(0))
         slots.append(same)
         if step < ROUNDS:
@@ -122,8 +123,8 @@
     weights = ring(up_weight)
     by_depth = lax.ppermute(features, ("row", "col"), depth_moves())
     by_token = lax.ppermute(features, ("row", "col"), token_moves())
-    by_depth = to_all_cols(after(by_depth, weights[1]))
-    by_token = to_all_cols(after(by_token, weights[3], by_depth))
+    by_depth = to_all_cols(by_depth)
+    by_token = to_all_cols(after(by_token, by_depth))
 
     both = 0.0
     for slot, weight in enumerate(weights):
@@ -131,7 +132,6 @@
         both += lax.dot_general(
             block, weight, (((0,), (0,)), ((), ())), preferred_element_type=jnp.float32
         )
-    both = after(both, by_token)
     hidden = both[:tokens] + to_other_core(both[tokens:].astype(jnp.bfloat16)).astype(jnp.float32)
     normal_cdf = 0.5 * (1.0 + jax.scipy.special.erf(hidden / math.sqrt(2.0)))
     density = jnp.exp(-0.5 * hidden * hidden) / math.sqrt(2.0 * math.pi)
@@ -140,8 +140,9 @@
         jnp.bfloat16
     )
 
+    grads = ring(hidden_grad)
     chip_grad = jnp.concatenate([hidden_grad, to_other_core(hidden_grad)], axis=0)
-    pieces = input_grad_pieces(chip_grad, weights)
+    pieces = input_grad_pieces(after(chip_grad, grads[1], grads[2]), weights)
     pieces = lax.all_to_all(pieces, "col", 0, 0, tiled=True)
     feature_grad = jnp.sum(pieces.astype(jnp.float32), axis=0).astype(jnp.bfloat16)
     feature_grad = lax.ppermute(
@@ -149,20 +150,16 @@
     )
 
     total = 0.0
-    for slot, grad in enumerate(ring(hidden_grad)):
+    for slot, grad in enumerate(grads):
         block = by_token[2 * slot : 2 * slot + 2].reshape(2 * depth, tokens)
         total += jnp.dot(block, grad, preferred_element_type=jnp.float32)
-    total = after(total, pieces)
-    width = hidden_units // PARTS
-    weight_grad = []
-    for part in range(PARTS):
-        share = total[:, part * width : (part + 1) * width]
-        own = share[:depth] + to_other_core(share[depth:].astype(jnp.bfloat16)).astype(jnp.float32)
-        own = after(own.astype(jnp.bfloat16), feature_grad)
-        replica = lax.ppermute(own, "dp", [(0, 1), (1, 0)])
-        weight_grad.append(own.astype(jnp.float32) + replica.astype(jnp.float32))
+    total = after(total, feature_grad)
+    own = total[:depth] + to_other_core(total[depth:].astype(jnp.bfloat16)).astype(jnp.float32)
+    own = own.astype(jnp.bfloat16)
+    replica = lax.ppermute(own, "dp", [(0, 1), (1, 0)])
+    weight_grad = own.astype(jnp.float32) + replica.astype(jnp.float32)
     feature_grad = feature_grad.T
-    return (gelu_out, feature_grad, jnp.concatenate(weight_grad, axis=1))
+    return (gelu_out, feature_grad, weight_grad)
 
 
 def solution(mesh):

time: 216 us -> 210 us (0.972)
  matrix products: 14.3 us -> 19.5 us
  waiting for transfers between devices: 88.4 us -> 84.8 us
  other arithmetic: 6.2 us -> 3.91 us
    all_to_all x2, waiting for transfers between devices: 11.5 us -> 0.01 us  [to_all_cols(): return lax.all_to_all(copies, 'col', 0, 0, tiled=True)]
    ppermute x6, waiting for transfers between devices: 16.2 us -> 7.38 us  [ring(): cross = lax.ppermute(cross, 'row', ring_moves(1 if step == 1 else 0))]
    ppermute x2 -> x1, waiting for transfers between devices: 20.8 us -> 28.8 us  [per_device(): replica = lax.ppermute(own, 'dp', [(0, 1), (1, 0)])]
    ppermute x8, waiting for transfers between devices: 32.9 us -> 40.9 us  [ring(): same = lax.ppermute(same, 'row', ring_moves(0))]
    ppermute x6, starting transfers between devices: 14.2 us -> 22.1 us  [ring(): cross = lax.ppermute(cross, 'row', ring_moves(1 if step == 1 else 0))]
    dot_general x8, matrix products: 8.94 us -> 16.4 us  [per_device(): total += jnp.dot(block, grad, preferred_element_type=jnp.float32)]
    ppermute x2 -> x1, starting transfers between devices: 9.74 us -> 4.97 us  [per_device(): replica = lax.ppermute(own, 'dp', [(0, 1), (1, 0)])]
    ppermute x1, starting transfers between devices: 4.63 us -> 1.92 us  [per_device(): by_token = lax.ppermute(features, ('row', 'col'), token_moves())]
  transfers between devices with their start and end apart: 26 -> 24, of which waited for: 15 -> 12; matrix products, arithmetic and copies ran while one was open for 10% -> 13% of each run, Pallas kernels for 2% -> 1%
where the time goes in v4:
time: 210 us; the launch traced here: 208 us
  starting transfers between devices  88.2 us (42%)
  waiting for transfers between devices  84.8 us (40%)
  matrix products  19.5 us (9%)
  local copies, waits for them, and re-layouts  7.57 us (4%)
  other arithmetic  3.91 us (2%)
  Pallas kernels  3.06 us (1%)
    ppermute x8, waiting for transfers between devices, ring(): same = lax.ppermute(same, 'row', ring_moves(0))  40.9 us
    ppermute x1, waiting for transfers between devices, per_device(): replica = lax.ppermute(own, 'dp', [(0, 1), (1, 0)])  28.8 us
    ppermute x6, starting transfers between devices, ring(): cross = lax.ppermute(cross, 'row', ring_moves(1 if step == 1 else 0))  22.1 us
    ppermute x8, starting transfers between devices, ring(): same = lax.ppermute(same, 'row', ring_moves(0))  19.3 us
    dot_general x8, matrix products, per_device(): total += jnp.dot(block, grad, preferred_element_type=jnp.float32)  16.4 us
    all_to_all x2, starting transfers between devices, to_all_cols(): return lax.all_to_all(copies, 'col', 0, 0, tiled=True)  14 us
    all_to_all x1, starting transfers between devices, per_device(): pieces = lax.all_to_all(pieces, 'col', 0, 0, tiled=True)  7.65 us
    ppermute x6, waiting for transfers between devices, ring(): cross = lax.ppermute(cross, 'row', ring_moves(1 if step == 1 else 0))  7.38 us
  transfers between devices with their start and end apart: 24, of which 12 were waited for; matrix products, arithmetic and copies ran while one was open for 13% of the time, Pallas kernels for 1%

profile of v4, /device:TPU:56, one launch (start us, length us, event | category | flops | bytes accessed | tf_op | source)
XLA Modules:
  0.0 208.2 jit_solution(13376344228985754600)
XLA Ops:
  0.6 6.6 %collective-permute-start = (bf16[192,128]{1,0:T(8,128)(2,1)}, bf16[192,128]{1,0:T(8,128)(2,1)S(1)}, u32[]{:S(2)}, u32[]{:S(2)}) collective-permute-start(bf16[192,128]{1,0:T(8,128)(2,1)} %bitcast), channel_id=1, source_target_pairs={{0,0},{16,1},{14,2},{30,3},{15,4},{31,5},{12,6},{28,7},{13,8},{29,... | collective-permute-start | bytes 147464 | tf_op jit(solution)/shard_map/ppermute | solution.py:124
  7.3 2.3 %collective-permute-done = bf16[192,128]{1,0:T(8,128)(2,1)S(1)} collective-permute-done((bf16[192,128]{1,0:T(8,128)(2,1)}, bf16[192,128]{1,0:T(8,128)(2,1)S(1)}, u32[]{:S(2)}, u32[]{:S(2)}) %collective-permute-start) | collective-permute-done | bytes 49184 | tf_op jit(solution)/shard_map/ppermute | solution.py:124
  10.6 8.0 %all-to-all-start = ((bf16[16,192,128]{2,1,0:T(8,128)(2,1)}), bf16[16,192,128]{2,1,0:T(8,128)(2,1)}, u32[]{:S(2)}, u32[]{:S(2)}) async-start(bf16[16,192,128]{2,1,0:T(8,128)(2,1)} %broadcast_in_dim.4), calls=%async_computation | async-start | bytes 1572864 | tf_op jit(solution)/shard_map/all_to_all | solution.py:80
  18.7 3.5 %collective-permute-start.1 = (bf16[192,1536]{1,0:T(8,128)(2,1)S(1)}, bf16[192,1536]{1,0:T(8,128)(2,1)S(1)}, u32[]{:S(2)}, u32[]{:S(2)}) collective-permute-start(bf16[192,1536]{1,0:T(8,128)(2,1)S(1)} %copy-done), channel_id=1, source_target_pairs={{0,32},{16,240},{32,64},{48,16},{64,96},{80,48},{96,128},{112,80},... | collective-permute-start | bytes 1769480 | tf_op jit(solution)/shard_map/ppermute | solution.py:66
  22.2 8.2 %collective-permute-start.2 = (bf16[192,1536]{1,0:T(8,128)(2,1)S(1)}, bf16[192,1536]{1,0:T(8,128)(2,1)S(1)}, u32[]{:S(2)}, u32[]{:S(2)}) collective-permute-start(bf16[192,1536]{1,0:T(8,128)(2,1)S(1)} %copy-done), channel_id=1, source_target_pairs={{16,32},{0,240},{48,64},{32,16},{80,96},{64,48},{112,128},{96,80},... | collective-permute-start | bytes 1769480 | tf_op jit(solution)/shard_map/ppermute | solution.py:69
  30.3 13.9 %collective-permute-done.1.refs_1_ = bf16[192,1536]{1,0:T(8,128)(2,1)S(1)} collective-permute-done((bf16[192,1536]{1,0:T(8,128)(2,1)S(1)}, bf16[192,1536]{1,0:T(8,128)(2,1)S(1)}, u32[]{:S(2)}, u32[]{:S(2)}) %collective-permute-start.1) | collective-permute-done | bytes 589856 | tf_op jit(solution)/shard_map/ppermute | solution.py:66
  48.1 1.9 collective-permute-start.13
  50.0 7.7 %collective-permute-done.3.refs_3_ = bf16[192,1536]{1,0:T(8,128)(2,1)S(1)} collective-permute-done((bf16[192,1536]{1,0:T(8,128)(2,1)S(1)}, bf16[192,1536]{1,0:T(8,128)(2,1)S(1)}, u32[]{:S(2)}, u32[]{:S(2)}) %collective-permute-start.3) | collective-permute-done | bytes 589856 | tf_op jit(solution)/shard_map/ppermute | solution.py:66
  59.7 7.0 %collective-permute-done.4.refs_4_ = bf16[192,1536]{1,0:T(8,128)(2,1)S(1)} collective-permute-done((bf16[192,1536]{1,0:T(8,128)(2,1)S(1)}, bf16[192,1536]{1,0:T(8,128)(2,1)S(1)}, u32[]{:S(2)}, u32[]{:S(2)}) %collective-permute-start.4) | collective-permute-done | bytes 589856 | tf_op jit(solution)/shard_map/ppermute | solution.py:69
  70.4 6.0 %all-to-all-start.2 = ((bf16[16,192,128]{2,1,0:T(8,128)(2,1)}), bf16[16,192,128]{2,1,0:T(8,128)(2,1)}, u32[]{:S(2)}, u32[]{:S(2)}) async-start(bf16[16,192,128]{2,1,0:T(8,128)(2,1)} %broadcast_in_dim.5), calls=%async_computation.2 | async-start | bytes 1572864 | tf_op jit(solution)/shard_map/all_to_all | solution.py:80
  82.7 10.2 %collective-permute-done.7.refs_7_ = bf16[192,1536]{1,0:T(8,128)(2,1)S(1)} collective-permute-done((bf16[192,1536]{1,0:T(8,128)(2,1)S(1)}, bf16[192,1536]{1,0:T(8,128)(2,1)S(1)}, u32[]{:S(2)}, u32[]{:S(2)}) %collective-permute-start.7) | collective-permute-done | bytes 589856 | tf_op jit(solution)/shard_map/ppermute | solution.py:66
  98.7 3.7 %collective-permute-start.11 = (bf16[128,1536]{1,0:T(8,128)(2,1)}, bf16[128,1536]{1,0:T(8,128)(2,1)}, u32[]{:S(2)}, u32[]{:S(2)}) collective-permute-start(bf16[128,1536]{1,0:T(8,128)(2,1)} %get-tuple-element.13), channel_id=1, source_target_pairs={{16,32},{0,240},{48,64},{32,16},{80,96},{64,48},{112,128},{96,80},... | collective-permute-start | bytes 1179656 | tf_op jit(solution)/shard_map/ppermute | solution.py:69
  102.4 1.9 collective-permute-start.10
  104.3 3.2 %collective-permute-start.9 = (bf16[128,1536]{1,0:T(8,128)(2,1)}, bf16[128,1536]{1,0:T(8,128)(2,1)}, u32[]{:S(2)}, u32[]{:S(2)}) collective-permute-start(bf16[128,1536]{1,0:T(8,128)(2,1)} %get-tuple-element.13), channel_id=1, source_target_pairs={{0,16},{16,0},{32,48},{48,32},{64,80},{80,64},{96,112},{112,96},{1... | collective-permute-start | bytes 1179656 | tf_op jit(solution)/shard_map/ppermute | solution.py:75
  107.5 2.1 fusion.48
  109.6 3.0 %fusion.49 = f32[384,1536]{1,0:T(8,128)} fusion(bf16[384,128]{1,0:T(8,128)(2,1)S(1)} %bitcast.70, bf16[128,1536]{1,0:T(8,128)(2,1)} %get-tuple-element.13), kind=kOutput, calls=%fused_computation.82 | convolution fusion | flops 150994944 | bytes 2850816 | tf_op jit(solution)/shard_map/dot_general | solution.py:155
  113.8 1.9 collective-permute-start.15
  115.7 1.9 collective-permute-start.14
  117.6 3.1 %shard_map.58 = bf16[16,192,128]{2,1,0:T(8,128)(2,1)} custom-call(bf16[256,1536]{1,0:T(8,128)(2,1)S(1)} %pad_maximum_fusion.grad_ref, bf16[192,1536]{1,0:T(8,128)(2,1)S(1)} %copy-done, bf16[192,1536]{1,0:T(8,128)(2,1)S(1)} %copy-done.2, bf16[192,1536]{1,0:T(8,128)(2,1)S(1)} %copy-done.5, bf16[192,1536]{1,0:T(8,128)(2,1)S(1)} %collective-permute-done.3.refs_3_, ...), custom_call_target="tpu_custom_call" | custom-call | flops 1207959552 | bytes 6291456 | tf_op jit(solution)/shard_map/pallas_call | solution.py:105
  120.7 7.7 %all-to-all-start.1 = ((bf16[16,192,128]{2,1,0:T(8,128)(2,1)}), bf16[16,192,128]{2,1,0:T(8,128)(2,1)S(1)}, u32[]{:S(2)}, u32[]{:S(2)}) async-start(bf16[16,192,128]{2,1,0:T(8,128)(2,1)} %shard_map.58), calls=%async_computation.1 | async-start | bytes 1572864 | tf_op jit(solution)/shard_map/all_to_all | solution.py:146
  128.4 2.3 %convolution_add_fusion.3 = f32[384,1536]{1,0:T(8,128)S(1)} fusion(f32[384,1536]{1,0:T(8,128)} %fusion.49, bf16[384,128]{1,0:T(8,128)(2,1)S(1)} %bitcast.72, bf16[128,1536]{1,0:T(8,128)(2,1)} %collective-permute-done.10), kind=kOutput, calls=%fused_computation.6 | convolution fusion | flops 151584768 | bytes 5210112 | tf_op jit(solution)/shard_map/dot_general | solution.py:155
  130.7 4.5 %collective-permute-start.17 = (bf16[128,1536]{1,0:T(8,128)(2,1)}, bf16[128,1536]{1,0:T(8,128)(2,1)S(1)}, u32[]{:S(2)}, u32[]{:S(2)}) collective-permute-start(bf16[128,1536]{1,0:T(8,128)(2,1)} %collective-permute-done.15), channel_id=1, source_target_pairs={{0,32},{16,240},{32,64},{48,16},{64,96},{80,48},{96,128},{112,80},... | collective-permute-start | bytes 1179656 | tf_op jit(solution)/shard_map/ppermute | solution.py:69
  135.2 3.2 %collective-permute-start.16 = (bf16[128,1536]{1,0:T(8,128)(2,1)}, bf16[128,1536]{1,0:T(8,128)(2,1)S(1)}, u32[]{:S(2)}, u32[]{:S(2)}) collective-permute-start(bf16[128,1536]{1,0:T(8,128)(2,1)} %collective-permute-done.14), channel_id=1, source_target_pairs={{0,32},{16,240},{32,64},{48,16},{64,96},{80,48},{96,128},{112,80},... | collective-permute-start | bytes 1179656 | tf_op jit(solution)/shard_map/ppermute | solution.py:66
  141.8 4.5 %collective-permute-done.16 = bf16[128,1536]{1,0:T(8,128)(2,1)S(1)} collective-permute-done((bf16[128,1536]{1,0:T(8,128)(2,1)}, bf16[128,1536]{1,0:T(8,128)(2,1)S(1)}, u32[]{:S(2)}, u32[]{:S(2)}) %collective-permute-start.16) | collective-permute-done | bytes 393248 | tf_op jit(solution)/shard_map/ppermute | solution.py:66
  146.3 3.0 %collective-permute-start.18 = (bf16[128,1536]{1,0:T(8,128)(2,1)S(1)}, bf16[128,1536]{1,0:T(8,128)(2,1)S(1)}, u32[]{:S(2)}, u32[]{:S(2)}) collective-permute-start(bf16[128,1536]{1,0:T(8,128)(2,1)S(1)} %collective-permute-done.16), channel_id=1, source_target_pairs={{0,32},{16,240},{32,64},{48,16},{64,96},{80,48},{96,128},{112,80},... | collective-permute-start | bytes 1179656 | tf_op jit(solution)/shard_map/ppermute | solution.py:66
  149.3 2.9 %fusion.2 = f32[384,1536]{1,0:T(8,128)} fusion(f32[384,1536]{1,0:T(8,128)S(1)} %fusion.50, f32[384,1536]{1,0:T(8,128)S(1)} %convolution_add_fusion.2, bf16[384,128]{1,0:T(8,128)(2,1)S(1)} %bitcast.73, bf16[128,1536]{1,0:T(8,128)(2,1)} %collective-permute-done.14), kind=kOutput, calls=%fused_computation.4 | convolution fusion | flops 152174592 | bytes 7569408 | tf_op jit(solution)/shard_map/dot_general | solution.py:155
  152.7 4.5 %collective-permute-done.18 = bf16[128,1536]{1,0:T(8,128)(2,1)S(1)} collective-permute-done((bf16[128,1536]{1,0:T(8,128)(2,1)S(1)}, bf16[128,1536]{1,0:T(8,128)(2,1)S(1)}, u32[]{:S(2)}, u32[]{:S(2)}) %collective-permute-start.18) | collective-permute-done | bytes 393248 | tf_op jit(solution)/shard_map/ppermute | solution.py:66
  159.2 4.6 %collective-permute-start.12 = (bf16[192,128]{1,0:T(8,128)(2,1)S(1)}, bf16[192,128]{1,0:T(8,128)(2,1)S(1)}, u32[]{:S(2)}, u32[]{:S(2)}) collective-permute-start(bf16[192,128]{1,0:T(8,128)(2,1)S(1)} %reduce_sum.12), channel_id=1, source_target_pairs={{0,0},{1,16},{2,14},{3,30},{4,15},{5,31},{6,12},{7,28},{8,13},{9,2... | collective-permute-start | bytes 147464 | tf_op jit(solution)/shard_map/ppermute | solution.py:148
  163.8 3.0 %fusion.1 = f32[384,1536]{1,0:T(8,128)S(1)} fusion(f32[384,1536]{1,0:T(8,128)} %fusion.52, f32[384,1536]{1,0:T(8,128)S(1)} %fusion.51, f32[384,1536]{1,0:T(8,128)} %fusion.2, bf16[384,128]{1,0:T(8,128)(2,1)S(1)} %bitcast.66, bf16[128,1536]{1,0:T(8,128)(2,1)} %copy-done.7), kind=kOutput, calls=%fused_computation.2 | convolution fusion | flops 152764416 | bytes 9928704 | tf_op jit(solution)/shard_map/dot_general | solution.py:155
  170.4 2.0 collective-permute-done.19
  172.6 5.0 %collective-permute-start.20 = (bf16[192,1536]{1,0:T(8,128)(2,1)S(1)}, bf16[192,1536]{1,0:T(8,128)(2,1)S(1)}, u32[]{:S(2)}, u32[]{:S(2)}) collective-permute-start(bf16[192,1536]{1,0:T(8,128)(2,1)S(1)} %add_convert_fusion), channel_id=1, source_target_pairs={{0,256},{256,0},{1,257},{257,1},{2,258},{258,2},{3,259},{259,3},{4... | collective-permute-start | bytes 1769480 | tf_op jit(solution)/shard_map/ppermute | solution.py:159
  177.5 28.8 %collective-permute-done.20 = bf16[192,1536]{1,0:T(8,128)(2,1)S(1)} collective-permute-done((bf16[192,1536]{1,0:T(8,128)(2,1)S(1)}, bf16[192,1536]{1,0:T(8,128)(2,1)S(1)}, u32[]{:S(2)}, u32[]{:S(2)}) %collective-permute-start.20) | collective-permute-done | bytes 589856 | tf_op jit(solution)/shard_map/ppermute | solution.py:159
  (75 shorter events, 35.0 us)
Async XLA Ops:
  0.6 18.0 %copy-start = (bf16[192,1536]{1,0:T(8,128)(2,1)S(1)}, bf16[192,1536]{1,0:T(8,128)(2,1)}, u32[]{:S(2)}) copy-start(bf16[192,1536]{1,0:T(8,128)(2,1)} %refs_0_.1) | copy-start | bytes 1769476
  0.6 9.0 %collective-permute-start = (bf16[192,128]{1,0:T(8,128)(2,1)}, bf16[192,128]{1,0:T(8,128)(2,1)S(1)}, u32[]{:S(2)}, u32[]{:S(2)}) collective-permute-start(bf16[192,128]{1,0:T(8,128)(2,1)} %bitcast), channel_id=1, source_target_pairs={{0,0},{16,1},{14,2},{30,3},{15,4},{31,5},{12,6},{28,7},{13,8},{29,... | collective-permute-start | bytes 147464 | tf_op jit(solution)/shard_map/ppermute | solution.py:124
  10.6 58.0 %all-to-all-start = ((bf16[16,192,128]{2,1,0:T(8,128)(2,1)}), bf16[16,192,128]{2,1,0:T(8,128)(2,1)}, u32[]{:S(2)}, u32[]{:S(2)}) async-start(bf16[16,192,128]{2,1,0:T(8,128)(2,1)} %broadcast_in_dim.4), calls=%async_computation | async-start | bytes 1572864 | tf_op jit(solution)/shard_map/all_to_all | solution.py:80
  18.7 25.6 %collective-permute-start.1 = (bf16[192,1536]{1,0:T(8,128)(2,1)S(1)}, bf16[192,1536]{1,0:T(8,128)(2,1)S(1)}, u32[]{:S(2)}, u32[]{:S(2)}) collective-permute-start(bf16[192,1536]{1,0:T(8,128)(2,1)S(1)} %copy-done), channel_id=1, source_target_pairs={{0,32},{16,240},{32,64},{48,16},{64,96},{80,48},{96,128},{112,80},... | collective-permute-start | bytes 1769480 | tf_op jit(solution)/shard_map/ppermute | solution.py:66
  22.2 24.0 %collective-permute-start.2 = (bf16[192,1536]{1,0:T(8,128)(2,1)S(1)}, bf16[192,1536]{1,0:T(8,128)(2,1)S(1)}, u32[]{:S(2)}, u32[]{:S(2)}) collective-permute-start(bf16[192,1536]{1,0:T(8,128)(2,1)S(1)} %copy-done), channel_id=1, source_target_pairs={{16,32},{0,240},{48,64},{32,16},{80,96},{64,48},{112,128},{96,80},... | collective-permute-start | bytes 1769480 | tf_op jit(solution)/shard_map/ppermute | solution.py:69
  44.2 33.8 %copy-start.1 = (bf16[192,1536]{1,0:T(8,128)(2,1)}, bf16[192,1536]{1,0:T(8,128)(2,1)S(1)}, u32[]{:S(2)}) copy-start(bf16[192,1536]{1,0:T(8,128)(2,1)S(1)} %collective-permute-done.1.refs_1_) | copy-start | bytes 1769476
  44.2 13.5 %collective-permute-start.3 = (bf16[192,1536]{1,0:T(8,128)(2,1)S(1)}, bf16[192,1536]{1,0:T(8,128)(2,1)S(1)}, u32[]{:S(2)}, u32[]{:S(2)}) collective-permute-start(bf16[192,1536]{1,0:T(8,128)(2,1)S(1)} %collective-permute-done.1.refs_1_), channel_id=1, source_target_pairs={{0,32},{16,240},{32,64},{48,16},{64,96},{80,48},{96,128},{112,80},... | collective-permute-start | bytes 1769480 | tf_op jit(solution)/shard_map/ppermute | solution.py:66
  46.1 13.5 %copy-start.3 = (bf16[192,1536]{1,0:T(8,128)(2,1)}, bf16[192,1536]{1,0:T(8,128)(2,1)S(1)}, u32[]{:S(2)}) copy-start(bf16[192,1536]{1,0:T(8,128)(2,1)S(1)} %collective-permute-done.2.refs_2_) | copy-start | bytes 1769476
  46.2 20.5 %collective-permute-start.4 = (bf16[192,1536]{1,0:T(8,128)(2,1)S(1)}, bf16[192,1536]{1,0:T(8,128)(2,1)S(1)}, u32[]{:S(2)}, u32[]{:S(2)}) collective-permute-start(bf16[192,1536]{1,0:T(8,128)(2,1)S(1)} %collective-permute-done.2.refs_2_), channel_id=1, source_target_pairs={{0,32},{16,240},{32,64},{48,16},{64,96},{80,48},{96,128},{112,80},... | collective-permute-start | bytes 1769480 | tf_op jit(solution)/shard_map/ppermute | solution.py:69
  48.1 20.5 %collective-permute-start.13 = (bf16[192,128]{1,0:T(8,128)(2,1)}, bf16[192,128]{1,0:T(8,128)(2,1)}, u32[]{:S(2)}, u32[]{:S(2)}) collective-permute-start(bf16[192,128]{1,0:T(8,128)(2,1)} %bitcast), channel_id=1, source_target_pairs={{0,0},{1,1},{224,2},{225,3},{240,4},{241,5},{192,6},{193,7},{208,8... | collective-permute-start | bytes 147464 | tf_op jit(solution)/shard_map/ppermute | solution.py:125
  57.7 22.2 %collective-permute-start.5 = (bf16[192,1536]{1,0:T(8,128)(2,1)S(1)}, bf16[192,1536]{1,0:T(8,128)(2,1)S(1)}, u32[]{:S(2)}, u32[]{:S(2)}) collective-permute-start(bf16[192,1536]{1,0:T(8,128)(2,1)S(1)} %collective-permute-done.3.refs_3_), channel_id=1, source_target_pairs={{0,32},{16,240},{32,64},{48,16},{64,96},{80,48},{96,128},{112,80},... | collective-permute-start | bytes 1769480 | tf_op jit(solution)/shard_map/ppermute | solution.py:66
  66.7 13.2 %collective-permute-start.6 = (bf16[192,1536]{1,0:T(8,128)(2,1)S(1)}, bf16[192,1536]{1,0:T(8,128)(2,1)S(1)}, u32[]{:S(2)}, u32[]{:S(2)}) collective-permute-start(bf16[192,1536]{1,0:T(8,128)(2,1)S(1)} %collective-permute-done.4.refs_4_), channel_id=1, source_target_pairs={{0,32},{16,240},{32,64},{48,16},{64,96},{80,48},{96,128},{112,80},... | collective-permute-start | bytes 1769480 | tf_op jit(solution)/shard_map/ppermute | solution.py:69
  70.4 37.1 %all-to-all-start.2 = ((bf16[16,192,128]{2,1,0:T(8,128)(2,1)}), bf16[16,192,128]{2,1,0:T(8,128)(2,1)}, u32[]{:S(2)}, u32[]{:S(2)}) async-start(bf16[16,192,128]{2,1,0:T(8,128)(2,1)} %broadcast_in_dim.5), calls=%async_computation.2 | async-start | bytes 1572864 | tf_op jit(solution)/shard_map/all_to_all | solution.py:80
  79.9 13.0 %collective-permute-start.7 = (bf16[192,1536]{1,0:T(8,128)(2,1)S(1)}, bf16[192,1536]{1,0:T(8,128)(2,1)S(1)}, u32[]{:S(2)}, u32[]{:S(2)}) collective-permute-start(bf16[192,1536]{1,0:T(8,128)(2,1)S(1)} %collective-permute-done.5.refs_5_), channel_id=1, source_target_pairs={{0,32},{16,240},{32,64},{48,16},{64,96},{80,48},{96,128},{112,80},... | collective-permute-start | bytes 1769480 | tf_op jit(solution)/shard_map/ppermute | solution.py:66
  93.8 3.6 %collective-permute-start.8 = (bf16[128,1536]{1,0:T(8,128)(2,1)S(1)}, bf16[128,1536]{1,0:T(8,128)(2,1)S(1)}, u32[]{:S(2)}, u32[]{:S(2)}) collective-permute-start(bf16[128,1536]{1,0:T(8,128)(2,1)S(1)} %slice.172), channel_id=1, source_target_pairs={{0,16},{16,0},{32,48},{48,32},{64,80},{80,64},{96,112},{112,96},{1... | collective-permute-start | bytes 1179656 | tf_op jit(solution)/shard_map/ppermute | solution.py:75
  98.7 15.0 %collective-permute-start.11 = (bf16[128,1536]{1,0:T(8,128)(2,1)}, bf16[128,1536]{1,0:T(8,128)(2,1)}, u32[]{:S(2)}, u32[]{:S(2)}) collective-permute-start(bf16[128,1536]{1,0:T(8,128)(2,1)} %get-tuple-element.13), channel_id=1, source_target_pairs={{16,32},{0,240},{48,64},{32,16},{80,96},{64,48},{112,128},{96,80},... | collective-permute-start | bytes 1179656 | tf_op jit(solution)/shard_map/ppermute | solution.py:69
  102.4 11.4 %collective-permute-start.10 = (bf16[128,1536]{1,0:T(8,128)(2,1)}, bf16[128,1536]{1,0:T(8,128)(2,1)}, u32[]{:S(2)}, u32[]{:S(2)}) collective-permute-start(bf16[128,1536]{1,0:T(8,128)(2,1)} %get-tuple-element.13), channel_id=1, source_target_pairs={{0,32},{16,240},{32,64},{48,16},{64,96},{80,48},{96,128},{112,80},... | collective-permute-start | bytes 1179656 | tf_op jit(solution)/shard_map/ppermute | solution.py:66
  104.3 8.3 %collective-permute-start.9 = (bf16[128,1536]{1,0:T(8,128)(2,1)}, bf16[128,1536]{1,0:T(8,128)(2,1)}, u32[]{:S(2)}, u32[]{:S(2)}) collective-permute-start(bf16[128,1536]{1,0:T(8,128)(2,1)} %get-tuple-element.13), channel_id=1, source_target_pairs={{0,16},{16,0},{32,48},{48,32},{64,80},{80,64},{96,112},{112,96},{1... | collective-permute-start | bytes 1179656 | tf_op jit(solution)/shard_map/ppermute | solution.py:75
  109.6 8.0 %copy-start.2 = (bf16[192,1536]{1,0:T(8,128)(2,1)S(1)}, bf16[192,1536]{1,0:T(8,128)(2,1)}, u32[]{:S(2)}) copy-start(bf16[192,1536]{1,0:T(8,128)(2,1)} %copy-done.1) | copy-start | bytes 1769476
  109.6 8.0 %copy-start.5 = (bf16[192,1536]{1,0:T(8,128)(2,1)S(1)}, bf16[192,1536]{1,0:T(8,128)(2,1)}, u32[]{:S(2)}) copy-start(bf16[192,1536]{1,0:T(8,128)(2,1)} %copy-done.3) | copy-start | bytes 1769476
  113.8 16.9 %collective-permute-start.15 = (bf16[128,1536]{1,0:T(8,128)(2,1)}, bf16[128,1536]{1,0:T(8,128)(2,1)}, u32[]{:S(2)}, u32[]{:S(2)}) collective-permute-start(bf16[128,1536]{1,0:T(8,128)(2,1)} %collective-permute-done.11), channel_id=1, source_target_pairs={{0,32},{16,240},{32,64},{48,16},{64,96},{80,48},{96,128},{112,80},... | collective-permute-start | bytes 1179656 | tf_op jit(solution)/shard_map/ppermute | solution.py:69
  115.7 19.5 %collective-permute-start.14 = (bf16[128,1536]{1,0:T(8,128)(2,1)}, bf16[128,1536]{1,0:T(8,128)(2,1)}, u32[]{:S(2)}, u32[]{:S(2)}) collective-permute-start(bf16[128,1536]{1,0:T(8,128)(2,1)} %collective-permute-done.10), channel_id=1, source_target_pairs={{0,32},{16,240},{32,64},{48,16},{64,96},{80,48},{96,128},{112,80},... | collective-permute-start | bytes 1179656 | tf_op jit(solution)/shard_map/ppermute | solution.py:66
  120.7 7.7 %copy-start.13 = (bf16[2,192,128]{2,1,0:T(8,128)(2,1)S(1)}, bf16[2,192,128]{2,1,0:T(8,128)(2,1)}, u32[]{:S(2)}) copy-start(bf16[2,192,128]{2,1,0:T(8,128)(2,1)} %get-tuple-element.21) | copy-start | bytes 294916
  120.7 38.4 %all-to-all-start.1 = ((bf16[16,192,128]{2,1,0:T(8,128)(2,1)}), bf16[16,192,128]{2,1,0:T(8,128)(2,1)S(1)}, u32[]{:S(2)}, u32[]{:S(2)}) async-start(bf16[16,192,128]{2,1,0:T(8,128)(2,1)} %shard_map.58), calls=%async_computation.1 | async-start | bytes 1572864 | tf_op jit(solution)/shard_map/all_to_all | solution.py:146
  128.4 10.0 %copy-start.12 = (bf16[2,192,128]{2,1,0:T(8,128)(2,1)S(1)}, bf16[2,192,128]{2,1,0:T(8,128)(2,1)}, u32[]{:S(2)}) copy-start(bf16[2,192,128]{2,1,0:T(8,128)(2,1)} %get-tuple-element.20) | copy-start | bytes 294916
  130.7 11.1 %collective-permute-start.17 = (bf16[128,1536]{1,0:T(8,128)(2,1)}, bf16[128,1536]{1,0:T(8,128)(2,1)S(1)}, u32[]{:S(2)}, u32[]{:S(2)}) collective-permute-start(bf16[128,1536]{1,0:T(8,128)(2,1)} %collective-permute-done.15), channel_id=1, source_target_pairs={{0,32},{16,240},{32,64},{48,16},{64,96},{80,48},{96,128},{112,80},... | collective-permute-start | bytes 1179656 | tf_op jit(solution)/shard_map/ppermute | solution.py:69
  135.2 11.1 %collective-permute-start.16 = (bf16[128,1536]{1,0:T(8,128)(2,1)}, bf16[128,1536]{1,0:T(8,128)(2,1)S(1)}, u32[]{:S(2)}, u32[]{:S(2)}) collective-permute-start(bf16[128,1536]{1,0:T(8,128)(2,1)} %collective-permute-done.14), channel_id=1, source_target_pairs={{0,32},{16,240},{32,64},{48,16},{64,96},{80,48},{96,128},{112,80},... | collective-permute-start | bytes 1179656 | tf_op jit(solution)/shard_map/ppermute | solution.py:66
  139.9 9.4 %copy-start.14 = (bf16[2,192,128]{2,1,0:T(8,128)(2,1)S(1)}, bf16[2,192,128]{2,1,0:T(8,128)(2,1)}, u32[]{:S(2)}) copy-start(bf16[2,192,128]{2,1,0:T(8,128)(2,1)} %get-tuple-element.19) | copy-start | bytes 294916
  146.3 10.9 %collective-permute-start.18 = (bf16[128,1536]{1,0:T(8,128)(2,1)S(1)}, bf16[128,1536]{1,0:T(8,128)(2,1)S(1)}, u32[]{:S(2)}, u32[]{:S(2)}) collective-permute-start(bf16[128,1536]{1,0:T(8,128)(2,1)S(1)} %collective-permute-done.16), channel_id=1, source_target_pairs={{0,32},{16,240},{32,64},{48,16},{64,96},{80,48},{96,128},{112,80},... | collective-permute-start | bytes 1179656 | tf_op jit(solution)/shard_map/ppermute | solution.py:66
  159.2 9.3 %collective-permute-start.12 = (bf16[192,128]{1,0:T(8,128)(2,1)S(1)}, bf16[192,128]{1,0:T(8,128)(2,1)S(1)}, u32[]{:S(2)}, u32[]{:S(2)}) collective-permute-start(bf16[192,128]{1,0:T(8,128)(2,1)S(1)} %reduce_sum.12), channel_id=1, source_target_pairs={{0,0},{1,16},{2,14},{3,30},{4,15},{5,31},{6,12},{7,28},{8,13},{9,2... | collective-permute-start | bytes 147464 | tf_op jit(solution)/shard_map/ppermute | solution.py:148
  168.5 3.9 %collective-permute-start.19 = (bf16[192,1536]{1,0:T(8,128)(2,1)S(1)}, bf16[192,1536]{1,0:T(8,128)(2,1)S(1)}, u32[]{:S(2)}, u32[]{:S(2)}) collective-permute-start(bf16[192,1536]{1,0:T(8,128)(2,1)S(1)} %slice.171), channel_id=1, source_target_pairs={{0,16},{16,0},{32,48},{48,32},{64,80},{80,64},{96,112},{112,96},{1... | collective-permute-start | bytes 1769480 | tf_op jit(solution)/shard_map/ppermute | solution.py:75
  172.6 33.8 %collective-permute-start.20 = (bf16[192,1536]{1,0:T(8,128)(2,1)S(1)}, bf16[192,1536]{1,0:T(8,128)(2,1)S(1)}, u32[]{:S(2)}, u32[]{:S(2)}) collective-permute-start(bf16[192,1536]{1,0:T(8,128)(2,1)S(1)} %add_convert_fusion), channel_id=1, source_target_pairs={{0,256},{256,0},{1,257},{257,1},{2,258},{258,2},{3,259},{259,3},{4... | collective-permute-start | bytes 1769480 | tf_op jit(solution)/shard_map/ppermute | solution.py:159
  (7 other events, 27.1 us)

commit v5 on v4

--- a/solution.py
+++ b/solution.py
@@ -1,3 +1,4 @@
+import functools
 import math
 
 import jax
@@ -12,6 +13,7 @@
 CHIPS = ROWS // 2
 ROUNDS = CHIPS // 2
 SLOTS = CHIPS
+LANES = 256
 
 
 def held_from(chip, core, slot):
@@ -84,28 +86,26 @@
     return lax.optimization_barrier((value,) + others)[0]
 
 
-def input_grad_kernel(grad_ref, *refs):
+def input_grad_kernel(own_ref, other_ref, *refs):
     *weight_refs, pieces_ref = refs
-    tokens = pieces_ref.shape[2]
     for slot, weight_ref in enumerate(weight_refs):
-        piece = lax.dot_general(
-            weight_ref[...],
-            grad_ref[...],
-            (((1,), (1,)), ((), ())),
-            preferred_element_type=jnp.float32,
-        ).astype(jnp.bfloat16)
-        pieces_ref[2 * slot] = piece[:, :tokens]
-        pieces_ref[2 * slot + 1] = piece[:, tokens:]
-
-
-def input_grad_pieces(chip_grad, weights):
+        for half, grad_ref in enumerate((own_ref, other_ref)):
+            pieces_ref[2 * slot + half] = lax.dot_general(
+                weight_ref[...],
+                grad_ref[...],
+                (((1,), (1,)), ((), ())),
+                preferred_element_type=jnp.float32,
+            ).astype(jnp.bfloat16)
+
+
+def input_grad_pieces(own, other, weights):
     depth, hidden_units = weights[0].shape
-    tokens = chip_grad.shape[0] // 2
-    moved = (SLOTS * depth * hidden_units + chip_grad.size + SLOTS * depth * 2 * tokens) * 2
+    tokens = own.shape[0]
+    moved = (SLOTS * depth * hidden_units + 2 * own.size + SLOTS * depth * 2 * tokens) * 2
     return pl.pallas_call(
         input_grad_kernel,
         out_shape=jax.ShapeDtypeStruct((2 * SLOTS, depth, tokens), jnp.bfloat16),
-        in_specs=[pl.BlockSpec(memory_space=pltpu.VMEM)] * (1 + SLOTS),
+        in_specs=[pl.BlockSpec(memory_space=pltpu.VMEM)] * (2 + SLOTS),
         out_specs=pl.BlockSpec(memory_space=pltpu.VMEM),
         compiler_params=pltpu.CompilerParams(vmem_limit_bytes=16 * 2**20),
         cost_estimate=pl.CostEstimate(
@@ -113,7 +113,45 @@
             bytes_accessed=moved,
             transcendentals=0,
         ),
-    )(chip_grad, *weights)
+    )(own, other, *weights)
+
+
+def token_sum_kernel(slots, first, block_ref, *refs):
+    grad_refs = refs[: len(slots)]
+    before = None if first else refs[len(slots) : len(slots) + 2]
+    outs = refs[-2:]
+    hidden_units = grad_refs[0].shape[1]
+    for half in range(2):
+        for start in range(0, hidden_units, LANES):
+            units = pl.ds(start, LANES)
+            total = None if first else before[half][:, units]
+            for slot, grad_ref in zip(slots, grad_refs):
+                term = jnp.dot(
+                    block_ref[2 * slot + half],
+                    grad_ref[:, units],
+                    preferred_element_type=jnp.float32,
+                )
+                total = term if total is None else total + term
+            outs[half][:, units] = total.astype(outs[half].dtype)
+
+
+def token_sum(slots, blocks, grads, before, kinds):
+    depth, tokens = blocks.shape[1:]
+    hidden_units = grads[0].shape[1]
+    operands = (blocks, *grads, *before)
+    return pl.pallas_call(
+        functools.partial(token_sum_kernel, slots, not before),
+        out_shape=[jax.ShapeDtypeStruct((depth, hidden_units), kind) for kind in kinds],
+        in_specs=[pl.BlockSpec(memory_space=pltpu.VMEM)] * len(operands),
+        out_specs=[pl.BlockSpec(memory_space=pltpu.VMEM)] * 2,
+        compiler_params=pltpu.CompilerParams(vmem_limit_bytes=16 * 2**20),
+        cost_estimate=pl.CostEstimate(
+            flops=4 * len(slots) * depth * hidden_units * tokens,
+            bytes_accessed=2 * (blocks.size + len(slots) * tokens * hidden_units)
+            + 4 * 2 * depth * hidden_units,
+            transcendentals=0,
+        ),
+    )(*operands)
 
 
 def per_device(features, up_weight, out_grad):
@@ -123,8 +161,9 @@
     weights = ring(up_weight)
     by_depth = lax.ppermute(features, ("row", "col"), depth_moves())
     by_token = lax.ppermute(features, ("row", "col"), token_moves())
-    by_depth = to_all_cols(by_depth)
-    by_token = to_all_cols(after(by_token, by_depth))
+    both_ways = jnp.concatenate([by_depth, by_token], axis=0)
+    both_ways = to_all_cols(after(both_ways, weights[1]))
+    by_depth, by_token = both_ways[:, :depth], both_ways[:, depth:]
 
     both = 0.0
     for slot, weight in enumerate(weights):
@@ -141,21 +180,22 @@
     )
 
     grads = ring(hidden_grad)
-    chip_grad = jnp.concatenate([hidden_grad, to_other_core(hidden_grad)], axis=0)
-    pieces = input_grad_pieces(after(chip_grad, grads[1], grads[2]), weights)
+    own_grad = after(hidden_grad, grads[1], grads[2])
+    pieces = input_grad_pieces(own_grad, to_other_core(hidden_grad), weights)
     pieces = lax.all_to_all(pieces, "col", 0, 0, tiled=True)
     feature_grad = jnp.sum(pieces.astype(jnp.float32), axis=0).astype(jnp.bfloat16)
     feature_grad = lax.ppermute(
         feature_grad, ("row", "col"), [(to, source) for source, to in depth_moves()]
     )
 
-    total = 0.0
-    for slot, grad in enumerate(grads):
-        block = by_token[2 * slot : 2 * slot + 2].reshape(2 * depth, tokens)
-        total += jnp.dot(block, grad, preferred_element_type=jnp.float32)
-    total = after(total, feature_grad)
-    own = total[:depth] + to_other_core(total[depth:].astype(jnp.bfloat16)).astype(jnp.float32)
-    own = own.astype(jnp.bfloat16)
+    split = SLOTS - 3
+    wide = jnp.float32
+    sums = token_sum(range(split), by_token, grads[:split], (), (wide, wide))
+    last = after(grads[-1], feature_grad)
+    own, other = token_sum(
+        range(split, SLOTS), by_token, [*grads[split:-1], last], sums, (wide, jnp.bfloat16)
+    )
+    own = (own + to_other_core(other).astype(jnp.float32)).astype(jnp.bfloat16)
     replica = lax.ppermute(own, "dp", [(0, 1), (1, 0)])
     weight_grad = own.astype(jnp.float32) + replica.astype(jnp.float32)
     feature_grad = feature_grad.T

time: 210 us -> 205 us (0.976)
  matrix products: 19.5 us -> 3.11 us
  waiting for transfers between devices: 84.8 us -> 91.7 us
  Pallas kernels: 3.06 us -> 6.2 us
    ppermute x6, waiting for transfers between devices: 7.38 us -> 28.8 us  [ring(): cross = lax.ppermute(cross, 'row', ring_moves(1 if step == 1 else 0))]
    dot_general x8 -> x0, matrix products: 16.4 us -> none  [per_device(): total += jnp.dot(block, grad, preferred_element_type=jnp.float32)]
    ppermute x8, waiting for transfers between devices: 40.9 us -> 25.2 us  [ring(): same = lax.ppermute(same, 'row', ring_moves(0))]
    ppermute x1, starting transfers between devices: 1.92 us -> 7.27 us  [per_device(): by_token = lax.ppermute(features, ('row', 'col'), token_moves())]
    all_to_all x2 -> x1, starting transfers between devices: 14 us -> 9.71 us  [to_all_cols(): return lax.all_to_all(copies, 'col', 0, 0, tiled=True)]
    ppermute x1, waiting for transfers between devices: 0.01 us -> 4.24 us  [per_device(): by_token = lax.ppermute(features, ('row', 'col'), token_moves())]
    unnamed x31 -> x29, local copies, waits for them, and re-layouts: 1.34 us -> 5.26 us
    ppermute x6, starting transfers between devices: 22.1 us -> 19.3 us  [ring(): cross = lax.ppermute(cross, 'row', ring_moves(1 if step == 1 else 0))]
  transfers between devices with their start and end apart: 24 -> 23, of which waited for: 12 -> 16; matrix products, arithmetic and copies ran while one was open for 13% -> 3% of each run, Pallas kernels for 1% -> 1%
where the time goes in v5:
time: 205 us; the launch traced here: 203 us
  waiting for transfers between devices  91.7 us (45%)
  starting transfers between devices  87.4 us (43%)
  local copies, waits for them, and re-layouts  9.13 us (4%)
  Pallas kernels  6.2 us (3%)
  other arithmetic  4.35 us (2%)
  matrix products  3.11 us (2%)
    ppermute x6, waiting for transfers between devices, ring(): cross = lax.ppermute(cross, 'row', ring_moves(1 if step == 1 else 0))  28.8 us
    ppermute x1, waiting for transfers between devices, per_device(): replica = lax.ppermute(own, 'dp', [(0, 1), (1, 0)])  27.6 us
    ppermute x8, waiting for transfers between devices, ring(): same = lax.ppermute(same, 'row', ring_moves(0))  25.2 us
    ppermute x8, starting transfers between devices, ring(): same = lax.ppermute(same, 'row', ring_moves(0))  20.2 us
    ppermute x6, starting transfers between devices, ring(): cross = lax.ppermute(cross, 'row', ring_moves(1 if step == 1 else 0))  19.3 us
    all_to_all x1, starting transfers between devices, to_all_cols(): return lax.all_to_all(copies, 'col', 0, 0, tiled=True)  9.71 us
    all_to_all x1, starting transfers between devices, per_device(): pieces = lax.all_to_all(pieces, 'col', 0, 0, tiled=True)  7.65 us
    ppermute x1, starting transfers between devices, per_device(): by_token = lax.ppermute(features, ('row', 'col'), token_moves())  7.27 us
  transfers between devices with their start and end apart: 23, of which 16 were waited for; matrix products, arithmetic and copies ran while one was open for 3% of the time, Pallas kernels for 1%

profile of v5, /device:TPU:56, one launch (start us, length us, event | category | flops | bytes accessed | tf_op | source)
XLA Modules:
  0.0 202.9 jit_solution(10143558126229752705)
XLA Ops:
  0.6 4.3 %collective-permute-start.2 = (bf16[192,1536]{1,0:T(8,128)(2,1)}, bf16[192,1536]{1,0:T(8,128)(2,1)S(1)}, u32[]{:S(2)}, u32[]{:S(2)}) collective-permute-start(bf16[192,1536]{1,0:T(8,128)(2,1)} %refs_0_.1), channel_id=1, source_target_pairs={{0,32},{16,240},{32,64},{48,16},{64,96},{80,48},{96,128},{112,80},... | collective-permute-start | bytes 1769480 | tf_op jit(solution)/shard_map/ppermute | solution.py:68
  4.9 6.5 %collective-permute-start = (bf16[192,128]{1,0:T(8,128)(2,1)}, bf16[192,128]{1,0:T(8,128)(2,1)S(1)}, u32[]{:S(2)}, u32[]{:S(2)}) collective-permute-start(bf16[192,128]{1,0:T(8,128)(2,1)} %bitcast.43), channel_id=1, source_target_pairs={{0,0},{16,1},{14,2},{30,3},{15,4},{31,5},{12,6},{28,7},{13,8},{29,... | collective-permute-start | bytes 147464 | tf_op jit(solution)/shard_map/ppermute | solution.py:162
  11.4 7.3 %collective-permute-start.1 = (bf16[192,128]{1,0:T(8,128)(2,1)}, bf16[192,128]{1,0:T(8,128)(2,1)S(1)}, u32[]{:S(2)}, u32[]{:S(2)}) collective-permute-start(bf16[192,128]{1,0:T(8,128)(2,1)} %bitcast.44), channel_id=1, source_target_pairs={{0,0},{1,1},{224,2},{225,3},{240,4},{241,5},{192,6},{193,7},{208,8... | collective-permute-start | bytes 147464 | tf_op jit(solution)/shard_map/ppermute | solution.py:163
  18.7 4.2 %collective-permute-done.1 = bf16[192,128]{1,0:T(8,128)(2,1)S(1)} collective-permute-done((bf16[192,128]{1,0:T(8,128)(2,1)}, bf16[192,128]{1,0:T(8,128)(2,1)S(1)}, u32[]{:S(2)}, u32[]{:S(2)}) %collective-permute-start.1) | collective-permute-done | bytes 49184 | tf_op jit(solution)/shard_map/ppermute | solution.py:163
  24.4 9.7 %all-to-all-start = ((bf16[16,384,128]{2,1,0:T(8,128)(2,1)}), bf16[16,384,128]{2,1,0:T(8,128)(2,1)}, u32[]{:S(2)}, u32[]{:S(2)}) async-start(bf16[16,384,128]{2,1,0:T(8,128)(2,1)} %broadcast_in_dim.2), calls=%async_computation | async-start | bytes 3145728 | tf_op jit(solution)/shard_map/all_to_all | solution.py:82
  34.2 3.6 %collective-permute-start.3 = (bf16[192,1536]{1,0:T(8,128)(2,1)S(1)}, bf16[192,1536]{1,0:T(8,128)(2,1)S(1)}, u32[]{:S(2)}, u32[]{:S(2)}) collective-permute-start(bf16[192,1536]{1,0:T(8,128)(2,1)S(1)} %copy-done), channel_id=1, source_target_pairs={{16,32},{0,240},{48,64},{32,16},{80,96},{64,48},{112,128},{96,80},... | collective-permute-start | bytes 1769480 | tf_op jit(solution)/shard_map/ppermute | solution.py:71
  37.8 3.3 %collective-permute-start.4 = (bf16[192,1536]{1,0:T(8,128)(2,1)S(1)}, bf16[192,1536]{1,0:T(8,128)(2,1)S(1)}, u32[]{:S(2)}, u32[]{:S(2)}) collective-permute-start(bf16[192,1536]{1,0:T(8,128)(2,1)S(1)} %collective-permute-done.2.refs_1_), channel_id=1, source_target_pairs={{0,32},{16,240},{32,64},{48,16},{64,96},{80,48},{96,128},{112,80},... | collective-permute-start | bytes 1769480 | tf_op jit(solution)/shard_map/ppermute | solution.py:68
  41.0 7.7 %collective-permute-done.3.refs_2_ = bf16[192,1536]{1,0:T(8,128)(2,1)S(1)} collective-permute-done((bf16[192,1536]{1,0:T(8,128)(2,1)S(1)}, bf16[192,1536]{1,0:T(8,128)(2,1)S(1)}, u32[]{:S(2)}, u32[]{:S(2)}) %collective-permute-start.3) | collective-permute-done | bytes 589856 | tf_op jit(solution)/shard_map/ppermute | solution.py:71
  48.7 4.5 %collective-permute-start.5 = (bf16[192,1536]{1,0:T(8,128)(2,1)S(1)}, bf16[192,1536]{1,0:T(8,128)(2,1)S(1)}, u32[]{:S(2)}, u32[]{:S(2)}) collective-permute-start(bf16[192,1536]{1,0:T(8,128)(2,1)S(1)} %collective-permute-done.3.refs_2_), channel_id=1, source_target_pairs={{0,32},{16,240},{32,64},{48,16},{64,96},{80,48},{96,128},{112,80},... | collective-permute-start | bytes 1769480 | tf_op jit(solution)/shard_map/ppermute | solution.py:71
  53.3 1.9 collective-permute-start.6
  55.2 6.5 %collective-permute-done.5.refs_4_ = bf16[192,1536]{1,0:T(8,128)(2,1)S(1)} collective-permute-done((bf16[192,1536]{1,0:T(8,128)(2,1)S(1)}, bf16[192,1536]{1,0:T(8,128)(2,1)S(1)}, u32[]{:S(2)}, u32[]{:S(2)}) %collective-permute-start.5) | collective-permute-done | bytes 589856 | tf_op jit(solution)/shard_map/ppermute | solution.py:71
  61.7 3.3 %collective-permute-start.7 = (bf16[192,1536]{1,0:T(8,128)(2,1)S(1)}, bf16[192,1536]{1,0:T(8,128)(2,1)S(1)}, u32[]{:S(2)}, u32[]{:S(2)}) collective-permute-start(bf16[192,1536]{1,0:T(8,128)(2,1)S(1)} %collective-permute-done.5.refs_4_), channel_id=1, source_target_pairs={{0,32},{16,240},{32,64},{48,16},{64,96},{80,48},{96,128},{112,80},... | collective-permute-start | bytes 1769480 | tf_op jit(solution)/shard_map/ppermute | solution.py:71
  65.1 3.0 %collective-permute-done.6.refs_5_ = bf16[192,1536]{1,0:T(8,128)(2,1)S(1)} collective-permute-done((bf16[192,1536]{1,0:T(8,128)(2,1)S(1)}, bf16[192,1536]{1,0:T(8,128)(2,1)S(1)}, u32[]{:S(2)}, u32[]{:S(2)}) %collective-permute-start.6) | collective-permute-done | bytes 589856 | tf_op jit(solution)/shard_map/ppermute | solution.py:68
  68.0 6.7 %collective-permute-done.7.refs_6_ = bf16[192,1536]{1,0:T(8,128)(2,1)S(1)} collective-permute-done((bf16[192,1536]{1,0:T(8,128)(2,1)S(1)}, bf16[192,1536]{1,0:T(8,128)(2,1)S(1)}, u32[]{:S(2)}, u32[]{:S(2)}) %collective-permute-start.7) | collective-permute-done | bytes 589856 | tf_op jit(solution)/shard_map/ppermute | solution.py:71
  74.7 3.0 %collective-permute-start.8 = (bf16[192,1536]{1,0:T(8,128)(2,1)S(1)}, bf16[192,1536]{1,0:T(8,128)(2,1)S(1)}, u32[]{:S(2)}, u32[]{:S(2)}) collective-permute-start(bf16[192,1536]{1,0:T(8,128)(2,1)S(1)} %collective-permute-done.6.refs_5_), channel_id=1, source_target_pairs={{0,32},{16,240},{32,64},{48,16},{64,96},{80,48},{96,128},{112,80},... | collective-permute-start | bytes 1769480 | tf_op jit(solution)/shard_map/ppermute | solution.py:68
  82.2 5.5 %collective-permute-done.8.refs_7_ = bf16[192,1536]{1,0:T(8,128)(2,1)S(1)} collective-permute-done((bf16[192,1536]{1,0:T(8,128)(2,1)S(1)}, bf16[192,1536]{1,0:T(8,128)(2,1)S(1)}, u32[]{:S(2)}, u32[]{:S(2)}) %collective-permute-start.8) | collective-permute-done | bytes 589856 | tf_op jit(solution)/shard_map/ppermute | solution.py:68
  88.9 1.9 collective-permute-start.9
  95.6 4.0 %collective-permute-start.11 = (bf16[128,1536]{1,0:T(8,128)(2,1)S(1)}, bf16[128,1536]{1,0:T(8,128)(2,1)S(1)}, u32[]{:S(2)}, u32[]{:S(2)}) collective-permute-start(bf16[128,1536]{1,0:T(8,128)(2,1)S(1)} %get-tuple-element.14.own_ref.refs_0_), channel_id=1, source_target_pairs={{16,32},{0,240},{48,64},{32,16},{80,96},{64,48},{112,128},{96,80},... | collective-permute-start | bytes 1179656 | tf_op jit(solution)/shard_map/ppermute | solution.py:71
  99.7 1.9 collective-permute-start.12
  101.6 5.8 %collective-permute-done.10.refs_1_ = bf16[128,1536]{1,0:T(8,128)(2,1)S(1)} collective-permute-done((bf16[128,1536]{1,0:T(8,128)(2,1)S(1)}, bf16[128,1536]{1,0:T(8,128)(2,1)S(1)}, u32[]{:S(2)}, u32[]{:S(2)}) %collective-permute-start.10) | collective-permute-done | bytes 393248 | tf_op jit(solution)/shard_map/ppermute | solution.py:68
  109.6 3.5 %shard_map.58 = bf16[16,192,128]{2,1,0:T(8,128)(2,1)} custom-call(bf16[128,1536]{1,0:T(8,128)(2,1)S(1)} %get-tuple-element.14.own_ref.refs_0_, bf16[128,1536]{1,0:T(8,128)(2,1)S(1)} %collective-permute-done.12.other_ref, bf16[192,1536]{1,0:T(8,128)(2,1)S(1)} %copy-done, bf16[192,1536]{1,0:T(8,128)(2,1)S(1)} %copy-done.2, bf16[192,1536]{1,0:T(8,128)(2,1)S(1)} %copy-done.4, ...), custom_call_target="tpu_custom_call" | custom-call | flops 1207959552 | bytes 6291456 | tf_op jit(solution)/shard_map/pallas_call | solution.py:105
  113.8 7.6 %all-to-all-start.1 = ((bf16[16,192,128]{2,1,0:T(8,128)(2,1)}), bf16[16,192,128]{2,1,0:T(8,128)(2,1)}, u32[]{:S(2)}, u32[]{:S(2)}) async-start(bf16[16,192,128]{2,1,0:T(8,128)(2,1)} %shard_map.58), calls=%async_computation.1 | async-start | bytes 1572864 | tf_op jit(solution)/shard_map/all_to_all | solution.py:185
  121.5 2.1 %collective-permute-start.14 = (bf16[128,1536]{1,0:T(8,128)(2,1)S(1)}, bf16[128,1536]{1,0:T(8,128)(2,1)S(1)}, u32[]{:S(2)}, u32[]{:S(2)}) collective-permute-start(bf16[128,1536]{1,0:T(8,128)(2,1)S(1)} %copy-done.8), channel_id=1, source_target_pairs={{0,32},{16,240},{32,64},{48,16},{64,96},{80,48},{96,128},{112,80},... | collective-permute-start | bytes 1179656 | tf_op jit(solution)/shard_map/ppermute | solution.py:68
  125.5 7.0 %collective-permute-done.14.refs_3_ = bf16[128,1536]{1,0:T(8,128)(2,1)S(1)} collective-permute-done((bf16[128,1536]{1,0:T(8,128)(2,1)S(1)}, bf16[128,1536]{1,0:T(8,128)(2,1)S(1)}, u32[]{:S(2)}, u32[]{:S(2)}) %collective-permute-start.14) | collective-permute-done | bytes 393248 | tf_op jit(solution)/shard_map/ppermute | solution.py:68
  134.4 2.3 %collective-permute-done.16.refs_4_ = bf16[128,1536]{1,0:T(8,128)(2,1)S(1)} collective-permute-done((bf16[128,1536]{1,0:T(8,128)(2,1)S(1)}, bf16[128,1536]{1,0:T(8,128)(2,1)S(1)}, u32[]{:S(2)}, u32[]{:S(2)}) %collective-permute-start.16) | collective-permute-done | bytes 393248 | tf_op jit(solution)/shard_map/ppermute | solution.py:71
  139.4 4.0 %collective-permute-done.15.refs_0_ = bf16[128,1536]{1,0:T(8,128)(2,1)S(1)} collective-permute-done((bf16[128,1536]{1,0:T(8,128)(2,1)S(1)}, bf16[128,1536]{1,0:T(8,128)(2,1)S(1)}, u32[]{:S(2)}, u32[]{:S(2)}) %collective-permute-start.15) | collective-permute-done | bytes 393248 | tf_op jit(solution)/shard_map/ppermute | solution.py:68
  143.4 4.2 %collective-permute-done.17.refs_1_ = bf16[128,1536]{1,0:T(8,128)(2,1)S(1)} collective-permute-done((bf16[128,1536]{1,0:T(8,128)(2,1)S(1)}, bf16[128,1536]{1,0:T(8,128)(2,1)S(1)}, u32[]{:S(2)}, u32[]{:S(2)}) %collective-permute-start.17) | collective-permute-done | bytes 393248 | tf_op jit(solution)/shard_map/ppermute | solution.py:71
  152.6 4.6 %collective-permute-start.13 = (bf16[192,128]{1,0:T(8,128)(2,1)}, bf16[192,128]{1,0:T(8,128)(2,1)S(1)}, u32[]{:S(2)}, u32[]{:S(2)}) collective-permute-start(bf16[192,128]{1,0:T(8,128)(2,1)} %reduce_sum.12), channel_id=1, source_target_pairs={{0,0},{1,16},{2,14},{3,30},{4,15},{5,31},{6,12},{7,28},{8,13},{9,2... | collective-permute-start | bytes 147464 | tf_op jit(solution)/shard_map/ppermute | solution.py:187
  159.9 2.2 %collective-permute-done.13 = bf16[192,128]{1,0:T(8,128)(2,1)S(1)} collective-permute-done((bf16[192,128]{1,0:T(8,128)(2,1)}, bf16[192,128]{1,0:T(8,128)(2,1)S(1)}, u32[]{:S(2)}, u32[]{:S(2)}) %collective-permute-start.13) | collective-permute-done | bytes 49184 | tf_op jit(solution)/shard_map/ppermute | solution.py:187
  165.1 2.0 collective-permute-done.19
  167.2 6.3 %collective-permute-start.20 = (bf16[192,1536]{1,0:T(8,128)(2,1)S(1)}, bf16[192,1536]{1,0:T(8,128)(2,1)S(1)}, u32[]{:S(2)}, u32[]{:S(2)}) collective-permute-start(bf16[192,1536]{1,0:T(8,128)(2,1)S(1)} %add_convert_fusion), channel_id=1, source_target_pairs={{0,256},{256,0},{1,257},{257,1},{2,258},{258,2},{3,259},{259,3},{4... | collective-permute-start | bytes 1769480 | tf_op jit(solution)/shard_map/ppermute | solution.py:199
  173.5 27.6 %collective-permute-done.20 = bf16[192,1536]{1,0:T(8,128)(2,1)S(1)} collective-permute-done((bf16[192,1536]{1,0:T(8,128)(2,1)S(1)}, bf16[192,1536]{1,0:T(8,128)(2,1)S(1)}, u32[]{:S(2)}, u32[]{:S(2)}) %collective-permute-start.20) | collective-permute-done | bytes 589856 | tf_op jit(solution)/shard_map/ppermute | solution.py:199
  (63 shorter events, 33.9 us)
Async XLA Ops:
  0.6 22.3 %collective-permute-start.2 = (bf16[192,1536]{1,0:T(8,128)(2,1)}, bf16[192,1536]{1,0:T(8,128)(2,1)S(1)}, u32[]{:S(2)}, u32[]{:S(2)}) collective-permute-start(bf16[192,1536]{1,0:T(8,128)(2,1)} %refs_0_.1), channel_id=1, source_target_pairs={{0,32},{16,240},{32,64},{48,16},{64,96},{80,48},{96,128},{112,80},... | collective-permute-start | bytes 1769480 | tf_op jit(solution)/shard_map/ppermute | solution.py:68
  4.9 13.8 %collective-permute-start = (bf16[192,128]{1,0:T(8,128)(2,1)}, bf16[192,128]{1,0:T(8,128)(2,1)S(1)}, u32[]{:S(2)}, u32[]{:S(2)}) collective-permute-start(bf16[192,128]{1,0:T(8,128)(2,1)} %bitcast.43), channel_id=1, source_target_pairs={{0,0},{16,1},{14,2},{30,3},{15,4},{31,5},{12,6},{28,7},{13,8},{29,... | collective-permute-start | bytes 147464 | tf_op jit(solution)/shard_map/ppermute | solution.py:162
  11.4 11.5 %collective-permute-start.1 = (bf16[192,128]{1,0:T(8,128)(2,1)}, bf16[192,128]{1,0:T(8,128)(2,1)S(1)}, u32[]{:S(2)}, u32[]{:S(2)}) collective-permute-start(bf16[192,128]{1,0:T(8,128)(2,1)} %bitcast.44), channel_id=1, source_target_pairs={{0,0},{1,1},{224,2},{225,3},{240,4},{241,5},{192,6},{193,7},{208,8... | collective-permute-start | bytes 147464 | tf_op jit(solution)/shard_map/ppermute | solution.py:163
  23.0 14.8 %copy-start.1 = (bf16[192,1536]{1,0:T(8,128)(2,1)}, bf16[192,1536]{1,0:T(8,128)(2,1)S(1)}, u32[]{:S(2)}) copy-start(bf16[192,1536]{1,0:T(8,128)(2,1)S(1)} %collective-permute-done.2.refs_1_) | copy-start | bytes 1769476
  24.4 9.7 %copy-start = (bf16[192,1536]{1,0:T(8,128)(2,1)S(1)}, bf16[192,1536]{1,0:T(8,128)(2,1)}, u32[]{:S(2)}) copy-start(bf16[192,1536]{1,0:T(8,128)(2,1)} %refs_0_.1) | copy-start | bytes 1769476
  24.4 53.3 %all-to-all-start = ((bf16[16,384,128]{2,1,0:T(8,128)(2,1)}), bf16[16,384,128]{2,1,0:T(8,128)(2,1)}, u32[]{:S(2)}, u32[]{:S(2)}) async-start(bf16[16,384,128]{2,1,0:T(8,128)(2,1)} %broadcast_in_dim.2), calls=%async_computation | async-start | bytes 3145728 | tf_op jit(solution)/shard_map/all_to_all | solution.py:82
  34.2 14.6 %collective-permute-start.3 = (bf16[192,1536]{1,0:T(8,128)(2,1)S(1)}, bf16[192,1536]{1,0:T(8,128)(2,1)S(1)}, u32[]{:S(2)}, u32[]{:S(2)}) collective-permute-start(bf16[192,1536]{1,0:T(8,128)(2,1)S(1)} %copy-done), channel_id=1, source_target_pairs={{16,32},{0,240},{48,64},{32,16},{80,96},{64,48},{112,128},{96,80},... | collective-permute-start | bytes 1769480 | tf_op jit(solution)/shard_map/ppermute | solution.py:71
  37.8 15.5 %collective-permute-start.4 = (bf16[192,1536]{1,0:T(8,128)(2,1)S(1)}, bf16[192,1536]{1,0:T(8,128)(2,1)S(1)}, u32[]{:S(2)}, u32[]{:S(2)}) collective-permute-start(bf16[192,1536]{1,0:T(8,128)(2,1)S(1)} %collective-permute-done.2.refs_1_), channel_id=1, source_target_pairs={{0,32},{16,240},{32,64},{48,16},{64,96},{80,48},{96,128},{112,80},... | collective-permute-start | bytes 1769480 | tf_op jit(solution)/shard_map/ppermute | solution.py:68
  48.7 26.0 %copy-start.3 = (bf16[192,1536]{1,0:T(8,128)(2,1)}, bf16[192,1536]{1,0:T(8,128)(2,1)S(1)}, u32[]{:S(2)}) copy-start(bf16[192,1536]{1,0:T(8,128)(2,1)S(1)} %collective-permute-done.3.refs_2_) | copy-start | bytes 1769476
  48.7 13.0 %collective-permute-start.5 = (bf16[192,1536]{1,0:T(8,128)(2,1)S(1)}, bf16[192,1536]{1,0:T(8,128)(2,1)S(1)}, u32[]{:S(2)}, u32[]{:S(2)}) collective-permute-start(bf16[192,1536]{1,0:T(8,128)(2,1)S(1)} %collective-permute-done.3.refs_2_), channel_id=1, source_target_pairs={{0,32},{16,240},{32,64},{48,16},{64,96},{80,48},{96,128},{112,80},... | collective-permute-start | bytes 1769480 | tf_op jit(solution)/shard_map/ppermute | solution.py:71
  53.3 14.7 %collective-permute-start.6 = (bf16[192,1536]{1,0:T(8,128)(2,1)S(1)}, bf16[192,1536]{1,0:T(8,128)(2,1)S(1)}, u32[]{:S(2)}, u32[]{:S(2)}) collective-permute-start(bf16[192,1536]{1,0:T(8,128)(2,1)S(1)} %collective-permute-done.4.refs_3_), channel_id=1, source_target_pairs={{0,32},{16,240},{32,64},{48,16},{64,96},{80,48},{96,128},{112,80},... | collective-permute-start | bytes 1769480 | tf_op jit(solution)/shard_map/ppermute | solution.py:68
  61.7 13.0 %collective-permute-start.7 = (bf16[192,1536]{1,0:T(8,128)(2,1)S(1)}, bf16[192,1536]{1,0:T(8,128)(2,1)S(1)}, u32[]{:S(2)}, u32[]{:S(2)}) collective-permute-start(bf16[192,1536]{1,0:T(8,128)(2,1)S(1)} %collective-permute-done.5.refs_4_), channel_id=1, source_target_pairs={{0,32},{16,240},{32,64},{48,16},{64,96},{80,48},{96,128},{112,80},... | collective-permute-start | bytes 1769480 | tf_op jit(solution)/shard_map/ppermute | solution.py:71
  74.7 13.0 %collective-permute-start.8 = (bf16[192,1536]{1,0:T(8,128)(2,1)S(1)}, bf16[192,1536]{1,0:T(8,128)(2,1)S(1)}, u32[]{:S(2)}, u32[]{:S(2)}) collective-permute-start(bf16[192,1536]{1,0:T(8,128)(2,1)S(1)} %collective-permute-done.6.refs_5_), channel_id=1, source_target_pairs={{0,32},{16,240},{32,64},{48,16},{64,96},{80,48},{96,128},{112,80},... | collective-permute-start | bytes 1769480 | tf_op jit(solution)/shard_map/ppermute | solution.py:68
  79.3 1.1 copy-start.2
  88.5 4.1 %copy-start.13 = (bf16[128,1536]{1,0:T(8,128)(2,1)S(1)}, bf16[128,1536]{1,0:T(8,128)(2,1)}, u32[]{:S(2)}) copy-start(bf16[128,1536]{1,0:T(8,128)(2,1)} %param.5) | copy-start | bytes 1179652
  88.9 3.6 %collective-permute-start.9 = (bf16[128,1536]{1,0:T(8,128)(2,1)S(1)}, bf16[128,1536]{1,0:T(8,128)(2,1)S(1)}, u32[]{:S(2)}, u32[]{:S(2)}) collective-permute-start(bf16[128,1536]{1,0:T(8,128)(2,1)S(1)} %slice.141), channel_id=1, source_target_pairs={{0,16},{16,0},{32,48},{48,32},{64,80},{80,64},{96,112},{112,96},{1... | collective-permute-start | bytes 1179656 | tf_op jit(solution)/shard_map/ppermute | solution.py:77
  93.7 13.7 %collective-permute-start.10 = (bf16[128,1536]{1,0:T(8,128)(2,1)S(1)}, bf16[128,1536]{1,0:T(8,128)(2,1)S(1)}, u32[]{:S(2)}, u32[]{:S(2)}) collective-permute-start(bf16[128,1536]{1,0:T(8,128)(2,1)S(1)} %get-tuple-element.14.own_ref.refs_0_), channel_id=1, source_target_pairs={{0,32},{16,240},{32,64},{48,16},{64,96},{80,48},{96,128},{112,80},... | collective-permute-start | bytes 1179656 | tf_op jit(solution)/shard_map/ppermute | solution.py:68
  95.6 13.2 %collective-permute-start.11 = (bf16[128,1536]{1,0:T(8,128)(2,1)S(1)}, bf16[128,1536]{1,0:T(8,128)(2,1)S(1)}, u32[]{:S(2)}, u32[]{:S(2)}) collective-permute-start(bf16[128,1536]{1,0:T(8,128)(2,1)S(1)} %get-tuple-element.14.own_ref.refs_0_), channel_id=1, source_target_pairs={{16,32},{0,240},{48,64},{32,16},{80,96},{64,48},{112,128},{96,80},... | collective-permute-start | bytes 1179656 | tf_op jit(solution)/shard_map/ppermute | solution.py:71
  99.7 9.9 %collective-permute-start.12 = (bf16[128,1536]{1,0:T(8,128)(2,1)S(1)}, bf16[128,1536]{1,0:T(8,128)(2,1)S(1)}, u32[]{:S(2)}, u32[]{:S(2)}) collective-permute-start(bf16[128,1536]{1,0:T(8,128)(2,1)S(1)} %get-tuple-element.14.own_ref.refs_0_), channel_id=1, source_target_pairs={{0,16},{16,0},{32,48},{48,32},{64,80},{80,64},{96,112},{112,96},{1... | collective-permute-start | bytes 1179656 | tf_op jit(solution)/shard_map/ppermute | solution.py:77
  107.4 2.2 %copy-start.7 = (bf16[128,1536]{1,0:T(8,128)(2,1)}, bf16[128,1536]{1,0:T(8,128)(2,1)S(1)}, u32[]{:S(2)}) copy-start(bf16[128,1536]{1,0:T(8,128)(2,1)S(1)} %collective-permute-done.10.refs_1_) | copy-start | bytes 1179652
  113.8 7.7 %copy-start.8 = (bf16[128,1536]{1,0:T(8,128)(2,1)S(1)}, bf16[128,1536]{1,0:T(8,128)(2,1)}, u32[]{:S(2)}) copy-start(bf16[128,1536]{1,0:T(8,128)(2,1)} %copy-done.7) | copy-start | bytes 1179652
  113.8 9.7 %copy-start.10 = (bf16[128,1536]{1,0:T(8,128)(2,1)S(1)}, bf16[128,1536]{1,0:T(8,128)(2,1)}, u32[]{:S(2)}) copy-start(bf16[128,1536]{1,0:T(8,128)(2,1)} %copy-done.9) | copy-start | bytes 1179652
  113.8 36.9 %all-to-all-start.1 = ((bf16[16,192,128]{2,1,0:T(8,128)(2,1)}), bf16[16,192,128]{2,1,0:T(8,128)(2,1)}, u32[]{:S(2)}, u32[]{:S(2)}) async-start(bf16[16,192,128]{2,1,0:T(8,128)(2,1)} %shard_map.58), calls=%async_computation.1 | async-start | bytes 1572864 | tf_op jit(solution)/shard_map/all_to_all | solution.py:185
  121.5 35.7 %copy-start.6 = (bf16[128,1536]{1,0:T(8,128)(2,1)S(1)}, bf16[128,1536]{1,0:T(8,128)(2,1)}, u32[]{:S(2)}) copy-start(bf16[128,1536]{1,0:T(8,128)(2,1)} %copy-done.5) | copy-start | bytes 1179652
  121.5 11.0 %collective-permute-start.14 = (bf16[128,1536]{1,0:T(8,128)(2,1)S(1)}, bf16[128,1536]{1,0:T(8,128)(2,1)S(1)}, u32[]{:S(2)}, u32[]{:S(2)}) collective-permute-start(bf16[128,1536]{1,0:T(8,128)(2,1)S(1)} %copy-done.8), channel_id=1, source_target_pairs={{0,32},{16,240},{32,64},{48,16},{64,96},{80,48},{96,128},{112,80},... | collective-permute-start | bytes 1179656 | tf_op jit(solution)/shard_map/ppermute | solution.py:68
  123.6 13.2 %collective-permute-start.16 = (bf16[128,1536]{1,0:T(8,128)(2,1)S(1)}, bf16[128,1536]{1,0:T(8,128)(2,1)S(1)}, u32[]{:S(2)}, u32[]{:S(2)}) collective-permute-start(bf16[128,1536]{1,0:T(8,128)(2,1)S(1)} %copy-done.10), channel_id=1, source_target_pairs={{0,32},{16,240},{32,64},{48,16},{64,96},{80,48},{96,128},{112,80},... | collective-permute-start | bytes 1179656 | tf_op jit(solution)/shard_map/ppermute | solution.py:71
  132.5 10.9 %collective-permute-start.15 = (bf16[128,1536]{1,0:T(8,128)(2,1)S(1)}, bf16[128,1536]{1,0:T(8,128)(2,1)S(1)}, u32[]{:S(2)}, u32[]{:S(2)}) collective-permute-start(bf16[128,1536]{1,0:T(8,128)(2,1)S(1)} %collective-permute-done.14.refs_3_), channel_id=1, source_target_pairs={{0,32},{16,240},{32,64},{48,16},{64,96},{80,48},{96,128},{112,80},... | collective-permute-start | bytes 1179656 | tf_op jit(solution)/shard_map/ppermute | solution.py:68
  136.7 10.9 %collective-permute-start.17 = (bf16[128,1536]{1,0:T(8,128)(2,1)S(1)}, bf16[128,1536]{1,0:T(8,128)(2,1)S(1)}, u32[]{:S(2)}, u32[]{:S(2)}) collective-permute-start(bf16[128,1536]{1,0:T(8,128)(2,1)S(1)} %collective-permute-done.16.refs_4_), channel_id=1, source_target_pairs={{0,32},{16,240},{32,64},{48,16},{64,96},{80,48},{96,128},{112,80},... | collective-permute-start | bytes 1179656 | tf_op jit(solution)/shard_map/ppermute | solution.py:71
  147.6 12.3 %collective-permute-start.18 = (bf16[128,1536]{1,0:T(8,128)(2,1)S(1)}, bf16[128,1536]{1,0:T(8,128)(2,1)S(1)}, u32[]{:S(2)}, u32[]{:S(2)}) collective-permute-start(bf16[128,1536]{1,0:T(8,128)(2,1)S(1)} %collective-permute-done.15.refs_0_), channel_id=1, source_target_pairs={{0,32},{16,240},{32,64},{48,16},{64,96},{80,48},{96,128},{112,80},... | collective-permute-start | bytes 1179656 | tf_op jit(solution)/shard_map/ppermute | solution.py:68
  152.6 9.5 %collective-permute-start.13 = (bf16[192,128]{1,0:T(8,128)(2,1)}, bf16[192,128]{1,0:T(8,128)(2,1)S(1)}, u32[]{:S(2)}, u32[]{:S(2)}) collective-permute-start(bf16[192,128]{1,0:T(8,128)(2,1)} %reduce_sum.12), channel_id=1, source_target_pairs={{0,0},{1,16},{2,14},{3,30},{4,15},{5,31},{6,12},{7,28},{8,13},{9,2... | collective-permute-start | bytes 147464 | tf_op jit(solution)/shard_map/ppermute | solution.py:187
  163.1 3.9 %collective-permute-start.19 = (bf16[192,1536]{1,0:T(8,128)(2,1)S(1)}, bf16[192,1536]{1,0:T(8,128)(2,1)S(1)}, u32[]{:S(2)}, u32[]{:S(2)}) collective-permute-start(bf16[192,1536]{1,0:T(8,128)(2,1)S(1)} %get-tuple-element.20), channel_id=1, source_target_pairs={{0,16},{16,0},{32,48},{48,32},{64,80},{80,64},{96,112},{112,96},{1... | collective-permute-start | bytes 1769480 | tf_op jit(solution)/shard_map/ppermute | solution.py:77
  167.2 33.9 %collective-permute-start.20 = (bf16[192,1536]{1,0:T(8,128)(2,1)S(1)}, bf16[192,1536]{1,0:T(8,128)(2,1)S(1)}, u32[]{:S(2)}, u32[]{:S(2)}) collective-permute-start(bf16[192,1536]{1,0:T(8,128)(2,1)S(1)} %add_convert_fusion), channel_id=1, source_target_pairs={{0,256},{256,0},{1,257},{257,1},{2,258},{258,2},{3,259},{259,3},{4... | collective-permute-start | bytes 1769480 | tf_op jit(solution)/shard_map/ppermute | solution.py:199
  (5 other events, 4.4 us)

commit v6 on v5

--- a/solution.py
+++ b/solution.py
@@ -14,6 +14,7 @@
 ROUNDS = CHIPS // 2
 SLOTS = CHIPS
 LANES = 256
+EXCHANGE_FLOPS = 10**10
 
 
 def held_from(chip, core, slot):
@@ -77,13 +78,31 @@
     return lax.ppermute(value, "row", [(row, row ^ 1) for row in range(ROWS)])
 
 
-def to_all_cols(block):
-    copies = jnp.broadcast_to(block[None], (COLS,) + block.shape)
-    return lax.all_to_all(copies, "col", 0, 0, tiled=True)
-
-
 def after(value, *others):
     return lax.optimization_barrier((value,) + others)[0]
+
+
+def copies_kernel(first_ref, second_ref, copies_ref):
+    depth = first_ref.shape[0]
+    for col in range(COLS):
+        copies_ref[col, :depth] = first_ref[...]
+        copies_ref[col, depth:] = second_ref[...]
+
+
+def copies_for_cols(first, second):
+    depth, tokens = first.shape
+    return pl.pallas_call(
+        copies_kernel,
+        out_shape=jax.ShapeDtypeStruct((COLS, 2 * depth, tokens), first.dtype),
+        in_specs=[pl.BlockSpec(memory_space=pltpu.VMEM)] * 2,
+        out_specs=pl.BlockSpec(memory_space=pltpu.VMEM),
+        compiler_params=pltpu.CompilerParams(vmem_limit_bytes=16 * 2**20),
+        cost_estimate=pl.CostEstimate(
+            flops=EXCHANGE_FLOPS,
+            bytes_accessed=4 * COLS * depth * tokens,
+            transcendentals=0,
+        ),
+    )(first, second)
 
 
 def input_grad_kernel(own_ref, other_ref, *refs):
@@ -109,7 +128,7 @@
         out_specs=pl.BlockSpec(memory_space=pltpu.VMEM),
         compiler_params=pltpu.CompilerParams(vmem_limit_bytes=16 * 2**20),
         cost_estimate=pl.CostEstimate(
-            flops=4 * SLOTS * depth * hidden_units * tokens,
+            flops=4 * SLOTS * depth * hidden_units * tokens + EXCHANGE_FLOPS,
             bytes_accessed=moved,
             transcendentals=0,
         ),
@@ -161,8 +180,7 @@
     weights = ring(up_weight)
     by_depth = lax.ppermute(features, ("row", "col"), depth_moves())
     by_token = lax.ppermute(features, ("row", "col"), token_moves())
-    both_ways = jnp.concatenate([by_depth, by_token], axis=0)
-    both_ways = to_all_cols(after(both_ways, weights[1]))
+    both_ways = lax.all_to_all(copies_for_cols(by_depth, by_token), "col", 0, 0, tiled=True)
     by_depth, by_token = both_ways[:, :depth], both_ways[:, depth:]
 
     both = 0.0

time: 205 us -> 210 us (1.024)
  waiting for transfers between devices: 91.7 us -> 103 us
  starting transfers between devices: 87.4 us -> 82.5 us
    ppermute x8, waiting for transfers between devices: 25.2 us -> 45.2 us  [ring(): same = lax.ppermute(same, 'row', ring_moves(0))]
    ppermute x6, waiting for transfers between devices: 28.8 us -> 19.4 us  [ring(): cross = lax.ppermute(cross, 'row', ring_moves(1 if step == 1 else 0))]
    ppermute x8, starting transfers between devices: 20.2 us -> 15.4 us  [ring(): same = lax.ppermute(same, 'row', ring_moves(0))]
  transfers between devices with their start and end apart: 23 -> 23, of which waited for: 16 -> 18; matrix products, arithmetic and copies ran while one was open for 3% -> 3% of each run, Pallas kernels for 1% -> 1%
where the time goes in v6:
time: 210 us; the launch traced here: 209 us
  waiting for transfers between devices  103 us (49%)
  starting transfers between devices  82.5 us (39%)
  local copies, waits for them, and re-layouts  7.69 us (4%)
  Pallas kernels  7.54 us (4%)
  other arithmetic  4.34 us (2%)
  matrix products  3.09 us (1%)
    ppermute x8, waiting for transfers between devices, ring(): same = lax.ppermute(same, 'row', ring_moves(0))  45.2 us
    ppermute x1, waiting for transfers between devices, per_device(): replica = lax.ppermute(own, 'dp', [(0, 1), (1, 0)])  28.9 us
    ppermute x6, waiting for transfers between devices, ring(): cross = lax.ppermute(cross, 'row', ring_moves(1 if step == 1 else 0))  19.4 us
    ppermute x6, starting transfers between devices, ring(): cross = lax.ppermute(cross, 'row', ring_moves(1 if step == 1 else 0))  18.8 us
    ppermute x8, starting transfers between devices, ring(): same = lax.ppermute(same, 'row', ring_moves(0))  15.4 us
    all_to_all x1, starting transfers between devices, per_device(): lax.all_to_all(copies_for_cols(by_depth, by_token), 'col', 0, 0, tiled=True)  10.7 us
    ppermute x1, starting transfers between devices, per_device(): by_token = lax.ppermute(features, ('row', 'col'), token_moves())  8.17 us
    all_to_all x1, starting transfers between devices, per_device(): pieces = lax.all_to_all(pieces, 'col', 0, 0, tiled=True)  7.65 us
  transfers between devices with their start and end apart: 23, of which 18 were waited for; matrix products, arithmetic and copies ran while one was open for 3% of the time, Pallas kernels for 1%

profile of v6, /device:TPU:56, one launch (start us, length us, event | category | flops | bytes accessed | tf_op | source)
XLA Modules:
  0.0 208.7 jit_solution(12059501798637665841)
XLA Ops:
  0.6 6.5 %collective-permute-start = (bf16[192,128]{1,0:T(8,128)(2,1)}, bf16[192,128]{1,0:T(8,128)(2,1)S(1)}, u32[]{:S(2)}, u32[]{:S(2)}) collective-permute-start(bf16[192,128]{1,0:T(8,128)(2,1)} %bitcast.43), channel_id=1, source_target_pairs={{0,0},{16,1},{14,2},{30,3},{15,4},{31,5},{12,6},{28,7},{13,8},{29,... | collective-permute-start | bytes 147464 | tf_op jit(solution)/shard_map/ppermute | solution.py:181
  7.1 8.2 %collective-permute-start.1 = (bf16[192,128]{1,0:T(8,128)(2,1)}, bf16[192,128]{1,0:T(8,128)(2,1)S(1)}, u32[]{:S(2)}, u32[]{:S(2)}) collective-permute-start(bf16[192,128]{1,0:T(8,128)(2,1)} %bitcast.44), channel_id=1, source_target_pairs={{0,0},{1,1},{224,2},{225,3},{240,4},{241,5},{192,6},{193,7},{208,8... | collective-permute-start | bytes 147464 | tf_op jit(solution)/shard_map/ppermute | solution.py:182
  15.3 3.2 %collective-permute-done.1.second_ref = bf16[192,128]{1,0:T(8,128)(2,1)S(1)} collective-permute-done((bf16[192,128]{1,0:T(8,128)(2,1)}, bf16[192,128]{1,0:T(8,128)(2,1)S(1)}, u32[]{:S(2)}, u32[]{:S(2)}) %collective-permute-start.1) | collective-permute-done | bytes 49184 | tf_op jit(solution)/shard_map/ppermute | solution.py:182
  19.9 10.7 %all-to-all-start = ((bf16[16,384,128]{2,1,0:T(8,128)(2,1)}), bf16[16,384,128]{2,1,0:T(8,128)(2,1)}, u32[]{:S(2)}, u32[]{:S(2)}) async-start(bf16[16,384,128]{2,1,0:T(8,128)(2,1)} %shard_map.58), calls=%async_computation | async-start | bytes 3145728 | tf_op jit(solution)/shard_map/all_to_all | solution.py:183
  30.6 1.9 collective-permute-start.2
  32.6 6.1 %collective-permute-start.3 = (bf16[192,1536]{1,0:T(8,128)(2,1)S(1)}, bf16[192,1536]{1,0:T(8,128)(2,1)S(1)}, u32[]{:S(2)}, u32[]{:S(2)}) collective-permute-start(bf16[192,1536]{1,0:T(8,128)(2,1)S(1)} %copy-done), channel_id=1, source_target_pairs={{16,32},{0,240},{48,64},{32,16},{80,96},{64,48},{112,128},{96,80},... | collective-permute-start | bytes 1769480 | tf_op jit(solution)/shard_map/ppermute | solution.py:72
  38.7 8.6 %collective-permute-done.2.refs_1_ = bf16[192,1536]{1,0:T(8,128)(2,1)S(1)} collective-permute-done((bf16[192,1536]{1,0:T(8,128)(2,1)S(1)}, bf16[192,1536]{1,0:T(8,128)(2,1)S(1)}, u32[]{:S(2)}, u32[]{:S(2)}) %collective-permute-start.2) | collective-permute-done | bytes 589856 | tf_op jit(solution)/shard_map/ppermute | solution.py:69
  47.3 1.9 collective-permute-start.4
  49.9 3.7 %collective-permute-start.5 = (bf16[192,1536]{1,0:T(8,128)(2,1)S(1)}, bf16[192,1536]{1,0:T(8,128)(2,1)S(1)}, u32[]{:S(2)}, u32[]{:S(2)}) collective-permute-start(bf16[192,1536]{1,0:T(8,128)(2,1)S(1)} %collective-permute-done.3.refs_2_), channel_id=1, source_target_pairs={{0,32},{16,240},{32,64},{48,16},{64,96},{80,48},{96,128},{112,80},... | collective-permute-start | bytes 1769480 | tf_op jit(solution)/shard_map/ppermute | solution.py:72
  53.6 7.7 %collective-permute-done.4.refs_3_ = bf16[192,1536]{1,0:T(8,128)(2,1)S(1)} collective-permute-done((bf16[192,1536]{1,0:T(8,128)(2,1)S(1)}, bf16[192,1536]{1,0:T(8,128)(2,1)S(1)}, u32[]{:S(2)}, u32[]{:S(2)}) %collective-permute-start.4) | collective-permute-done | bytes 589856 | tf_op jit(solution)/shard_map/ppermute | solution.py:69
  63.3 4.4 %collective-permute-done.5.refs_4_ = bf16[192,1536]{1,0:T(8,128)(2,1)S(1)} collective-permute-done((bf16[192,1536]{1,0:T(8,128)(2,1)S(1)}, bf16[192,1536]{1,0:T(8,128)(2,1)S(1)}, u32[]{:S(2)}, u32[]{:S(2)}) %collective-permute-start.5) | collective-permute-done | bytes 589856 | tf_op jit(solution)/shard_map/ppermute | solution.py:72
  69.6 4.7 %collective-permute-done.6.refs_5_ = bf16[192,1536]{1,0:T(8,128)(2,1)S(1)} collective-permute-done((bf16[192,1536]{1,0:T(8,128)(2,1)S(1)}, bf16[192,1536]{1,0:T(8,128)(2,1)S(1)}, u32[]{:S(2)}, u32[]{:S(2)}) %collective-permute-start.6) | collective-permute-done | bytes 589856 | tf_op jit(solution)/shard_map/ppermute | solution.py:69
  74.3 6.3 %collective-permute-done.7.refs_6_ = bf16[192,1536]{1,0:T(8,128)(2,1)S(1)} collective-permute-done((bf16[192,1536]{1,0:T(8,128)(2,1)S(1)}, bf16[192,1536]{1,0:T(8,128)(2,1)S(1)}, u32[]{:S(2)}, u32[]{:S(2)}) %collective-permute-start.7) | collective-permute-done | bytes 589856 | tf_op jit(solution)/shard_map/ppermute | solution.py:72
  87.1 6.6 %collective-permute-done.8.refs_7_ = bf16[192,1536]{1,0:T(8,128)(2,1)S(1)} collective-permute-done((bf16[192,1536]{1,0:T(8,128)(2,1)S(1)}, bf16[192,1536]{1,0:T(8,128)(2,1)S(1)}, u32[]{:S(2)}, u32[]{:S(2)}) %collective-permute-start.8) | collective-permute-done | bytes 589856 | tf_op jit(solution)/shard_map/ppermute | solution.py:69
  94.9 1.9 collective-permute-start.9
  101.6 3.3 %collective-permute-start.11 = (bf16[128,1536]{1,0:T(8,128)(2,1)S(1)}, bf16[128,1536]{1,0:T(8,128)(2,1)S(1)}, u32[]{:S(2)}, u32[]{:S(2)}) collective-permute-start(bf16[128,1536]{1,0:T(8,128)(2,1)S(1)} %get-tuple-element.12.own_ref.refs_0_), channel_id=1, source_target_pairs={{16,32},{0,240},{48,64},{32,16},{80,96},{64,48},{112,128},{96,80},... | collective-permute-start | bytes 1179656 | tf_op jit(solution)/shard_map/ppermute | solution.py:72
  104.9 1.9 collective-permute-start.12
  106.8 6.5 %collective-permute-done.10.refs_1_ = bf16[128,1536]{1,0:T(8,128)(2,1)S(1)} collective-permute-done((bf16[128,1536]{1,0:T(8,128)(2,1)S(1)}, bf16[128,1536]{1,0:T(8,128)(2,1)S(1)}, u32[]{:S(2)}, u32[]{:S(2)}) %collective-permute-start.10) | collective-permute-done | bytes 393248 | tf_op jit(solution)/shard_map/ppermute | solution.py:69
  115.5 3.5 %shard_map.59 = bf16[16,192,128]{2,1,0:T(8,128)(2,1)} custom-call(bf16[128,1536]{1,0:T(8,128)(2,1)S(1)} %get-tuple-element.12.own_ref.refs_0_, bf16[128,1536]{1,0:T(8,128)(2,1)S(1)} %collective-permute-done.12.other_ref, bf16[192,1536]{1,0:T(8,128)(2,1)S(1)} %copy-done, bf16[192,1536]{1,0:T(8,128)(2,1)S(1)} %copy-done.2, bf16[192,1536]{1,0:T(8,128)(2,1)S(1)} %copy-done.4, ...), custom_call_target="tpu_custom_call" | custom-call | flops 11207959552 | bytes 6291456 | tf_op jit(solution)/shard_map/pallas_call | solution.py:124
  119.8 7.7 %all-to-all-start.1 = ((bf16[16,192,128]{2,1,0:T(8,128)(2,1)}), bf16[16,192,128]{2,1,0:T(8,128)(2,1)}, u32[]{:S(2)}, u32[]{:S(2)}) async-start(bf16[16,192,128]{2,1,0:T(8,128)(2,1)} %shard_map.59), calls=%async_computation.1 | async-start | bytes 1572864 | tf_op jit(solution)/shard_map/all_to_all | solution.py:203
  127.5 2.1 collective-permute-start.14
  129.5 1.9 collective-permute-start.16
  131.5 7.0 %collective-permute-done.14.refs_3_ = bf16[128,1536]{1,0:T(8,128)(2,1)S(1)} collective-permute-done((bf16[128,1536]{1,0:T(8,128)(2,1)S(1)}, bf16[128,1536]{1,0:T(8,128)(2,1)S(1)}, u32[]{:S(2)}, u32[]{:S(2)}) %collective-permute-start.14) | collective-permute-done | bytes 393248 | tf_op jit(solution)/shard_map/ppermute | solution.py:69
  140.4 2.3 %collective-permute-done.16.refs_4_ = bf16[128,1536]{1,0:T(8,128)(2,1)S(1)} collective-permute-done((bf16[128,1536]{1,0:T(8,128)(2,1)S(1)}, bf16[128,1536]{1,0:T(8,128)(2,1)S(1)}, u32[]{:S(2)}, u32[]{:S(2)}) %collective-permute-start.16) | collective-permute-done | bytes 393248 | tf_op jit(solution)/shard_map/ppermute | solution.py:72
  145.4 4.0 %collective-permute-done.15.refs_0_ = bf16[128,1536]{1,0:T(8,128)(2,1)S(1)} collective-permute-done((bf16[128,1536]{1,0:T(8,128)(2,1)S(1)}, bf16[128,1536]{1,0:T(8,128)(2,1)S(1)}, u32[]{:S(2)}, u32[]{:S(2)}) %collective-permute-start.15) | collective-permute-done | bytes 393248 | tf_op jit(solution)/shard_map/ppermute | solution.py:69
  149.4 4.2 %collective-permute-done.17.refs_1_ = bf16[128,1536]{1,0:T(8,128)(2,1)S(1)} collective-permute-done((bf16[128,1536]{1,0:T(8,128)(2,1)S(1)}, bf16[128,1536]{1,0:T(8,128)(2,1)S(1)}, u32[]{:S(2)}, u32[]{:S(2)}) %collective-permute-start.17) | collective-permute-done | bytes 393248 | tf_op jit(solution)/shard_map/ppermute | solution.py:72
  158.6 4.6 %collective-permute-start.13 = (bf16[192,128]{1,0:T(8,128)(2,1)}, bf16[192,128]{1,0:T(8,128)(2,1)S(1)}, u32[]{:S(2)}, u32[]{:S(2)}) collective-permute-start(bf16[192,128]{1,0:T(8,128)(2,1)} %reduce_sum.12), channel_id=1, source_target_pairs={{0,0},{1,16},{2,14},{3,30},{4,15},{5,31},{6,12},{7,28},{8,13},{9,2... | collective-permute-start | bytes 147464 | tf_op jit(solution)/shard_map/ppermute | solution.py:205
  165.8 2.2 %collective-permute-done.13 = bf16[192,128]{1,0:T(8,128)(2,1)S(1)} collective-permute-done((bf16[192,128]{1,0:T(8,128)(2,1)}, bf16[192,128]{1,0:T(8,128)(2,1)S(1)}, u32[]{:S(2)}, u32[]{:S(2)}) %collective-permute-start.13) | collective-permute-done | bytes 49184 | tf_op jit(solution)/shard_map/ppermute | solution.py:205
  169.1 1.9 collective-permute-start.19
  171.0 2.0 collective-permute-done.19
  173.1 4.9 %collective-permute-start.20 = (bf16[192,1536]{1,0:T(8,128)(2,1)S(1)}, bf16[192,1536]{1,0:T(8,128)(2,1)S(1)}, u32[]{:S(2)}, u32[]{:S(2)}) collective-permute-start(bf16[192,1536]{1,0:T(8,128)(2,1)S(1)} %add_convert_fusion), channel_id=1, source_target_pairs={{0,256},{256,0},{1,257},{257,1},{2,258},{258,2},{3,259},{259,3},{4... | collective-permute-start | bytes 1769480 | tf_op jit(solution)/shard_map/ppermute | solution.py:217
  178.0 28.9 %collective-permute-done.20 = bf16[192,1536]{1,0:T(8,128)(2,1)S(1)} collective-permute-done((bf16[192,1536]{1,0:T(8,128)(2,1)S(1)}, bf16[192,1536]{1,0:T(8,128)(2,1)S(1)}, u32[]{:S(2)}, u32[]{:S(2)}) %collective-permute-start.20) | collective-permute-done | bytes 589856 | tf_op jit(solution)/shard_map/ppermute | solution.py:217
  (62 shorter events, 36.4 us)
Async XLA Ops:
  0.6 14.7 %collective-permute-start = (bf16[192,128]{1,0:T(8,128)(2,1)}, bf16[192,128]{1,0:T(8,128)(2,1)S(1)}, u32[]{:S(2)}, u32[]{:S(2)}) collective-permute-start(bf16[192,128]{1,0:T(8,128)(2,1)} %bitcast.43), channel_id=1, source_target_pairs={{0,0},{16,1},{14,2},{30,3},{15,4},{31,5},{12,6},{28,7},{13,8},{29,... | collective-permute-start | bytes 147464 | tf_op jit(solution)/shard_map/ppermute | solution.py:181
  7.1 11.4 %collective-permute-start.1 = (bf16[192,128]{1,0:T(8,128)(2,1)}, bf16[192,128]{1,0:T(8,128)(2,1)S(1)}, u32[]{:S(2)}, u32[]{:S(2)}) collective-permute-start(bf16[192,128]{1,0:T(8,128)(2,1)} %bitcast.44), channel_id=1, source_target_pairs={{0,0},{1,1},{224,2},{225,3},{240,4},{241,5},{192,6},{193,7},{208,8... | collective-permute-start | bytes 147464 | tf_op jit(solution)/shard_map/ppermute | solution.py:182
  19.9 10.7 %copy-start = (bf16[192,1536]{1,0:T(8,128)(2,1)S(1)}, bf16[192,1536]{1,0:T(8,128)(2,1)}, u32[]{:S(2)}) copy-start(bf16[192,1536]{1,0:T(8,128)(2,1)} %refs_0_.1) | copy-start | bytes 1769476
  19.9 62.7 %all-to-all-start = ((bf16[16,384,128]{2,1,0:T(8,128)(2,1)}), bf16[16,384,128]{2,1,0:T(8,128)(2,1)}, u32[]{:S(2)}, u32[]{:S(2)}) async-start(bf16[16,384,128]{2,1,0:T(8,128)(2,1)} %shard_map.58), calls=%async_computation | async-start | bytes 3145728 | tf_op jit(solution)/shard_map/all_to_all | solution.py:183
  30.6 16.6 %collective-permute-start.2 = (bf16[192,1536]{1,0:T(8,128)(2,1)S(1)}, bf16[192,1536]{1,0:T(8,128)(2,1)S(1)}, u32[]{:S(2)}, u32[]{:S(2)}) collective-permute-start(bf16[192,1536]{1,0:T(8,128)(2,1)S(1)} %copy-done), channel_id=1, source_target_pairs={{0,32},{16,240},{32,64},{48,16},{64,96},{80,48},{96,128},{112,80},... | collective-permute-start | bytes 1769480 | tf_op jit(solution)/shard_map/ppermute | solution.py:69
  32.6 17.4 %collective-permute-start.3 = (bf16[192,1536]{1,0:T(8,128)(2,1)S(1)}, bf16[192,1536]{1,0:T(8,128)(2,1)S(1)}, u32[]{:S(2)}, u32[]{:S(2)}) collective-permute-start(bf16[192,1536]{1,0:T(8,128)(2,1)S(1)} %copy-done), channel_id=1, source_target_pairs={{16,32},{0,240},{48,64},{32,16},{80,96},{64,48},{112,128},{96,80},... | collective-permute-start | bytes 1769480 | tf_op jit(solution)/shard_map/ppermute | solution.py:72
  47.3 33.4 %copy-start.1 = (bf16[192,1536]{1,0:T(8,128)(2,1)}, bf16[192,1536]{1,0:T(8,128)(2,1)S(1)}, u32[]{:S(2)}) copy-start(bf16[192,1536]{1,0:T(8,128)(2,1)S(1)} %collective-permute-done.2.refs_1_) | copy-start | bytes 1769476
  47.3 14.1 %collective-permute-start.4 = (bf16[192,1536]{1,0:T(8,128)(2,1)S(1)}, bf16[192,1536]{1,0:T(8,128)(2,1)S(1)}, u32[]{:S(2)}, u32[]{:S(2)}) collective-permute-start(bf16[192,1536]{1,0:T(8,128)(2,1)S(1)} %collective-permute-done.2.refs_1_), channel_id=1, source_target_pairs={{0,32},{16,240},{32,64},{48,16},{64,96},{80,48},{96,128},{112,80},... | collective-permute-start | bytes 1769480 | tf_op jit(solution)/shard_map/ppermute | solution.py:69
  49.9 30.7 %copy-start.3 = (bf16[192,1536]{1,0:T(8,128)(2,1)}, bf16[192,1536]{1,0:T(8,128)(2,1)S(1)}, u32[]{:S(2)}) copy-start(bf16[192,1536]{1,0:T(8,128)(2,1)S(1)} %collective-permute-done.3.refs_2_) | copy-start | bytes 1769476
  49.9 17.7 %collective-permute-start.5 = (bf16[192,1536]{1,0:T(8,128)(2,1)S(1)}, bf16[192,1536]{1,0:T(8,128)(2,1)S(1)}, u32[]{:S(2)}, u32[]{:S(2)}) collective-permute-start(bf16[192,1536]{1,0:T(8,128)(2,1)S(1)} %collective-permute-done.3.refs_2_), channel_id=1, source_target_pairs={{0,32},{16,240},{32,64},{48,16},{64,96},{80,48},{96,128},{112,80},... | collective-permute-start | bytes 1769480 | tf_op jit(solution)/shard_map/ppermute | solution.py:72
  61.4 13.0 %collective-permute-start.6 = (bf16[192,1536]{1,0:T(8,128)(2,1)S(1)}, bf16[192,1536]{1,0:T(8,128)(2,1)S(1)}, u32[]{:S(2)}, u32[]{:S(2)}) collective-permute-start(bf16[192,1536]{1,0:T(8,128)(2,1)S(1)} %collective-permute-done.4.refs_3_), channel_id=1, source_target_pairs={{0,32},{16,240},{32,64},{48,16},{64,96},{80,48},{96,128},{112,80},... | collective-permute-start | bytes 1769480 | tf_op jit(solution)/shard_map/ppermute | solution.py:69
  67.7 13.0 %collective-permute-start.7 = (bf16[192,1536]{1,0:T(8,128)(2,1)S(1)}, bf16[192,1536]{1,0:T(8,128)(2,1)S(1)}, u32[]{:S(2)}, u32[]{:S(2)}) collective-permute-start(bf16[192,1536]{1,0:T(8,128)(2,1)S(1)} %collective-permute-done.5.refs_4_), channel_id=1, source_target_pairs={{0,32},{16,240},{32,64},{48,16},{64,96},{80,48},{96,128},{112,80},... | collective-permute-start | bytes 1769480 | tf_op jit(solution)/shard_map/ppermute | solution.py:72
  80.7 13.0 %collective-permute-start.8 = (bf16[192,1536]{1,0:T(8,128)(2,1)S(1)}, bf16[192,1536]{1,0:T(8,128)(2,1)S(1)}, u32[]{:S(2)}, u32[]{:S(2)}) collective-permute-start(bf16[192,1536]{1,0:T(8,128)(2,1)S(1)} %collective-permute-done.6.refs_5_), channel_id=1, source_target_pairs={{0,32},{16,240},{32,64},{48,16},{64,96},{80,48},{96,128},{112,80},... | collective-permute-start | bytes 1769480 | tf_op jit(solution)/shard_map/ppermute | solution.py:69
  84.2 1.1 copy-start.2
  94.4 4.1 %copy-start.13 = (bf16[128,1536]{1,0:T(8,128)(2,1)S(1)}, bf16[128,1536]{1,0:T(8,128)(2,1)}, u32[]{:S(2)}) copy-start(bf16[128,1536]{1,0:T(8,128)(2,1)} %param.5) | copy-start | bytes 1179652
  94.9 3.6 %collective-permute-start.9 = (bf16[128,1536]{1,0:T(8,128)(2,1)S(1)}, bf16[128,1536]{1,0:T(8,128)(2,1)S(1)}, u32[]{:S(2)}, u32[]{:S(2)}) collective-permute-start(bf16[128,1536]{1,0:T(8,128)(2,1)S(1)} %slice.141), channel_id=1, source_target_pairs={{0,16},{16,0},{32,48},{48,32},{64,80},{80,64},{96,112},{112,96},{1... | collective-permute-start | bytes 1179656 | tf_op jit(solution)/shard_map/ppermute | solution.py:78
  99.7 13.7 %collective-permute-start.10 = (bf16[128,1536]{1,0:T(8,128)(2,1)S(1)}, bf16[128,1536]{1,0:T(8,128)(2,1)S(1)}, u32[]{:S(2)}, u32[]{:S(2)}) collective-permute-start(bf16[128,1536]{1,0:T(8,128)(2,1)S(1)} %get-tuple-element.12.own_ref.refs_0_), channel_id=1, source_target_pairs={{0,32},{16,240},{32,64},{48,16},{64,96},{80,48},{96,128},{112,80},... | collective-permute-start | bytes 1179656 | tf_op jit(solution)/shard_map/ppermute | solution.py:69
  101.6 13.2 %collective-permute-start.11 = (bf16[128,1536]{1,0:T(8,128)(2,1)S(1)}, bf16[128,1536]{1,0:T(8,128)(2,1)S(1)}, u32[]{:S(2)}, u32[]{:S(2)}) collective-permute-start(bf16[128,1536]{1,0:T(8,128)(2,1)S(1)} %get-tuple-element.12.own_ref.refs_0_), channel_id=1, source_target_pairs={{16,32},{0,240},{48,64},{32,16},{80,96},{64,48},{112,128},{96,80},... | collective-permute-start | bytes 1179656 | tf_op jit(solution)/shard_map/ppermute | solution.py:72
  104.9 10.6 %collective-permute-start.12 = (bf16[128,1536]{1,0:T(8,128)(2,1)S(1)}, bf16[128,1536]{1,0:T(8,128)(2,1)S(1)}, u32[]{:S(2)}, u32[]{:S(2)}) collective-permute-start(bf16[128,1536]{1,0:T(8,128)(2,1)S(1)} %get-tuple-element.12.own_ref.refs_0_), channel_id=1, source_target_pairs={{0,16},{16,0},{32,48},{48,32},{64,80},{80,64},{96,112},{112,96},{1... | collective-permute-start | bytes 1179656 | tf_op jit(solution)/shard_map/ppermute | solution.py:78
  113.4 1.4 copy-start.7
  119.8 7.7 %copy-start.8 = (bf16[128,1536]{1,0:T(8,128)(2,1)S(1)}, bf16[128,1536]{1,0:T(8,128)(2,1)}, u32[]{:S(2)}) copy-start(bf16[128,1536]{1,0:T(8,128)(2,1)} %copy-done.7) | copy-start | bytes 1179652
  119.8 9.7 %copy-start.10 = (bf16[128,1536]{1,0:T(8,128)(2,1)S(1)}, bf16[128,1536]{1,0:T(8,128)(2,1)}, u32[]{:S(2)}) copy-start(bf16[128,1536]{1,0:T(8,128)(2,1)} %copy-done.9) | copy-start | bytes 1179652
  119.8 36.9 %all-to-all-start.1 = ((bf16[16,192,128]{2,1,0:T(8,128)(2,1)}), bf16[16,192,128]{2,1,0:T(8,128)(2,1)}, u32[]{:S(2)}, u32[]{:S(2)}) async-start(bf16[16,192,128]{2,1,0:T(8,128)(2,1)} %shard_map.59), calls=%async_computation.1 | async-start | bytes 1572864 | tf_op jit(solution)/shard_map/all_to_all | solution.py:203
  127.5 35.7 %copy-start.6 = (bf16[128,1536]{1,0:T(8,128)(2,1)S(1)}, bf16[128,1536]{1,0:T(8,128)(2,1)}, u32[]{:S(2)}) copy-start(bf16[128,1536]{1,0:T(8,128)(2,1)} %copy-done.5) | copy-start | bytes 1179652
  127.5 11.0 %collective-permute-start.14 = (bf16[128,1536]{1,0:T(8,128)(2,1)S(1)}, bf16[128,1536]{1,0:T(8,128)(2,1)S(1)}, u32[]{:S(2)}, u32[]{:S(2)}) collective-permute-start(bf16[128,1536]{1,0:T(8,128)(2,1)S(1)} %copy-done.8), channel_id=1, source_target_pairs={{0,32},{16,240},{32,64},{48,16},{64,96},{80,48},{96,128},{112,80},... | collective-permute-start | bytes 1179656 | tf_op jit(solution)/shard_map/ppermute | solution.py:69
  129.5 13.2 %collective-permute-start.16 = (bf16[128,1536]{1,0:T(8,128)(2,1)S(1)}, bf16[128,1536]{1,0:T(8,128)(2,1)S(1)}, u32[]{:S(2)}, u32[]{:S(2)}) collective-permute-start(bf16[128,1536]{1,0:T(8,128)(2,1)S(1)} %copy-done.10), channel_id=1, source_target_pairs={{0,32},{16,240},{32,64},{48,16},{64,96},{80,48},{96,128},{112,80},... | collective-permute-start | bytes 1179656 | tf_op jit(solution)/shard_map/ppermute | solution.py:72
  138.5 10.9 %collective-permute-start.15 = (bf16[128,1536]{1,0:T(8,128)(2,1)S(1)}, bf16[128,1536]{1,0:T(8,128)(2,1)S(1)}, u32[]{:S(2)}, u32[]{:S(2)}) collective-permute-start(bf16[128,1536]{1,0:T(8,128)(2,1)S(1)} %collective-permute-done.14.refs_3_), channel_id=1, source_target_pairs={{0,32},{16,240},{32,64},{48,16},{64,96},{80,48},{96,128},{112,80},... | collective-permute-start | bytes 1179656 | tf_op jit(solution)/shard_map/ppermute | solution.py:69
  142.7 10.9 %collective-permute-start.17 = (bf16[128,1536]{1,0:T(8,128)(2,1)S(1)}, bf16[128,1536]{1,0:T(8,128)(2,1)S(1)}, u32[]{:S(2)}, u32[]{:S(2)}) collective-permute-start(bf16[128,1536]{1,0:T(8,128)(2,1)S(1)} %collective-permute-done.16.refs_4_), channel_id=1, source_target_pairs={{0,32},{16,240},{32,64},{48,16},{64,96},{80,48},{96,128},{112,80},... | collective-permute-start | bytes 1179656 | tf_op jit(solution)/shard_map/ppermute | solution.py:72
  153.6 12.3 %collective-permute-start.18 = (bf16[128,1536]{1,0:T(8,128)(2,1)S(1)}, bf16[128,1536]{1,0:T(8,128)(2,1)S(1)}, u32[]{:S(2)}, u32[]{:S(2)}) collective-permute-start(bf16[128,1536]{1,0:T(8,128)(2,1)S(1)} %collective-permute-done.15.refs_0_), channel_id=1, source_target_pairs={{0,32},{16,240},{32,64},{48,16},{64,96},{80,48},{96,128},{112,80},... | collective-permute-start | bytes 1179656 | tf_op jit(solution)/shard_map/ppermute | solution.py:69
  158.6 9.5 %collective-permute-start.13 = (bf16[192,128]{1,0:T(8,128)(2,1)}, bf16[192,128]{1,0:T(8,128)(2,1)S(1)}, u32[]{:S(2)}, u32[]{:S(2)}) collective-permute-start(bf16[192,128]{1,0:T(8,128)(2,1)} %reduce_sum.12), channel_id=1, source_target_pairs={{0,0},{1,16},{2,14},{3,30},{4,15},{5,31},{6,12},{7,28},{8,13},{9,2... | collective-permute-start | bytes 147464 | tf_op jit(solution)/shard_map/ppermute | solution.py:205
  169.1 3.9 %collective-permute-start.19 = (bf16[192,1536]{1,0:T(8,128)(2,1)S(1)}, bf16[192,1536]{1,0:T(8,128)(2,1)S(1)}, u32[]{:S(2)}, u32[]{:S(2)}) collective-permute-start(bf16[192,1536]{1,0:T(8,128)(2,1)S(1)} %get-tuple-element.18), channel_id=1, source_target_pairs={{0,16},{16,0},{32,48},{48,32},{64,80},{80,64},{96,112},{112,96},{1... | collective-permute-start | bytes 1769480 | tf_op jit(solution)/shard_map/ppermute | solution.py:78
  173.1 33.8 %collective-permute-start.20 = (bf16[192,1536]{1,0:T(8,128)(2,1)S(1)}, bf16[192,1536]{1,0:T(8,128)(2,1)S(1)}, u32[]{:S(2)}, u32[]{:S(2)}) collective-permute-start(bf16[192,1536]{1,0:T(8,128)(2,1)S(1)} %add_convert_fusion), channel_id=1, source_target_pairs={{0,256},{256,0},{1,257},{257,1},{2,258},{258,2},{3,259},{259,3},{4... | collective-permute-start | bytes 1769480 | tf_op jit(solution)/shard_map/ppermute | solution.py:217
  (5 other events, 4.4 us)

commit v7 on v1

v7 whole, which is shorter than its diff:
```python
import functools
import math

import jax
import jax.numpy as jnp
from jax import lax
from jax.experimental import pallas as pl
from jax.experimental.pallas import tpu as pltpu
from jax.sharding import PartitionSpec as P

ROWS = 16
COLS = 16
LANES = 256
VMEM_BYTES = 32 * 2**20


def after(value, *others):
    return lax.optimization_barrier((value,) + others)[0]


def local_kernel(kernel, out_shape, flops, operands):
    moved = sum(x.size * x.dtype.itemsize for x in (*operands, out_shape))
    return pl.pallas_call(
        kernel,
        out_shape=out_shape,
        in_specs=[pl.BlockSpec(memory_space=pltpu.VMEM)] * len(operands),
        out_specs=pl.BlockSpec(memory_space=pltpu.VMEM),
        compiler_params=pltpu.CompilerParams(vmem_limit_bytes=VMEM_BYTES),
        cost_estimate=pl.CostEstimate(flops=flops, bytes_accessed=moved, transcendentals=0),
    )(*operands)


def input_grad_kernel(weight_ref, grad_ref, pieces_ref):
    depth = pieces_ref.shape[1]
    for col in range(COLS):
        pieces_ref[col] = lax.dot_general(
            weight_ref[pl.ds(col * depth, depth), :],
            grad_ref[...],
            (((1,), (1,)), ((), ())),
            preferred_element_type=jnp.float32,
        ).astype(jnp.bfloat16)


def input_grad_pieces(weight, grad):
    tokens, hidden_units = grad.shape
    depth = weight.shape[0] // COLS
    out_shape = jax.ShapeDtypeStruct((COLS, depth, tokens), jnp.bfloat16)
    flops = 2 * weight.size * tokens
    return local_kernel(input_grad_kernel, out_shape, flops, (weight, grad))


def token_sum_kernel(block_ref, grad_ref, total_ref):
    rows, _, tokens = block_ref.shape
    for start in range(0, total_ref.shape[1], LANES):
        units = pl.ds(start, LANES)
        total = None
        for row in range(rows):
            term = jnp.dot(
                block_ref[row],
                grad_ref[pl.ds(row * tokens, tokens), units],
                preferred_element_type=jnp.float32,
            )
            total = term if total is None else total + term
        total_ref[:, units] = total.astype(total_ref.dtype)


def token_sum(blocks, grads):
    depth = blocks.shape[1]
    out_shape = jax.ShapeDtypeStruct((depth, grads.shape[1]), jnp.bfloat16)
    flops = 2 * depth * grads.size
    return local_kernel(token_sum_kernel, out_shape, flops, (blocks, grads))


def per_device(features, up_weight, out_grad):
    tokens, depth = features.shape
    features = features.T
    weight = lax.all_gather(up_weight, "row", axis=0, tiled=True)
    swap = [(r * COLS + c, c * COLS + r) for r in range(ROWS) for c in range(COLS)]
    turned = lax.ppermute(features, ("row", "col"), swap)
    block = jnp.concatenate([features, turned], axis=0)
    copies = jnp.broadcast_to(block[None], (COLS,) + block.shape)
    both_ways = lax.all_to_all(copies, "col", 0, 0, tiled=True)
    by_depth = both_ways[:, :depth].reshape(COLS * depth, tokens)
    by_token = both_ways[:, depth:]

    hidden = lax.dot_general(
        by_depth, weight, (((0,), (0,)), ((), ())), preferred_element_type=jnp.float32
    )
    normal_cdf = 0.5 * (1.0 + jax.scipy.special.erf(hidden / math.sqrt(2.0)))
    density = jnp.exp(-0.5 * hidden * hidden) / math.sqrt(2.0 * math.pi)
    gelu_out = (hidden * normal_cdf).astype(jnp.bfloat16)
    hidden_grad = (out_grad.astype(jnp.float32) * (normal_cdf + hidden * density)).astype(
        jnp.bfloat16
    )
    grads = lax.all_gather(hidden_grad, "row", axis=0, tiled=True)

    pieces = input_grad_pieces(weight, hidden_grad)
    pieces = lax.all_to_all(pieces, "col", 0, 0, tiled=True)
    feature_grad = jnp.sum(pieces.astype(jnp.float32), axis=0).astype(jnp.bfloat16)

    own = token_sum(by_token, after(grads, feature_grad))
    replica = lax.ppermute(own, "dp", [(0, 1), (1, 0)])
    weight_grad = own.astype(jnp.float32) + replica.astype(jnp.float32)
    return (gelu_out, feature_grad.T, weight_grad)


def solution(mesh):
    placed = (P(("dp", "row"), "col"), P("row", "col"), P(("dp", "row"), "col"))
    return jax.shard_map(
        per_device,
        mesh=mesh,
        in_specs=placed,
        out_specs=(P(("dp", "row"), "col"), P(("dp", "row"), "col"), P("row", "col")),
        check_vma=False,
    )
```

time: 202 us -> 181 us (0.90)
  the two profiles are of different devices: /device:TPU:128 before, /device:TPU:17 now
where the time goes in v7:
time: 181 us; the launch traced here: 180 us
  blocking collectives  70.2 us (39%)
  waiting for transfers between devices  56.7 us (31%)
  starting transfers between devices  17.3 us (10%)
  between operations  14.1 us (8%)
  local copies, waits for them, and re-layouts  7.86 us (4%)
  matrix products  6.28 us (3%)
  Pallas kernels  5.16 us (3%)
  other arithmetic  2.71 us (1%)
    all_to_all x1, blocking collectives, per_device(): both_ways = lax.all_to_all(copies, 'col', 0, 0, tiled=True)  43.2 us
    ppermute x1, waiting for transfers between devices, per_device(): replica = lax.ppermute(own, 'dp', [(0, 1), (1, 0)])  28.4 us
    all_to_all x1, blocking collectives, per_device(): pieces = lax.all_to_all(pieces, 'col', 0, 0, tiled=True)  27 us
    all_gather x1, waiting for transfers between devices, per_device(): grads = lax.all_gather(hidden_grad, 'row', axis=0, tiled=True)  12.6 us
    all_gather x1, waiting for transfers between devices, per_device(): weight = lax.all_gather(up_weight, 'row', axis=0, tiled=True)  12.4 us
    ppermute x1, starting transfers between devices, per_device(): turned = lax.ppermute(features, ('row', 'col'), swap)  11.9 us
    unnamed x8, local copies, waits for them, and re-layouts  7.46 us
    dot_general x1, matrix products, per_device(): lax.dot_general(by_depth, weight, (((0,), (0,)), ((), ())), preferred_ele...  6.28 us
  transfers between devices with their start and end apart: 4, of which 4 were waited for; matrix products, arithmetic and copies ran while one was open for 1% of the time, Pallas kernels for 1%

profile of v7, /device:TPU:17, one launch (start us, length us, event | category | flops | bytes accessed | tf_op | source)
XLA Modules:
  0.0 180.3 jit_solution(13610489248964303403)
XLA Ops:
  7.2 0.0 all-gather.3.cloned.1.call-start
  7.2 0.7 all-gather.3.cloned.1.call-update
  7.9 0.0 all-gather.5.cloned.1.call-start
  7.9 11.9 %collective-permute-start = (bf16[192,128]{1,0:T(8,128)(2,1)}, bf16[192,128]{1,0:T(8,128)(2,1)S(1)}, u32[]{:S(2)}, u32[]{:S(2)}) collective-permute-start(bf16[192,128]{1,0:T(8,128)(2,1)} %bitcast.7), channel_id=1, source_target_pairs={{0,0},{1,16},{2,32},{3,48},{4,64},{5,80},{6,96},{7,112},{8,128},{9... | collective-permute-start | bytes 147464 | tf_op jit(solution)/shard_map/ppermute | solution.py:79
  19.8 2.7 %collective-permute-done = bf16[192,128]{1,0:T(8,128)(2,1)S(1)} collective-permute-done((bf16[192,128]{1,0:T(8,128)(2,1)}, bf16[192,128]{1,0:T(8,128)(2,1)S(1)}, u32[]{:S(2)}, u32[]{:S(2)}) %collective-permute-start) | collective-permute-done | bytes 49184 | tf_op jit(solution)/shard_map/ppermute | solution.py:79
  22.5 0.8 pad_maximum_fusion
  23.3 0.3 broadcast_in_dim.2
  23.6 43.2 %all_to_all.10 = bf16[16,384,128]{2,1,0:T(8,128)(2,1)S(1)} all-to-all(bf16[16,384,128]{2,1,0:T(8,128)(2,1)S(1)} %broadcast_in_dim.2), channel_id=1, replica_groups=mesh['dp'=2,'row'=16,'col'=16] {'col'}, dimensions={0} | all-to-all | bytes 3145728 | tf_op jit(solution)/shard_map/all_to_all | solution.py:82
  66.8 0.0 copy-start.3
  66.9 0.1 fusion.6
  67.0 12.4 %all-gather.3.cloned.1.call-done.weight_ref = bf16[3072,1536]{1,0:T(8,128)(2,1)} async-done(((bf16[192,1536]{1,0:T(8,128)(2,1)}), bf16[3072,1536]{1,0:T(8,128)(2,1)}) %all-gather.3.cloned.1.call-update) | async-done | bytes 9437200 | tf_op jit(solution)/shard_map/all_gather | solution.py:77
  79.3 0.0 copy-done.3
  79.3 6.3 %fusion.5 = (bf16[128,1536]{1,0:T(8,128)(2,1)}, bf16[128,1536]{1,0:T(8,128)(2,1)}) fusion(bf16[128,1536]{1,0:T(8,128)(2,1)S(1)} %copy-done.3, bf16[3072,128]{1,0:T(8,128)(2,1)S(1)} %bitcast.5, bf16[3072,1536]{1,0:T(8,128)(2,1)} %all-gather.3.cloned.1.call-done.weight_ref), kind=kOutput, calls=%fused_computation.7 | convolution fusion | flops 1210515456 | bytes 11403264 | tf_op jit(solution)/shard_map/dot_general | solution.py:86
  85.6 0.0 all-gather.5.cloned.1.call-update
  85.6 0.0 copy-start
  85.6 3.7 %copy-done = bf16[3072,1536]{1,0:T(8,128)(2,1)S(1)} copy-done((bf16[3072,1536]{1,0:T(8,128)(2,1)S(1)}, bf16[3072,1536]{1,0:T(8,128)(2,1)}, u32[]{:S(2)}) %copy-start) | copy-done | bytes 9437208
  89.3 0.0 copy-start.2
  89.3 1.0 copy-done.2
  90.3 2.6 %shard_map.58 = bf16[16,192,128]{2,1,0:T(8,128)(2,1)S(1)} custom-call(bf16[3072,1536]{1,0:T(8,128)(2,1)S(1)} %copy-done, bf16[128,1536]{1,0:T(8,128)(2,1)S(1)} %copy-done.2), custom_call_target="tpu_custom_call" | custom-call | flops 1207959552 | bytes 10616832 | tf_op jit(solution)/shard_map/pallas_call | solution.py:23
  92.9 27.0 %all_to_all.11 = bf16[16,192,128]{2,1,0:T(8,128)(2,1)S(1)} all-to-all(bf16[16,192,128]{2,1,0:T(8,128)(2,1)S(1)} %shard_map.58), channel_id=1, replica_groups=mesh['dp'=2,'row'=16,'col'=16] {'col'}, dimensions={0} | all-to-all | bytes 1572864 | tf_op jit(solution)/shard_map/all_to_all | solution.py:98
  119.9 0.7 reduce_sum.12
  120.7 12.6 %all-gather.5.cloned.1.call-done.grad_ref = bf16[2048,1536]{1,0:T(8,128)(2,1)} async-done(((bf16[128,1536]{1,0:T(8,128)(2,1)}), bf16[2048,1536]{1,0:T(8,128)(2,1)}) %all-gather.5.cloned.1.call-update) | async-done | bytes 6291472 | tf_op jit(solution)/shard_map/all_gather | solution.py:95
  133.3 0.0 copy-start.1
  133.3 2.8 %copy-done.1 = bf16[2048,1536]{1,0:T(8,128)(2,1)S(1)} copy-done((bf16[2048,1536]{1,0:T(8,128)(2,1)S(1)}, bf16[2048,1536]{1,0:T(8,128)(2,1)}, u32[]{:S(2)}) %copy-start.1) | copy-done | bytes 6291480
  136.1 2.6 %shard_map.59 = bf16[192,1536]{1,0:T(8,128)(2,1)S(1)} custom-call(bf16[16,192,128]{2,1,0:T(8,128)(2,1)S(1)} %get-tuple-element.5.block_ref, bf16[2048,1536]{1,0:T(8,128)(2,1)S(1)} %copy-done.1), custom_call_target="tpu_custom_call" | custom-call | flops 1207959552 | bytes 7667712 | tf_op jit(solution)/shard_map/pallas_call | solution.py:23
  138.6 5.3 %collective-permute-start.1 = (bf16[192,1536]{1,0:T(8,128)(2,1)S(1)}, bf16[192,1536]{1,0:T(8,128)(2,1)S(1)}, u32[]{:S(2)}, u32[]{:S(2)}) collective-permute-start(bf16[192,1536]{1,0:T(8,128)(2,1)S(1)} %shard_map.59), channel_id=1, source_target_pairs={{0,256},{256,0},{1,257},{257,1},{2,258},{258,2},{3,259},{259,3},{4... | collective-permute-start | bytes 1769480 | tf_op jit(solution)/shard_map/ppermute | solution.py:102
  144.0 28.4 %collective-permute-done.1 = bf16[192,1536]{1,0:T(8,128)(2,1)S(1)} collective-permute-done((bf16[192,1536]{1,0:T(8,128)(2,1)S(1)}, bf16[192,1536]{1,0:T(8,128)(2,1)S(1)}, u32[]{:S(2)}, u32[]{:S(2)}) %collective-permute-start.1) | collective-permute-done | bytes 589856 | tf_op jit(solution)/shard_map/ppermute | solution.py:102
  172.3 1.2 convert_add_fusion
Async XLA Ops:
  7.2 72.2 %all-gather.3.cloned.1.call-start = ((), (), s32[]{:S(2)}) async-start(), calls=%async_computation.2 | async-start | bytes 10027008 | tf_op jit(solution)/shard_map/all_gather | solution.py:77
  7.9 125.4 %all-gather.5.cloned.1.call-start = ((), (), s32[]{:S(2)}) async-start(), calls=%async_computation.3 | async-start | bytes 6684672 | tf_op jit(solution)/shard_map/all_gather | solution.py:95
  7.9 14.6 %collective-permute-start = (bf16[192,128]{1,0:T(8,128)(2,1)}, bf16[192,128]{1,0:T(8,128)(2,1)S(1)}, u32[]{:S(2)}, u32[]{:S(2)}) collective-permute-start(bf16[192,128]{1,0:T(8,128)(2,1)} %bitcast.7), channel_id=1, source_target_pairs={{0,0},{1,16},{2,32},{3,48},{4,64},{5,80},{6,96},{7,112},{8,128},{9... | collective-permute-start | bytes 147464 | tf_op jit(solution)/shard_map/ppermute | solution.py:79
  66.8 12.5 %copy-start.3 = (bf16[128,1536]{1,0:T(8,128)(2,1)S(1)}, bf16[128,1536]{1,0:T(8,128)(2,1)}, u32[]{:S(2)}) copy-start(bf16[128,1536]{1,0:T(8,128)(2,1)} %param.5) | copy-start | bytes 1179652
  85.6 3.7 %copy-start = (bf16[3072,1536]{1,0:T(8,128)(2,1)S(1)}, bf16[3072,1536]{1,0:T(8,128)(2,1)}, u32[]{:S(2)}) copy-start(bf16[3072,1536]{1,0:T(8,128)(2,1)} %all-gather.3.cloned.1.call-done.weight_ref) | copy-start | bytes 28311556
  89.3 1.0 copy-start.2
  133.3 2.8 %copy-start.1 = (bf16[2048,1536]{1,0:T(8,128)(2,1)S(1)}, bf16[2048,1536]{1,0:T(8,128)(2,1)}, u32[]{:S(2)}) copy-start(bf16[2048,1536]{1,0:T(8,128)(2,1)} %all-gather.5.cloned.1.call-done.grad_ref) | copy-start | bytes 18874372
  138.6 33.7 %collective-permute-start.1 = (bf16[192,1536]{1,0:T(8,128)(2,1)S(1)}, bf16[192,1536]{1,0:T(8,128)(2,1)S(1)}, u32[]{:S(2)}, u32[]{:S(2)}) collective-permute-start(bf16[192,1536]{1,0:T(8,128)(2,1)S(1)} %shard_map.59), channel_id=1, source_target_pairs={{0,256},{256,0},{1,257},{257,1},{2,258},{258,2},{3,259},{259,3},{4... | collective-permute-start | bytes 1769480 | tf_op jit(solution)/shard_map/ppermute | solution.py:102
Sparse Core Ops, SparseCore 0:
  10.1 69.1 all-gather.2
  85.8 47.4 all-gather.4

commit v8 on v7

v8 whole, which is shorter than its diff:
```python
import math

import jax
import jax.numpy as jnp
from jax import lax
from jax.experimental import pallas as pl
from jax.experimental.pallas import tpu as pltpu
from jax.sharding import PartitionSpec as P

ROWS = 16
COLS = 16
CHIPS = ROWS // 2
ROUNDS = CHIPS // 2
EARLY = 5
LANES = 256
RING_UNITS = 768
VMEM_BYTES = 32 * 2**20


def after(value, *others):
    return lax.optimization_barrier((value,) + others)[0]


def held_from(chip, core, slot):
    steps = (slot + 1) // 2
    parity = core if slot % 2 or slot == 0 else 1 - core
    away = -steps if core == 0 else steps
    return 2 * ((chip + away) % CHIPS) + parity


def places():
    table = []
    for row in range(ROWS):
        chip, core = divmod(row, 2)
        mine = [held_from(chip, core, slot) for slot in range(CHIPS)]
        other = [held_from(chip, 1 - core, slot) for slot in range(CHIPS)]
        table.append(mine + other)
    return jnp.array(table, jnp.int32)[lax.axis_index("row")]


def ring_moves(cross):
    moves = []
    for chip in range(CHIPS):
        moves.append((2 * chip + cross, 2 * ((chip + 1) % CHIPS)))
        moves.append((2 * chip + 1 - cross, 2 * ((chip - 1) % CHIPS) + 1))
    return moves


def to_other_core(value):
    return lax.ppermute(value, "row", [(row, row ^ 1) for row in range(ROWS)])


def ring_gather(block):
    mine = [block]
    same = cross = block
    for step in range(1, ROUNDS + 1):
        if step == ROUNDS:
            same = after(same, cross)
        same = lax.ppermute(same, "row", ring_moves(0))
        mine.append(same)
        if step < ROUNDS:
            cross = lax.ppermute(cross, "row", ring_moves(1 if step == 1 else 0))
            mine.append(cross)
    early = to_other_core(jnp.concatenate(mine[:EARLY]))
    late = to_other_core(jnp.concatenate(mine[EARLY:]))
    return mine + [early, late]


def ring_blocks(refs, depth):
    *mine, early, late = refs
    for ref in mine:
        yield ref[...]
    for stack in (early, late):
        for start in range(0, stack.shape[0], depth):
            yield stack[pl.ds(start, depth), :]


def local_kernel(kernel, out_shape, flops, operands, indices=None):
    moved = sum(x.size * x.dtype.itemsize for x in (*operands, out_shape))
    in_specs = [pl.BlockSpec(memory_space=pltpu.VMEM)] * len(operands)
    if indices is not None:
        in_specs = [pl.BlockSpec(memory_space=pltpu.SMEM)] + in_specs
        operands = (indices, *operands)
    return pl.pallas_call(
        kernel,
        out_shape=out_shape,
        in_specs=in_specs,
        out_specs=pl.BlockSpec(memory_space=pltpu.VMEM),
        compiler_params=pltpu.CompilerParams(vmem_limit_bytes=VMEM_BYTES),
        cost_estimate=pl.CostEstimate(flops=flops, bytes_accessed=moved, transcendentals=0),
    )(*operands)


def ring_hidden_kernel(place_ref, by_depth_ref, *refs):
    *weight_refs, hidden_ref = refs
    depth = by_depth_ref.shape[1]
    total = None
    for slot, weight in enumerate(ring_blocks(weight_refs, depth)):
        term = lax.dot_general(
            by_depth_ref[place_ref[slot]],
            weight,
            (((0,), (0,)), ((), ())),
            preferred_element_type=jnp.float32,
        )
        total = term if total is None else total + term
    hidden_ref[...] = total


def input_grad_kernel(place_ref, ring_grad_ref, grad_ref, weight_ref, *refs):
    *ring_refs, pieces_ref = refs
    depth = pieces_ref.shape[1]
    contract_last = (((1,), (1,)), ((), ()))
    for slot, ring_weight in enumerate(ring_blocks(ring_refs, depth)):
        place = place_ref[slot]
        start = pl.multiple_of(place * depth, depth)
        first = lax.dot_general(
            ring_weight, ring_grad_ref[...], contract_last, preferred_element_type=jnp.float32
        )
        second = lax.dot_general(
            weight_ref[pl.ds(start, depth), :],
            grad_ref[...],
            contract_last,
            preferred_element_type=jnp.float32,
        )
        pieces_ref[place] = (first + second).astype(jnp.bfloat16)


def ring_sum_kernel(place_ref, by_token_ref, *refs):
    *grad_refs, total_ref = refs
    tokens = by_token_ref.shape[2]
    total = None
    for slot, grad in enumerate(ring_blocks(grad_refs, tokens)):
        term = jnp.dot(by_token_ref[place_ref[slot]], grad, preferred_element_type=jnp.float32)
        total = term if total is None else total + term
    total_ref[...] = total.astype(total_ref.dtype)


def token_sum_kernel(by_token_ref, grad_ref, total_ref):
    rows, _, tokens = by_token_ref.shape
    for start in range(0, total_ref.shape[1], LANES):
        units = pl.ds(start, LANES)
        total = None
        for row in range(rows):
            term = jnp.dot(
                by_token_ref[row],
                grad_ref[pl.ds(row * tokens, tokens), units],
                preferred_element_type=jnp.float32,
            )
            total = term if total is None else total + term
        total_ref[:, units] = total.astype(total_ref.dtype)


def gelu_parts(hidden, out_grad):
    normal_cdf = 0.5 * (1.0 + jax.scipy.special.erf(hidden / math.sqrt(2.0)))
    density = jnp.exp(-0.5 * hidden * hidden) / math.sqrt(2.0 * math.pi)
    gelu_out = (hidden * normal_cdf).astype(jnp.bfloat16)
    hidden_grad = out_grad.astype(jnp.float32) * (normal_cdf + hidden * density)
    return gelu_out, hidden_grad.astype(jnp.bfloat16)


def replica_sum(own):
    replica = lax.ppermute(own, "dp", [(0, 1), (1, 0)])
    return own.astype(jnp.float32) + replica.astype(jnp.float32)


def per_device(features, up_weight, out_grad):
    tokens, depth = features.shape
    rest = up_weight.shape[1] - RING_UNITS
    place = places()
    features = features.T
    weight = lax.all_gather(up_weight[:, RING_UNITS:], "row", axis=0, tiled=True)
    ring_weight = ring_gather(up_weight[:, :RING_UNITS])
    swap = [(r * COLS + c, c * COLS + r) for r in range(ROWS) for c in range(COLS)]
    turned = lax.ppermute(features, ("row", "col"), swap)
    block = jnp.concatenate([features, turned], axis=0)
    copies = jnp.broadcast_to(block[None], (COLS,) + block.shape)
    both_ways = lax.all_to_all(copies, "col", 0, 0, tiled=True)
    by_depth, by_token = both_ways[:, :depth], both_ways[:, depth:]

    ring_hidden = local_kernel(
        ring_hidden_kernel,
        jax.ShapeDtypeStruct((tokens, RING_UNITS), jnp.float32),
        2 * tokens * ROWS * depth * RING_UNITS,
        (by_depth, *ring_weight),
        place,
    )
    ring_gelu, ring_grad = gelu_parts(ring_hidden, out_grad[:, :RING_UNITS])
    ring_grads = ring_gather(ring_grad)

    hidden = lax.dot_general(
        by_depth.reshape(COLS * depth, tokens),
        weight,
        (((0,), (0,)), ((), ())),
        preferred_element_type=jnp.float32,
    )
    gelu_out, grad = gelu_parts(hidden, out_grad[:, RING_UNITS:])
    grads = lax.all_gather(grad, "row", axis=0, tiled=True)

    pieces = local_kernel(
        input_grad_kernel,
        jax.ShapeDtypeStruct((COLS, depth, tokens), jnp.bfloat16),
        2 * tokens * ROWS * depth * (RING_UNITS + rest),
        (ring_grad, grad, weight, *ring_weight),
        place,
    )
    pieces = lax.all_to_all(pieces, "col", 0, 0, tiled=True)
    feature_grad = jnp.sum(pieces.astype(jnp.float32), axis=0).astype(jnp.bfloat16)

    ring_own = local_kernel(
        ring_sum_kernel,
        jax.ShapeDtypeStruct((depth, RING_UNITS), jnp.bfloat16),
        2 * tokens * ROWS * depth * RING_UNITS,
        (by_token, *ring_grads),
        place,
    )
    ring_total = replica_sum(ring_own)
    own = local_kernel(
        token_sum_kernel,
        jax.ShapeDtypeStruct((depth, rest), jnp.bfloat16),
        2 * tokens * ROWS * depth * rest,
        (by_token, after(grads, feature_grad)),
    )
    total = replica_sum(own)
    gelu_out = jnp.concatenate([ring_gelu, gelu_out], axis=1)
    weight_grad = jnp.concatenate([ring_total, total], axis=1)
    return (gelu_out, feature_grad.T, weight_grad)


def solution(mesh):
    placed = (P(("dp", "row"), "col"), P("row", "col"), P(("dp", "row"), "col"))
    return jax.shard_map(
        per_device,
        mesh=mesh,
        in_specs=placed,
        out_specs=(P(("dp", "row"), "col"), P(("dp", "row"), "col"), P("row", "col")),
        check_vma=False,
    )
```

time: 181 us -> 251 us (1.39)
  the two profiles are of different devices: /device:TPU:17 before, /device:TPU:1 now
where the time goes in v8:
time: 251 us; the launch traced here: 249 us
  starting transfers between devices  101 us (40%)
  blocking collectives  51.2 us (20%)
  waiting for transfers between devices  39.3 us (16%)
  local copies, waits for them, and re-layouts  22.5 us (9%)
  between operations  14.6 us (6%)
  Pallas kernels  11.3 us (5%)
  other arithmetic  5.75 us (2%)
  matrix products  4.06 us (2%)
    all_to_all x1, blocking collectives, per_device(): both_ways = lax.all_to_all(copies, 'col', 0, 0, tiled=True)  51.2 us
    ppermute x8, starting transfers between devices, ring_gather(): same = lax.ppermute(same, 'row', ring_moves(0))  34.7 us
    ppermute x4, starting transfers between devices, to_other_core(): return lax.ppermute(value, 'row', [(row, row ^ 1) for row in range(ROWS)])  27 us
    ppermute x2, waiting for transfers between devices, replica_sum(): replica = lax.ppermute(own, 'dp', [(0, 1), (1, 0)])  23.2 us
    ppermute x6, starting transfers between devices, ring_gather(): cross = lax.ppermute(cross, 'row', ring_moves(1 if step == 1 else 0))  19.3 us
    unnamed x71, local copies, waits for them, and re-layouts  19.1 us
    pallas_call x4, Pallas kernels, local_kernel(): pl.pallas_call(kernel, out_shape=out_shape, in_specs=in_specs, out_specs=...  11.3 us
    ppermute x8, waiting for transfers between devices, ring_gather(): same = lax.ppermute(same, 'row', ring_moves(0))  10.5 us
  transfers between devices with their start and end apart: 24, of which 11 were waited for; matrix products, arithmetic and copies ran while one was open for 5% of the time, Pallas kernels for 5%

profile of v8, /device:TPU:1, one launch (start us, length us, event | category | flops | bytes accessed | tf_op | source)
XLA Modules:
  0.0 249.4 jit_solution(9289120884822428093)
XLA Ops:
  7.2 1.9 constant_dynamic-update-slice_fusion.4
  9.2 4.5 %collective-permute-start = (bf16[192,128]{1,0:T(8,128)(2,1)S(1)}, bf16[192,128]{1,0:T(8,128)(2,1)S(1)}, u32[]{:S(2)}, u32[]{:S(2)}) collective-permute-start(bf16[192,128]{1,0:T(8,128)(2,1)S(1)} %bitcast.11), channel_id=1, source_target_pairs={{0,0},{1,16},{2,32},{3,48},{4,64},{5,80},{6,96},{7,112},{8,128},{9... | collective-permute-start | bytes 147464 | tf_op jit(solution)/shard_map/ppermute | solution.py:174
  15.8 51.2 %all_to_all.10 = bf16[16,384,128]{2,1,0:T(8,128)(2,1)S(1)} all-to-all(bf16[16,384,128]{2,1,0:T(8,128)(2,1)S(1)} %broadcast_in_dim.2), channel_id=1, replica_groups=mesh['dp'=2,'row'=16,'col'=16] {'col'}, dimensions={0} | all-to-all | bytes 3145728 | tf_op jit(solution)/shard_map/all_to_all | solution.py:177
  68.0 4.1 %fusion.11 = (bf16[128,768]{1,0:T(8,128)(2,1)}, bf16[128,768]{1,0:T(8,128)(2,1)}) fusion(bf16[128,1536]{1,0:T(8,128)(2,1)S(1)} %copy-done.27, bf16[3072,128]{1,0:T(8,128)(2,1)S(1)} %bitcast.9, bf16[3072,768]{1,0:T(8,128)(2,1)} %all-gather.3.cloned.1.call-done.weight_ref), kind=kOutput, calls=%fused_computation.18 | convolution fusion | flops 605257728 | bytes 6094848 | tf_op jit(solution)/shard_map/dot_general | solution.py:190
  72.1 7.4 %collective-permute-start.1 = (bf16[192,768]{1,0:T(8,128)(2,1)S(1)}, bf16[192,768]{1,0:T(8,128)(2,1)S(1)}, u32[]{:S(2)}, u32[]{:S(2)}) collective-permute-start(bf16[192,768]{1,0:T(8,128)(2,1)S(1)} %get-tuple-element.15.refs_0_), channel_id=1, source_target_pairs={{0,32},{16,240},{32,64},{48,16},{64,96},{80,48},{96,128},{112,80},... | collective-permute-start | bytes 884744 | tf_op jit(solution)/shard_map/ppermute | solution.py:59
  79.5 4.1 %collective-permute-start.2 = (bf16[192,768]{1,0:T(8,128)(2,1)S(1)}, bf16[192,768]{1,0:T(8,128)(2,1)S(1)}, u32[]{:S(2)}, u32[]{:S(2)}) collective-permute-start(bf16[192,768]{1,0:T(8,128)(2,1)S(1)} %get-tuple-element.15.refs_0_), channel_id=1, source_target_pairs={{16,32},{0,240},{48,64},{32,16},{80,96},{64,48},{112,128},{96,80},... | collective-permute-start | bytes 884744 | tf_op jit(solution)/shard_map/ppermute | solution.py:62
  83.7 4.5 %collective-permute-start.3 = (bf16[192,768]{1,0:T(8,128)(2,1)S(1)}, bf16[192,768]{1,0:T(8,128)(2,1)S(1)}, u32[]{:S(2)}, u32[]{:S(2)}) collective-permute-start(bf16[192,768]{1,0:T(8,128)(2,1)S(1)} %collective-permute-done.1.refs_1_), channel_id=1, source_target_pairs={{0,32},{16,240},{32,64},{48,16},{64,96},{80,48},{96,128},{112,80},... | collective-permute-start | bytes 884744 | tf_op jit(solution)/shard_map/ppermute | solution.py:59
  88.3 3.0 %collective-permute-start.4 = (bf16[192,768]{1,0:T(8,128)(2,1)S(1)}, bf16[192,768]{1,0:T(8,128)(2,1)S(1)}, u32[]{:S(2)}, u32[]{:S(2)}) collective-permute-start(bf16[192,768]{1,0:T(8,128)(2,1)S(1)} %collective-permute-done.2.refs_2_), channel_id=1, source_target_pairs={{0,32},{16,240},{32,64},{48,16},{64,96},{80,48},{96,128},{112,80},... | collective-permute-start | bytes 884744 | tf_op jit(solution)/shard_map/ppermute | solution.py:62
  93.9 5.1 %collective-permute-start.5 = (bf16[192,768]{1,0:T(8,128)(2,1)S(1)}, bf16[192,768]{1,0:T(8,128)(2,1)S(1)}, u32[]{:S(2)}, u32[]{:S(2)}) collective-permute-start(bf16[192,768]{1,0:T(8,128)(2,1)S(1)} %collective-permute-done.3.refs_3_), channel_id=1, source_target_pairs={{0,32},{16,240},{32,64},{48,16},{64,96},{80,48},{96,128},{112,80},... | collective-permute-start | bytes 884744 | tf_op jit(solution)/shard_map/ppermute | solution.py:59
  99.5 5.2 %collective-permute-start.6 = (bf16[192,768]{1,0:T(8,128)(2,1)S(1)}, bf16[192,768]{1,0:T(8,128)(2,1)S(1)}, u32[]{:S(2)}, u32[]{:S(2)}) collective-permute-start(bf16[192,768]{1,0:T(8,128)(2,1)S(1)} %collective-permute-done.4.refs_4_), channel_id=1, source_target_pairs={{0,32},{16,240},{32,64},{48,16},{64,96},{80,48},{96,128},{112,80},... | collective-permute-start | bytes 884744 | tf_op jit(solution)/shard_map/ppermute | solution.py:62
  106.1 9.5 %collective-permute-start.8 = (bf16[960,768]{1,0:T(8,128)(2,1)}, bf16[960,768]{1,0:T(8,128)(2,1)}, u32[]{:S(2)}, u32[]{:S(2)}) collective-permute-start(bf16[960,768]{1,0:T(8,128)(2,1)} %constant_dynamic-update-slice_fusion), channel_id=1, source_target_pairs={{0,16},{16,0},{32,48},{48,32},{64,80},{80,64},{96,112},{112,96},{1... | collective-permute-start | bytes 4423688 | tf_op jit(solution)/shard_map/ppermute | solution.py:50
  115.6 4.9 %collective-permute-start.7 = (bf16[192,768]{1,0:T(8,128)(2,1)S(1)}, bf16[192,768]{1,0:T(8,128)(2,1)S(1)}, u32[]{:S(2)}, u32[]{:S(2)}) collective-permute-start(bf16[192,768]{1,0:T(8,128)(2,1)S(1)} %collective-permute-done.5.refs_5_), channel_id=1, source_target_pairs={{0,32},{16,240},{32,64},{48,16},{64,96},{80,48},{96,128},{112,80},... | collective-permute-start | bytes 884744 | tf_op jit(solution)/shard_map/ppermute | solution.py:59
  120.5 3.6 %collective-permute-done.7.refs_7_ = bf16[192,768]{1,0:T(8,128)(2,1)S(1)} collective-permute-done((bf16[192,768]{1,0:T(8,128)(2,1)S(1)}, bf16[192,768]{1,0:T(8,128)(2,1)S(1)}, u32[]{:S(2)}, u32[]{:S(2)}) %collective-permute-start.7) | collective-permute-done | bytes 294944 | tf_op jit(solution)/shard_map/ppermute | solution.py:59
  125.8 9.6 %collective-permute-start.9 = (bf16[576,768]{1,0:T(8,128)(2,1)}, bf16[576,768]{1,0:T(8,128)(2,1)S(1)}, u32[]{:S(2)}, u32[]{:S(2)}) collective-permute-start(bf16[576,768]{1,0:T(8,128)(2,1)} %pad_maximum_fusion.1), channel_id=1, source_target_pairs={{0,16},{16,0},{32,48},{48,32},{64,80},{80,64},{96,112},{112,96},{1... | collective-permute-start | bytes 2654216 | tf_op jit(solution)/shard_map/ppermute | solution.py:50
  145.3 2.5 shard_map.67
  148.7 1.9 collective-permute-start.10
  150.6 1.9 collective-permute-start.11
  152.6 2.9 %collective-permute-done.10.refs_1_ = bf16[128,768]{1,0:T(8,128)(2,1)S(1)} collective-permute-done((bf16[128,768]{1,0:T(8,128)(2,1)S(1)}, bf16[128,768]{1,0:T(8,128)(2,1)S(1)}, u32[]{:S(2)}, u32[]{:S(2)}) %collective-permute-start.10) | collective-permute-done | bytes 196640 | tf_op jit(solution)/shard_map/ppermute | solution.py:59
  155.4 2.8 %collective-permute-start.12 = (bf16[128,768]{1,0:T(8,128)(2,1)S(1)}, bf16[128,768]{1,0:T(8,128)(2,1)}, u32[]{:S(2)}, u32[]{:S(2)}) collective-permute-start(bf16[128,768]{1,0:T(8,128)(2,1)S(1)} %collective-permute-done.10.refs_1_), channel_id=1, source_target_pairs={{0,32},{16,240},{32,64},{48,16},{64,96},{80,48},{96,128},{112,80},... | collective-permute-start | bytes 589832 | tf_op jit(solution)/shard_map/ppermute | solution.py:59
  158.3 2.8 %collective-permute-start.13 = (bf16[128,768]{1,0:T(8,128)(2,1)S(1)}, bf16[128,768]{1,0:T(8,128)(2,1)}, u32[]{:S(2)}, u32[]{:S(2)}) collective-permute-start(bf16[128,768]{1,0:T(8,128)(2,1)S(1)} %collective-permute-done.11.refs_2_), channel_id=1, source_target_pairs={{0,32},{16,240},{32,64},{48,16},{64,96},{80,48},{96,128},{112,80},... | collective-permute-start | bytes 589832 | tf_op jit(solution)/shard_map/ppermute | solution.py:62
  163.1 3.3 %collective-permute-start.14 = (bf16[128,768]{1,0:T(8,128)(2,1)}, bf16[128,768]{1,0:T(8,128)(2,1)}, u32[]{:S(2)}, u32[]{:S(2)}) collective-permute-start(bf16[128,768]{1,0:T(8,128)(2,1)} %collective-permute-done.12.refs_3_), channel_id=1, source_target_pairs={{0,32},{16,240},{32,64},{48,16},{64,96},{80,48},{96,128},{112,80},... | collective-permute-start | bytes 589832 | tf_op jit(solution)/shard_map/ppermute | solution.py:59
  166.4 2.3 collective-permute-start.15
  168.9 4.9 %shard_map.68 = bf16[16,192,128]{2,1,0:T(8,128)(2,1)} custom-call(s32[16]{0:T(128)S(1)} %dynamic-slice_bitcast_fusion.place_ref, bf16[128,768]{1,0:T(8,128)(2,1)S(1)} %get-tuple-element.10.ring_grad_ref.refs_0_, bf16[128,768]{1,0:T(8,128)(2,1)S(1)} %copy-done.21, bf16[3072,768]{1,0:T(8,128)(2,1)S(1)} %bitcast.8, bf16[192,768]{1,0:T(8,128)(2,1)S(1)} %copy-done.20, ...), custom_call_target="tpu_custom_call" | custom-call | flops 1207959552 | bytes 10616832 | tf_op jit(solution)/shard_map/pallas_call | solution.py:84
  173.8 5.9 %all-to-all-start.1 = ((bf16[16,192,128]{2,1,0:T(8,128)(2,1)}), bf16[16,192,128]{2,1,0:T(8,128)(2,1)S(1)}, u32[]{:S(2)}, u32[]{:S(2)}) async-start(bf16[16,192,128]{2,1,0:T(8,128)(2,1)} %shard_map.68), calls=%async_computation.1 | async-start | bytes 1572864 | tf_op jit(solution)/shard_map/all_to_all | solution.py:206
  182.9 4.8 %collective-permute-start.17 = (bf16[640,768]{1,0:T(8,128)(2,1)}, bf16[640,768]{1,0:T(8,128)(2,1)S(1)}, u32[]{:S(2)}, u32[]{:S(2)}) collective-permute-start(bf16[640,768]{1,0:T(8,128)(2,1)} %constant_dynamic-update-slice_fusion.5), channel_id=1, source_target_pairs={{0,16},{16,0},{32,48},{48,32},{64,80},{80,64},{96,112},{112,96},{1... | collective-permute-start | bytes 2949128 | tf_op jit(solution)/shard_map/ppermute | solution.py:50
  187.8 4.9 %collective-permute-start.16 = (bf16[128,768]{1,0:T(8,128)(2,1)}, bf16[128,768]{1,0:T(8,128)(2,1)S(1)}, u32[]{:S(2)}, u32[]{:S(2)}) collective-permute-start(bf16[128,768]{1,0:T(8,128)(2,1)} %collective-permute-done.14.refs_5_), channel_id=1, source_target_pairs={{0,32},{16,240},{32,64},{48,16},{64,96},{80,48},{96,128},{112,80},... | collective-permute-start | bytes 589832 | tf_op jit(solution)/shard_map/ppermute | solution.py:59
  192.6 2.9 %collective-permute-done.16.refs_7_ = bf16[128,768]{1,0:T(8,128)(2,1)S(1)} collective-permute-done((bf16[128,768]{1,0:T(8,128)(2,1)}, bf16[128,768]{1,0:T(8,128)(2,1)S(1)}, u32[]{:S(2)}, u32[]{:S(2)}) %collective-permute-start.16) | collective-permute-done | bytes 196640 | tf_op jit(solution)/shard_map/ppermute | solution.py:59
  196.6 3.1 %collective-permute-start.18 = (bf16[384,768]{1,0:T(8,128)(2,1)S(1)}, bf16[384,768]{1,0:T(8,128)(2,1)S(1)}, u32[]{:S(2)}, u32[]{:S(2)}) collective-permute-start(bf16[384,768]{1,0:T(8,128)(2,1)S(1)} %pad_maximum_fusion.2), channel_id=1, source_target_pairs={{0,16},{16,0},{32,48},{48,32},{64,80},{80,64},{96,112},{112,96},{1... | collective-permute-start | bytes 1769480 | tf_op jit(solution)/shard_map/ppermute | solution.py:50
  201.4 2.6 %shard_map.69 = bf16[192,768]{1,0:T(8,128)(2,1)S(1)} custom-call(s32[16]{0:T(128)S(1)} %dynamic-slice_bitcast_fusion.place_ref, bf16[16,192,128]{2,1,0:T(8,128)(2,1)S(1)} %get-tuple-element.11.by_token_ref, bf16[128,768]{1,0:T(8,128)(2,1)S(1)} %get-tuple-element.10.ring_grad_ref.refs_0_, bf16[128,768]{1,0:T(8,128)(2,1)S(1)} %copy-done.23, ...), custom_call_target="tpu_custom_call" | custom-call | flops 603979776 | bytes 4227072 | tf_op jit(solution)/shard_map/pallas_call | solution.py:84
  204.0 6.4 %collective-permute-start.19 = (bf16[192,768]{1,0:T(8,128)(2,1)S(1)}, bf16[192,768]{1,0:T(8,128)(2,1)S(1)}, u32[]{:S(2)}, u32[]{:S(2)}) collective-permute-start(bf16[192,768]{1,0:T(8,128)(2,1)S(1)} %shard_map.69), channel_id=1, source_target_pairs={{0,256},{256,0},{1,257},{257,1},{2,258},{258,2},{3,259},{259,3},{4... | collective-permute-start | bytes 884744 | tf_op jit(solution)/shard_map/ppermute | solution.py:162
  214.5 2.8 %collective-permute-start.20 = (bf16[192,768]{1,0:T(8,128)(2,1)S(1)}, bf16[192,768]{1,0:T(8,128)(2,1)S(1)}, u32[]{:S(2)}, u32[]{:S(2)}) collective-permute-start(bf16[192,768]{1,0:T(8,128)(2,1)S(1)} %shard_map.70), channel_id=1, source_target_pairs={{0,256},{256,0},{1,257},{257,1},{2,258},{258,2},{3,259},{259,3},{4... | collective-permute-start | bytes 884744 | tf_op jit(solution)/shard_map/ppermute | solution.py:162
  218.9 22.4 %collective-permute-done.20 = bf16[192,768]{1,0:T(8,128)(2,1)S(1)} collective-permute-done((bf16[192,768]{1,0:T(8,128)(2,1)S(1)}, bf16[192,768]{1,0:T(8,128)(2,1)S(1)}, u32[]{:S(2)}, u32[]{:S(2)}) %collective-permute-start.20) | collective-permute-done | bytes 294944 | tf_op jit(solution)/shard_map/ppermute | solution.py:162
  (111 shorter events, 35.3 us)
Async XLA Ops:
  7.2 60.0 %all-gather.3.cloned.1.call-start = ((), (), s32[]{:S(2)}) async-start(), calls=%async_computation.2 | async-start | bytes 5013504 | tf_op jit(solution)/shard_map/all_gather | solution.py:171
  9.1 70.4 %copy-start.19 = (bf16[192,768]{1,0:T(8,128)(2,1)}, bf16[192,768]{1,0:T(8,128)(2,1)S(1)}, u32[]{:S(2)}) copy-start(bf16[192,768]{1,0:T(8,128)(2,1)S(1)} %get-tuple-element.15.refs_0_) | copy-start | bytes 884740
  9.2 202.0 %all-gather.5.cloned.1.call-start = ((), (), s32[]{:S(2)}) async-start(), calls=%async_computation.3 | async-start | bytes 3342336 | tf_op jit(solution)/shard_map/all_gather | solution.py:197
  9.2 6.3 %collective-permute-start = (bf16[192,128]{1,0:T(8,128)(2,1)S(1)}, bf16[192,128]{1,0:T(8,128)(2,1)S(1)}, u32[]{:S(2)}, u32[]{:S(2)}) collective-permute-start(bf16[192,128]{1,0:T(8,128)(2,1)S(1)} %bitcast.11), channel_id=1, source_target_pairs={{0,0},{1,16},{2,32},{3,48},{4,64},{5,80},{6,96},{7,112},{8,128},{9... | collective-permute-start | bytes 147464 | tf_op jit(solution)/shard_map/ppermute | solution.py:174
  72.1 11.5 %collective-permute-start.1 = (bf16[192,768]{1,0:T(8,128)(2,1)S(1)}, bf16[192,768]{1,0:T(8,128)(2,1)S(1)}, u32[]{:S(2)}, u32[]{:S(2)}) collective-permute-start(bf16[192,768]{1,0:T(8,128)(2,1)S(1)} %get-tuple-element.15.refs_0_), channel_id=1, source_target_pairs={{0,32},{16,240},{32,64},{48,16},{64,96},{80,48},{96,128},{112,80},... | collective-permute-start | bytes 884744 | tf_op jit(solution)/shard_map/ppermute | solution.py:59
  79.5 8.8 %collective-permute-start.2 = (bf16[192,768]{1,0:T(8,128)(2,1)S(1)}, bf16[192,768]{1,0:T(8,128)(2,1)S(1)}, u32[]{:S(2)}, u32[]{:S(2)}) collective-permute-start(bf16[192,768]{1,0:T(8,128)(2,1)S(1)} %get-tuple-element.15.refs_0_), channel_id=1, source_target_pairs={{16,32},{0,240},{48,64},{32,16},{80,96},{64,48},{112,128},{96,80},... | collective-permute-start | bytes 884744 | tf_op jit(solution)/shard_map/ppermute | solution.py:62
  83.7 36.8 %copy-start.10 = (bf16[192,768]{1,0:T(8,128)(2,1)}, bf16[192,768]{1,0:T(8,128)(2,1)S(1)}, u32[]{:S(2)}) copy-start(bf16[192,768]{1,0:T(8,128)(2,1)S(1)} %collective-permute-done.1.refs_1_) | copy-start | bytes 884740
  83.7 10.2 %collective-permute-start.3 = (bf16[192,768]{1,0:T(8,128)(2,1)S(1)}, bf16[192,768]{1,0:T(8,128)(2,1)S(1)}, u32[]{:S(2)}, u32[]{:S(2)}) collective-permute-start(bf16[192,768]{1,0:T(8,128)(2,1)S(1)} %collective-permute-done.1.refs_1_), channel_id=1, source_target_pairs={{0,32},{16,240},{32,64},{48,16},{64,96},{80,48},{96,128},{112,80},... | collective-permute-start | bytes 884744 | tf_op jit(solution)/shard_map/ppermute | solution.py:59
  88.3 32.1 %copy-start.12 = (bf16[192,768]{1,0:T(8,128)(2,1)}, bf16[192,768]{1,0:T(8,128)(2,1)S(1)}, u32[]{:S(2)}) copy-start(bf16[192,768]{1,0:T(8,128)(2,1)S(1)} %collective-permute-done.2.refs_2_) | copy-start | bytes 884740
  88.3 11.1 %collective-permute-start.4 = (bf16[192,768]{1,0:T(8,128)(2,1)S(1)}, bf16[192,768]{1,0:T(8,128)(2,1)S(1)}, u32[]{:S(2)}, u32[]{:S(2)}) collective-permute-start(bf16[192,768]{1,0:T(8,128)(2,1)S(1)} %collective-permute-done.2.refs_2_), channel_id=1, source_target_pairs={{0,32},{16,240},{32,64},{48,16},{64,96},{80,48},{96,128},{112,80},... | collective-permute-start | bytes 884744 | tf_op jit(solution)/shard_map/ppermute | solution.py:62
  93.9 26.6 %copy-start.14 = (bf16[192,768]{1,0:T(8,128)(2,1)}, bf16[192,768]{1,0:T(8,128)(2,1)S(1)}, u32[]{:S(2)}) copy-start(bf16[192,768]{1,0:T(8,128)(2,1)S(1)} %collective-permute-done.3.refs_3_) | copy-start | bytes 884740
  93.9 21.7 %collective-permute-start.5 = (bf16[192,768]{1,0:T(8,128)(2,1)S(1)}, bf16[192,768]{1,0:T(8,128)(2,1)S(1)}, u32[]{:S(2)}, u32[]{:S(2)}) collective-permute-start(bf16[192,768]{1,0:T(8,128)(2,1)S(1)} %collective-permute-done.3.refs_3_), channel_id=1, source_target_pairs={{0,32},{16,240},{32,64},{48,16},{64,96},{80,48},{96,128},{112,80},... | collective-permute-start | bytes 884744 | tf_op jit(solution)/shard_map/ppermute | solution.py:59
  99.5 16.1 %collective-permute-start.6 = (bf16[192,768]{1,0:T(8,128)(2,1)S(1)}, bf16[192,768]{1,0:T(8,128)(2,1)S(1)}, u32[]{:S(2)}, u32[]{:S(2)}) collective-permute-start(bf16[192,768]{1,0:T(8,128)(2,1)S(1)} %collective-permute-done.4.refs_4_), channel_id=1, source_target_pairs={{0,32},{16,240},{32,64},{48,16},{64,96},{80,48},{96,128},{112,80},... | collective-permute-start | bytes 884744 | tf_op jit(solution)/shard_map/ppermute | solution.py:62
  106.1 31.6 %collective-permute-start.8 = (bf16[960,768]{1,0:T(8,128)(2,1)}, bf16[960,768]{1,0:T(8,128)(2,1)}, u32[]{:S(2)}, u32[]{:S(2)}) collective-permute-start(bf16[960,768]{1,0:T(8,128)(2,1)} %constant_dynamic-update-slice_fusion), channel_id=1, source_target_pairs={{0,16},{16,0},{32,48},{48,32},{64,80},{80,64},{96,112},{112,96},{1... | collective-permute-start | bytes 4423688 | tf_op jit(solution)/shard_map/ppermute | solution.py:50
  115.6 8.5 %collective-permute-start.7 = (bf16[192,768]{1,0:T(8,128)(2,1)S(1)}, bf16[192,768]{1,0:T(8,128)(2,1)S(1)}, u32[]{:S(2)}, u32[]{:S(2)}) collective-permute-start(bf16[192,768]{1,0:T(8,128)(2,1)S(1)} %collective-permute-done.5.refs_5_), channel_id=1, source_target_pairs={{0,32},{16,240},{32,64},{48,16},{64,96},{80,48},{96,128},{112,80},... | collective-permute-start | bytes 884744 | tf_op jit(solution)/shard_map/ppermute | solution.py:59
  124.1 44.7 %slice-start = ((s8[4718592]{0:T(1024)(128)(4,1)}), s8[524288]{0:T(1024)(128)(4,1)S(1)}, s32[]{:S(2)}) async-start(s8[4718592]{0:T(1024)(128)(4,1)} %bitcast.7), calls=%async_computation.4 | async-start | bytes 1048576
  125.8 11.8 %collective-permute-start.9 = (bf16[576,768]{1,0:T(8,128)(2,1)}, bf16[576,768]{1,0:T(8,128)(2,1)S(1)}, u32[]{:S(2)}, u32[]{:S(2)}) collective-permute-start(bf16[576,768]{1,0:T(8,128)(2,1)} %pad_maximum_fusion.1), channel_id=1, source_target_pairs={{0,16},{16,0},{32,48},{48,32},{64,80},{80,64},{96,112},{112,96},{1... | collective-permute-start | bytes 2654216 | tf_op jit(solution)/shard_map/ppermute | solution.py:50
  136.1 32.7 %slice-start.1 = ((s8[4718592]{0:T(1024)(128)(4,1)}), s8[4194304]{0:T(1024)(128)(4,1)S(1)}, s32[]{:S(2)}) async-start(s8[4718592]{0:T(1024)(128)(4,1)} %bitcast.7), calls=%async_computation.5 | async-start | bytes 8388608
  148.7 6.7 %collective-permute-start.10 = (bf16[128,768]{1,0:T(8,128)(2,1)S(1)}, bf16[128,768]{1,0:T(8,128)(2,1)S(1)}, u32[]{:S(2)}, u32[]{:S(2)}) collective-permute-start(bf16[128,768]{1,0:T(8,128)(2,1)S(1)} %get-tuple-element.10.ring_grad_ref.refs_0_), channel_id=1, source_target_pairs={{0,32},{16,240},{32,64},{48,16},{64,96},{80,48},{96,128},{112,80},... | collective-permute-start | bytes 589832 | tf_op jit(solution)/shard_map/ppermute | solution.py:59
  150.6 7.6 %collective-permute-start.11 = (bf16[128,768]{1,0:T(8,128)(2,1)S(1)}, bf16[128,768]{1,0:T(8,128)(2,1)S(1)}, u32[]{:S(2)}, u32[]{:S(2)}) collective-permute-start(bf16[128,768]{1,0:T(8,128)(2,1)S(1)} %get-tuple-element.10.ring_grad_ref.refs_0_), channel_id=1, source_target_pairs={{16,32},{0,240},{48,64},{32,16},{80,96},{64,48},{112,128},{96,80},... | collective-permute-start | bytes 589832 | tf_op jit(solution)/shard_map/ppermute | solution.py:62
  155.4 7.7 %collective-permute-start.12 = (bf16[128,768]{1,0:T(8,128)(2,1)S(1)}, bf16[128,768]{1,0:T(8,128)(2,1)}, u32[]{:S(2)}, u32[]{:S(2)}) collective-permute-start(bf16[128,768]{1,0:T(8,128)(2,1)S(1)} %collective-permute-done.10.refs_1_), channel_id=1, source_target_pairs={{0,32},{16,240},{32,64},{48,16},{64,96},{80,48},{96,128},{112,80},... | collective-permute-start | bytes 589832 | tf_op jit(solution)/shard_map/ppermute | solution.py:59
  158.3 8.2 %collective-permute-start.13 = (bf16[128,768]{1,0:T(8,128)(2,1)S(1)}, bf16[128,768]{1,0:T(8,128)(2,1)}, u32[]{:S(2)}, u32[]{:S(2)}) collective-permute-start(bf16[128,768]{1,0:T(8,128)(2,1)S(1)} %collective-permute-done.11.refs_2_), channel_id=1, source_target_pairs={{0,32},{16,240},{32,64},{48,16},{64,96},{80,48},{96,128},{112,80},... | collective-permute-start | bytes 589832 | tf_op jit(solution)/shard_map/ppermute | solution.py:62
  163.1 24.6 %collective-permute-start.14 = (bf16[128,768]{1,0:T(8,128)(2,1)}, bf16[128,768]{1,0:T(8,128)(2,1)}, u32[]{:S(2)}, u32[]{:S(2)}) collective-permute-start(bf16[128,768]{1,0:T(8,128)(2,1)} %collective-permute-done.12.refs_3_), channel_id=1, source_target_pairs={{0,32},{16,240},{32,64},{48,16},{64,96},{80,48},{96,128},{112,80},... | collective-permute-start | bytes 589832 | tf_op jit(solution)/shard_map/ppermute | solution.py:59
  166.4 21.3 %collective-permute-start.15 = (bf16[128,768]{1,0:T(8,128)(2,1)}, bf16[128,768]{1,0:T(8,128)(2,1)}, u32[]{:S(2)}, u32[]{:S(2)}) collective-permute-start(bf16[128,768]{1,0:T(8,128)(2,1)} %collective-permute-done.13.refs_4_), channel_id=1, source_target_pairs={{0,32},{16,240},{32,64},{48,16},{64,96},{80,48},{96,128},{112,80},... | collective-permute-start | bytes 589832 | tf_op jit(solution)/shard_map/ppermute | solution.py:62
  173.8 27.6 %copy-start.23 = (bf16[128,768]{1,0:T(8,128)(2,1)S(1)}, bf16[128,768]{1,0:T(8,128)(2,1)}, u32[]{:S(2)}) copy-start(bf16[128,768]{1,0:T(8,128)(2,1)} %copy-done.22) | copy-start | bytes 589828
  173.8 27.6 %copy-start.25 = (bf16[128,768]{1,0:T(8,128)(2,1)S(1)}, bf16[128,768]{1,0:T(8,128)(2,1)}, u32[]{:S(2)}) copy-start(bf16[128,768]{1,0:T(8,128)(2,1)} %copy-done.24) | copy-start | bytes 589828
  173.8 36.7 %all-to-all-start.1 = ((bf16[16,192,128]{2,1,0:T(8,128)(2,1)}), bf16[16,192,128]{2,1,0:T(8,128)(2,1)S(1)}, u32[]{:S(2)}, u32[]{:S(2)}) async-start(bf16[16,192,128]{2,1,0:T(8,128)(2,1)} %shard_map.68), calls=%async_computation.1 | async-start | bytes 1572864 | tf_op jit(solution)/shard_map/all_to_all | solution.py:206
  182.9 18.4 %collective-permute-start.17 = (bf16[640,768]{1,0:T(8,128)(2,1)}, bf16[640,768]{1,0:T(8,128)(2,1)S(1)}, u32[]{:S(2)}, u32[]{:S(2)}) collective-permute-start(bf16[640,768]{1,0:T(8,128)(2,1)} %constant_dynamic-update-slice_fusion.5), channel_id=1, source_target_pairs={{0,16},{16,0},{32,48},{48,32},{64,80},{80,64},{96,112},{112,96},{1... | collective-permute-start | bytes 2949128 | tf_op jit(solution)/shard_map/ppermute | solution.py:50
  187.8 7.8 %collective-permute-start.16 = (bf16[128,768]{1,0:T(8,128)(2,1)}, bf16[128,768]{1,0:T(8,128)(2,1)S(1)}, u32[]{:S(2)}, u32[]{:S(2)}) collective-permute-start(bf16[128,768]{1,0:T(8,128)(2,1)} %collective-permute-done.14.refs_5_), channel_id=1, source_target_pairs={{0,32},{16,240},{32,64},{48,16},{64,96},{80,48},{96,128},{112,80},... | collective-permute-start | bytes 589832 | tf_op jit(solution)/shard_map/ppermute | solution.py:59
  196.6 4.8 %collective-permute-start.18 = (bf16[384,768]{1,0:T(8,128)(2,1)S(1)}, bf16[384,768]{1,0:T(8,128)(2,1)S(1)}, u32[]{:S(2)}, u32[]{:S(2)}) collective-permute-start(bf16[384,768]{1,0:T(8,128)(2,1)S(1)} %pad_maximum_fusion.2), channel_id=1, source_target_pairs={{0,16},{16,0},{32,48},{48,32},{64,80},{80,64},{96,112},{112,96},{1... | collective-permute-start | bytes 1769480 | tf_op jit(solution)/shard_map/ppermute | solution.py:50
  204.0 14.1 %collective-permute-start.19 = (bf16[192,768]{1,0:T(8,128)(2,1)S(1)}, bf16[192,768]{1,0:T(8,128)(2,1)S(1)}, u32[]{:S(2)}, u32[]{:S(2)}) collective-permute-start(bf16[192,768]{1,0:T(8,128)(2,1)S(1)} %shard_map.69), channel_id=1, source_target_pairs={{0,256},{256,0},{1,257},{257,1},{2,258},{258,2},{3,259},{259,3},{4... | collective-permute-start | bytes 884744 | tf_op jit(solution)/shard_map/ppermute | solution.py:162
  214.5 26.9 %collective-permute-start.20 = (bf16[192,768]{1,0:T(8,128)(2,1)S(1)}, bf16[192,768]{1,0:T(8,128)(2,1)S(1)}, u32[]{:S(2)}, u32[]{:S(2)}) collective-permute-start(bf16[192,768]{1,0:T(8,128)(2,1)S(1)} %shard_map.70), channel_id=1, source_target_pairs={{0,256},{256,0},{1,257},{257,1},{2,258},{258,2},{3,259},{259,3},{4... | collective-permute-start | bytes 884744 | tf_op jit(solution)/shard_map/ppermute | solution.py:162
  (24 other events, 179.0 us)
Sparse Core Ops, SparseCore 0:
  10.7 51.9 all-gather.2
  72.2 50.2 all-gather.4

commit v9 on v2

v9 whole, which is shorter than its diff:
```python
import functools
import math

import jax
import jax.numpy as jnp
from jax import lax
from jax.experimental import pallas as pl
from jax.experimental.pallas import tpu as pltpu
from jax.sharding import PartitionSpec as P

ROWS = 16
COLS = 16
SIDE = 4
CHIPS = ROWS // 2
ROUNDS = CHIPS // 2
SLOTS = CHIPS
SPLIT = 5
LANES = 256
VMEM_BYTES = 24 * 2**20


def after(value, *others):
    return lax.optimization_barrier((value,) + others)[0]


def held_from(chip, core, slot):
    steps = (slot + 1) // 2
    parity = core if slot % 2 or slot == 0 else 1 - core
    away = -steps if core == 0 else steps
    return 2 * ((chip + away) % CHIPS) + parity


def every_place():
    for chip in range(CHIPS):
        for core in range(2):
            for slot in range(SLOTS):
                for other in range(2):
                    yield chip, core, slot, other


def depth_moves():
    return [
        (
            (2 * chip + (core ^ other)) * COLS + held_from(chip, core, slot),
            (2 * chip + core) * COLS + 2 * slot + other,
        )
        for chip, core, slot, other in every_place()
    ]


def token_moves():
    return [
        (
            held_from(chip, core, slot) * COLS + 2 * chip + (core ^ other),
            (2 * chip + core) * COLS + 2 * slot + other,
        )
        for chip, core, slot, other in every_place()
    ]


def ring_moves(cross):
    moves = []
    for chip in range(CHIPS):
        moves.append((2 * chip + cross, 2 * ((chip + 1) % CHIPS)))
        moves.append((2 * chip + 1 - cross, 2 * ((chip - 1) % CHIPS) + 1))
    return moves


def ring(block):
    slots = [block]
    same = cross = block
    for step in range(1, ROUNDS + 1):
        if step == ROUNDS:
            same = after(same, cross)
        same = lax.ppermute(same, "row", ring_moves(0))
        slots.append(same)
        if step < ROUNDS:
            cross = lax.ppermute(cross, "row", ring_moves(1 if step == 1 else 0))
            slots.append(cross)
    return slots


def to_other_core(value):
    return lax.ppermute(value, "row", [(row, row ^ 1) for row in range(ROWS)])


def along_y(value, steps):
    moves = [(c, (c + SIDE * steps) % COLS) for c in range(COLS)]
    return lax.ppermute(value, "col", moves)


def along_x(value, steps):
    moves = [(c, c // SIDE * SIDE + (c + steps) % SIDE) for c in range(COLS)]
    return lax.ppermute(value, "col", moves)


def from_all_cols(block):
    line = jnp.stack([block] + [along_y(block, d) for d in range(1, SIDE)])
    return jnp.concatenate([line] + [along_x(line, e) for e in range(1, SIDE)])


def sum_to_cols(pieces):
    line = pieces[:SIDE].astype(jnp.float32)
    for e in range(1, SIDE):
        line += along_x(pieces[SIDE * e : SIDE * (e + 1)], e).astype(jnp.float32)
    line = line.astype(jnp.bfloat16)
    total = line[0].astype(jnp.float32)
    for d in range(1, SIDE):
        total += along_y(line[d], d).astype(jnp.float32)
    return total.astype(jnp.bfloat16)


def places(sign):
    tables = []
    for col in range(COLS):
        y, x = divmod(col, SIDE)
        tables.append(
            [
                SIDE * ((sign * (c % SIDE - x)) % SIDE) + (sign * (c // SIDE - y)) % SIDE
                for c in range(COLS)
            ]
        )
    return jnp.array(tables, jnp.int32)[lax.axis_index("col")]


def local_kernel(kernel, out_shapes, flops, place, operands):
    moved = sum(x.size * x.dtype.itemsize for x in (*operands, *out_shapes))
    vmem = pl.BlockSpec(memory_space=pltpu.VMEM)
    return pl.pallas_call(
        kernel,
        out_shape=out_shapes,
        in_specs=[pl.BlockSpec(memory_space=pltpu.SMEM)] + [vmem] * len(operands),
        out_specs=[vmem] * len(out_shapes),
        compiler_params=pltpu.CompilerParams(vmem_limit_bytes=VMEM_BYTES),
        cost_estimate=pl.CostEstimate(flops=flops, bytes_accessed=moved, transcendentals=0),
    )(place, *operands)


def slot_sum_kernel(slots, by_depth, place_ref, block_ref, *refs):
    value_refs = refs[: len(slots)]
    before = refs[len(slots) : -2]
    outs = refs[-2:]
    depth = block_ref.shape[1] // 2
    for half in range(2):
        blocks = []
        for slot in slots:
            rows = pl.ds(0 if by_depth else depth, depth)
            blocks.append(block_ref[place_ref[2 * slot + half], rows, :])
        for start in range(0, value_refs[0].shape[1], LANES):
            units = pl.ds(start, LANES)
            total = before[half][:, units] if before else None
            for block, value_ref in zip(blocks, value_refs):
                term = lax.dot_general(
                    block,
                    value_ref[:, units],
                    (((0 if by_depth else 1,), (0,)), ((), ())),
                    preferred_element_type=jnp.float32,
                )
                total = term if total is None else total + term
            outs[half][:, units] = total.astype(outs[half].dtype)


def slot_sums(by_depth, place, blocks, values, last):
    depth, tokens = blocks.shape[1] // 2, blocks.shape[2]
    rows = tokens if by_depth else depth
    width = values[0].shape[1]
    wide = jax.ShapeDtypeStruct((rows, width), jnp.float32)
    narrow = jax.ShapeDtypeStruct((rows, width), jnp.bfloat16)
    sums = ()
    parts = (range(SPLIT), (wide, wide)), (range(SPLIT, SLOTS), (wide, narrow))
    for slots, out_shapes in parts:
        given = [values[slot] for slot in slots]
        if sums:
            given[-1] = last(given[-1])
        sums = local_kernel(
            functools.partial(slot_sum_kernel, slots, by_depth),
            out_shapes,
            4 * len(slots) * depth * tokens * width,
            place,
            (blocks, *given, *sums),
        )
    return sums


def input_grad_kernel(place_ref, own_ref, other_ref, *refs):
    *weight_refs, pieces_ref = refs
    for slot, weight_ref in enumerate(weight_refs):
        for half, grad_ref in enumerate((own_ref, other_ref)):
            pieces_ref[place_ref[2 * slot + half]] = lax.dot_general(
                weight_ref[...],
                grad_ref[...],
                (((1,), (1,)), ((), ())),
                preferred_element_type=jnp.float32,
            ).astype(jnp.bfloat16)


def per_device(features, up_weight, out_grad):
    tokens, depth = features.shape
    hidden_units = up_weight.shape[1]
    back, ahead = places(-1), places(1)
    features = features.T
    weights = ring(up_weight)
    turned = [
        lax.ppermute(features, ("row", "col"), moves()) for moves in (depth_moves, token_moves)
    ]
    blocks = from_all_cols(jnp.concatenate(turned))

    own, other = slot_sums(True, back, blocks, weights, lambda value: value)
    hidden = own + to_other_core(other).astype(jnp.float32)
    normal_cdf = 0.5 * (1.0 + jax.scipy.special.erf(hidden / math.sqrt(2.0)))
    density = jnp.exp(-0.5 * hidden * hidden) / math.sqrt(2.0 * math.pi)
    gelu_out = (hidden * normal_cdf).astype(jnp.bfloat16)
    hidden_grad = (out_grad.astype(jnp.float32) * (normal_cdf + hidden * density)).astype(
        jnp.bfloat16
    )

    grads = ring(hidden_grad)
    (pieces,) = local_kernel(
        input_grad_kernel,
        [jax.ShapeDtypeStruct((COLS, depth, tokens), jnp.bfloat16)],
        4 * SLOTS * depth * hidden_units * tokens,
        ahead,
        (hidden_grad, to_other_core(hidden_grad), *weights),
    )
    feature_grad = lax.ppermute(
        sum_to_cols(pieces), ("row", "col"), [(to, source) for source, to in depth_moves()]
    )

    own, other = slot_sums(False, back, blocks, grads, lambda value: value)
    own = (own + to_other_core(other).astype(jnp.float32)).astype(jnp.bfloat16)
    own = after(own, feature_grad)
    replica = lax.ppermute(own, "dp", [(0, 1), (1, 0)])
    weight_grad = own.astype(jnp.float32) + replica.astype(jnp.float32)
    return (gelu_out, feature_grad.T, weight_grad)


def solution(mesh):
    placed = (P(("dp", "row"), "col"), P("row", "col"), P(("dp", "row"), "col"))
    return jax.shard_map(
        per_device,
        mesh=mesh,
        in_specs=placed,
        out_specs=(P(("dp", "row"), "col"), P(("dp", "row"), "col"), P("row", "col")),
        check_vma=False,
    )
```

time: 231 us -> 209 us (0.905)
  matrix products: 23 us -> 0 us
  waiting for transfers between devices: 66.6 us -> 80.5 us
  local copies, waits for them, and re-layouts: 15.4 us -> 2.31 us
  starting transfers between devices: 121 us -> 110 us
  Pallas kernels: 0 us -> 10.1 us
    ppermute x3 -> x15, starting transfers between devices: 18.4 us -> 58.5 us  [the longest x6 25.1 us: along_x(): return lax.ppermute(value, 'col', moves)]
    dot_general x32 -> x0, matrix products: 23 us -> none  [the longest x16 12.3 us: per_device(): total += jnp.dot(block, grad, preferred_element_type=jnp.float32)]
    all_to_all x3 -> x0, starting transfers between devices: 21.6 us -> none  [the longest x2 14 us: to_all_cols(): return lax.all_to_all(copies, 'col', 0, 0, tiled=True)]
    ppermute x3 -> x15, waiting for transfers between devices: 5.68 us -> 24.9 us  [the longest x6 10.7 us: along_x(): return lax.ppermute(value, 'col', moves)]
    ppermute x9 -> x6, starting transfers between devices: 33.3 us -> 18.8 us  [ring(): cross = lax.ppermute(cross, 'row', ring_moves(1 if step == 1 else 0))]
    unnamed x50 -> x12, local copies, waits for them, and re-layouts: 11.8 us -> 0.8 us
    pallas_call x0 -> x5, Pallas kernels: none -> 10.1 us  [local_kernel(): pl.pallas_call(kernel, out_shape=out_shapes, in_specs=[pl.BlockSpec(memor...]
    ppermute x9 -> x6, waiting for transfers between devices: 13.1 us -> 6.44 us  [ring(): cross = lax.ppermute(cross, 'row', ring_moves(1 if step == 1 else 0))]
  transfers between devices with their start and end apart: 33 -> 33, of which waited for: 12 -> 15; matrix products, arithmetic and copies ran while one was open for 16% -> 1% of each run, Pallas kernels for 0% -> 4%
where the time goes in v9:
time: 209 us; the launch traced here: 207 us
  starting transfers between devices  110 us (53%)
  waiting for transfers between devices  80.5 us (39%)
  Pallas kernels  10.1 us (5%)
  other arithmetic  2.66 us (1%)
  local copies, waits for them, and re-layouts  2.31 us (1%)
    ppermute x1, waiting for transfers between devices, per_device(): replica = lax.ppermute(own, 'dp', [(0, 1), (1, 0)])  26.6 us
    ppermute x6, starting transfers between devices, along_x(): return lax.ppermute(value, 'col', moves)  25.1 us
    ppermute x8, starting transfers between devices, ring(): same = lax.ppermute(same, 'row', ring_moves(0))  23.8 us
    ppermute x8, waiting for transfers between devices, ring(): same = lax.ppermute(same, 'row', ring_moves(0))  20.9 us
    ppermute x6, starting transfers between devices, along_y(): return lax.ppermute(value, 'col', moves)  19.1 us
    ppermute x6, starting transfers between devices, ring(): cross = lax.ppermute(cross, 'row', ring_moves(1 if step == 1 else 0))  18.8 us
    ppermute x6, waiting for transfers between devices, along_x(): return lax.ppermute(value, 'col', moves)  10.7 us
    ppermute x2, starting transfers between devices, per_device(): lax.ppermute(features, ('row', 'col'), moves())  10.3 us
  transfers between devices with their start and end apart: 33, of which 15 were waited for; matrix products, arithmetic and copies ran while one was open for 1% of the time, Pallas kernels for 4%

profile of v9, /device:TPU:56, one launch (start us, length us, event | category | flops | bytes accessed | tf_op | source)
XLA Modules:
  0.0 207.1 jit_solution(8718084929061548932)
XLA Ops:
  0.6 4.3 %collective-permute-start.8 = (bf16[192,1536]{1,0:T(8,128)(2,1)}, bf16[192,1536]{1,0:T(8,128)(2,1)S(1)}, u32[]{:S(2)}, u32[]{:S(2)}) collective-permute-start(bf16[192,1536]{1,0:T(8,128)(2,1)} %refs_0_.3), channel_id=1, source_target_pairs={{0,32},{16,240},{32,64},{48,16},{64,96},{80,48},{96,128},{112,80},... | collective-permute-start | bytes 1769480 | tf_op jit(solution)/shard_map/ppermute | solution.py:75
  4.9 8.3 %collective-permute-start.11 = (bf16[192,1536]{1,0:T(8,128)(2,1)}, bf16[192,1536]{1,0:T(8,128)(2,1)S(1)}, u32[]{:S(2)}, u32[]{:S(2)}) collective-permute-start(bf16[192,1536]{1,0:T(8,128)(2,1)} %refs_0_.3), channel_id=1, source_target_pairs={{16,32},{0,240},{48,64},{32,16},{80,96},{64,48},{112,128},{96,80},... | collective-permute-start | bytes 1769480 | tf_op jit(solution)/shard_map/ppermute | solution.py:78
  13.2 11.4 %collective-permute-done.8.refs_1_ = bf16[192,1536]{1,0:T(8,128)(2,1)S(1)} collective-permute-done((bf16[192,1536]{1,0:T(8,128)(2,1)}, bf16[192,1536]{1,0:T(8,128)(2,1)S(1)}, u32[]{:S(2)}, u32[]{:S(2)}) %collective-permute-start.8) | collective-permute-done | bytes 589856 | tf_op jit(solution)/shard_map/ppermute | solution.py:75
  28.4 6.5 %collective-permute-start = (bf16[192,128]{1,0:T(8,128)(2,1)}, bf16[192,128]{1,0:T(8,128)(2,1)S(1)}, u32[]{:S(2)}, u32[]{:S(2)}) collective-permute-start(bf16[192,128]{1,0:T(8,128)(2,1)} %bitcast.30), channel_id=1, source_target_pairs={{0,0},{16,1},{14,2},{30,3},{15,4},{31,5},{12,6},{28,7},{13,8},{29,... | collective-permute-start | bytes 147464 | tf_op jit(solution)/shard_map/ppermute | solution.py:204
  34.9 3.8 %collective-permute-start.1 = (bf16[192,128]{1,0:T(8,128)(2,1)}, bf16[192,128]{1,0:T(8,128)(2,1)S(1)}, u32[]{:S(2)}, u32[]{:S(2)}) collective-permute-start(bf16[192,128]{1,0:T(8,128)(2,1)} %bitcast.31), channel_id=1, source_target_pairs={{0,0},{1,1},{224,2},{225,3},{240,4},{241,5},{192,6},{193,7},{208,8... | collective-permute-start | bytes 147464 | tf_op jit(solution)/shard_map/ppermute | solution.py:204
  39.5 7.3 %collective-permute-done.1 = bf16[192,128]{1,0:T(8,128)(2,1)S(1)} collective-permute-done((bf16[192,128]{1,0:T(8,128)(2,1)}, bf16[192,128]{1,0:T(8,128)(2,1)S(1)}, u32[]{:S(2)}, u32[]{:S(2)}) %collective-permute-start.1) | collective-permute-done | bytes 49184 | tf_op jit(solution)/shard_map/ppermute | solution.py:204
  50.6 3.9 %collective-permute-start.4 = (bf16[384,128]{1,0:T(8,128)(2,1)S(1)}, bf16[384,128]{1,0:T(8,128)(2,1)S(1)}, u32[]{:S(2)}, u32[]{:S(2)}) collective-permute-start(bf16[384,128]{1,0:T(8,128)(2,1)S(1)} %constant_dynamic-update-slice_fusion), channel_id=1, source_target_pairs={{0,12},{1,13},{2,14},{3,15},{4,0},{5,1},{6,2},{7,3},{8,4},{9,5},{1... | collective-permute-start | bytes 294920 | tf_op jit(solution)/shard_map/ppermute | solution.py:89
  54.6 3.3 %collective-permute-start.10 = (bf16[192,1536]{1,0:T(8,128)(2,1)S(1)}, bf16[192,1536]{1,0:T(8,128)(2,1)S(1)}, u32[]{:S(2)}, u32[]{:S(2)}) collective-permute-start(bf16[192,1536]{1,0:T(8,128)(2,1)S(1)} %collective-permute-done.9.refs_3_), channel_id=1, source_target_pairs={{0,32},{16,240},{32,64},{48,16},{64,96},{80,48},{96,128},{112,80},... | collective-permute-start | bytes 1769480 | tf_op jit(solution)/shard_map/ppermute | solution.py:75
  60.0 2.2 %collective-permute-start.5 = (bf16[4,384,128]{2,1,0:T(8,128)(2,1)S(1)}, bf16[4,384,128]{2,1,0:T(8,128)(2,1)S(1)}, u32[]{:S(2)}, u32[]{:S(2)}) collective-permute-start(bf16[4,384,128]{2,1,0:T(8,128)(2,1)S(1)} %pad_maximum_fusion), channel_id=1, source_target_pairs={{0,1},{1,2},{2,3},{3,0},{4,5},{5,6},{6,7},{7,4},{8,9},{9,10},{10,1... | collective-permute-start | bytes 1179656 | tf_op jit(solution)/shard_map/ppermute | solution.py:94
  62.1 7.4 %collective-permute-start.6 = (bf16[4,384,128]{2,1,0:T(8,128)(2,1)S(1)}, bf16[4,384,128]{2,1,0:T(8,128)(2,1)S(1)}, u32[]{:S(2)}, u32[]{:S(2)}) collective-permute-start(bf16[4,384,128]{2,1,0:T(8,128)(2,1)S(1)} %pad_maximum_fusion), channel_id=1, source_target_pairs={{0,2},{1,3},{2,0},{3,1},{4,6},{5,7},{6,4},{7,5},{8,10},{9,11},{10,... | collective-permute-start | bytes 1179656 | tf_op jit(solution)/shard_map/ppermute | solution.py:94
  69.5 3.5 %collective-permute-start.7 = (bf16[4,384,128]{2,1,0:T(8,128)(2,1)S(1)}, bf16[4,384,128]{2,1,0:T(8,128)(2,1)S(1)}, u32[]{:S(2)}, u32[]{:S(2)}) collective-permute-start(bf16[4,384,128]{2,1,0:T(8,128)(2,1)S(1)} %pad_maximum_fusion), channel_id=1, source_target_pairs={{0,3},{1,0},{2,1},{3,2},{4,7},{5,4},{6,5},{7,6},{8,11},{9,8},{10,9... | collective-permute-start | bytes 1179656 | tf_op jit(solution)/shard_map/ppermute | solution.py:94
  73.9 2.1 %collective-permute-start.14 = (bf16[192,1536]{1,0:T(8,128)(2,1)S(1)}, bf16[192,1536]{1,0:T(8,128)(2,1)S(1)}, u32[]{:S(2)}, u32[]{:S(2)}) collective-permute-start(bf16[192,1536]{1,0:T(8,128)(2,1)S(1)} %collective-permute-done.10.refs_0_.refs_5_), channel_id=1, source_target_pairs={{0,32},{16,240},{32,64},{48,16},{64,96},{80,48},{96,128},{112,80},... | collective-permute-start | bytes 1769480 | tf_op jit(solution)/shard_map/ppermute | solution.py:75
  76.5 8.1 %collective-permute-done.6 = bf16[4,384,128]{2,1,0:T(8,128)(2,1)S(1)} collective-permute-done((bf16[4,384,128]{2,1,0:T(8,128)(2,1)S(1)}, bf16[4,384,128]{2,1,0:T(8,128)(2,1)S(1)}, u32[]{:S(2)}, u32[]{:S(2)}) %collective-permute-start.6) | collective-permute-done | bytes 393248 | tf_op jit(solution)/shard_map/ppermute | solution.py:94
  94.5 3.6 %collective-permute-start.24 = (bf16[128,1536]{1,0:T(8,128)(2,1)S(1)}, bf16[128,1536]{1,0:T(8,128)(2,1)S(1)}, u32[]{:S(2)}, u32[]{:S(2)}) collective-permute-start(bf16[128,1536]{1,0:T(8,128)(2,1)S(1)} %get-tuple-element.25.own_ref.refs_0_), channel_id=1, source_target_pairs={{0,32},{16,240},{32,64},{48,16},{64,96},{80,48},{96,128},{112,80},... | collective-permute-start | bytes 1179656 | tf_op jit(solution)/shard_map/ppermute | solution.py:75
  100.1 6.4 %collective-permute-done.24.refs_1_ = bf16[128,1536]{1,0:T(8,128)(2,1)S(1)} collective-permute-done((bf16[128,1536]{1,0:T(8,128)(2,1)S(1)}, bf16[128,1536]{1,0:T(8,128)(2,1)S(1)}, u32[]{:S(2)}, u32[]{:S(2)}) %collective-permute-start.24) | collective-permute-done | bytes 393248 | tf_op jit(solution)/shard_map/ppermute | solution.py:75
  106.5 4.0 %collective-permute-start.25 = (bf16[128,1536]{1,0:T(8,128)(2,1)S(1)}, bf16[128,1536]{1,0:T(8,128)(2,1)S(1)}, u32[]{:S(2)}, u32[]{:S(2)}) collective-permute-start(bf16[128,1536]{1,0:T(8,128)(2,1)S(1)} %collective-permute-done.24.refs_1_), channel_id=1, source_target_pairs={{0,32},{16,240},{32,64},{48,16},{64,96},{80,48},{96,128},{112,80},... | collective-permute-start | bytes 1179656 | tf_op jit(solution)/shard_map/ppermute | solution.py:75
  114.4 3.0 %collective-permute-done.25.refs_3_ = bf16[128,1536]{1,0:T(8,128)(2,1)S(1)} collective-permute-done((bf16[128,1536]{1,0:T(8,128)(2,1)S(1)}, bf16[128,1536]{1,0:T(8,128)(2,1)S(1)}, u32[]{:S(2)}, u32[]{:S(2)}) %collective-permute-start.25) | collective-permute-done | bytes 393248 | tf_op jit(solution)/shard_map/ppermute | solution.py:75
  117.4 2.8 %collective-permute-start.26 = (bf16[128,1536]{1,0:T(8,128)(2,1)S(1)}, bf16[128,1536]{1,0:T(8,128)(2,1)S(1)}, u32[]{:S(2)}, u32[]{:S(2)}) collective-permute-start(bf16[128,1536]{1,0:T(8,128)(2,1)S(1)} %collective-permute-done.25.refs_3_), channel_id=1, source_target_pairs={{0,32},{16,240},{32,64},{48,16},{64,96},{80,48},{96,128},{112,80},... | collective-permute-start | bytes 1179656 | tf_op jit(solution)/shard_map/ppermute | solution.py:75
  121.6 2.8 %collective-permute-start.29 = (bf16[128,1536]{1,0:T(8,128)(2,1)S(1)}, bf16[128,1536]{1,0:T(8,128)(2,1)S(1)}, u32[]{:S(2)}, u32[]{:S(2)}) collective-permute-start(bf16[128,1536]{1,0:T(8,128)(2,1)S(1)} %collective-permute-done.28.refs_4_), channel_id=1, source_target_pairs={{0,32},{16,240},{32,64},{48,16},{64,96},{80,48},{96,128},{112,80},... | collective-permute-start | bytes 1179656 | tf_op jit(solution)/shard_map/ppermute | solution.py:78
  125.1 3.1 %shard_map.78 = bf16[16,192,128]{2,1,0:T(8,128)(2,1)S(1)} custom-call(s32[16]{0:T(128)S(1)} %dynamic-slice_bitcast_fusion.place_ref, bf16[128,1536]{1,0:T(8,128)(2,1)S(1)} %get-tuple-element.25.own_ref.refs_0_, bf16[128,1536]{1,0:T(8,128)(2,1)S(1)} %collective-permute-done.16.other_ref, bf16[192,1536]{1,0:T(8,128)(2,1)S(1)} %copy-done, ...), custom_call_target="tpu_custom_call" | custom-call | flops 1207959552 | bytes 6291456 | tf_op jit(solution)/shard_map/pallas_call | solution.py:129
  128.3 4.2 %collective-permute-done.29.refs_1_ = bf16[128,1536]{1,0:T(8,128)(2,1)S(1)} collective-permute-done((bf16[128,1536]{1,0:T(8,128)(2,1)S(1)}, bf16[128,1536]{1,0:T(8,128)(2,1)S(1)}, u32[]{:S(2)}, u32[]{:S(2)}) %collective-permute-start.29) | collective-permute-done | bytes 393248 | tf_op jit(solution)/shard_map/ppermute | solution.py:78
  134.5 4.6 %collective-permute-start.19 = (bf16[4,192,128]{2,1,0:T(8,128)(2,1)S(1)}, bf16[4,192,128]{2,1,0:T(8,128)(2,1)S(1)}, u32[]{:S(2)}, u32[]{:S(2)}) collective-permute-start(bf16[4,192,128]{2,1,0:T(8,128)(2,1)S(1)} %get-tuple-element.28), channel_id=1, source_target_pairs={{0,3},{1,0},{2,1},{3,2},{4,7},{5,4},{6,5},{7,6},{8,11},{9,8},{10,9... | collective-permute-start | bytes 589832 | tf_op jit(solution)/shard_map/ppermute | solution.py:94
  139.1 4.1 %collective-permute-start.18 = (bf16[4,192,128]{2,1,0:T(8,128)(2,1)S(1)}, bf16[4,192,128]{2,1,0:T(8,128)(2,1)S(1)}, u32[]{:S(2)}, u32[]{:S(2)}) collective-permute-start(bf16[4,192,128]{2,1,0:T(8,128)(2,1)S(1)} %get-tuple-element.29), channel_id=1, source_target_pairs={{0,2},{1,3},{2,0},{3,1},{4,6},{5,7},{6,4},{7,5},{8,10},{9,11},{10,... | collective-permute-start | bytes 589832 | tf_op jit(solution)/shard_map/ppermute | solution.py:94
  143.2 3.3 %collective-permute-start.17 = (bf16[4,192,128]{2,1,0:T(8,128)(2,1)S(1)}, bf16[4,192,128]{2,1,0:T(8,128)(2,1)S(1)}, u32[]{:S(2)}, u32[]{:S(2)}) collective-permute-start(bf16[4,192,128]{2,1,0:T(8,128)(2,1)S(1)} %get-tuple-element.27), channel_id=1, source_target_pairs={{0,1},{1,2},{2,3},{3,0},{4,5},{5,6},{6,7},{7,4},{8,9},{9,10},{10,1... | collective-permute-start | bytes 589832 | tf_op jit(solution)/shard_map/ppermute | solution.py:94
  146.5 2.2 %shard_map.79 = (f32[192,1536]{1,0:T(8,128)S(1)}, f32[192,1536]{1,0:T(8,128)S(1)}) custom-call(s32[16]{0:T(128)S(1)} %dynamic-slice_bitcast_fusion.1.place_ref, bf16[16,384,128]{2,1,0:T(8,128)(2,1)S(1)} %constant_dynamic-update-slice_fusion.2.block_ref, bf16[128,1536]{1,0:T(8,128)(2,1)S(1)} %get-tuple-element.25.own_ref.refs_0_, ...), custom_call_target="tpu_custom_call" | custom-call | flops 754974720 | bytes 5898240 | tf_op jit(solution)/shard_map/pallas_call | solution.py:129
  152.7 3.2 %collective-permute-start.22 = (bf16[192,128]{1,0:T(8,128)(2,1)S(1)}, bf16[192,128]{1,0:T(8,128)(2,1)S(1)}, u32[]{:S(2)}, u32[]{:S(2)}) collective-permute-start(bf16[192,128]{1,0:T(8,128)(2,1)S(1)} %get-tuple-element.31), channel_id=1, source_target_pairs={{0,12},{1,13},{2,14},{3,15},{4,0},{5,1},{6,2},{7,3},{8,4},{9,5},{1... | collective-permute-start | bytes 147464 | tf_op jit(solution)/shard_map/ppermute | solution.py:89
  155.8 3.9 %collective-permute-start.21 = (bf16[192,128]{1,0:T(8,128)(2,1)S(1)}, bf16[192,128]{1,0:T(8,128)(2,1)S(1)}, u32[]{:S(2)}, u32[]{:S(2)}) collective-permute-start(bf16[192,128]{1,0:T(8,128)(2,1)S(1)} %get-tuple-element.32), channel_id=1, source_target_pairs={{0,8},{1,9},{2,10},{3,11},{4,12},{5,13},{6,14},{7,15},{8,0},{9,1},... | collective-permute-start | bytes 147464 | tf_op jit(solution)/shard_map/ppermute | solution.py:89
  159.7 4.3 %collective-permute-start.20 = (bf16[192,128]{1,0:T(8,128)(2,1)S(1)}, bf16[192,128]{1,0:T(8,128)(2,1)S(1)}, u32[]{:S(2)}, u32[]{:S(2)}) collective-permute-start(bf16[192,128]{1,0:T(8,128)(2,1)S(1)} %get-tuple-element.30), channel_id=1, source_target_pairs={{0,4},{1,5},{2,6},{3,7},{4,8},{5,9},{6,10},{7,11},{8,12},{9,13},{1... | collective-permute-start | bytes 147464 | tf_op jit(solution)/shard_map/ppermute | solution.py:89
  165.8 4.0 %collective-permute-start.23 = (bf16[192,128]{1,0:T(8,128)(2,1)S(1)}, bf16[192,128]{1,0:T(8,128)(2,1)S(1)}, u32[]{:S(2)}, u32[]{:S(2)}) collective-permute-start(bf16[192,128]{1,0:T(8,128)(2,1)S(1)} %fusion.8), channel_id=1, source_target_pairs={{0,0},{1,16},{2,14},{3,30},{4,15},{5,31},{6,12},{7,28},{8,13},{9,2... | collective-permute-start | bytes 147464 | tf_op jit(solution)/shard_map/ppermute | solution.py:225
  170.0 5.2 %collective-permute-done.23 = bf16[192,128]{1,0:T(8,128)(2,1)S(1)} collective-permute-done((bf16[192,128]{1,0:T(8,128)(2,1)S(1)}, bf16[192,128]{1,0:T(8,128)(2,1)S(1)}, u32[]{:S(2)}, u32[]{:S(2)}) %collective-permute-start.23) | collective-permute-done | bytes 49184 | tf_op jit(solution)/shard_map/ppermute | solution.py:225
  175.2 3.5 %collective-permute-start.32 = (bf16[192,1536]{1,0:T(8,128)(2,1)S(1)}, bf16[192,1536]{1,0:T(8,128)(2,1)S(1)}, u32[]{:S(2)}, u32[]{:S(2)}) collective-permute-start(bf16[192,1536]{1,0:T(8,128)(2,1)S(1)} %add_convert_fusion), channel_id=1, source_target_pairs={{0,256},{256,0},{1,257},{257,1},{2,258},{258,2},{3,259},{259,3},{4... | collective-permute-start | bytes 1769480 | tf_op jit(solution)/shard_map/ppermute | solution.py:232
  178.8 26.6 %collective-permute-done.32 = bf16[192,1536]{1,0:T(8,128)(2,1)S(1)} collective-permute-done((bf16[192,1536]{1,0:T(8,128)(2,1)S(1)}, bf16[192,1536]{1,0:T(8,128)(2,1)S(1)}, u32[]{:S(2)}, u32[]{:S(2)}) %collective-permute-start.32) | collective-permute-done | bytes 589856 | tf_op jit(solution)/shard_map/ppermute | solution.py:232
  (63 shorter events, 39.1 us)
Async XLA Ops:
  0.6 24.0 %collective-permute-start.8 = (bf16[192,1536]{1,0:T(8,128)(2,1)}, bf16[192,1536]{1,0:T(8,128)(2,1)S(1)}, u32[]{:S(2)}, u32[]{:S(2)}) collective-permute-start(bf16[192,1536]{1,0:T(8,128)(2,1)} %refs_0_.3), channel_id=1, source_target_pairs={{0,32},{16,240},{32,64},{48,16},{64,96},{80,48},{96,128},{112,80},... | collective-permute-start | bytes 1769480 | tf_op jit(solution)/shard_map/ppermute | solution.py:75
  4.9 21.6 %collective-permute-start.11 = (bf16[192,1536]{1,0:T(8,128)(2,1)}, bf16[192,1536]{1,0:T(8,128)(2,1)S(1)}, u32[]{:S(2)}, u32[]{:S(2)}) collective-permute-start(bf16[192,1536]{1,0:T(8,128)(2,1)} %refs_0_.3), channel_id=1, source_target_pairs={{16,32},{0,240},{48,64},{32,16},{80,96},{64,48},{112,128},{96,80},... | collective-permute-start | bytes 1769480 | tf_op jit(solution)/shard_map/ppermute | solution.py:78
  24.6 30.0 %collective-permute-start.9 = (bf16[192,1536]{1,0:T(8,128)(2,1)S(1)}, bf16[192,1536]{1,0:T(8,128)(2,1)S(1)}, u32[]{:S(2)}, u32[]{:S(2)}) collective-permute-start(bf16[192,1536]{1,0:T(8,128)(2,1)S(1)} %collective-permute-done.8.refs_1_), channel_id=1, source_target_pairs={{0,32},{16,240},{32,64},{48,16},{64,96},{80,48},{96,128},{112,80},... | collective-permute-start | bytes 1769480 | tf_op jit(solution)/shard_map/ppermute | solution.py:75
  26.5 31.4 %collective-permute-start.12 = (bf16[192,1536]{1,0:T(8,128)(2,1)S(1)}, bf16[192,1536]{1,0:T(8,128)(2,1)S(1)}, u32[]{:S(2)}, u32[]{:S(2)}) collective-permute-start(bf16[192,1536]{1,0:T(8,128)(2,1)S(1)} %collective-permute-done.11.refs_2_), channel_id=1, source_target_pairs={{0,32},{16,240},{32,64},{48,16},{64,96},{80,48},{96,128},{112,80},... | collective-permute-start | bytes 1769480 | tf_op jit(solution)/shard_map/ppermute | solution.py:78
  28.4 11.0 %collective-permute-start = (bf16[192,128]{1,0:T(8,128)(2,1)}, bf16[192,128]{1,0:T(8,128)(2,1)S(1)}, u32[]{:S(2)}, u32[]{:S(2)}) collective-permute-start(bf16[192,128]{1,0:T(8,128)(2,1)} %bitcast.30), channel_id=1, source_target_pairs={{0,0},{16,1},{14,2},{30,3},{15,4},{31,5},{12,6},{28,7},{13,8},{29,... | collective-permute-start | bytes 147464 | tf_op jit(solution)/shard_map/ppermute | solution.py:204
  34.9 11.8 %collective-permute-start.1 = (bf16[192,128]{1,0:T(8,128)(2,1)}, bf16[192,128]{1,0:T(8,128)(2,1)S(1)}, u32[]{:S(2)}, u32[]{:S(2)}) collective-permute-start(bf16[192,128]{1,0:T(8,128)(2,1)} %bitcast.31), channel_id=1, source_target_pairs={{0,0},{1,1},{224,2},{225,3},{240,4},{241,5},{192,6},{193,7},{208,8... | collective-permute-start | bytes 147464 | tf_op jit(solution)/shard_map/ppermute | solution.py:204
  46.8 13.1 %collective-permute-start.2 = (bf16[384,128]{1,0:T(8,128)(2,1)S(1)}, bf16[384,128]{1,0:T(8,128)(2,1)S(1)}, u32[]{:S(2)}, u32[]{:S(2)}) collective-permute-start(bf16[384,128]{1,0:T(8,128)(2,1)S(1)} %constant_dynamic-update-slice_fusion), channel_id=1, source_target_pairs={{0,4},{1,5},{2,6},{3,7},{4,8},{5,9},{6,10},{7,11},{8,12},{9,13},{1... | collective-permute-start | bytes 294920 | tf_op jit(solution)/shard_map/ppermute | solution.py:89
  48.7 11.2 %collective-permute-start.3 = (bf16[384,128]{1,0:T(8,128)(2,1)S(1)}, bf16[384,128]{1,0:T(8,128)(2,1)S(1)}, u32[]{:S(2)}, u32[]{:S(2)}) collective-permute-start(bf16[384,128]{1,0:T(8,128)(2,1)S(1)} %constant_dynamic-update-slice_fusion), channel_id=1, source_target_pairs={{0,8},{1,9},{2,10},{3,11},{4,12},{5,13},{6,14},{7,15},{8,0},{9,1},... | collective-permute-start | bytes 294920 | tf_op jit(solution)/shard_map/ppermute | solution.py:89
  50.6 9.2 %collective-permute-start.4 = (bf16[384,128]{1,0:T(8,128)(2,1)S(1)}, bf16[384,128]{1,0:T(8,128)(2,1)S(1)}, u32[]{:S(2)}, u32[]{:S(2)}) collective-permute-start(bf16[384,128]{1,0:T(8,128)(2,1)S(1)} %constant_dynamic-update-slice_fusion), channel_id=1, source_target_pairs={{0,12},{1,13},{2,14},{3,15},{4,0},{5,1},{6,2},{7,3},{8,4},{9,5},{1... | collective-permute-start | bytes 294920 | tf_op jit(solution)/shard_map/ppermute | solution.py:89
  54.6 18.5 %collective-permute-start.10 = (bf16[192,1536]{1,0:T(8,128)(2,1)S(1)}, bf16[192,1536]{1,0:T(8,128)(2,1)S(1)}, u32[]{:S(2)}, u32[]{:S(2)}) collective-permute-start(bf16[192,1536]{1,0:T(8,128)(2,1)S(1)} %collective-permute-done.9.refs_3_), channel_id=1, source_target_pairs={{0,32},{16,240},{32,64},{48,16},{64,96},{80,48},{96,128},{112,80},... | collective-permute-start | bytes 1769480 | tf_op jit(solution)/shard_map/ppermute | solution.py:75
  57.9 16.0 %collective-permute-start.13 = (bf16[192,1536]{1,0:T(8,128)(2,1)S(1)}, bf16[192,1536]{1,0:T(8,128)(2,1)S(1)}, u32[]{:S(2)}, u32[]{:S(2)}) collective-permute-start(bf16[192,1536]{1,0:T(8,128)(2,1)S(1)} %collective-permute-done.12.refs_4_), channel_id=1, source_target_pairs={{0,32},{16,240},{32,64},{48,16},{64,96},{80,48},{96,128},{112,80},... | collective-permute-start | bytes 1769480 | tf_op jit(solution)/shard_map/ppermute | solution.py:78
  60.0 16.5 %collective-permute-start.5 = (bf16[4,384,128]{2,1,0:T(8,128)(2,1)S(1)}, bf16[4,384,128]{2,1,0:T(8,128)(2,1)S(1)}, u32[]{:S(2)}, u32[]{:S(2)}) collective-permute-start(bf16[4,384,128]{2,1,0:T(8,128)(2,1)S(1)} %pad_maximum_fusion), channel_id=1, source_target_pairs={{0,1},{1,2},{2,3},{3,0},{4,5},{5,6},{6,7},{7,4},{8,9},{9,10},{10,1... | collective-permute-start | bytes 1179656 | tf_op jit(solution)/shard_map/ppermute | solution.py:94
  62.1 22.4 %collective-permute-start.6 = (bf16[4,384,128]{2,1,0:T(8,128)(2,1)S(1)}, bf16[4,384,128]{2,1,0:T(8,128)(2,1)S(1)}, u32[]{:S(2)}, u32[]{:S(2)}) collective-permute-start(bf16[4,384,128]{2,1,0:T(8,128)(2,1)S(1)} %pad_maximum_fusion), channel_id=1, source_target_pairs={{0,2},{1,3},{2,0},{3,1},{4,6},{5,7},{6,4},{7,5},{8,10},{9,11},{10,... | collective-permute-start | bytes 1179656 | tf_op jit(solution)/shard_map/ppermute | solution.py:94
  69.5 17.0 %collective-permute-start.7 = (bf16[4,384,128]{2,1,0:T(8,128)(2,1)S(1)}, bf16[4,384,128]{2,1,0:T(8,128)(2,1)S(1)}, u32[]{:S(2)}, u32[]{:S(2)}) collective-permute-start(bf16[4,384,128]{2,1,0:T(8,128)(2,1)S(1)} %pad_maximum_fusion), channel_id=1, source_target_pairs={{0,3},{1,0},{2,1},{3,2},{4,7},{5,4},{6,5},{7,6},{8,11},{9,8},{10,9... | collective-permute-start | bytes 1179656 | tf_op jit(solution)/shard_map/ppermute | solution.py:94
  73.9 14.5 %collective-permute-start.14 = (bf16[192,1536]{1,0:T(8,128)(2,1)S(1)}, bf16[192,1536]{1,0:T(8,128)(2,1)S(1)}, u32[]{:S(2)}, u32[]{:S(2)}) collective-permute-start(bf16[192,1536]{1,0:T(8,128)(2,1)S(1)} %collective-permute-done.10.refs_0_.refs_5_), channel_id=1, source_target_pairs={{0,32},{16,240},{32,64},{48,16},{64,96},{80,48},{96,128},{112,80},... | collective-permute-start | bytes 1769480 | tf_op jit(solution)/shard_map/ppermute | solution.py:75
  94.5 12.0 %collective-permute-start.24 = (bf16[128,1536]{1,0:T(8,128)(2,1)S(1)}, bf16[128,1536]{1,0:T(8,128)(2,1)S(1)}, u32[]{:S(2)}, u32[]{:S(2)}) collective-permute-start(bf16[128,1536]{1,0:T(8,128)(2,1)S(1)} %get-tuple-element.25.own_ref.refs_0_), channel_id=1, source_target_pairs={{0,32},{16,240},{32,64},{48,16},{64,96},{80,48},{96,128},{112,80},... | collective-permute-start | bytes 1179656 | tf_op jit(solution)/shard_map/ppermute | solution.py:75
  98.1 12.4 %collective-permute-start.27 = (bf16[128,1536]{1,0:T(8,128)(2,1)S(1)}, bf16[128,1536]{1,0:T(8,128)(2,1)S(1)}, u32[]{:S(2)}, u32[]{:S(2)}) collective-permute-start(bf16[128,1536]{1,0:T(8,128)(2,1)S(1)} %get-tuple-element.25.own_ref.refs_0_), channel_id=1, source_target_pairs={{16,32},{0,240},{48,64},{32,16},{80,96},{64,48},{112,128},{96,80},... | collective-permute-start | bytes 1179656 | tf_op jit(solution)/shard_map/ppermute | solution.py:78
  106.5 10.9 %collective-permute-start.25 = (bf16[128,1536]{1,0:T(8,128)(2,1)S(1)}, bf16[128,1536]{1,0:T(8,128)(2,1)S(1)}, u32[]{:S(2)}, u32[]{:S(2)}) collective-permute-start(bf16[128,1536]{1,0:T(8,128)(2,1)S(1)} %collective-permute-done.24.refs_1_), channel_id=1, source_target_pairs={{0,32},{16,240},{32,64},{48,16},{64,96},{80,48},{96,128},{112,80},... | collective-permute-start | bytes 1179656 | tf_op jit(solution)/shard_map/ppermute | solution.py:75
  110.5 11.1 %collective-permute-start.28 = (bf16[128,1536]{1,0:T(8,128)(2,1)S(1)}, bf16[128,1536]{1,0:T(8,128)(2,1)S(1)}, u32[]{:S(2)}, u32[]{:S(2)}) collective-permute-start(bf16[128,1536]{1,0:T(8,128)(2,1)S(1)} %collective-permute-done.27.refs_2_), channel_id=1, source_target_pairs={{0,32},{16,240},{32,64},{48,16},{64,96},{80,48},{96,128},{112,80},... | collective-permute-start | bytes 1179656 | tf_op jit(solution)/shard_map/ppermute | solution.py:78
  112.5 12.6 %collective-permute-start.16 = (bf16[128,1536]{1,0:T(8,128)(2,1)S(1)}, bf16[128,1536]{1,0:T(8,128)(2,1)S(1)}, u32[]{:S(2)}, u32[]{:S(2)}) collective-permute-start(bf16[128,1536]{1,0:T(8,128)(2,1)S(1)} %get-tuple-element.25.own_ref.refs_0_), channel_id=1, source_target_pairs={{0,16},{16,0},{32,48},{48,32},{64,80},{80,64},{96,112},{112,96},{1... | collective-permute-start | bytes 1179656 | tf_op jit(solution)/shard_map/ppermute | solution.py:84
  117.4 10.9 %collective-permute-start.26 = (bf16[128,1536]{1,0:T(8,128)(2,1)S(1)}, bf16[128,1536]{1,0:T(8,128)(2,1)S(1)}, u32[]{:S(2)}, u32[]{:S(2)}) collective-permute-start(bf16[128,1536]{1,0:T(8,128)(2,1)S(1)} %collective-permute-done.25.refs_3_), channel_id=1, source_target_pairs={{0,32},{16,240},{32,64},{48,16},{64,96},{80,48},{96,128},{112,80},... | collective-permute-start | bytes 1179656 | tf_op jit(solution)/shard_map/ppermute | solution.py:75
  121.6 10.9 %collective-permute-start.29 = (bf16[128,1536]{1,0:T(8,128)(2,1)S(1)}, bf16[128,1536]{1,0:T(8,128)(2,1)S(1)}, u32[]{:S(2)}, u32[]{:S(2)}) collective-permute-start(bf16[128,1536]{1,0:T(8,128)(2,1)S(1)} %collective-permute-done.28.refs_4_), channel_id=1, source_target_pairs={{0,32},{16,240},{32,64},{48,16},{64,96},{80,48},{96,128},{112,80},... | collective-permute-start | bytes 1179656 | tf_op jit(solution)/shard_map/ppermute | solution.py:78
  132.5 16.2 %collective-permute-start.30 = (bf16[128,1536]{1,0:T(8,128)(2,1)S(1)}, bf16[128,1536]{1,0:T(8,128)(2,1)S(1)}, u32[]{:S(2)}, u32[]{:S(2)}) collective-permute-start(bf16[128,1536]{1,0:T(8,128)(2,1)S(1)} %collective-permute-done.26.refs_0_), channel_id=1, source_target_pairs={{0,32},{16,240},{32,64},{48,16},{64,96},{80,48},{96,128},{112,80},... | collective-permute-start | bytes 1179656 | tf_op jit(solution)/shard_map/ppermute | solution.py:75
  134.5 17.8 %collective-permute-start.19 = (bf16[4,192,128]{2,1,0:T(8,128)(2,1)S(1)}, bf16[4,192,128]{2,1,0:T(8,128)(2,1)S(1)}, u32[]{:S(2)}, u32[]{:S(2)}) collective-permute-start(bf16[4,192,128]{2,1,0:T(8,128)(2,1)S(1)} %get-tuple-element.28), channel_id=1, source_target_pairs={{0,3},{1,0},{2,1},{3,2},{4,7},{5,4},{6,5},{7,6},{8,11},{9,8},{10,9... | collective-permute-start | bytes 589832 | tf_op jit(solution)/shard_map/ppermute | solution.py:94
  139.1 13.2 %collective-permute-start.18 = (bf16[4,192,128]{2,1,0:T(8,128)(2,1)S(1)}, bf16[4,192,128]{2,1,0:T(8,128)(2,1)S(1)}, u32[]{:S(2)}, u32[]{:S(2)}) collective-permute-start(bf16[4,192,128]{2,1,0:T(8,128)(2,1)S(1)} %get-tuple-element.29), channel_id=1, source_target_pairs={{0,2},{1,3},{2,0},{3,1},{4,6},{5,7},{6,4},{7,5},{8,10},{9,11},{10,... | collective-permute-start | bytes 589832 | tf_op jit(solution)/shard_map/ppermute | solution.py:94
  143.2 9.4 %collective-permute-start.17 = (bf16[4,192,128]{2,1,0:T(8,128)(2,1)S(1)}, bf16[4,192,128]{2,1,0:T(8,128)(2,1)S(1)}, u32[]{:S(2)}, u32[]{:S(2)}) collective-permute-start(bf16[4,192,128]{2,1,0:T(8,128)(2,1)S(1)} %get-tuple-element.27), channel_id=1, source_target_pairs={{0,1},{1,2},{2,3},{3,0},{4,5},{5,6},{6,7},{7,4},{8,9},{9,10},{10,1... | collective-permute-start | bytes 589832 | tf_op jit(solution)/shard_map/ppermute | solution.py:94
  150.3 19.5 %collective-permute-start.31 = (bf16[192,1536]{1,0:T(8,128)(2,1)S(1)}, bf16[192,1536]{1,0:T(8,128)(2,1)S(1)}, u32[]{:S(2)}, u32[]{:S(2)}) collective-permute-start(bf16[192,1536]{1,0:T(8,128)(2,1)S(1)} %get-tuple-element.23), channel_id=1, source_target_pairs={{0,16},{16,0},{32,48},{48,32},{64,80},{80,64},{96,112},{112,96},{1... | collective-permute-start | bytes 1769480 | tf_op jit(solution)/shard_map/ppermute | solution.py:84
  152.7 11.4 %collective-permute-start.22 = (bf16[192,128]{1,0:T(8,128)(2,1)S(1)}, bf16[192,128]{1,0:T(8,128)(2,1)S(1)}, u32[]{:S(2)}, u32[]{:S(2)}) collective-permute-start(bf16[192,128]{1,0:T(8,128)(2,1)S(1)} %get-tuple-element.31), channel_id=1, source_target_pairs={{0,12},{1,13},{2,14},{3,15},{4,0},{5,1},{6,2},{7,3},{8,4},{9,5},{1... | collective-permute-start | bytes 147464 | tf_op jit(solution)/shard_map/ppermute | solution.py:89
  155.8 8.2 %collective-permute-start.21 = (bf16[192,128]{1,0:T(8,128)(2,1)S(1)}, bf16[192,128]{1,0:T(8,128)(2,1)S(1)}, u32[]{:S(2)}, u32[]{:S(2)}) collective-permute-start(bf16[192,128]{1,0:T(8,128)(2,1)S(1)} %get-tuple-element.32), channel_id=1, source_target_pairs={{0,8},{1,9},{2,10},{3,11},{4,12},{5,13},{6,14},{7,15},{8,0},{9,1},... | collective-permute-start | bytes 147464 | tf_op jit(solution)/shard_map/ppermute | solution.py:89
  159.7 6.0 %collective-permute-start.20 = (bf16[192,128]{1,0:T(8,128)(2,1)S(1)}, bf16[192,128]{1,0:T(8,128)(2,1)S(1)}, u32[]{:S(2)}, u32[]{:S(2)}) collective-permute-start(bf16[192,128]{1,0:T(8,128)(2,1)S(1)} %get-tuple-element.30), channel_id=1, source_target_pairs={{0,4},{1,5},{2,6},{3,7},{4,8},{5,9},{6,10},{7,11},{8,12},{9,13},{1... | collective-permute-start | bytes 147464 | tf_op jit(solution)/shard_map/ppermute | solution.py:89
  165.8 9.4 %collective-permute-start.23 = (bf16[192,128]{1,0:T(8,128)(2,1)S(1)}, bf16[192,128]{1,0:T(8,128)(2,1)S(1)}, u32[]{:S(2)}, u32[]{:S(2)}) collective-permute-start(bf16[192,128]{1,0:T(8,128)(2,1)S(1)} %fusion.8), channel_id=1, source_target_pairs={{0,0},{1,16},{2,14},{3,30},{4,15},{5,31},{6,12},{7,28},{8,13},{9,2... | collective-permute-start | bytes 147464 | tf_op jit(solution)/shard_map/ppermute | solution.py:225
  175.2 30.1 %collective-permute-start.32 = (bf16[192,1536]{1,0:T(8,128)(2,1)S(1)}, bf16[192,1536]{1,0:T(8,128)(2,1)S(1)}, u32[]{:S(2)}, u32[]{:S(2)}) collective-permute-start(bf16[192,1536]{1,0:T(8,128)(2,1)S(1)} %add_convert_fusion), channel_id=1, source_target_pairs={{0,256},{256,0},{1,257},{257,1},{2,258},{258,2},{3,259},{259,3},{4... | collective-permute-start | bytes 1769480 | tf_op jit(solution)/shard_map/ppermute | solution.py:232
  (3 other events, 35.2 us)

commit v10 on v7

v10 whole, which is shorter than its diff:
```python
import math

import jax
import jax.numpy as jnp
from jax import lax
from jax.experimental import pallas as pl
from jax.experimental.pallas import tpu as pltpu
from jax.sharding import Mesh
from jax.sharding import PartitionSpec as P

ROWS = 16
COLS = 16
SIDE = 4
LANES = 256
VMEM_BYTES = 32 * 2**20
COL = ("y", "x")


def after(value, *others):
    return lax.optimization_barrier((value,) + others)[0]


def local_kernel(kernel, out_shape, flops, operands):
    moved = sum(x.size * x.dtype.itemsize for x in (*operands, out_shape))
    return pl.pallas_call(
        kernel,
        out_shape=out_shape,
        in_specs=[pl.BlockSpec(memory_space=pltpu.VMEM)] * len(operands),
        out_specs=pl.BlockSpec(memory_space=pltpu.VMEM),
        compiler_params=pltpu.CompilerParams(vmem_limit_bytes=VMEM_BYTES),
        cost_estimate=pl.CostEstimate(flops=flops, bytes_accessed=moved, transcendentals=0),
    )(*operands)


def input_grad_kernel(weight_ref, grad_ref, pieces_ref):
    depth = pieces_ref.shape[2]
    for col in range(COLS):
        pieces_ref[col % SIDE, col // SIDE] = lax.dot_general(
            weight_ref[pl.ds(col * depth, depth), :],
            grad_ref[...],
            (((1,), (1,)), ((), ())),
            preferred_element_type=jnp.float32,
        ).astype(jnp.bfloat16)


def input_grad_pieces(weight, grad):
    depth = weight.shape[0] // COLS
    out_shape = jax.ShapeDtypeStruct((SIDE, SIDE, depth, grad.shape[0]), jnp.bfloat16)
    return local_kernel(input_grad_kernel, out_shape, 2 * weight.size * grad.shape[0], (weight, grad))


def token_sum_kernel(block_ref, grad_ref, total_ref):
    rows, _, tokens = block_ref.shape
    for start in range(0, total_ref.shape[1], LANES):
        units = pl.ds(start, LANES)
        total = None
        for row in range(rows):
            term = jnp.dot(
                block_ref[row],
                grad_ref[pl.ds(row * tokens, tokens), units],
                preferred_element_type=jnp.float32,
            )
            total = term if total is None else total + term
        total_ref[:, units] = total.astype(total_ref.dtype)


def token_sum(blocks, grads):
    depth = blocks.shape[1]
    out_shape = jax.ShapeDtypeStruct((depth, grads.shape[1]), jnp.bfloat16)
    return local_kernel(token_sum_kernel, out_shape, 2 * depth * grads.size, (blocks, grads))


def to_replica(value):
    return lax.ppermute(value, "dp", [(0, 1), (1, 0)])


def to_all_cols(block):
    copies = jnp.broadcast_to(block[None], (COLS,) + block.shape)
    return lax.all_to_all(copies, COL, 0, 0, tiled=True)


def sum_along(pieces, axis):
    pieces = lax.all_to_all(pieces, axis, 0, 0, tiled=True)
    return jnp.sum(pieces.astype(jnp.float32), axis=0).astype(jnp.bfloat16)


def turn_moves(replicas):
    moves = []
    for d in range(2 if replicas else 1):
        for r in range(ROWS):
            for c in range(COLS):
                target = c * COLS + r
                if replicas:
                    target += (1 - d) * ROWS * COLS
                moves.append(((d * ROWS + r) * COLS + c, target))
    return moves


def per_device(features, up_weight, out_grad):
    tokens, depth = features.shape
    half = up_weight.shape[1] // 2
    replica = lax.axis_index("dp")
    features = features.T

    def half_of(value, which):
        return lax.dynamic_slice_in_dim(value, which * half, half, axis=1)

    weight = lax.all_gather(half_of(up_weight, replica), "row", axis=0, tiled=True)
    by_depth = to_all_cols(jnp.concatenate([features, to_replica(features)], axis=1))
    turned = [
        lax.ppermute(features, ("row",) + COL, turn_moves(False)),
        lax.ppermute(features, ("dp", "row") + COL, turn_moves(True)),
    ]
    out_grad = jnp.concatenate(
        [half_of(out_grad, replica), to_replica(half_of(out_grad, 1 - replica))], axis=0
    )

    hidden = lax.dot_general(
        by_depth.reshape(COLS * depth, 2 * tokens),
        weight,
        (((0,), (0,)), ((), ())),
        preferred_element_type=jnp.float32,
    )
    normal_cdf = 0.5 * (1.0 + jax.scipy.special.erf(hidden / math.sqrt(2.0)))
    density = jnp.exp(-0.5 * hidden * hidden) / math.sqrt(2.0 * math.pi)
    gelu_half = (hidden * normal_cdf).astype(jnp.bfloat16)
    hidden_grad = (out_grad.astype(jnp.float32) * (normal_cdf + hidden * density)).astype(
        jnp.bfloat16
    )
    grads = lax.all_gather(hidden_grad, "row", axis=0, tiled=True)

    def halves(mine, other):
        parts = jnp.where(replica == 0, mine, other), jnp.where(replica == 0, other, mine)
        return jnp.concatenate(parts, axis=1)

    gelu_out = halves(gelu_half[:tokens], to_replica(gelu_half[tokens:]))
    by_token = to_all_cols(after(jnp.concatenate(turned, axis=1), hidden_grad))

    pieces = input_grad_pieces(weight, hidden_grad)
    feature_grad = sum_along(sum_along(pieces, "x"), "y")
    feature_grad = feature_grad[:, :tokens].astype(jnp.float32) + to_replica(
        feature_grad[:, tokens:]
    ).astype(jnp.float32)
    feature_grad = feature_grad.astype(jnp.bfloat16).T

    own = token_sum(by_token, grads)
    weight_grad = halves(own, to_replica(own)).astype(jnp.float32)
    return (gelu_out, feature_grad, weight_grad)


def solution(mesh):
    names = ("dp", "row") + COL
    fine = Mesh(mesh.devices.reshape(2, ROWS, SIDE, SIDE), names)
    by_tokens = P(("dp", "row"), COL)
    placed = (by_tokens, P("row", COL), by_tokens)
    return jax.shard_map(
        per_device,
        mesh=fine,
        in_specs=placed,
        out_specs=(by_tokens, by_tokens, P("row", COL)),
        check_vma=False,
    )
```

time: 181 us -> 221 us (1.22)
  the two profiles are of different devices: /device:TPU:17 before, /device:TPU:77 now
where the time goes in v10:
time: 221 us; the launch traced here: 220 us
  waiting for transfers between devices  103 us (47%)
  starting transfers between devices  59.5 us (27%)
  blocking collectives  20.5 us (9%)
  between operations  14.2 us (6%)
  local copies, waits for them, and re-layouts  10.5 us (5%)
  matrix products  4.76 us (2%)
  other arithmetic  4.63 us (2%)
  Pallas kernels  3.55 us (2%)
    ppermute x5, waiting for transfers between devices, to_replica(): return lax.ppermute(value, 'dp', [(0, 1), (1, 0)])  60.5 us
    all_to_all x2, waiting for transfers between devices, to_all_cols(): return lax.all_to_all(copies, COL, 0, 0, tiled=True)  32.9 us
    ppermute x5, starting transfers between devices, to_replica(): return lax.ppermute(value, 'dp', [(0, 1), (1, 0)])  25 us
    all_to_all x1, blocking collectives, sum_along(): pieces = lax.all_to_all(pieces, axis, 0, 0, tiled=True)  20.5 us
    all_to_all x2, starting transfers between devices, to_all_cols(): return lax.all_to_all(copies, COL, 0, 0, tiled=True)  18.3 us
    ppermute x1, starting transfers between devices, per_device(): lax.ppermute(features, ('dp', 'row') + COL, turn_moves(True))  10.8 us
    ppermute x1, waiting for transfers between devices, per_device(): lax.ppermute(features, ('row',) + COL, turn_moves(False))  8.97 us
    unnamed x12, local copies, waits for them, and re-layouts  7.13 us
  transfers between devices with their start and end apart: 12, of which 8 were waited for; matrix products, arithmetic and copies ran while one was open for 3% of the time, Pallas kernels for 2%

profile of v10, /device:TPU:77, one launch (start us, length us, event | category | flops | bytes accessed | tf_op | source)
XLA Modules:
  0.0 220.2 jit_solution(15523672792032085333)
XLA Ops:
  7.2 1.0 copy-done
  8.2 0.7 constant_dynamic-slice_fusion.2
  9.0 6.6 %collective-permute-start = (bf16[192,128]{1,0:T(8,128)(2,1)}, bf16[192,128]{1,0:T(8,128)(2,1)S(1)}, u32[]{:S(2)}, u32[]{:S(2)}) collective-permute-start(bf16[192,128]{1,0:T(8,128)(2,1)} %bitcast.7), channel_id=1, source_target_pairs={{0,256},{256,0},{1,257},{257,1},{2,258},{258,2},{3,259},{259,3},{4... | collective-permute-start | bytes 147464 | tf_op jit(solution)/shard_map/ppermute | solution.py:74
  15.6 2.5 %collective-permute-done = bf16[192,128]{1,0:T(8,128)(2,1)S(1)} collective-permute-done((bf16[192,128]{1,0:T(8,128)(2,1)}, bf16[192,128]{1,0:T(8,128)(2,1)S(1)}, u32[]{:S(2)}, u32[]{:S(2)}) %collective-permute-start) | collective-permute-done | bytes 49184 | tf_op jit(solution)/shard_map/ppermute | solution.py:74
  18.0 0.8 pad_maximum_fusion.1
  18.9 1.3 broadcast_in_dim.4
  20.2 7.6 %all-to-all-start = ((bf16[16,192,256]{2,1,0:T(8,128)(2,1)}), bf16[16,192,256]{2,1,0:T(8,128)(2,1)S(1)}, u32[]{:S(2)}, u32[]{:S(2)}) async-start(bf16[16,192,256]{2,1,0:T(8,128)(2,1)} %broadcast_in_dim.4), calls=%async_computation | async-start | bytes 3145728 | tf_op jit(solution)/shard_map/all_to_all | solution.py:79
  27.9 4.9 %collective-permute-start.2 = (bf16[128,768]{1,0:T(8,128)(2,1)S(1)}, bf16[128,768]{1,0:T(8,128)(2,1)S(1)}, u32[]{:S(2)}, u32[]{:S(2)}) collective-permute-start(bf16[128,768]{1,0:T(8,128)(2,1)S(1)} %get-tuple-element.12), channel_id=1, source_target_pairs={{0,256},{256,0},{1,257},{257,1},{2,258},{258,2},{3,259},{259,3},{4... | collective-permute-start | bytes 589832 | tf_op jit(solution)/shard_map/ppermute | solution.py:74
  32.8 21.5 %collective-permute-done.2 = bf16[128,768]{1,0:T(8,128)(2,1)S(1)} collective-permute-done((bf16[128,768]{1,0:T(8,128)(2,1)S(1)}, bf16[128,768]{1,0:T(8,128)(2,1)S(1)}, u32[]{:S(2)}, u32[]{:S(2)}) %collective-permute-start.2) | collective-permute-done | bytes 196640 | tf_op jit(solution)/shard_map/ppermute | solution.py:74
  54.3 17.9 %all-to-all-done = bf16[16,192,256]{2,1,0:T(8,128)(2,1)S(1)} async-done(((bf16[16,192,256]{2,1,0:T(8,128)(2,1)}), bf16[16,192,256]{2,1,0:T(8,128)(2,1)S(1)}, u32[]{:S(2)}, u32[]{:S(2)}) %all-to-all-start) | async-done | bytes 1572896 | tf_op jit(solution)/shard_map/all_to_all | solution.py:79
  72.2 4.8 %fusion.5 = (bf16[256,768]{1,0:T(8,128)(2,1)}, bf16[256,768]{1,0:T(8,128)(2,1)S(1)}) fusion(bf16[128,768]{1,0:T(8,128)(2,1)S(1)} %collective-permute-done.2, bf16[128,768]{1,0:T(8,128)(2,1)S(1)} %get-tuple-element.11, bf16[3072,256]{1,0:T(8,128)(2,1)S(1)} %bitcast.6, bf16[3072,768]{1,0:T(8,128)(2,1)} %all-gather.3.cloned.1.call-done.weight_ref), kind=kOutput, calls=%fused_computation.6 | convolution fusion | flops 1211105280 | bytes 7471104 | tf_op jit(solution)/shard_map/dot_general | solution.py:118
  77.0 2.3 %copy-done.2 = bf16[3072,768]{1,0:T(8,128)(2,1)S(1)} copy-done((bf16[3072,768]{1,0:T(8,128)(2,1)S(1)}, bf16[3072,768]{1,0:T(8,128)(2,1)}, u32[]{:S(2)}) %copy-start.2) | copy-done | bytes 4718616
  79.3 1.0 copy-done.3
  80.3 2.2 shard_map.58
  82.5 20.5 %all_to_all.20 = bf16[4,4,192,256]{3,2,1,0:T(8,128)(2,1)S(1)} all-to-all(bf16[4,4,192,256]{3,2,1,0:T(8,128)(2,1)S(1)} %shard_map.58), channel_id=1, replica_groups=mesh['dp'=2,'row'=16,'y'=4,'x'=4] {'x'}, dimensions={0} | all-to-all | bytes 3145728 | tf_op jit(solution)/shard_map/all_to_all | solution.py:83
  103.0 1.1 reduce_sum.24
  104.0 3.5 %all-to-all-start.2 = ((bf16[4,192,256]{2,1,0:T(8,128)(2,1)}), bf16[4,192,256]{2,1,0:T(8,128)(2,1)S(1)}, u32[]{:S(2)}, u32[]{:S(2)}) async-start(bf16[4,192,256]{2,1,0:T(8,128)(2,1)} %reduce_sum.24), calls=%async_computation.2 | async-start | bytes 786432 | tf_op jit(solution)/shard_map/all_to_all | solution.py:83
  107.5 10.8 %collective-permute-start.5 = (bf16[192,128]{1,0:T(8,128)(2,1)S(1)}, bf16[192,128]{1,0:T(8,128)(2,1)S(1)}, u32[]{:S(2)}, u32[]{:S(2)}) collective-permute-start(bf16[192,128]{1,0:T(8,128)(2,1)S(1)} %bitcast.9), channel_id=1, source_target_pairs={{0,256},{1,272},{2,288},{3,304},{4,320},{5,336},{6,352},{7,368},{8... | collective-permute-start | bytes 147464 | tf_op jit(solution)/shard_map/ppermute | solution.py:112
  118.3 1.9 collective-permute-start.4
  120.4 9.0 %collective-permute-done.4 = bf16[192,128]{1,0:T(8,128)(2,1)S(1)} collective-permute-done((bf16[192,128]{1,0:T(8,128)(2,1)S(1)}, bf16[192,128]{1,0:T(8,128)(2,1)S(1)}, u32[]{:S(2)}, u32[]{:S(2)}) %collective-permute-start.4) | collective-permute-done | bytes 49184 | tf_op jit(solution)/shard_map/ppermute | solution.py:111
  129.4 1.3 broadcast_in_dim.5
  130.7 10.7 %all-to-all-start.3 = ((bf16[16,192,256]{2,1,0:T(8,128)(2,1)}), bf16[16,192,256]{2,1,0:T(8,128)(2,1)S(1)}, u32[]{:S(2)}, u32[]{:S(2)}) async-start(bf16[16,192,256]{2,1,0:T(8,128)(2,1)} %broadcast_in_dim.5), calls=%async_computation.3 | async-start | bytes 3145728 | tf_op jit(solution)/shard_map/all_to_all | solution.py:79
  141.4 4.3 %collective-permute-start.1 = (bf16[128,768]{1,0:T(8,128)(2,1)S(1)}, bf16[128,768]{1,0:T(8,128)(2,1)S(1)}, u32[]{:S(2)}, u32[]{:S(2)}) collective-permute-start(bf16[128,768]{1,0:T(8,128)(2,1)S(1)} %slice.17), channel_id=1, source_target_pairs={{0,256},{256,0},{1,257},{257,1},{2,258},{258,2},{3,259},{259,3},{4... | collective-permute-start | bytes 589832 | tf_op jit(solution)/shard_map/ppermute | solution.py:74
  145.7 21.6 %collective-permute-done.1 = bf16[128,768]{1,0:T(8,128)(2,1)S(1)} collective-permute-done((bf16[128,768]{1,0:T(8,128)(2,1)S(1)}, bf16[128,768]{1,0:T(8,128)(2,1)S(1)}, u32[]{:S(2)}, u32[]{:S(2)}) %collective-permute-start.1) | collective-permute-done | bytes 196640 | tf_op jit(solution)/shard_map/ppermute | solution.py:74
  167.5 5.0 %collective-permute-start.3 = (bf16[192,128]{1,0:T(8,128)(2,1)S(1)}, bf16[192,128]{1,0:T(8,128)(2,1)S(1)}, u32[]{:S(2)}, u32[]{:S(2)}) collective-permute-start(bf16[192,128]{1,0:T(8,128)(2,1)S(1)} %slice.19), channel_id=1, source_target_pairs={{0,256},{256,0},{1,257},{257,1},{2,258},{258,2},{3,259},{259,3},{4... | collective-permute-start | bytes 147464 | tf_op jit(solution)/shard_map/ppermute | solution.py:74
  172.4 15.0 %all-to-all-done.3.block_ref = bf16[16,192,256]{2,1,0:T(8,128)(2,1)S(1)} async-done(((bf16[16,192,256]{2,1,0:T(8,128)(2,1)}), bf16[16,192,256]{2,1,0:T(8,128)(2,1)S(1)}, u32[]{:S(2)}, u32[]{:S(2)}) %all-to-all-start.3) | async-done | bytes 1572896 | tf_op jit(solution)/shard_map/all_to_all | solution.py:79
  187.4 2.8 %copy-done.1 = bf16[4096,768]{1,0:T(8,128)(2,1)S(1)} copy-done((bf16[4096,768]{1,0:T(8,128)(2,1)S(1)}, bf16[4096,768]{1,0:T(8,128)(2,1)}, u32[]{:S(2)}) %copy-start.1) | copy-done | bytes 6291480
  190.2 1.4 shard_map.59
  191.6 4.3 %collective-permute-start.6 = (bf16[192,768]{1,0:T(8,128)(2,1)S(1)}, bf16[192,768]{1,0:T(8,128)(2,1)S(1)}, u32[]{:S(2)}, u32[]{:S(2)}) collective-permute-start(bf16[192,768]{1,0:T(8,128)(2,1)S(1)} %shard_map.59), channel_id=1, source_target_pairs={{0,256},{256,0},{1,257},{257,1},{2,258},{258,2},{3,259},{259,3},{4... | collective-permute-start | bytes 884744 | tf_op jit(solution)/shard_map/ppermute | solution.py:74
  195.9 0.8 pad_maximum_fusion
  197.3 14.9 %collective-permute-done.6 = bf16[192,768]{1,0:T(8,128)(2,1)S(1)} collective-permute-done((bf16[192,768]{1,0:T(8,128)(2,1)S(1)}, bf16[192,768]{1,0:T(8,128)(2,1)S(1)}, u32[]{:S(2)}, u32[]{:S(2)}) %collective-permute-start.6) | collective-permute-done | bytes 294944 | tf_op jit(solution)/shard_map/ppermute | solution.py:74
  212.2 1.1 maximum_convert_fusion
  (25 shorter events, 1.2 us)
Async XLA Ops:
  7.2 1.1 copy-start
  7.2 65.0 %all-gather.3.cloned.1.call-start = ((), (), s32[]{:S(2)}) async-start(), calls=%async_computation.4 | async-start | bytes 5013504 | tf_op jit(solution)/shard_map/all_gather | solution.py:108
  9.0 9.1 %collective-permute-start = (bf16[192,128]{1,0:T(8,128)(2,1)}, bf16[192,128]{1,0:T(8,128)(2,1)S(1)}, u32[]{:S(2)}, u32[]{:S(2)}) collective-permute-start(bf16[192,128]{1,0:T(8,128)(2,1)} %bitcast.7), channel_id=1, source_target_pairs={{0,256},{256,0},{1,257},{257,1},{2,258},{258,2},{3,259},{259,3},{4... | collective-permute-start | bytes 147464 | tf_op jit(solution)/shard_map/ppermute | solution.py:74
  20.2 7.6 %copy-start.4 = (bf16[128,1536]{1,0:T(8,128)(2,1)S(1)}, bf16[128,1536]{1,0:T(8,128)(2,1)}, u32[]{:S(2)}) copy-start(bf16[128,1536]{1,0:T(8,128)(2,1)} %param.5) | copy-start | bytes 1179652
  20.2 52.0 %all-to-all-start = ((bf16[16,192,256]{2,1,0:T(8,128)(2,1)}), bf16[16,192,256]{2,1,0:T(8,128)(2,1)S(1)}, u32[]{:S(2)}, u32[]{:S(2)}) async-start(bf16[16,192,256]{2,1,0:T(8,128)(2,1)} %broadcast_in_dim.4), calls=%async_computation | async-start | bytes 3145728 | tf_op jit(solution)/shard_map/all_to_all | solution.py:79
  27.8 159.6 %all-gather.5.cloned.1.call-start = ((), (), s32[]{:S(2)}) async-start(), calls=%async_computation.5 | async-start | bytes 6684672 | tf_op jit(solution)/shard_map/all_gather | solution.py:130
  27.9 26.4 %collective-permute-start.2 = (bf16[128,768]{1,0:T(8,128)(2,1)S(1)}, bf16[128,768]{1,0:T(8,128)(2,1)S(1)}, u32[]{:S(2)}, u32[]{:S(2)}) collective-permute-start(bf16[128,768]{1,0:T(8,128)(2,1)S(1)} %get-tuple-element.12), channel_id=1, source_target_pairs={{0,256},{256,0},{1,257},{257,1},{2,258},{258,2},{3,259},{259,3},{4... | collective-permute-start | bytes 589832 | tf_op jit(solution)/shard_map/ppermute | solution.py:74
  77.0 2.3 %copy-start.2 = (bf16[3072,768]{1,0:T(8,128)(2,1)S(1)}, bf16[3072,768]{1,0:T(8,128)(2,1)}, u32[]{:S(2)}) copy-start(bf16[3072,768]{1,0:T(8,128)(2,1)} %all-gather.3.cloned.1.call-done.weight_ref) | copy-start | bytes 14155780
  79.3 1.0 copy-start.3
  103.0 4.5 %copy-start.5 = (bf16[128,192]{0,1:T(8,128)(2,1)S(1)}, bf16[128,192]{0,1:T(8,128)(2,1)}, u32[]{:S(2)}) copy-start(bf16[128,192]{0,1:T(8,128)(2,1)} %param.3) | copy-start | bytes 147460
  104.0 25.3 %all-to-all-start.2 = ((bf16[4,192,256]{2,1,0:T(8,128)(2,1)}), bf16[4,192,256]{2,1,0:T(8,128)(2,1)S(1)}, u32[]{:S(2)}, u32[]{:S(2)}) async-start(bf16[4,192,256]{2,1,0:T(8,128)(2,1)} %reduce_sum.24), calls=%async_computation.2 | async-start | bytes 786432 | tf_op jit(solution)/shard_map/all_to_all | solution.py:83
  107.5 12.9 %collective-permute-start.5 = (bf16[192,128]{1,0:T(8,128)(2,1)S(1)}, bf16[192,128]{1,0:T(8,128)(2,1)S(1)}, u32[]{:S(2)}, u32[]{:S(2)}) collective-permute-start(bf16[192,128]{1,0:T(8,128)(2,1)S(1)} %bitcast.9), channel_id=1, source_target_pairs={{0,256},{1,272},{2,288},{3,304},{4,320},{5,336},{6,352},{7,368},{8... | collective-permute-start | bytes 147464 | tf_op jit(solution)/shard_map/ppermute | solution.py:112
  118.3 11.1 %collective-permute-start.4 = (bf16[192,128]{1,0:T(8,128)(2,1)S(1)}, bf16[192,128]{1,0:T(8,128)(2,1)S(1)}, u32[]{:S(2)}, u32[]{:S(2)}) collective-permute-start(bf16[192,128]{1,0:T(8,128)(2,1)S(1)} %bitcast.10), channel_id=1, source_target_pairs={{0,0},{1,16},{2,32},{3,48},{4,64},{5,80},{6,96},{7,112},{8,128},{9... | collective-permute-start | bytes 147464 | tf_op jit(solution)/shard_map/ppermute | solution.py:111
  130.7 56.7 %all-to-all-start.3 = ((bf16[16,192,256]{2,1,0:T(8,128)(2,1)}), bf16[16,192,256]{2,1,0:T(8,128)(2,1)S(1)}, u32[]{:S(2)}, u32[]{:S(2)}) async-start(bf16[16,192,256]{2,1,0:T(8,128)(2,1)} %broadcast_in_dim.5), calls=%async_computation.3 | async-start | bytes 3145728 | tf_op jit(solution)/shard_map/all_to_all | solution.py:79
  141.4 26.0 %collective-permute-start.1 = (bf16[128,768]{1,0:T(8,128)(2,1)S(1)}, bf16[128,768]{1,0:T(8,128)(2,1)S(1)}, u32[]{:S(2)}, u32[]{:S(2)}) collective-permute-start(bf16[128,768]{1,0:T(8,128)(2,1)S(1)} %slice.17), channel_id=1, source_target_pairs={{0,256},{256,0},{1,257},{257,1},{2,258},{258,2},{3,259},{259,3},{4... | collective-permute-start | bytes 589832 | tf_op jit(solution)/shard_map/ppermute | solution.py:74
  167.5 29.2 %collective-permute-start.3 = (bf16[192,128]{1,0:T(8,128)(2,1)S(1)}, bf16[192,128]{1,0:T(8,128)(2,1)S(1)}, u32[]{:S(2)}, u32[]{:S(2)}) collective-permute-start(bf16[192,128]{1,0:T(8,128)(2,1)S(1)} %slice.19), channel_id=1, source_target_pairs={{0,256},{256,0},{1,257},{257,1},{2,258},{258,2},{3,259},{259,3},{4... | collective-permute-start | bytes 147464 | tf_op jit(solution)/shard_map/ppermute | solution.py:74
  187.4 2.8 %copy-start.1 = (bf16[4096,768]{1,0:T(8,128)(2,1)S(1)}, bf16[4096,768]{1,0:T(8,128)(2,1)}, u32[]{:S(2)}) copy-start(bf16[4096,768]{1,0:T(8,128)(2,1)} %all-gather.5.cloned.1.call-done.grad_ref) | copy-start | bytes 18874372
  191.6 20.6 %collective-permute-start.6 = (bf16[192,768]{1,0:T(8,128)(2,1)S(1)}, bf16[192,768]{1,0:T(8,128)(2,1)S(1)}, u32[]{:S(2)}, u32[]{:S(2)}) collective-permute-start(bf16[192,768]{1,0:T(8,128)(2,1)S(1)} %shard_map.59), channel_id=1, source_target_pairs={{0,256},{256,0},{1,257},{257,1},{2,258},{258,2},{3,259},{259,3},{4... | collective-permute-start | bytes 884744 | tf_op jit(solution)/shard_map/ppermute | solution.py:74
Sparse Core Ops, SparseCore 0:
  10.7 49.4 all-gather.2
  77.1 59.1 all-gather.4

commit v11 on v10

v11 whole, which is shorter than its diff:
```python
import math

import jax
import jax.numpy as jnp
from jax import lax
from jax.experimental import pallas as pl
from jax.experimental.pallas import tpu as pltpu
from jax.sharding import Mesh
from jax.sharding import PartitionSpec as P

ROWS = 16
COLS = 16
SIDE = 4
LANES = 256
VMEM_BYTES = 32 * 2**20
COL = ("y", "x")


def after(value, *others):
    return lax.optimization_barrier((value,) + others)[0]


def local_kernel(kernel, out_shape, flops, operands):
    moved = sum(x.size * x.dtype.itemsize for x in (*operands, out_shape))
    return pl.pallas_call(
        kernel,
        out_shape=out_shape,
        in_specs=[pl.BlockSpec(memory_space=pltpu.VMEM)] * len(operands),
        out_specs=pl.BlockSpec(memory_space=pltpu.VMEM),
        compiler_params=pltpu.CompilerParams(vmem_limit_bytes=VMEM_BYTES),
        cost_estimate=pl.CostEstimate(flops=flops, bytes_accessed=moved, transcendentals=0),
    )(*operands)


def both_replicas(block_ref, col):
    y, x = divmod(col, SIDE)
    return jnp.concatenate([block_ref[x, y], block_ref[x, SIDE + y]], axis=1)


def hidden_kernel(block_ref, weight_ref, hidden_ref):
    depth = block_ref.shape[2]
    blocks = [both_replicas(block_ref, col) for col in range(COLS)]
    for start in range(0, hidden_ref.shape[1], LANES):
        units = pl.ds(start, LANES)
        total = None
        for col, block in enumerate(blocks):
            term = lax.dot_general(
                block,
                weight_ref[pl.ds(col * depth, depth), units],
                (((0,), (0,)), ((), ())),
                preferred_element_type=jnp.float32,
            )
            total = term if total is None else total + term
        hidden_ref[:, units] = total


def hidden_sum(blocks, weight):
    tokens = 2 * blocks.shape[3]
    out_shape = jax.ShapeDtypeStruct((tokens, weight.shape[1]), jnp.float32)
    return local_kernel(hidden_kernel, out_shape, 2 * tokens * weight.size, (blocks, weight))


def input_grad_kernel(weight_ref, grad_ref, pieces_ref):
    depth, tokens = pieces_ref.shape[2:]
    for col in range(COLS):
        y, x = divmod(col, SIDE)
        piece = lax.dot_general(
            weight_ref[pl.ds(col * depth, depth), :],
            grad_ref[...],
            (((1,), (1,)), ((), ())),
            preferred_element_type=jnp.float32,
        ).astype(jnp.bfloat16)
        pieces_ref[x, y] = piece[:, :tokens]
        pieces_ref[x, SIDE + y] = piece[:, tokens:]


def input_grad_pieces(weight, grad):
    depth = weight.shape[0] // COLS
    out_shape = jax.ShapeDtypeStruct((SIDE, 2 * SIDE, depth, grad.shape[0] // 2), jnp.bfloat16)
    return local_kernel(input_grad_kernel, out_shape, 2 * weight.size * grad.shape[0], (weight, grad))


def token_sum_kernel(block_ref, grad_ref, total_ref):
    tokens = 2 * block_ref.shape[3]
    blocks = [both_replicas(block_ref, row) for row in range(ROWS)]
    for start in range(0, total_ref.shape[1], LANES):
        units = pl.ds(start, LANES)
        total = None
        for row, block in enumerate(blocks):
            term = jnp.dot(
                block,
                grad_ref[pl.ds(row * tokens, tokens), units],
                preferred_element_type=jnp.float32,
            )
            total = term if total is None else total + term
        total_ref[:, units] = total.astype(total_ref.dtype)


def token_sum(blocks, grads):
    depth = blocks.shape[2]
    out_shape = jax.ShapeDtypeStruct((depth, grads.shape[1]), jnp.bfloat16)
    return local_kernel(token_sum_kernel, out_shape, 2 * depth * grads.size, (blocks, grads))


def to_replica(value):
    return lax.ppermute(value, "dp", [(0, 1), (1, 0)])


def to_all(block, axis, size):
    copies = jnp.broadcast_to(block[None], (size,) + block.shape)
    return lax.all_to_all(copies, axis, 0, 0, tiled=True)


def sum_along(pieces, axis):
    pieces = lax.all_to_all(pieces, axis, 0, 0, tiled=True)
    return jnp.sum(pieces.astype(jnp.float32), axis=0).astype(jnp.bfloat16)


def per_device(features, up_weight, out_grad):
    tokens, depth = features.shape
    half = up_weight.shape[1] // 2
    replica = lax.axis_index("dp")
    features = features.T

    def half_of(value, which):
        return lax.dynamic_slice_in_dim(value, which * half, half, axis=1)

    def by_replica(mine, other, axis):
        parts = jnp.where(replica == 0, mine, other), jnp.where(replica == 0, other, mine)
        return jnp.concatenate(parts, axis=axis)

    weight = lax.all_gather(half_of(up_weight, replica), "row", axis=0, tiled=True)
    line = to_all(features, ("dp", "y"), 2 * SIDE)
    by_depth = to_all(line, "x", SIDE)
    turns = [(r * COLS + c, c * COLS + r) for r in range(ROWS) for c in range(COLS)]
    turned = lax.ppermute(features, ("row",) + COL, turns)
    turned_line = to_all(after(turned, line), ("dp", "y"), 2 * SIDE)
    out_grad = by_replica(
        half_of(out_grad, replica), to_replica(half_of(out_grad, 1 - replica)), 0
    )

    hidden = hidden_sum(by_depth, weight)
    normal_cdf = 0.5 * (1.0 + jax.scipy.special.erf(hidden / math.sqrt(2.0)))
    density = jnp.exp(-0.5 * hidden * hidden) / math.sqrt(2.0 * math.pi)
    gelu_half = (hidden * normal_cdf).astype(jnp.bfloat16)
    hidden_grad = (out_grad.astype(jnp.float32) * (normal_cdf + hidden * density)).astype(
        jnp.bfloat16
    )
    grads = lax.all_gather(hidden_grad, "row", axis=0, tiled=True)

    by_token = to_all(after(turned_line, hidden_grad), "x", SIDE)
    pieces = input_grad_pieces(weight, after(hidden_grad, by_token))
    feature_grad = sum_along(sum_along(pieces, "x"), ("dp", "y")).T

    mine, other = (
        lax.dynamic_slice_in_dim(gelu_half, which * tokens, tokens, axis=0)
        for which in (replica, 1 - replica)
    )
    gelu_out = by_replica(mine, to_replica(other), 1)
    own = token_sum(by_token, grads)
    weight_grad = by_replica(own, to_replica(own), 1).astype(jnp.float32)
    return (gelu_out, feature_grad, weight_grad)


def solution(mesh):
    names = ("dp", "row") + COL
    fine = Mesh(mesh.devices.reshape(2, ROWS, SIDE, SIDE), names)
    by_tokens = P(("dp", "row"), COL)
    placed = (by_tokens, P("row", COL), by_tokens)
    return jax.shard_map(
        per_device,
        mesh=fine,
        in_specs=placed,
        out_specs=(by_tokens, by_tokens, P("row", COL)),
        check_vma=False,
    )
```

time: 221 us -> 200 us (0.905)
  the two profiles are of different devices: /device:TPU:77 before, /device:TPU:56 now
where the time goes in v11:
time: 200 us; the launch traced here: 198 us
  waiting for transfers between devices  60.5 us (30%)
  blocking collectives  59.2 us (30%)
  starting transfers between devices  40.3 us (20%)
  between operations  14.2 us (7%)
  local copies, waits for them, and re-layouts  9.68 us (5%)
  other arithmetic  7.36 us (4%)
  Pallas kernels  6.66 us (3%)
    all_to_all x3, blocking collectives, to_all(): return lax.all_to_all(copies, axis, 0, 0, tiled=True)  59.2 us
    ppermute x3, waiting for transfers between devices, to_replica(): return lax.ppermute(value, 'dp', [(0, 1), (1, 0)])  21.3 us
    all_to_all x2, waiting for transfers between devices, sum_along(): pieces = lax.all_to_all(pieces, axis, 0, 0, tiled=True)  19.1 us
    ppermute x3, starting transfers between devices, to_replica(): return lax.ppermute(value, 'dp', [(0, 1), (1, 0)])  15.6 us
    all_to_all x2, starting transfers between devices, sum_along(): pieces = lax.all_to_all(pieces, axis, 0, 0, tiled=True)  13.4 us
    all_gather x1, waiting for transfers between devices, per_device(): lax.all_gather(half_of(up_weight, replica), 'row', axis=0, tiled=True)  9.53 us
    ppermute x1, starting transfers between devices, per_device(): turned = lax.ppermute(features, ('row',) + COL, turns)  6.73 us
    pallas_call x3, Pallas kernels, local_kernel(): pl.pallas_call(kernel, out_shape=out_shape, in_specs=[pl.BlockSpec(memory...  6.66 us
  transfers between devices with their start and end apart: 9, of which 7 were waited for; matrix products, arithmetic and copies ran while one was open for 4% of the time, Pallas kernels for 2%

profile of v11, /device:TPU:56, one launch (start us, length us, event | category | flops | bytes accessed | tf_op | source)
XLA Modules:
  0.0 198.0 jit_solution(9668174996257382759)
XLA Ops:
  7.2 1.0 copy-done
  8.2 0.7 constant_dynamic-slice_fusion.2
  9.0 0.9 broadcast_in_dim.8
  9.8 17.1 %all_to_all.30 = bf16[8,192,128]{2,1,0:T(8,128)(2,1)S(1)} all-to-all(bf16[8,192,128]{2,1,0:T(8,128)(2,1)S(1)} %broadcast_in_dim.8), channel_id=1, replica_groups=mesh['dp'=2,'row'=16,'y'=4,'x'=4] {'dp','y'}, dimensions={0} | all-to-all | bytes 786432 | tf_op jit(solution)/shard_map/all_to_all | solution.py:111
  27.0 1.5 broadcast_in_dim.9
  28.5 4.6 %all-to-all-start.1 = ((bf16[4,8,192,128]{3,2,1,0:T(8,128)(2,1)}), bf16[4,8,192,128]{3,2,1,0:T(8,128)(2,1)S(1)}, u32[]{:S(2)}, u32[]{:S(2)}) async-start(bf16[4,8,192,128]{3,2,1,0:T(8,128)(2,1)} %broadcast_in_dim.9), calls=%async_computation.1 | async-start | bytes 3145728 | tf_op jit(solution)/shard_map/all_to_all | solution.py:111
  33.1 5.8 %collective-permute-start.1 = (bf16[128,768]{1,0:T(8,128)(2,1)S(1)}, bf16[128,768]{1,0:T(8,128)(2,1)S(1)}, u32[]{:S(2)}, u32[]{:S(2)}) collective-permute-start(bf16[128,768]{1,0:T(8,128)(2,1)S(1)} %constant_dynamic-slice_fusion), channel_id=1, source_target_pairs={{0,256},{256,0},{1,257},{257,1},{2,258},{258,2},{3,259},{259,3},{4... | collective-permute-start | bytes 589832 | tf_op jit(solution)/shard_map/ppermute | solution.py:106
  38.9 6.3 %collective-permute-done.1 = bf16[128,768]{1,0:T(8,128)(2,1)S(1)} collective-permute-done((bf16[128,768]{1,0:T(8,128)(2,1)S(1)}, bf16[128,768]{1,0:T(8,128)(2,1)S(1)}, u32[]{:S(2)}, u32[]{:S(2)}) %collective-permute-start.1) | collective-permute-done | bytes 196640 | tf_op jit(solution)/shard_map/ppermute | solution.py:106
  45.4 6.0 %all-to-all-done.1.block_ref = bf16[4,8,192,128]{3,2,1,0:T(8,128)(2,1)S(1)} async-done(((bf16[4,8,192,128]{3,2,1,0:T(8,128)(2,1)}), bf16[4,8,192,128]{3,2,1,0:T(8,128)(2,1)S(1)}, u32[]{:S(2)}, u32[]{:S(2)}) %all-to-all-start.1) | async-done | bytes 1572896 | tf_op jit(solution)/shard_map/all_to_all | solution.py:111
  51.4 9.5 %all-gather.3.cloned.1.call-done.weight_ref = bf16[3072,768]{1,0:T(8,128)(2,1)} async-done(((bf16[192,768]{1,0:T(8,128)(2,1)}), bf16[3072,768]{1,0:T(8,128)(2,1)}) %all-gather.3.cloned.1.call-update) | async-done | bytes 4718608 | tf_op jit(solution)/shard_map/all_gather | solution.py:132
  60.9 2.3 %copy-done.1 = bf16[3072,768]{1,0:T(8,128)(2,1)S(1)} copy-done((bf16[3072,768]{1,0:T(8,128)(2,1)S(1)}, bf16[3072,768]{1,0:T(8,128)(2,1)}, u32[]{:S(2)}) %copy-start.1) | copy-done | bytes 4718616
  63.3 1.8 shard_map.58
  65.1 1.1 fusion.5
  66.3 6.7 %collective-permute-start.2 = (bf16[192,128]{1,0:T(8,128)(2,1)S(1)}, bf16[192,128]{1,0:T(8,128)(2,1)S(1)}, u32[]{:S(2)}, u32[]{:S(2)}) collective-permute-start(bf16[192,128]{1,0:T(8,128)(2,1)S(1)} %bitcast.3), channel_id=1, source_target_pairs={{0,0},{1,16},{2,32},{3,48},{4,64},{5,80},{6,96},{7,112},{8,128},{9... | collective-permute-start | bytes 147464 | tf_op jit(solution)/shard_map/ppermute | solution.py:136
  73.0 4.5 %collective-permute-done.2 = bf16[192,128]{1,0:T(8,128)(2,1)S(1)} collective-permute-done((bf16[192,128]{1,0:T(8,128)(2,1)S(1)}, bf16[192,128]{1,0:T(8,128)(2,1)S(1)}, u32[]{:S(2)}, u32[]{:S(2)}) %collective-permute-start.2) | collective-permute-done | bytes 49184 | tf_op jit(solution)/shard_map/ppermute | solution.py:136
  77.5 17.0 %all_to_all.31 = bf16[8,192,128]{2,1,0:T(8,128)(2,1)S(1)} all-to-all(bf16[8,192,128]{2,1,0:T(8,128)(2,1)S(1)} %broadcast_in_dim.10), channel_id=1, replica_groups=mesh['dp'=2,'row'=16,'y'=4,'x'=4] {'dp','y'}, dimensions={0} | all-to-all | bytes 786432 | tf_op jit(solution)/shard_map/all_to_all | solution.py:111
  94.9 25.1 %all_to_all.32.block_ref = bf16[4,8,192,128]{3,2,1,0:T(8,128)(2,1)S(1)} all-to-all(bf16[4,8,192,128]{3,2,1,0:T(8,128)(2,1)S(1)} %broadcast_in_dim.11), channel_id=1, replica_groups=mesh['dp'=2,'row'=16,'y'=4,'x'=4] {'x'}, dimensions={0} | all-to-all | bytes 3145728 | tf_op jit(solution)/shard_map/all_to_all | solution.py:111
  120.0 3.4 %shard_map.59 = bf16[4,8,192,128]{3,2,1,0:T(8,128)(2,1)} custom-call(bf16[3072,768]{1,0:T(8,128)(2,1)S(1)} %copy-done.2, bf16[256,768]{1,0:T(8,128)(2,1)S(1)} %copy-done.4), custom_call_target="tpu_custom_call" | custom-call | flops 1207959552 | bytes 6684672 | tf_op jit(solution)/shard_map/pallas_call | solution.py:25
  123.4 4.3 %all-to-all-start.4 = ((bf16[4,8,192,128]{3,2,1,0:T(8,128)(2,1)}), bf16[4,8,192,128]{3,2,1,0:T(8,128)(2,1)}, u32[]{:S(2)}, u32[]{:S(2)}) async-start(bf16[4,8,192,128]{3,2,1,0:T(8,128)(2,1)} %shard_map.59), calls=%async_computation.4 | async-start | bytes 3145728 | tf_op jit(solution)/shard_map/all_to_all | solution.py:115
  127.8 19.1 %all-to-all-done.4 = bf16[4,8,192,128]{3,2,1,0:T(8,128)(2,1)} async-done(((bf16[4,8,192,128]{3,2,1,0:T(8,128)(2,1)}), bf16[4,8,192,128]{3,2,1,0:T(8,128)(2,1)}, u32[]{:S(2)}, u32[]{:S(2)}) %all-to-all-start.4) | async-done | bytes 1572896 | tf_op jit(solution)/shard_map/all_to_all | solution.py:115
  146.9 2.5 %reduce_sum.24 = bf16[8,192,128]{2,1,0:T(8,128)(2,1)} reduce(bf16[4,8,192,128]{3,2,1,0:T(8,128)(2,1)} %all-to-all-done.4, bf16[]{:T(256)} %constant.33.clone.1), dimensions={0}, to_apply=%region_0.1 | reduce | flops 589824 | bytes 1966082 | tf_op jit(solution)/shard_map/reduce_sum | solution.py:116
  149.5 9.0 %all-to-all-start.5 = ((bf16[8,192,128]{2,1,0:T(8,128)(2,1)}), bf16[8,192,128]{2,1,0:T(8,128)(2,1)S(1)}, u32[]{:S(2)}, u32[]{:S(2)}) async-start(bf16[8,192,128]{2,1,0:T(8,128)(2,1)} %reduce_sum.24), calls=%async_computation.5 | async-start | bytes 786432 | tf_op jit(solution)/shard_map/all_to_all | solution.py:115
  158.5 5.1 %collective-permute-start = (bf16[128,768]{1,0:T(8,128)(2,1)S(1)}, bf16[128,768]{1,0:T(8,128)(2,1)}, u32[]{:S(2)}, u32[]{:S(2)}) collective-permute-start(bf16[128,768]{1,0:T(8,128)(2,1)S(1)} %constant_dynamic-slice_fusion.1), channel_id=1, source_target_pairs={{0,256},{256,0},{1,257},{257,1},{2,258},{258,2},{3,259},{259,3},{4... | collective-permute-start | bytes 589832 | tf_op jit(solution)/shard_map/ppermute | solution.py:106
  163.7 2.8 %copy-done.3 = bf16[4096,768]{1,0:T(8,128)(2,1)S(1)} copy-done((bf16[4096,768]{1,0:T(8,128)(2,1)S(1)}, bf16[4096,768]{1,0:T(8,128)(2,1)}, u32[]{:S(2)}) %copy-start.3) | copy-done | bytes 6291480
  166.5 1.4 shard_map.60
  167.9 4.6 %collective-permute-start.3 = (bf16[192,768]{1,0:T(8,128)(2,1)S(1)}, bf16[192,768]{1,0:T(8,128)(2,1)S(1)}, u32[]{:S(2)}, u32[]{:S(2)}) collective-permute-start(bf16[192,768]{1,0:T(8,128)(2,1)S(1)} %shard_map.60), channel_id=1, source_target_pairs={{0,256},{256,0},{1,257},{257,1},{2,258},{258,2},{3,259},{259,3},{4... | collective-permute-start | bytes 884744 | tf_op jit(solution)/shard_map/ppermute | solution.py:106
  172.5 7.2 %collective-permute-done = bf16[128,768]{1,0:T(8,128)(2,1)} collective-permute-done((bf16[128,768]{1,0:T(8,128)(2,1)S(1)}, bf16[128,768]{1,0:T(8,128)(2,1)}, u32[]{:S(2)}, u32[]{:S(2)}) %collective-permute-start) | collective-permute-done | bytes 196640 | tf_op jit(solution)/shard_map/ppermute | solution.py:106
  179.7 1.0 broadcast_select_fusion.5
  180.7 0.8 pad_maximum_fusion
  181.5 0.7 reduce_sum.25
  182.1 7.8 %collective-permute-done.3 = bf16[192,768]{1,0:T(8,128)(2,1)S(1)} collective-permute-done((bf16[192,768]{1,0:T(8,128)(2,1)S(1)}, bf16[192,768]{1,0:T(8,128)(2,1)S(1)}, u32[]{:S(2)}, u32[]{:S(2)}) %collective-permute-start.3) | collective-permute-done | bytes 294944 | tf_op jit(solution)/shard_map/ppermute | solution.py:106
  190.0 1.1 maximum_convert_fusion
  (23 shorter events, 0.7 us)
Async XLA Ops:
  7.2 1.1 copy-start
  7.2 53.7 %all-gather.3.cloned.1.call-start = ((), (), s32[]{:S(2)}) async-start(), calls=%async_computation.6 | async-start | bytes 5013504 | tf_op jit(solution)/shard_map/all_gather | solution.py:132
  28.5 4.6 %copy-start.5 = (bf16[128,1536]{1,0:T(8,128)(2,1)S(1)}, bf16[128,1536]{1,0:T(8,128)(2,1)}, u32[]{:S(2)}) copy-start(bf16[128,1536]{1,0:T(8,128)(2,1)} %param.5) | copy-start | bytes 1179652
  28.5 22.9 %all-to-all-start.1 = ((bf16[4,8,192,128]{3,2,1,0:T(8,128)(2,1)}), bf16[4,8,192,128]{3,2,1,0:T(8,128)(2,1)S(1)}, u32[]{:S(2)}, u32[]{:S(2)}) async-start(bf16[4,8,192,128]{3,2,1,0:T(8,128)(2,1)} %broadcast_in_dim.9), calls=%async_computation.1 | async-start | bytes 3145728 | tf_op jit(solution)/shard_map/all_to_all | solution.py:111
  33.0 130.6 %all-gather.5.cloned.1.call-start = ((), (), s32[]{:S(2)}) async-start(), calls=%async_computation.7 | async-start | bytes 6684672 | tf_op jit(solution)/shard_map/all_gather | solution.py:149
  33.1 12.2 %collective-permute-start.1 = (bf16[128,768]{1,0:T(8,128)(2,1)S(1)}, bf16[128,768]{1,0:T(8,128)(2,1)S(1)}, u32[]{:S(2)}, u32[]{:S(2)}) collective-permute-start(bf16[128,768]{1,0:T(8,128)(2,1)S(1)} %constant_dynamic-slice_fusion), channel_id=1, source_target_pairs={{0,256},{256,0},{1,257},{257,1},{2,258},{258,2},{3,259},{259,3},{4... | collective-permute-start | bytes 589832 | tf_op jit(solution)/shard_map/ppermute | solution.py:106
  60.9 2.3 %copy-start.1 = (bf16[3072,768]{1,0:T(8,128)(2,1)S(1)}, bf16[3072,768]{1,0:T(8,128)(2,1)}, u32[]{:S(2)}) copy-start(bf16[3072,768]{1,0:T(8,128)(2,1)} %all-gather.3.cloned.1.call-done.weight_ref) | copy-start | bytes 14155780
  65.1 1.2 copy-start.6
  66.3 11.2 %collective-permute-start.2 = (bf16[192,128]{1,0:T(8,128)(2,1)S(1)}, bf16[192,128]{1,0:T(8,128)(2,1)S(1)}, u32[]{:S(2)}, u32[]{:S(2)}) collective-permute-start(bf16[192,128]{1,0:T(8,128)(2,1)S(1)} %bitcast.3), channel_id=1, source_target_pairs={{0,0},{1,16},{2,32},{3,48},{4,64},{5,80},{6,96},{7,112},{8,128},{9... | collective-permute-start | bytes 147464 | tf_op jit(solution)/shard_map/ppermute | solution.py:136
  94.5 25.5 %copy-start.2 = (bf16[3072,768]{1,0:T(8,128)(2,1)S(1)}, bf16[3072,768]{1,0:T(8,128)(2,1)}, u32[]{:S(2)}) copy-start(bf16[3072,768]{1,0:T(8,128)(2,1)} %all-gather.3.cloned.1.call-done.weight_ref) | copy-start | bytes 14155780
  94.9 25.1 %copy-start.4 = (bf16[256,768]{1,0:T(8,128)(2,1)S(1)}, bf16[256,768]{1,0:T(8,128)(2,1)}, u32[]{:S(2)}) copy-start(bf16[256,768]{1,0:T(8,128)(2,1)} %get-tuple-element.8.grad_ref) | copy-start | bytes 1179652
  123.4 23.5 %all-to-all-start.4 = ((bf16[4,8,192,128]{3,2,1,0:T(8,128)(2,1)}), bf16[4,8,192,128]{3,2,1,0:T(8,128)(2,1)}, u32[]{:S(2)}, u32[]{:S(2)}) async-start(bf16[4,8,192,128]{3,2,1,0:T(8,128)(2,1)} %shard_map.59), calls=%async_computation.4 | async-start | bytes 3145728 | tf_op jit(solution)/shard_map/all_to_all | solution.py:115
  149.5 32.0 %all-to-all-start.5 = ((bf16[8,192,128]{2,1,0:T(8,128)(2,1)}), bf16[8,192,128]{2,1,0:T(8,128)(2,1)S(1)}, u32[]{:S(2)}, u32[]{:S(2)}) async-start(bf16[8,192,128]{2,1,0:T(8,128)(2,1)} %reduce_sum.24), calls=%async_computation.5 | async-start | bytes 786432 | tf_op jit(solution)/shard_map/all_to_all | solution.py:115
  158.5 21.2 %collective-permute-start = (bf16[128,768]{1,0:T(8,128)(2,1)S(1)}, bf16[128,768]{1,0:T(8,128)(2,1)}, u32[]{:S(2)}, u32[]{:S(2)}) collective-permute-start(bf16[128,768]{1,0:T(8,128)(2,1)S(1)} %constant_dynamic-slice_fusion.1), channel_id=1, source_target_pairs={{0,256},{256,0},{1,257},{257,1},{2,258},{258,2},{3,259},{259,3},{4... | collective-permute-start | bytes 589832 | tf_op jit(solution)/shard_map/ppermute | solution.py:106
  163.7 2.8 %copy-start.3 = (bf16[4096,768]{1,0:T(8,128)(2,1)S(1)}, bf16[4096,768]{1,0:T(8,128)(2,1)}, u32[]{:S(2)}) copy-start(bf16[4096,768]{1,0:T(8,128)(2,1)} %all-gather.5.cloned.1.call-done.grad_ref) | copy-start | bytes 18874372
  167.9 22.0 %collective-permute-start.3 = (bf16[192,768]{1,0:T(8,128)(2,1)S(1)}, bf16[192,768]{1,0:T(8,128)(2,1)S(1)}, u32[]{:S(2)}, u32[]{:S(2)}) collective-permute-start(bf16[192,768]{1,0:T(8,128)(2,1)S(1)} %shard_map.60), channel_id=1, source_target_pairs={{0,256},{256,0},{1,257},{257,1},{2,258},{258,2},{3,259},{259,3},{4... | collective-permute-start | bytes 884744 | tf_op jit(solution)/shard_map/ppermute | solution.py:106
Sparse Core Ops, SparseCore 0:
  10.7 50.1 all-gather.2
  66.4 47.7 all-gather.4

commit v12 on v11

--- a/solution.py
+++ b/solution.py
@@ -13,6 +13,7 @@
 SIDE = 4
 LANES = 256
 VMEM_BYTES = 32 * 2**20
+TILED_VMEM_BYTES = 56 * 2**20
 COL = ("y", "x")
 
 
@@ -20,16 +21,22 @@
     return lax.optimization_barrier((value,) + others)[0]
 
 
-def local_kernel(kernel, out_shape, flops, operands):
+def cost_of(flops, operands, out_shape):
     moved = sum(x.size * x.dtype.itemsize for x in (*operands, out_shape))
+    return pl.CostEstimate(flops=flops, bytes_accessed=moved, transcendentals=0)
+
+
+def tiled_kernel(kernel, out_shape, flops, blocks, value):
+    whole = pl.BlockSpec(blocks.shape, lambda tile: (0,) * blocks.ndim)
     return pl.pallas_call(
         kernel,
         out_shape=out_shape,
-        in_specs=[pl.BlockSpec(memory_space=pltpu.VMEM)] * len(operands),
-        out_specs=pl.BlockSpec(memory_space=pltpu.VMEM),
-        compiler_params=pltpu.CompilerParams(vmem_limit_bytes=VMEM_BYTES),
-        cost_estimate=pl.CostEstimate(flops=flops, bytes_accessed=moved, transcendentals=0),
-    )(*operands)
+        grid=(out_shape.shape[1] // LANES,),
+        in_specs=[whole, pl.BlockSpec((value.shape[0], LANES), lambda tile: (0, tile))],
+        out_specs=pl.BlockSpec((out_shape.shape[0], LANES), lambda tile: (0, tile)),
+        compiler_params=pltpu.CompilerParams(vmem_limit_bytes=TILED_VMEM_BYTES),
+        cost_estimate=cost_of(flops, (blocks, value), out_shape),
+    )(blocks, value)
 
 
 def both_replicas(block_ref, col):
@@ -39,25 +46,22 @@
 
 def hidden_kernel(block_ref, weight_ref, hidden_ref):
     depth = block_ref.shape[2]
-    blocks = [both_replicas(block_ref, col) for col in range(COLS)]
-    for start in range(0, hidden_ref.shape[1], LANES):
-        units = pl.ds(start, LANES)
-        total = None
-        for col, block in enumerate(blocks):
-            term = lax.dot_general(
-                block,
-                weight_ref[pl.ds(col * depth, depth), units],
-                (((0,), (0,)), ((), ())),
-                preferred_element_type=jnp.float32,
-            )
-            total = term if total is None else total + term
-        hidden_ref[:, units] = total
+    total = None
+    for col in range(COLS):
+        term = lax.dot_general(
+            both_replicas(block_ref, col),
+            weight_ref[pl.ds(col * depth, depth), :],
+            (((0,), (0,)), ((), ())),
+            preferred_element_type=jnp.float32,
+        )
+        total = term if total is None else total + term
+    hidden_ref[...] = total
 
 
 def hidden_sum(blocks, weight):
     tokens = 2 * blocks.shape[3]
     out_shape = jax.ShapeDtypeStruct((tokens, weight.shape[1]), jnp.float32)
-    return local_kernel(hidden_kernel, out_shape, 2 * tokens * weight.size, (blocks, weight))
+    return tiled_kernel(hidden_kernel, out_shape, 2 * tokens * weight.size, blocks, weight)
 
 
 def input_grad_kernel(weight_ref, grad_ref, pieces_ref):
@@ -77,29 +81,33 @@
 def input_grad_pieces(weight, grad):
     depth = weight.shape[0] // COLS
     out_shape = jax.ShapeDtypeStruct((SIDE, 2 * SIDE, depth, grad.shape[0] // 2), jnp.bfloat16)
-    return local_kernel(input_grad_kernel, out_shape, 2 * weight.size * grad.shape[0], (weight, grad))
+    return pl.pallas_call(
+        input_grad_kernel,
+        out_shape=out_shape,
+        in_specs=[pl.BlockSpec(memory_space=pltpu.VMEM)] * 2,
+        out_specs=pl.BlockSpec(memory_space=pltpu.VMEM),
+        compiler_params=pltpu.CompilerParams(vmem_limit_bytes=VMEM_BYTES),
+        cost_estimate=cost_of(2 * weight.size * grad.shape[0], (weight, grad), out_shape),
+    )(weight, grad)
 
 
 def token_sum_kernel(block_ref, grad_ref, total_ref):
     tokens = 2 * block_ref.shape[3]
-    blocks = [both_replicas(block_ref, row) for row in range(ROWS)]
-    for start in range(0, total_ref.shape[1], LANES):
-        units = pl.ds(start, LANES)
-        total = None
-        for row, block in enumerate(blocks):
-            term = jnp.dot(
-                block,
-                grad_ref[pl.ds(row * tokens, tokens), units],
-                preferred_element_type=jnp.float32,
-            )
-            total = term if total is None else total + term
-        total_ref[:, units] = total.astype(total_ref.dtype)
+    total = None
+    for row in range(ROWS):
+        term = jnp.dot(
+            both_replicas(block_ref, row),
+            grad_ref[pl.ds(row * tokens, tokens), :],
+            preferred_element_type=jnp.float32,
+        )
+        total = term if total is None else total + term
+    total_ref[...] = total.astype(total_ref.dtype)
 
 
 def token_sum(blocks, grads):
     depth = blocks.shape[2]
     out_shape = jax.ShapeDtypeStruct((depth, grads.shape[1]), jnp.bfloat16)
-    return local_kernel(token_sum_kernel, out_shape, 2 * depth * grads.size, (blocks, grads))
+    return tiled_kernel(token_sum_kernel, out_shape, 2 * depth * grads.size, blocks, grads)
 
 
 def to_replica(value):
@@ -139,7 +147,7 @@
         half_of(out_grad, replica), to_replica(half_of(out_grad, 1 - replica)), 0
     )
 
-    hidden = hidden_sum(by_depth, weight)
+    hidden = hidden_sum(after(by_depth, turned_line), weight)
     normal_cdf = 0.5 * (1.0 + jax.scipy.special.erf(hidden / math.sqrt(2.0)))
     density = jnp.exp(-0.5 * hidden * hidden) / math.sqrt(2.0 * math.pi)
     gelu_half = (hidden * normal_cdf).astype(jnp.bfloat16)
@@ -149,15 +157,15 @@
     grads = lax.all_gather(hidden_grad, "row", axis=0, tiled=True)
 
     by_token = to_all(after(turned_line, hidden_grad), "x", SIDE)
-    pieces = input_grad_pieces(weight, after(hidden_grad, by_token))
-    feature_grad = sum_along(sum_along(pieces, "x"), ("dp", "y")).T
+    pieces = input_grad_pieces(weight, hidden_grad)
+    own = token_sum(by_token, grads)
+    feature_grad = sum_along(after(sum_along(pieces, "x"), own), ("dp", "y")).T
 
     mine, other = (
         lax.dynamic_slice_in_dim(gelu_half, which * tokens, tokens, axis=0)
         for which in (replica, 1 - replica)
     )
     gelu_out = by_replica(mine, to_replica(other), 1)
-    own = token_sum(by_token, grads)
     weight_grad = by_replica(own, to_replica(own), 1).astype(jnp.float32)
     return (gelu_out, feature_grad, weight_grad)
 

time: 200 us -> 181 us (0.905)
  blocking collectives: 59.2 us -> 16.2 us
  starting transfers between devices: 40.3 us -> 54.5 us
  Pallas kernels: 6.66 us -> 14.5 us
    all_to_all x3 -> x1, blocking collectives: 59.2 us -> 16.2 us  [to_all(): return lax.all_to_all(copies, axis, 0, 0, tiled=True)]
    all_to_all x1 -> x3, waiting for transfers between devices: 6.04 us -> 21.9 us  [to_all(): return lax.all_to_all(copies, axis, 0, 0, tiled=True)]
    all_to_all x2, waiting for transfers between devices: 19.1 us -> 6.93 us  [sum_along(): pieces = lax.all_to_all(pieces, axis, 0, 0, tiled=True)]
    all_to_all x1 -> x3, starting transfers between devices: 4.56 us -> 16.1 us  [to_all(): return lax.all_to_all(copies, axis, 0, 0, tiled=True)]
    all_gather x1, waiting for transfers between devices: 0.02 us -> 10.9 us  [per_device(): grads = lax.all_gather(hidden_grad, 'row', axis=0, tiled=True)]
    all_gather x1, waiting for transfers between devices: 9.53 us -> 0.01 us  [per_device(): lax.all_gather(half_of(up_weight, replica), 'row', axis=0, tiled=True)]
    pallas_call x3, Pallas kernels: 6.66 us -> 14.5 us  [the longest x2 11.2 us: tiled_kernel(): pl.pallas_call(kernel, out_shape=out_shape, grid=(out_shape.shape[1] // L...]
    ppermute x3, waiting for transfers between devices: 21.3 us -> 13.8 us  [to_replica(): return lax.ppermute(value, 'dp', [(0, 1), (1, 0)])]
  transfers between devices with their start and end apart: 9 -> 11, of which waited for: 7 -> 7; matrix products, arithmetic and copies ran while one was open for 4% -> 5% of each run, Pallas kernels for 2% -> 5%
where the time goes in v12:
time: 181 us; the launch traced here: 179 us
  waiting for transfers between devices  61.3 us (34%)
  starting transfers between devices  54.5 us (30%)
  blocking collectives  16.2 us (9%)
  Pallas kernels  14.5 us (8%)
  between operations  14.2 us (8%)
  local copies, waits for them, and re-layouts  11.3 us (6%)
  other arithmetic  7.09 us (4%)
    all_to_all x3, waiting for transfers between devices, to_all(): return lax.all_to_all(copies, axis, 0, 0, tiled=True)  21.9 us
    ppermute x3, starting transfers between devices, to_replica(): return lax.ppermute(value, 'dp', [(0, 1), (1, 0)])  16.7 us
    all_to_all x1, blocking collectives, to_all(): return lax.all_to_all(copies, axis, 0, 0, tiled=True)  16.2 us
    all_to_all x3, starting transfers between devices, to_all(): return lax.all_to_all(copies, axis, 0, 0, tiled=True)  16.1 us
    ppermute x3, waiting for transfers between devices, to_replica(): return lax.ppermute(value, 'dp', [(0, 1), (1, 0)])  13.8 us
    ppermute x1, starting transfers between devices, per_device(): turned = lax.ppermute(features, ('row',) + COL, turns)  12 us
    pallas_call x2, Pallas kernels, tiled_kernel(): pl.pallas_call(kernel, out_shape=out_shape, grid=(out_shape.shape[1] // L...  11.2 us
    all_gather x1, waiting for transfers between devices, per_device(): grads = lax.all_gather(hidden_grad, 'row', axis=0, tiled=True)  10.9 us
  transfers between devices with their start and end apart: 11, of which 7 were waited for; matrix products, arithmetic and copies ran while one was open for 5% of the time, Pallas kernels for 5%

profile of v12, /device:TPU:56, one launch (start us, length us, event | category | flops | bytes accessed | tf_op | source)
XLA Modules:
  0.0 179.2 jit_solution(1538164170448581331)
XLA Ops:
  7.2 1.0 copy-done
  9.0 1.6 broadcast_in_dim.8
  10.6 8.5 %all-to-all-start = ((bf16[8,192,128]{2,1,0:T(8,128)(2,1)}), bf16[8,192,128]{2,1,0:T(8,128)(2,1)S(1)}, u32[]{:S(2)}, u32[]{:S(2)}) async-start(bf16[8,192,128]{2,1,0:T(8,128)(2,1)} %broadcast_in_dim.8), calls=%async_computation | async-start | bytes 786432 | tf_op jit(solution)/shard_map/all_to_all | solution.py:119
  19.1 12.0 %collective-permute-start = (bf16[192,128]{1,0:T(8,128)(2,1)S(1)}, bf16[192,128]{1,0:T(8,128)(2,1)S(1)}, u32[]{:S(2)}, u32[]{:S(2)}) collective-permute-start(bf16[192,128]{1,0:T(8,128)(2,1)S(1)} %bitcast.3), channel_id=1, source_target_pairs={{0,0},{1,16},{2,32},{3,48},{4,64},{5,80},{6,96},{7,112},{8,128},{9... | collective-permute-start | bytes 147464 | tf_op jit(solution)/shard_map/ppermute | solution.py:144
  31.1 7.8 %collective-permute-done = bf16[192,128]{1,0:T(8,128)(2,1)S(1)} collective-permute-done((bf16[192,128]{1,0:T(8,128)(2,1)S(1)}, bf16[192,128]{1,0:T(8,128)(2,1)S(1)}, u32[]{:S(2)}, u32[]{:S(2)}) %collective-permute-start) | collective-permute-done | bytes 49184 | tf_op jit(solution)/shard_map/ppermute | solution.py:144
  38.9 16.2 %all_to_all.30 = bf16[8,192,128]{2,1,0:T(8,128)(2,1)S(1)} all-to-all(bf16[8,192,128]{2,1,0:T(8,128)(2,1)S(1)} %broadcast_in_dim.10), channel_id=1, replica_groups=mesh['dp'=2,'row'=16,'y'=4,'x'=4] {'dp','y'}, dimensions={0} | all-to-all | bytes 786432 | tf_op jit(solution)/shard_map/all_to_all | solution.py:119
  55.2 1.6 broadcast_in_dim.9
  56.7 3.9 %all-to-all-start.1 = ((bf16[4,8,192,128]{3,2,1,0:T(8,128)(2,1)}), bf16[4,8,192,128]{3,2,1,0:T(8,128)(2,1)S(1)}, u32[]{:S(2)}, u32[]{:S(2)}) async-start(bf16[4,8,192,128]{3,2,1,0:T(8,128)(2,1)} %broadcast_in_dim.9), calls=%async_computation.1 | async-start | bytes 3145728 | tf_op jit(solution)/shard_map/all_to_all | solution.py:119
  60.7 6.0 %collective-permute-start.2 = (bf16[128,768]{1,0:T(8,128)(2,1)S(1)}, bf16[128,768]{1,0:T(8,128)(2,1)S(1)}, u32[]{:S(2)}, u32[]{:S(2)}) collective-permute-start(bf16[128,768]{1,0:T(8,128)(2,1)S(1)} %constant_dynamic-slice_fusion), channel_id=1, source_target_pairs={{0,256},{256,0},{1,257},{257,1},{2,258},{258,2},{3,259},{259,3},{4... | collective-permute-start | bytes 589832 | tf_op jit(solution)/shard_map/ppermute | solution.py:114
  66.7 6.0 %collective-permute-done.2 = bf16[128,768]{1,0:T(8,128)(2,1)S(1)} collective-permute-done((bf16[128,768]{1,0:T(8,128)(2,1)S(1)}, bf16[128,768]{1,0:T(8,128)(2,1)S(1)}, u32[]{:S(2)}, u32[]{:S(2)}) %collective-permute-start.2) | collective-permute-done | bytes 196640 | tf_op jit(solution)/shard_map/ppermute | solution.py:114
  72.8 8.2 %all-to-all-done.1.block_ref = bf16[4,8,192,128]{3,2,1,0:T(8,128)(2,1)S(1)} async-done(((bf16[4,8,192,128]{3,2,1,0:T(8,128)(2,1)}), bf16[4,8,192,128]{3,2,1,0:T(8,128)(2,1)S(1)}, u32[]{:S(2)}, u32[]{:S(2)}) %all-to-all-start.1) | async-done | bytes 1572896 | tf_op jit(solution)/shard_map/all_to_all | solution.py:119
  81.0 1.2 copy-done.3
  82.2 5.7 %shard_map.58 = f32[256,768]{1,0:T(8,128)} custom-call(bf16[4,8,192,128]{3,2,1,0:T(8,128)(2,1)} %copy-done.3, bf16[3072,768]{1,0:T(8,128)(2,1)} %all-gather.3.cloned.1.call-done.weight_ref), custom_call_target="tpu_custom_call" | custom-call | flops 1207959552 | bytes 7077888 | tf_op jit(solution)/shard_map/pallas_call | solution.py:31
  87.8 2.3 %fusion.5 = (bf16[256,768]{1,0:T(8,128)(2,1)}, bf16[256,768]{1,0:T(8,128)(2,1)S(1)}) fusion(f32[256,768]{1,0:T(8,128)} %shard_map.58, bf16[128,768]{1,0:T(8,128)(2,1)S(1)} %get-tuple-element.16, bf16[128,768]{1,0:T(8,128)(2,1)S(1)} %get-tuple-element.15), kind=kLoop, calls=%fused_computation.6 | loop fusion | flops 3145728 | bytes 1966080 | tf_op jit(solution)/shard_map/convert_element_type | solution.py:154
  90.1 1.6 broadcast_in_dim.11
  91.7 3.7 %all-to-all-start.4 = ((bf16[4,8,192,128]{3,2,1,0:T(8,128)(2,1)}), bf16[4,8,192,128]{3,2,1,0:T(8,128)(2,1)S(1)}, u32[]{:S(2)}, u32[]{:S(2)}) async-start(bf16[4,8,192,128]{3,2,1,0:T(8,128)(2,1)} %broadcast_in_dim.11), calls=%async_computation.4 | async-start | bytes 3145728 | tf_op jit(solution)/shard_map/all_to_all | solution.py:119
  95.4 2.3 %copy-done.1 = bf16[3072,768]{1,0:T(8,128)(2,1)S(1)} copy-done((bf16[3072,768]{1,0:T(8,128)(2,1)S(1)}, bf16[3072,768]{1,0:T(8,128)(2,1)}, u32[]{:S(2)}) %copy-start.1) | copy-done | bytes 4718616
  97.7 3.3 %shard_map.59 = bf16[4,8,192,128]{3,2,1,0:T(8,128)(2,1)} custom-call(bf16[3072,768]{1,0:T(8,128)(2,1)S(1)} %copy-done.1, bf16[256,768]{1,0:T(8,128)(2,1)S(1)} %copy-done.2), custom_call_target="tpu_custom_call" | custom-call | flops 1207959552 | bytes 6684672 | tf_op jit(solution)/shard_map/pallas_call | solution.py:84
  101.0 13.7 %all-to-all-done.4.block_ref = bf16[4,8,192,128]{3,2,1,0:T(8,128)(2,1)S(1)} async-done(((bf16[4,8,192,128]{3,2,1,0:T(8,128)(2,1)}), bf16[4,8,192,128]{3,2,1,0:T(8,128)(2,1)S(1)}, u32[]{:S(2)}, u32[]{:S(2)}) %all-to-all-start.4) | async-done | bytes 1572896 | tf_op jit(solution)/shard_map/all_to_all | solution.py:119
  114.7 1.3 copy-done.4
  116.0 3.6 %all-to-all-start.3 = ((bf16[4,8,192,128]{3,2,1,0:T(8,128)(2,1)}), bf16[4,8,192,128]{3,2,1,0:T(8,128)(2,1)S(1)}, u32[]{:S(2)}, u32[]{:S(2)}) async-start(bf16[4,8,192,128]{3,2,1,0:T(8,128)(2,1)} %shard_map.59), calls=%async_computation.3 | async-start | bytes 3145728 | tf_op jit(solution)/shard_map/all_to_all | solution.py:123
  119.6 5.7 %collective-permute-start.1 = (bf16[128,768]{1,0:T(8,128)(2,1)S(1)}, bf16[128,768]{1,0:T(8,128)(2,1)}, u32[]{:S(2)}, u32[]{:S(2)}) collective-permute-start(bf16[128,768]{1,0:T(8,128)(2,1)S(1)} %constant_dynamic-slice_fusion.1), channel_id=1, source_target_pairs={{0,256},{256,0},{1,257},{257,1},{2,258},{258,2},{3,259},{259,3},{4... | collective-permute-start | bytes 589832 | tf_op jit(solution)/shard_map/ppermute | solution.py:114
  125.3 10.9 %all-gather.5.cloned.1.call-done.grad_ref = bf16[4096,768]{1,0:T(8,128)(2,1)} async-done(((bf16[256,768]{1,0:T(8,128)(2,1)}), bf16[4096,768]{1,0:T(8,128)(2,1)}) %all-gather.5.cloned.1.call-update) | async-done | bytes 6291472 | tf_op jit(solution)/shard_map/all_gather | solution.py:157
  136.2 5.6 %shard_map.60 = bf16[192,768]{1,0:T(8,128)(2,1)} custom-call(bf16[4,8,192,128]{3,2,1,0:T(8,128)(2,1)} %copy-done.4, bf16[4096,768]{1,0:T(8,128)(2,1)} %all-gather.5.cloned.1.call-done.grad_ref), custom_call_target="tpu_custom_call" | custom-call | flops 1207959552 | bytes 8159232 | tf_op jit(solution)/shard_map/pallas_call | solution.py:31
  141.7 5.1 %collective-permute-start.3 = (bf16[192,768]{1,0:T(8,128)(2,1)}, bf16[192,768]{1,0:T(8,128)(2,1)S(1)}, u32[]{:S(2)}, u32[]{:S(2)}) collective-permute-start(bf16[192,768]{1,0:T(8,128)(2,1)} %shard_map.60), channel_id=1, source_target_pairs={{0,256},{256,0},{1,257},{257,1},{2,258},{258,2},{3,259},{259,3},{4... | collective-permute-start | bytes 884744 | tf_op jit(solution)/shard_map/ppermute | solution.py:114
  146.8 1.0 broadcast_select_fusion.5
  147.8 1.1 reduce_sum.24
  148.9 6.1 %all-to-all-start.5 = ((bf16[8,192,128]{2,1,0:T(8,128)(2,1)}), bf16[8,192,128]{2,1,0:T(8,128)(2,1)S(1)}, u32[]{:S(2)}, u32[]{:S(2)}) async-start(bf16[8,192,128]{2,1,0:T(8,128)(2,1)} %reduce_sum.24), calls=%async_computation.5 | async-start | bytes 786432 | tf_op jit(solution)/shard_map/all_to_all | solution.py:123
  155.0 0.8 pad_maximum_fusion
  155.8 7.8 %collective-permute-done.3 = bf16[192,768]{1,0:T(8,128)(2,1)S(1)} collective-permute-done((bf16[192,768]{1,0:T(8,128)(2,1)}, bf16[192,768]{1,0:T(8,128)(2,1)S(1)}, u32[]{:S(2)}, u32[]{:S(2)}) %collective-permute-start.3) | collective-permute-done | bytes 294944 | tf_op jit(solution)/shard_map/ppermute | solution.py:114
  163.6 1.1 maximum_convert_fusion
  164.8 6.9 %all-to-all-done.5 = bf16[8,192,128]{2,1,0:T(8,128)(2,1)S(1)} async-done(((bf16[8,192,128]{2,1,0:T(8,128)(2,1)}), bf16[8,192,128]{2,1,0:T(8,128)(2,1)S(1)}, u32[]{:S(2)}, u32[]{:S(2)}) %all-to-all-start.5) | async-done | bytes 393248 | tf_op jit(solution)/shard_map/all_to_all | solution.py:123
  (27 shorter events, 1.7 us)
Async XLA Ops:
  7.2 1.1 copy-start
  7.2 12.0 %copy-start.7 = (bf16[128,192]{0,1:T(8,128)(2,1)S(1)}, bf16[128,192]{0,1:T(8,128)(2,1)}, u32[]{:S(2)}) copy-start(bf16[128,192]{0,1:T(8,128)(2,1)} %param.3) | copy-start | bytes 147460
  7.2 73.8 %all-gather.3.cloned.1.call-start = ((), (), s32[]{:S(2)}) async-start(), calls=%async_computation.6 | async-start | bytes 5013504 | tf_op jit(solution)/shard_map/all_gather | solution.py:140
  10.6 28.3 %all-to-all-start = ((bf16[8,192,128]{2,1,0:T(8,128)(2,1)}), bf16[8,192,128]{2,1,0:T(8,128)(2,1)S(1)}, u32[]{:S(2)}, u32[]{:S(2)}) async-start(bf16[8,192,128]{2,1,0:T(8,128)(2,1)} %broadcast_in_dim.8), calls=%async_computation | async-start | bytes 786432 | tf_op jit(solution)/shard_map/all_to_all | solution.py:119
  19.1 19.7 %collective-permute-start = (bf16[192,128]{1,0:T(8,128)(2,1)S(1)}, bf16[192,128]{1,0:T(8,128)(2,1)S(1)}, u32[]{:S(2)}, u32[]{:S(2)}) collective-permute-start(bf16[192,128]{1,0:T(8,128)(2,1)S(1)} %bitcast.3), channel_id=1, source_target_pairs={{0,0},{1,16},{2,32},{3,48},{4,64},{5,80},{6,96},{7,112},{8,128},{9... | collective-permute-start | bytes 147464 | tf_op jit(solution)/shard_map/ppermute | solution.py:144
  56.7 3.9 %copy-start.6 = (bf16[128,1536]{1,0:T(8,128)(2,1)S(1)}, bf16[128,1536]{1,0:T(8,128)(2,1)}, u32[]{:S(2)}) copy-start(bf16[128,1536]{1,0:T(8,128)(2,1)} %param.5) | copy-start | bytes 1179652
  56.7 24.2 %all-to-all-start.1 = ((bf16[4,8,192,128]{3,2,1,0:T(8,128)(2,1)}), bf16[4,8,192,128]{3,2,1,0:T(8,128)(2,1)S(1)}, u32[]{:S(2)}, u32[]{:S(2)}) async-start(bf16[4,8,192,128]{3,2,1,0:T(8,128)(2,1)} %broadcast_in_dim.9), calls=%async_computation.1 | async-start | bytes 3145728 | tf_op jit(solution)/shard_map/all_to_all | solution.py:119
  60.7 75.5 %all-gather.5.cloned.1.call-start = ((), (), s32[]{:S(2)}) async-start(), calls=%async_computation.7 | async-start | bytes 6684672 | tf_op jit(solution)/shard_map/all_gather | solution.py:157
  60.7 12.0 %collective-permute-start.2 = (bf16[128,768]{1,0:T(8,128)(2,1)S(1)}, bf16[128,768]{1,0:T(8,128)(2,1)S(1)}, u32[]{:S(2)}, u32[]{:S(2)}) collective-permute-start(bf16[128,768]{1,0:T(8,128)(2,1)S(1)} %constant_dynamic-slice_fusion), channel_id=1, source_target_pairs={{0,256},{256,0},{1,257},{257,1},{2,258},{258,2},{3,259},{259,3},{4... | collective-permute-start | bytes 589832 | tf_op jit(solution)/shard_map/ppermute | solution.py:114
  81.0 1.2 copy-start.3
  91.7 3.7 %copy-start.2 = (bf16[256,768]{1,0:T(8,128)(2,1)S(1)}, bf16[256,768]{1,0:T(8,128)(2,1)}, u32[]{:S(2)}) copy-start(bf16[256,768]{1,0:T(8,128)(2,1)} %get-tuple-element.11.grad_ref) | copy-start | bytes 1179652
  91.7 23.1 %all-to-all-start.4 = ((bf16[4,8,192,128]{3,2,1,0:T(8,128)(2,1)}), bf16[4,8,192,128]{3,2,1,0:T(8,128)(2,1)S(1)}, u32[]{:S(2)}, u32[]{:S(2)}) async-start(bf16[4,8,192,128]{3,2,1,0:T(8,128)(2,1)} %broadcast_in_dim.11), calls=%async_computation.4 | async-start | bytes 3145728 | tf_op jit(solution)/shard_map/all_to_all | solution.py:119
  95.4 2.3 %copy-start.1 = (bf16[3072,768]{1,0:T(8,128)(2,1)S(1)}, bf16[3072,768]{1,0:T(8,128)(2,1)}, u32[]{:S(2)}) copy-start(bf16[3072,768]{1,0:T(8,128)(2,1)} %all-gather.3.cloned.1.call-done.weight_ref) | copy-start | bytes 14155780
  114.7 1.3 copy-start.4
  116.0 31.8 %all-to-all-start.3 = ((bf16[4,8,192,128]{3,2,1,0:T(8,128)(2,1)}), bf16[4,8,192,128]{3,2,1,0:T(8,128)(2,1)S(1)}, u32[]{:S(2)}, u32[]{:S(2)}) async-start(bf16[4,8,192,128]{3,2,1,0:T(8,128)(2,1)} %shard_map.59), calls=%async_computation.3 | async-start | bytes 3145728 | tf_op jit(solution)/shard_map/all_to_all | solution.py:123
  119.6 27.2 %collective-permute-start.1 = (bf16[128,768]{1,0:T(8,128)(2,1)S(1)}, bf16[128,768]{1,0:T(8,128)(2,1)}, u32[]{:S(2)}, u32[]{:S(2)}) collective-permute-start(bf16[128,768]{1,0:T(8,128)(2,1)S(1)} %constant_dynamic-slice_fusion.1), channel_id=1, source_target_pairs={{0,256},{256,0},{1,257},{257,1},{2,258},{258,2},{3,259},{259,3},{4... | collective-permute-start | bytes 589832 | tf_op jit(solution)/shard_map/ppermute | solution.py:114
  141.7 21.9 %collective-permute-start.3 = (bf16[192,768]{1,0:T(8,128)(2,1)}, bf16[192,768]{1,0:T(8,128)(2,1)S(1)}, u32[]{:S(2)}, u32[]{:S(2)}) collective-permute-start(bf16[192,768]{1,0:T(8,128)(2,1)} %shard_map.60), channel_id=1, source_target_pairs={{0,256},{256,0},{1,257},{257,1},{2,258},{258,2},{3,259},{259,3},{4... | collective-permute-start | bytes 884744 | tf_op jit(solution)/shard_map/ppermute | solution.py:114
  147.8 15.8 %copy-start.5 = (bf16[192,768]{1,0:T(8,128)(2,1)S(1)}, bf16[192,768]{1,0:T(8,128)(2,1)}, u32[]{:S(2)}) copy-start(bf16[192,768]{1,0:T(8,128)(2,1)} %shard_map.60) | copy-start | bytes 884740
  148.9 22.8 %all-to-all-start.5 = ((bf16[8,192,128]{2,1,0:T(8,128)(2,1)}), bf16[8,192,128]{2,1,0:T(8,128)(2,1)S(1)}, u32[]{:S(2)}, u32[]{:S(2)}) async-start(bf16[8,192,128]{2,1,0:T(8,128)(2,1)} %reduce_sum.24), calls=%async_computation.5 | async-start | bytes 786432 | tf_op jit(solution)/shard_map/all_to_all | solution.py:123
Sparse Core Ops, SparseCore 0:
  10.7 53.0 all-gather.2
  90.2 45.8 all-gather.4

commit v13 on v11

--- a/solution.py
+++ b/solution.py
@@ -134,12 +134,11 @@
     by_depth = to_all(line, "x", SIDE)
     turns = [(r * COLS + c, c * COLS + r) for r in range(ROWS) for c in range(COLS)]
     turned = lax.ppermute(features, ("row",) + COL, turns)
-    turned_line = to_all(after(turned, line), ("dp", "y"), 2 * SIDE)
     out_grad = by_replica(
         half_of(out_grad, replica), to_replica(half_of(out_grad, 1 - replica)), 0
     )
 
-    hidden = hidden_sum(by_depth, weight)
+    hidden = hidden_sum(after(by_depth, turned), weight)
     normal_cdf = 0.5 * (1.0 + jax.scipy.special.erf(hidden / math.sqrt(2.0)))
     density = jnp.exp(-0.5 * hidden * hidden) / math.sqrt(2.0 * math.pi)
     gelu_half = (hidden * normal_cdf).astype(jnp.bfloat16)
@@ -148,8 +147,10 @@
     )
     grads = lax.all_gather(hidden_grad, "row", axis=0, tiled=True)
 
-    by_token = to_all(after(turned_line, hidden_grad), "x", SIDE)
-    pieces = input_grad_pieces(weight, after(hidden_grad, by_token))
+    by_token = to_all(after(turned, hidden_grad), ("dp", "y"), 2 * SIDE)
+    by_token = to_all(by_token, "x", SIDE)
+    pieces = input_grad_pieces(weight, hidden_grad)
+    own = token_sum(by_token, grads)
     feature_grad = sum_along(sum_along(pieces, "x"), ("dp", "y")).T
 
     mine, other = (
@@ -157,7 +158,6 @@
         for which in (replica, 1 - replica)
     )
     gelu_out = by_replica(mine, to_replica(other), 1)
-    own = token_sum(by_token, grads)
     weight_grad = by_replica(own, to_replica(own), 1).astype(jnp.float32)
     return (gelu_out, feature_grad, weight_grad)
 

time: 200 us -> 189 us (0.945)
  blocking collectives: 59.2 us -> 43.6 us
  starting transfers between devices: 40.3 us -> 55.7 us
  waiting for transfers between devices: 60.5 us -> 46.4 us
  local copies, waits for them, and re-layouts: 9.68 us -> 14 us
    all_to_all x3 -> x1, blocking collectives: 59.2 us -> 17.1 us  [to_all(): return lax.all_to_all(copies, axis, 0, 0, tiled=True)]
    all_to_all x0 -> x1, blocking collectives: none -> 26.5 us  [sum_along(): pieces = lax.all_to_all(pieces, axis, 0, 0, tiled=True)]
    all_to_all x2 -> x1, waiting for transfers between devices: 19.1 us -> 0.01 us  [sum_along(): pieces = lax.all_to_all(pieces, axis, 0, 0, tiled=True)]
    all_to_all x1 -> x3, waiting for transfers between devices: 6.04 us -> 20.5 us  [to_all(): return lax.all_to_all(copies, axis, 0, 0, tiled=True)]
    all_to_all x1 -> x3, starting transfers between devices: 4.56 us -> 13.3 us  [to_all(): return lax.all_to_all(copies, axis, 0, 0, tiled=True)]
    ppermute x1, starting transfers between devices: 6.73 us -> 13.8 us  [per_device(): turned = lax.ppermute(features, ('row',) + COL, turns)]
    ppermute x3, waiting for transfers between devices: 21.3 us -> 15.1 us  [to_replica(): return lax.ppermute(value, 'dp', [(0, 1), (1, 0)])]
    all_gather x1, waiting for transfers between devices: 9.53 us -> 4.2 us  [per_device(): lax.all_gather(half_of(up_weight, replica), 'row', axis=0, tiled=True)]
  transfers between devices with their start and end apart: 9 -> 10, of which waited for: 7 -> 6; matrix products, arithmetic and copies ran while one was open for 4% -> 5% of each run, Pallas kernels for 2% -> 2%
where the time goes in v13:
time: 189 us; the launch traced here: 187 us
  starting transfers between devices  55.7 us (29%)
  waiting for transfers between devices  46.4 us (25%)
  blocking collectives  43.6 us (23%)
  between operations  14.2 us (8%)
  local copies, waits for them, and re-layouts  14 us (7%)
  other arithmetic  7.39 us (4%)
  Pallas kernels  5.4 us (3%)
    all_to_all x1, blocking collectives, sum_along(): pieces = lax.all_to_all(pieces, axis, 0, 0, tiled=True)  26.5 us
    all_to_all x3, waiting for transfers between devices, to_all(): return lax.all_to_all(copies, axis, 0, 0, tiled=True)  20.5 us
    all_to_all x1, blocking collectives, to_all(): return lax.all_to_all(copies, axis, 0, 0, tiled=True)  17.1 us
    ppermute x3, starting transfers between devices, to_replica(): return lax.ppermute(value, 'dp', [(0, 1), (1, 0)])  15.6 us
    ppermute x3, waiting for transfers between devices, to_replica(): return lax.ppermute(value, 'dp', [(0, 1), (1, 0)])  15.1 us
    ppermute x1, starting transfers between devices, per_device(): turned = lax.ppermute(features, ('row',) + COL, turns)  13.8 us
    all_to_all x3, starting transfers between devices, to_all(): return lax.all_to_all(copies, axis, 0, 0, tiled=True)  13.3 us
    all_to_all x1, starting transfers between devices, sum_along(): pieces = lax.all_to_all(pieces, axis, 0, 0, tiled=True)  12.9 us
  transfers between devices with their start and end apart: 10, of which 6 were waited for; matrix products, arithmetic and copies ran while one was open for 5% of the time, Pallas kernels for 2%

profile of v13, /device:TPU:56, one launch (start us, length us, event | category | flops | bytes accessed | tf_op | source)
XLA Modules:
  0.0 186.7 jit_solution(10095696337331225648)
XLA Ops:
  7.2 1.0 copy-done
  9.0 0.9 broadcast_in_dim.8
  9.8 17.1 %all_to_all.30 = bf16[8,192,128]{2,1,0:T(8,128)(2,1)S(1)} all-to-all(bf16[8,192,128]{2,1,0:T(8,128)(2,1)S(1)} %broadcast_in_dim.8), channel_id=1, replica_groups=mesh['dp'=2,'row'=16,'y'=4,'x'=4] {'dp','y'}, dimensions={0} | all-to-all | bytes 786432 | tf_op jit(solution)/shard_map/all_to_all | solution.py:111
  27.0 1.5 broadcast_in_dim.9
  28.5 4.6 %all-to-all-start.1 = ((bf16[4,8,192,128]{3,2,1,0:T(8,128)(2,1)}), bf16[4,8,192,128]{3,2,1,0:T(8,128)(2,1)S(1)}, u32[]{:S(2)}, u32[]{:S(2)}) async-start(bf16[4,8,192,128]{3,2,1,0:T(8,128)(2,1)} %broadcast_in_dim.9), calls=%async_computation.1 | async-start | bytes 3145728 | tf_op jit(solution)/shard_map/all_to_all | solution.py:111
  33.1 5.8 %collective-permute-start.2 = (bf16[128,768]{1,0:T(8,128)(2,1)S(1)}, bf16[128,768]{1,0:T(8,128)(2,1)S(1)}, u32[]{:S(2)}, u32[]{:S(2)}) collective-permute-start(bf16[128,768]{1,0:T(8,128)(2,1)S(1)} %constant_dynamic-slice_fusion), channel_id=1, source_target_pairs={{0,256},{256,0},{1,257},{257,1},{2,258},{258,2},{3,259},{259,3},{4... | collective-permute-start | bytes 589832 | tf_op jit(solution)/shard_map/ppermute | solution.py:106
  38.9 13.8 %collective-permute-start = (bf16[192,128]{1,0:T(8,128)(2,1)S(1)}, bf16[192,128]{1,0:T(8,128)(2,1)S(1)}, u32[]{:S(2)}, u32[]{:S(2)}) collective-permute-start(bf16[192,128]{1,0:T(8,128)(2,1)S(1)} %bitcast.3), channel_id=1, source_target_pairs={{0,0},{1,16},{2,32},{3,48},{4,64},{5,80},{6,96},{7,112},{8,128},{9... | collective-permute-start | bytes 147464 | tf_op jit(solution)/shard_map/ppermute | solution.py:136
  52.8 6.6 %collective-permute-done = bf16[192,128]{1,0:T(8,128)(2,1)S(1)} collective-permute-done((bf16[192,128]{1,0:T(8,128)(2,1)S(1)}, bf16[192,128]{1,0:T(8,128)(2,1)S(1)}, u32[]{:S(2)}, u32[]{:S(2)}) %collective-permute-start) | collective-permute-done | bytes 49184 | tf_op jit(solution)/shard_map/ppermute | solution.py:136
  59.5 4.2 %all-gather.3.cloned.1.call-done.weight_ref = bf16[3072,768]{1,0:T(8,128)(2,1)} async-done(((bf16[192,768]{1,0:T(8,128)(2,1)}), bf16[3072,768]{1,0:T(8,128)(2,1)}) %all-gather.3.cloned.1.call-update) | async-done | bytes 4718608 | tf_op jit(solution)/shard_map/all_gather | solution.py:132
  63.7 2.3 %copy-done.1 = bf16[3072,768]{1,0:T(8,128)(2,1)S(1)} copy-done((bf16[3072,768]{1,0:T(8,128)(2,1)S(1)}, bf16[3072,768]{1,0:T(8,128)(2,1)}, u32[]{:S(2)}) %copy-start.1) | copy-done | bytes 4718616
  66.0 1.8 shard_map.58
  67.9 1.1 fusion.5
  69.0 0.8 broadcast_in_dim.10
  69.8 5.2 %all-to-all-start.4 = ((bf16[8,192,128]{2,1,0:T(8,128)(2,1)}), bf16[8,192,128]{2,1,0:T(8,128)(2,1)S(1)}, u32[]{:S(2)}, u32[]{:S(2)}) async-start(bf16[8,192,128]{2,1,0:T(8,128)(2,1)} %broadcast_in_dim.10), calls=%async_computation.4 | async-start | bytes 786432 | tf_op jit(solution)/shard_map/all_to_all | solution.py:111
  75.0 2.3 %copy-done.2 = bf16[3072,768]{1,0:T(8,128)(2,1)S(1)} copy-done((bf16[3072,768]{1,0:T(8,128)(2,1)S(1)}, bf16[3072,768]{1,0:T(8,128)(2,1)}, u32[]{:S(2)}) %copy-start.2) | copy-done | bytes 4718616
  77.4 2.2 %shard_map.59 = bf16[4,8,192,128]{3,2,1,0:T(8,128)(2,1)S(1)} custom-call(bf16[3072,768]{1,0:T(8,128)(2,1)S(1)} %copy-done.2, bf16[256,768]{1,0:T(8,128)(2,1)S(1)} %copy-done.4), custom_call_target="tpu_custom_call" | custom-call | flops 1207959552 | bytes 6684672 | tf_op jit(solution)/shard_map/pallas_call | solution.py:25
  79.5 5.3 %all-to-all-done.4 = bf16[8,192,128]{2,1,0:T(8,128)(2,1)S(1)} async-done(((bf16[8,192,128]{2,1,0:T(8,128)(2,1)}), bf16[8,192,128]{2,1,0:T(8,128)(2,1)S(1)}, u32[]{:S(2)}, u32[]{:S(2)}) %all-to-all-start.4) | async-done | bytes 393248 | tf_op jit(solution)/shard_map/all_to_all | solution.py:111
  84.8 26.5 %all_to_all.31 = bf16[4,8,192,128]{3,2,1,0:T(8,128)(2,1)} all-to-all(bf16[4,8,192,128]{3,2,1,0:T(8,128)(2,1)S(1)} %shard_map.59), channel_id=1, replica_groups=mesh['dp'=2,'row'=16,'y'=4,'x'=4] {'x'}, dimensions={0} | all-to-all | bytes 3145728 | tf_op jit(solution)/shard_map/all_to_all | solution.py:115
  111.4 1.6 broadcast_in_dim.11
  113.0 3.6 %all-to-all-start.5 = ((bf16[4,8,192,128]{3,2,1,0:T(8,128)(2,1)}), bf16[4,8,192,128]{3,2,1,0:T(8,128)(2,1)S(1)}, u32[]{:S(2)}, u32[]{:S(2)}) async-start(bf16[4,8,192,128]{3,2,1,0:T(8,128)(2,1)} %broadcast_in_dim.11), calls=%async_computation.5 | async-start | bytes 3145728 | tf_op jit(solution)/shard_map/all_to_all | solution.py:111
  116.5 2.5 %reduce_sum.24 = bf16[8,192,128]{2,1,0:T(8,128)(2,1)} reduce(bf16[4,8,192,128]{3,2,1,0:T(8,128)(2,1)} %all_to_all.31, bf16[]{:T(256)} %constant.33.clone.1), dimensions={0}, to_apply=%region_0.1 | reduce | flops 589824 | bytes 1966082 | tf_op jit(solution)/shard_map/reduce_sum | solution.py:116
  119.1 15.1 %all-to-all-done.5.block_ref = bf16[4,8,192,128]{3,2,1,0:T(8,128)(2,1)S(1)} async-done(((bf16[4,8,192,128]{3,2,1,0:T(8,128)(2,1)}), bf16[4,8,192,128]{3,2,1,0:T(8,128)(2,1)S(1)}, u32[]{:S(2)}, u32[]{:S(2)}) %all-to-all-start.5) | async-done | bytes 1572896 | tf_op jit(solution)/shard_map/all_to_all | solution.py:111
  134.2 12.9 %all-to-all-start.3 = ((bf16[8,192,128]{2,1,0:T(8,128)(2,1)}), bf16[8,192,128]{2,1,0:T(8,128)(2,1)S(1)}, u32[]{:S(2)}, u32[]{:S(2)}) async-start(bf16[8,192,128]{2,1,0:T(8,128)(2,1)} %reduce_sum.24), calls=%async_computation.3 | async-start | bytes 786432 | tf_op jit(solution)/shard_map/all_to_all | solution.py:115
  147.2 5.1 %collective-permute-start.1 = (bf16[128,768]{1,0:T(8,128)(2,1)S(1)}, bf16[128,768]{1,0:T(8,128)(2,1)}, u32[]{:S(2)}, u32[]{:S(2)}) collective-permute-start(bf16[128,768]{1,0:T(8,128)(2,1)S(1)} %constant_dynamic-slice_fusion.1), channel_id=1, source_target_pairs={{0,256},{256,0},{1,257},{257,1},{2,258},{258,2},{3,259},{259,3},{4... | collective-permute-start | bytes 589832 | tf_op jit(solution)/shard_map/ppermute | solution.py:106
  152.4 2.8 %copy-done.3 = bf16[4096,768]{1,0:T(8,128)(2,1)S(1)} copy-done((bf16[4096,768]{1,0:T(8,128)(2,1)S(1)}, bf16[4096,768]{1,0:T(8,128)(2,1)}, u32[]{:S(2)}) %copy-start.3) | copy-done | bytes 6291480
  155.1 1.4 shard_map.60
  156.5 4.6 %collective-permute-start.3 = (bf16[192,768]{1,0:T(8,128)(2,1)S(1)}, bf16[192,768]{1,0:T(8,128)(2,1)S(1)}, u32[]{:S(2)}, u32[]{:S(2)}) collective-permute-start(bf16[192,768]{1,0:T(8,128)(2,1)S(1)} %shard_map.60), channel_id=1, source_target_pairs={{0,256},{256,0},{1,257},{257,1},{2,258},{258,2},{3,259},{259,3},{4... | collective-permute-start | bytes 884744 | tf_op jit(solution)/shard_map/ppermute | solution.py:106
  161.2 7.4 %collective-permute-done.1 = bf16[128,768]{1,0:T(8,128)(2,1)} collective-permute-done((bf16[128,768]{1,0:T(8,128)(2,1)S(1)}, bf16[128,768]{1,0:T(8,128)(2,1)}, u32[]{:S(2)}, u32[]{:S(2)}) %collective-permute-start.1) | collective-permute-done | bytes 196640 | tf_op jit(solution)/shard_map/ppermute | solution.py:106
  168.5 1.0 broadcast_select_fusion.5
  169.5 0.8 pad_maximum_fusion
  171.0 7.7 %collective-permute-done.3 = bf16[192,768]{1,0:T(8,128)(2,1)S(1)} collective-permute-done((bf16[192,768]{1,0:T(8,128)(2,1)S(1)}, bf16[192,768]{1,0:T(8,128)(2,1)S(1)}, u32[]{:S(2)}, u32[]{:S(2)}) %collective-permute-start.3) | collective-permute-done | bytes 294944 | tf_op jit(solution)/shard_map/ppermute | solution.py:106
  178.7 1.1 maximum_convert_fusion
  (24 shorter events, 1.7 us)
Async XLA Ops:
  7.2 1.1 copy-start
  7.2 56.5 %all-gather.3.cloned.1.call-start = ((), (), s32[]{:S(2)}) async-start(), calls=%async_computation.6 | async-start | bytes 5013504 | tf_op jit(solution)/shard_map/all_gather | solution.py:132
  28.5 4.6 %copy-start.5 = (bf16[128,1536]{1,0:T(8,128)(2,1)S(1)}, bf16[128,1536]{1,0:T(8,128)(2,1)}, u32[]{:S(2)}) copy-start(bf16[128,1536]{1,0:T(8,128)(2,1)} %param.5) | copy-start | bytes 1179652
  28.5 10.4 %copy-start.6 = (bf16[128,192]{0,1:T(8,128)(2,1)S(1)}, bf16[128,192]{0,1:T(8,128)(2,1)}, u32[]{:S(2)}) copy-start(bf16[128,192]{0,1:T(8,128)(2,1)} %param.3) | copy-start | bytes 147460
  28.5 31.0 %all-to-all-start.1 = ((bf16[4,8,192,128]{3,2,1,0:T(8,128)(2,1)}), bf16[4,8,192,128]{3,2,1,0:T(8,128)(2,1)S(1)}, u32[]{:S(2)}, u32[]{:S(2)}) async-start(bf16[4,8,192,128]{3,2,1,0:T(8,128)(2,1)} %broadcast_in_dim.9), calls=%async_computation.1 | async-start | bytes 3145728 | tf_op jit(solution)/shard_map/all_to_all | solution.py:111
  33.0 119.3 %all-gather.5.cloned.1.call-start = ((), (), s32[]{:S(2)}) async-start(), calls=%async_computation.7 | async-start | bytes 6684672 | tf_op jit(solution)/shard_map/all_gather | solution.py:148
  33.1 19.7 %collective-permute-start.2 = (bf16[128,768]{1,0:T(8,128)(2,1)S(1)}, bf16[128,768]{1,0:T(8,128)(2,1)S(1)}, u32[]{:S(2)}, u32[]{:S(2)}) collective-permute-start(bf16[128,768]{1,0:T(8,128)(2,1)S(1)} %constant_dynamic-slice_fusion), channel_id=1, source_target_pairs={{0,256},{256,0},{1,257},{257,1},{2,258},{258,2},{3,259},{259,3},{4... | collective-permute-start | bytes 589832 | tf_op jit(solution)/shard_map/ppermute | solution.py:106
  38.9 20.5 %collective-permute-start = (bf16[192,128]{1,0:T(8,128)(2,1)S(1)}, bf16[192,128]{1,0:T(8,128)(2,1)S(1)}, u32[]{:S(2)}, u32[]{:S(2)}) collective-permute-start(bf16[192,128]{1,0:T(8,128)(2,1)S(1)} %bitcast.3), channel_id=1, source_target_pairs={{0,0},{1,16},{2,32},{3,48},{4,64},{5,80},{6,96},{7,112},{8,128},{9... | collective-permute-start | bytes 147464 | tf_op jit(solution)/shard_map/ppermute | solution.py:136
  63.7 2.3 %copy-start.1 = (bf16[3072,768]{1,0:T(8,128)(2,1)S(1)}, bf16[3072,768]{1,0:T(8,128)(2,1)}, u32[]{:S(2)}) copy-start(bf16[3072,768]{1,0:T(8,128)(2,1)} %all-gather.3.cloned.1.call-done.weight_ref) | copy-start | bytes 14155780
  69.0 6.0 %copy-start.4 = (bf16[256,768]{1,0:T(8,128)(2,1)S(1)}, bf16[256,768]{1,0:T(8,128)(2,1)}, u32[]{:S(2)}) copy-start(bf16[256,768]{1,0:T(8,128)(2,1)} %get-tuple-element.7.grad_ref) | copy-start | bytes 1179652
  69.8 15.0 %all-to-all-start.4 = ((bf16[8,192,128]{2,1,0:T(8,128)(2,1)}), bf16[8,192,128]{2,1,0:T(8,128)(2,1)S(1)}, u32[]{:S(2)}, u32[]{:S(2)}) async-start(bf16[8,192,128]{2,1,0:T(8,128)(2,1)} %broadcast_in_dim.10), calls=%async_computation.4 | async-start | bytes 786432 | tf_op jit(solution)/shard_map/all_to_all | solution.py:111
  75.0 2.3 %copy-start.2 = (bf16[3072,768]{1,0:T(8,128)(2,1)S(1)}, bf16[3072,768]{1,0:T(8,128)(2,1)}, u32[]{:S(2)}) copy-start(bf16[3072,768]{1,0:T(8,128)(2,1)} %all-gather.3.cloned.1.call-done.weight_ref) | copy-start | bytes 14155780
  113.0 21.3 %all-to-all-start.5 = ((bf16[4,8,192,128]{3,2,1,0:T(8,128)(2,1)}), bf16[4,8,192,128]{3,2,1,0:T(8,128)(2,1)S(1)}, u32[]{:S(2)}, u32[]{:S(2)}) async-start(bf16[4,8,192,128]{3,2,1,0:T(8,128)(2,1)} %broadcast_in_dim.11), calls=%async_computation.5 | async-start | bytes 3145728 | tf_op jit(solution)/shard_map/all_to_all | solution.py:111
  134.2 36.1 %all-to-all-start.3 = ((bf16[8,192,128]{2,1,0:T(8,128)(2,1)}), bf16[8,192,128]{2,1,0:T(8,128)(2,1)S(1)}, u32[]{:S(2)}, u32[]{:S(2)}) async-start(bf16[8,192,128]{2,1,0:T(8,128)(2,1)} %reduce_sum.24), calls=%async_computation.3 | async-start | bytes 786432 | tf_op jit(solution)/shard_map/all_to_all | solution.py:115
  147.2 21.3 %collective-permute-start.1 = (bf16[128,768]{1,0:T(8,128)(2,1)S(1)}, bf16[128,768]{1,0:T(8,128)(2,1)}, u32[]{:S(2)}, u32[]{:S(2)}) collective-permute-start(bf16[128,768]{1,0:T(8,128)(2,1)S(1)} %constant_dynamic-slice_fusion.1), channel_id=1, source_target_pairs={{0,256},{256,0},{1,257},{257,1},{2,258},{258,2},{3,259},{259,3},{4... | collective-permute-start | bytes 589832 | tf_op jit(solution)/shard_map/ppermute | solution.py:106
  152.4 2.8 %copy-start.3 = (bf16[4096,768]{1,0:T(8,128)(2,1)S(1)}, bf16[4096,768]{1,0:T(8,128)(2,1)}, u32[]{:S(2)}) copy-start(bf16[4096,768]{1,0:T(8,128)(2,1)} %all-gather.5.cloned.1.call-done.grad_ref) | copy-start | bytes 18874372
  156.5 22.1 %collective-permute-start.3 = (bf16[192,768]{1,0:T(8,128)(2,1)S(1)}, bf16[192,768]{1,0:T(8,128)(2,1)S(1)}, u32[]{:S(2)}, u32[]{:S(2)}) collective-permute-start(bf16[192,768]{1,0:T(8,128)(2,1)S(1)} %shard_map.60), channel_id=1, source_target_pairs={{0,256},{256,0},{1,257},{257,1},{2,258},{258,2},{3,259},{259,3},{4... | collective-permute-start | bytes 884744 | tf_op jit(solution)/shard_map/ppermute | solution.py:106
Sparse Core Ops, SparseCore 0:
  10.7 52.9 all-gather.2
  69.1 48.6 all-gather.4

commit v14 on v13

--- a/solution.py
+++ b/solution.py
@@ -130,15 +130,15 @@
         return jnp.concatenate(parts, axis=axis)
 
     weight = lax.all_gather(half_of(up_weight, replica), "row", axis=0, tiled=True)
-    line = to_all(features, ("dp", "y"), 2 * SIDE)
-    by_depth = to_all(line, "x", SIDE)
     turns = [(r * COLS + c, c * COLS + r) for r in range(ROWS) for c in range(COLS)]
     turned = lax.ppermute(features, ("row",) + COL, turns)
+    lines = to_all(jnp.stack([features, turned]), ("dp", "y"), 2 * SIDE)
+    by_depth = to_all(lines[:, 0], "x", SIDE)
     out_grad = by_replica(
         half_of(out_grad, replica), to_replica(half_of(out_grad, 1 - replica)), 0
     )
 
-    hidden = hidden_sum(after(by_depth, turned), weight)
+    hidden = hidden_sum(by_depth, weight)
     normal_cdf = 0.5 * (1.0 + jax.scipy.special.erf(hidden / math.sqrt(2.0)))
     density = jnp.exp(-0.5 * hidden * hidden) / math.sqrt(2.0 * math.pi)
     gelu_half = (hidden * normal_cdf).astype(jnp.bfloat16)
@@ -147,11 +147,10 @@
     )
     grads = lax.all_gather(hidden_grad, "row", axis=0, tiled=True)
 
-    by_token = to_all(after(turned, hidden_grad), ("dp", "y"), 2 * SIDE)
-    by_token = to_all(by_token, "x", SIDE)
+    by_token = to_all(after(lines[:, 1], hidden_grad), "x", SIDE)
     pieces = input_grad_pieces(weight, hidden_grad)
     own = token_sum(by_token, grads)
-    feature_grad = sum_along(sum_along(pieces, "x"), ("dp", "y")).T
+    feature_grad = sum_along(after(sum_along(pieces, "x"), own), ("dp", "y")).T
 
     mine, other = (
         lax.dynamic_slice_in_dim(gelu_half, which * tokens, tokens, axis=0)

time: 189 us -> 177 us (0.937)
  blocking collectives: 43.6 us -> 23.4 us
  waiting for transfers between devices: 46.4 us -> 61.2 us
  starting transfers between devices: 55.7 us -> 49.4 us
    all_to_all x1 -> x0, blocking collectives: 26.5 us -> none  [sum_along(): pieces = lax.all_to_all(pieces, axis, 0, 0, tiled=True)]
    all_gather x1, waiting for transfers between devices: 0.02 us -> 15.7 us  [per_device(): grads = lax.all_gather(hidden_grad, 'row', axis=0, tiled=True)]
    all_to_all x1 -> x2, waiting for transfers between devices: 0.01 us -> 7.01 us  [sum_along(): pieces = lax.all_to_all(pieces, axis, 0, 0, tiled=True)]
    all_to_all x1, blocking collectives: 17.1 us -> 23.4 us  [to_all(): return lax.all_to_all(copies, axis, 0, 0, tiled=True)]
    all_to_all x3 -> x2, starting transfers between devices: 13.3 us -> 7.39 us  [to_all(): return lax.all_to_all(copies, axis, 0, 0, tiled=True)]
    all_gather x1, waiting for transfers between devices: 4.2 us -> 0.01 us  [per_device(): lax.all_gather(half_of(up_weight, replica), 'row', axis=0, tiled=True)]
    ppermute x1, waiting for transfers between devices: 6.62 us -> 3.86 us  [per_device(): turned = lax.ppermute(features, ('row',) + COL, turns)]
    ppermute x3, starting transfers between devices: 15.6 us -> 18.2 us  [to_replica(): return lax.ppermute(value, 'dp', [(0, 1), (1, 0)])]
  transfers between devices with their start and end apart: 10 -> 10, of which waited for: 6 -> 7; matrix products, arithmetic and copies ran while one was open for 5% -> 5% of each run, Pallas kernels for 2% -> 3%
where the time goes in v14:
time: 177 us; the launch traced here: 175 us
  waiting for transfers between devices  61.2 us (35%)
  starting transfers between devices  49.4 us (28%)
  blocking collectives  23.4 us (13%)
  between operations  14.2 us (8%)
  local copies, waits for them, and re-layouts  12.5 us (7%)
  other arithmetic  7.26 us (4%)
  Pallas kernels  6.65 us (4%)
    all_to_all x1, blocking collectives, to_all(): return lax.all_to_all(copies, axis, 0, 0, tiled=True)  23.4 us
    all_to_all x2, waiting for transfers between devices, to_all(): return lax.all_to_all(copies, axis, 0, 0, tiled=True)  22 us
    ppermute x3, starting transfers between devices, to_replica(): return lax.ppermute(value, 'dp', [(0, 1), (1, 0)])  18.2 us
    all_gather x1, waiting for transfers between devices, per_device(): grads = lax.all_gather(hidden_grad, 'row', axis=0, tiled=True)  15.7 us
    ppermute x1, starting transfers between devices, per_device(): turned = lax.ppermute(features, ('row',) + COL, turns)  13.3 us
    ppermute x3, waiting for transfers between devices, to_replica(): return lax.ppermute(value, 'dp', [(0, 1), (1, 0)])  12.6 us
    all_to_all x2, starting transfers between devices, sum_along(): pieces = lax.all_to_all(pieces, axis, 0, 0, tiled=True)  10.4 us
    unnamed x12, local copies, waits for them, and re-layouts  8.47 us
  transfers between devices with their start and end apart: 10, of which 7 were waited for; matrix products, arithmetic and copies ran while one was open for 5% of the time, Pallas kernels for 3%

profile of v14, /device:TPU:56, one launch (start us, length us, event | category | flops | bytes accessed | tf_op | source)
XLA Modules:
  0.0 174.7 jit_solution(14752406082177217650)
XLA Ops:
  7.2 1.0 copy-done
  8.2 0.7 constant_dynamic-slice_fusion.2
  9.0 13.3 %collective-permute-start = (bf16[192,128]{1,0:T(8,128)(2,1)}, bf16[192,128]{1,0:T(8,128)(2,1)S(1)}, u32[]{:S(2)}, u32[]{:S(2)}) collective-permute-start(bf16[192,128]{1,0:T(8,128)(2,1)} %bitcast.9), channel_id=1, source_target_pairs={{0,0},{1,16},{2,32},{3,48},{4,64},{5,80},{6,96},{7,112},{8,128},{9... | collective-permute-start | bytes 147464 | tf_op jit(solution)/shard_map/ppermute | solution.py:134
  22.3 3.9 %collective-permute-done = bf16[192,128]{1,0:T(8,128)(2,1)S(1)} collective-permute-done((bf16[192,128]{1,0:T(8,128)(2,1)}, bf16[192,128]{1,0:T(8,128)(2,1)S(1)}, u32[]{:S(2)}, u32[]{:S(2)}) %collective-permute-start) | collective-permute-done | bytes 49184 | tf_op jit(solution)/shard_map/ppermute | solution.py:134
  26.2 0.8 pad_maximum_fusion.1
  27.1 23.4 %all_to_all.25 = bf16[8,2,192,128]{3,2,1,0:T(8,128)(2,1)S(1)} all-to-all(bf16[8,2,192,128]{3,2,1,0:T(8,128)(2,1)S(1)} %broadcast_in_dim.8), channel_id=1, replica_groups=mesh['dp'=2,'row'=16,'y'=4,'x'=4] {'dp','y'}, dimensions={0} | all-to-all | bytes 1572864 | tf_op jit(solution)/shard_map/all_to_all | solution.py:111
  50.6 1.5 broadcast_in_dim.10
  52.1 3.7 %all-to-all-start.1 = ((bf16[4,8,192,128]{3,2,1,0:T(8,128)(2,1)}), bf16[4,8,192,128]{3,2,1,0:T(8,128)(2,1)S(1)}, u32[]{:S(2)}, u32[]{:S(2)}) async-start(bf16[4,8,192,128]{3,2,1,0:T(8,128)(2,1)} %broadcast_in_dim.10), calls=%async_computation.1 | async-start | bytes 3145728 | tf_op jit(solution)/shard_map/all_to_all | solution.py:111
  55.9 6.4 %collective-permute-start.2 = (bf16[128,768]{1,0:T(8,128)(2,1)S(1)}, bf16[128,768]{1,0:T(8,128)(2,1)S(1)}, u32[]{:S(2)}, u32[]{:S(2)}) collective-permute-start(bf16[128,768]{1,0:T(8,128)(2,1)S(1)} %constant_dynamic-slice_fusion), channel_id=1, source_target_pairs={{0,256},{256,0},{1,257},{257,1},{2,258},{258,2},{3,259},{259,3},{4... | collective-permute-start | bytes 589832 | tf_op jit(solution)/shard_map/ppermute | solution.py:106
  62.3 5.6 %collective-permute-done.2 = bf16[128,768]{1,0:T(8,128)(2,1)S(1)} collective-permute-done((bf16[128,768]{1,0:T(8,128)(2,1)S(1)}, bf16[128,768]{1,0:T(8,128)(2,1)S(1)}, u32[]{:S(2)}, u32[]{:S(2)}) %collective-permute-start.2) | collective-permute-done | bytes 196640 | tf_op jit(solution)/shard_map/ppermute | solution.py:106
  68.0 8.2 %all-to-all-done.1.block_ref = bf16[4,8,192,128]{3,2,1,0:T(8,128)(2,1)S(1)} async-done(((bf16[4,8,192,128]{3,2,1,0:T(8,128)(2,1)}), bf16[4,8,192,128]{3,2,1,0:T(8,128)(2,1)S(1)}, u32[]{:S(2)}, u32[]{:S(2)}) %all-to-all-start.1) | async-done | bytes 1572896 | tf_op jit(solution)/shard_map/all_to_all | solution.py:111
  76.3 2.3 %copy-done.1 = bf16[3072,768]{1,0:T(8,128)(2,1)S(1)} copy-done((bf16[3072,768]{1,0:T(8,128)(2,1)S(1)}, bf16[3072,768]{1,0:T(8,128)(2,1)}, u32[]{:S(2)}) %copy-start.1) | copy-done | bytes 4718616
  78.6 1.8 %shard_map.58 = f32[256,768]{1,0:T(8,128)S(1)} custom-call(bf16[4,8,192,128]{3,2,1,0:T(8,128)(2,1)S(1)} %all-to-all-done.1.block_ref, bf16[3072,768]{1,0:T(8,128)(2,1)S(1)} %copy-done.1), custom_call_target="tpu_custom_call" | custom-call | flops 1207959552 | bytes 7077888 | tf_op jit(solution)/shard_map/pallas_call | solution.py:25
  80.5 1.1 fusion.5
  81.6 1.6 broadcast_in_dim.22
  83.2 3.7 %all-to-all-start.3 = ((bf16[4,8,192,128]{3,2,1,0:T(8,128)(2,1)}), bf16[4,8,192,128]{3,2,1,0:T(8,128)(2,1)S(1)}, u32[]{:S(2)}, u32[]{:S(2)}) async-start(bf16[4,8,192,128]{3,2,1,0:T(8,128)(2,1)} %broadcast_in_dim.22), calls=%async_computation.3 | async-start | bytes 3145728 | tf_op jit(solution)/shard_map/all_to_all | solution.py:111
  86.9 2.3 %copy-done.2 = bf16[3072,768]{1,0:T(8,128)(2,1)S(1)} copy-done((bf16[3072,768]{1,0:T(8,128)(2,1)S(1)}, bf16[3072,768]{1,0:T(8,128)(2,1)}, u32[]{:S(2)}) %copy-start.2) | copy-done | bytes 4718616
  89.2 3.4 %shard_map.59 = bf16[4,8,192,128]{3,2,1,0:T(8,128)(2,1)} custom-call(bf16[3072,768]{1,0:T(8,128)(2,1)S(1)} %copy-done.2, bf16[256,768]{1,0:T(8,128)(2,1)S(1)} %copy-done.4), custom_call_target="tpu_custom_call" | custom-call | flops 1207959552 | bytes 6684672 | tf_op jit(solution)/shard_map/pallas_call | solution.py:25
  92.6 13.8 %all-to-all-done.3.block_ref = bf16[4,8,192,128]{3,2,1,0:T(8,128)(2,1)S(1)} async-done(((bf16[4,8,192,128]{3,2,1,0:T(8,128)(2,1)}), bf16[4,8,192,128]{3,2,1,0:T(8,128)(2,1)S(1)}, u32[]{:S(2)}, u32[]{:S(2)}) %all-to-all-start.3) | async-done | bytes 1572896 | tf_op jit(solution)/shard_map/all_to_all | solution.py:111
  106.4 4.4 %all-to-all-start.2 = ((bf16[4,8,192,128]{3,2,1,0:T(8,128)(2,1)}), bf16[4,8,192,128]{3,2,1,0:T(8,128)(2,1)}, u32[]{:S(2)}, u32[]{:S(2)}) async-start(bf16[4,8,192,128]{3,2,1,0:T(8,128)(2,1)} %shard_map.59), calls=%async_computation.2 | async-start | bytes 3145728 | tf_op jit(solution)/shard_map/all_to_all | solution.py:115
  110.8 6.7 %collective-permute-start.1 = (bf16[128,768]{1,0:T(8,128)(2,1)S(1)}, bf16[128,768]{1,0:T(8,128)(2,1)S(1)}, u32[]{:S(2)}, u32[]{:S(2)}) collective-permute-start(bf16[128,768]{1,0:T(8,128)(2,1)S(1)} %constant_dynamic-slice_fusion.1), channel_id=1, source_target_pairs={{0,256},{256,0},{1,257},{257,1},{2,258},{258,2},{3,259},{259,3},{4... | collective-permute-start | bytes 589832 | tf_op jit(solution)/shard_map/ppermute | solution.py:106
  117.5 15.7 %all-gather.5.cloned.1.call-done.grad_ref = bf16[4096,768]{1,0:T(8,128)(2,1)} async-done(((bf16[256,768]{1,0:T(8,128)(2,1)}), bf16[4096,768]{1,0:T(8,128)(2,1)}) %all-gather.5.cloned.1.call-update) | async-done | bytes 6291472 | tf_op jit(solution)/shard_map/all_gather | solution.py:148
  133.2 2.8 %copy-done.3 = bf16[4096,768]{1,0:T(8,128)(2,1)S(1)} copy-done((bf16[4096,768]{1,0:T(8,128)(2,1)S(1)}, bf16[4096,768]{1,0:T(8,128)(2,1)}, u32[]{:S(2)}) %copy-start.3) | copy-done | bytes 6291480
  136.0 1.4 shard_map.60
  137.4 5.1 %collective-permute-start.3 = (bf16[192,768]{1,0:T(8,128)(2,1)S(1)}, bf16[192,768]{1,0:T(8,128)(2,1)S(1)}, u32[]{:S(2)}, u32[]{:S(2)}) collective-permute-start(bf16[192,768]{1,0:T(8,128)(2,1)S(1)} %shard_map.60), channel_id=1, source_target_pairs={{0,256},{256,0},{1,257},{257,1},{2,258},{258,2},{3,259},{259,3},{4... | collective-permute-start | bytes 884744 | tf_op jit(solution)/shard_map/ppermute | solution.py:106
  142.6 2.5 %reduce_sum.24 = bf16[8,192,128]{2,1,0:T(8,128)(2,1)} reduce(bf16[4,8,192,128]{3,2,1,0:T(8,128)(2,1)} %all-to-all-done.2, bf16[]{:T(256)} %constant.33.clone.1), dimensions={0}, to_apply=%region_0.1 | reduce | flops 589824 | bytes 1966082 | tf_op jit(solution)/shard_map/reduce_sum | solution.py:116
  145.1 6.1 %all-to-all-start.4 = ((bf16[8,192,128]{2,1,0:T(8,128)(2,1)}), bf16[8,192,128]{2,1,0:T(8,128)(2,1)S(1)}, u32[]{:S(2)}, u32[]{:S(2)}) async-start(bf16[8,192,128]{2,1,0:T(8,128)(2,1)} %reduce_sum.24), calls=%async_computation.4 | async-start | bytes 786432 | tf_op jit(solution)/shard_map/all_to_all | solution.py:115
  151.2 0.8 pad_maximum_fusion
  152.0 7.0 %collective-permute-done.3 = bf16[192,768]{1,0:T(8,128)(2,1)S(1)} collective-permute-done((bf16[192,768]{1,0:T(8,128)(2,1)S(1)}, bf16[192,768]{1,0:T(8,128)(2,1)S(1)}, u32[]{:S(2)}, u32[]{:S(2)}) %collective-permute-start.3) | collective-permute-done | bytes 294944 | tf_op jit(solution)/shard_map/ppermute | solution.py:106
  159.0 1.1 maximum_convert_fusion
  160.2 7.0 %all-to-all-done.4 = bf16[8,192,128]{2,1,0:T(8,128)(2,1)S(1)} async-done(((bf16[8,192,128]{2,1,0:T(8,128)(2,1)}), bf16[8,192,128]{2,1,0:T(8,128)(2,1)S(1)}, u32[]{:S(2)}, u32[]{:S(2)}) %all-to-all-start.4) | async-done | bytes 393248 | tf_op jit(solution)/shard_map/all_to_all | solution.py:115
  167.2 0.7 reduce_sum.25
  (22 shorter events, 0.6 us)
Async XLA Ops:
  7.2 1.1 copy-start
  7.2 69.1 %all-gather.3.cloned.1.call-start = ((), (), s32[]{:S(2)}) async-start(), calls=%async_computation.5 | async-start | bytes 5013504 | tf_op jit(solution)/shard_map/all_gather | solution.py:132
  9.0 17.2 %collective-permute-start = (bf16[192,128]{1,0:T(8,128)(2,1)}, bf16[192,128]{1,0:T(8,128)(2,1)S(1)}, u32[]{:S(2)}, u32[]{:S(2)}) collective-permute-start(bf16[192,128]{1,0:T(8,128)(2,1)} %bitcast.9), channel_id=1, source_target_pairs={{0,0},{1,16},{2,32},{3,48},{4,64},{5,80},{6,96},{7,112},{8,128},{9... | collective-permute-start | bytes 147464 | tf_op jit(solution)/shard_map/ppermute | solution.py:134
  52.1 3.8 %copy-start.5 = (bf16[128,1536]{1,0:T(8,128)(2,1)S(1)}, bf16[128,1536]{1,0:T(8,128)(2,1)}, u32[]{:S(2)}) copy-start(bf16[128,1536]{1,0:T(8,128)(2,1)} %param.5) | copy-start | bytes 1179652
  52.1 24.2 %all-to-all-start.1 = ((bf16[4,8,192,128]{3,2,1,0:T(8,128)(2,1)}), bf16[4,8,192,128]{3,2,1,0:T(8,128)(2,1)S(1)}, u32[]{:S(2)}, u32[]{:S(2)}) async-start(bf16[4,8,192,128]{3,2,1,0:T(8,128)(2,1)} %broadcast_in_dim.10), calls=%async_computation.1 | async-start | bytes 3145728 | tf_op jit(solution)/shard_map/all_to_all | solution.py:111
  55.8 77.4 %all-gather.5.cloned.1.call-start = ((), (), s32[]{:S(2)}) async-start(), calls=%async_computation.6 | async-start | bytes 6684672 | tf_op jit(solution)/shard_map/all_gather | solution.py:148
  55.9 12.0 %collective-permute-start.2 = (bf16[128,768]{1,0:T(8,128)(2,1)S(1)}, bf16[128,768]{1,0:T(8,128)(2,1)S(1)}, u32[]{:S(2)}, u32[]{:S(2)}) collective-permute-start(bf16[128,768]{1,0:T(8,128)(2,1)S(1)} %constant_dynamic-slice_fusion), channel_id=1, source_target_pairs={{0,256},{256,0},{1,257},{257,1},{2,258},{258,2},{3,259},{259,3},{4... | collective-permute-start | bytes 589832 | tf_op jit(solution)/shard_map/ppermute | solution.py:106
  76.3 2.3 %copy-start.1 = (bf16[3072,768]{1,0:T(8,128)(2,1)S(1)}, bf16[3072,768]{1,0:T(8,128)(2,1)}, u32[]{:S(2)}) copy-start(bf16[3072,768]{1,0:T(8,128)(2,1)} %all-gather.3.cloned.1.call-done.weight_ref) | copy-start | bytes 14155780
  83.2 3.7 %copy-start.4 = (bf16[256,768]{1,0:T(8,128)(2,1)S(1)}, bf16[256,768]{1,0:T(8,128)(2,1)}, u32[]{:S(2)}) copy-start(bf16[256,768]{1,0:T(8,128)(2,1)} %get-tuple-element.9.grad_ref) | copy-start | bytes 1179652
  83.2 23.2 %all-to-all-start.3 = ((bf16[4,8,192,128]{3,2,1,0:T(8,128)(2,1)}), bf16[4,8,192,128]{3,2,1,0:T(8,128)(2,1)S(1)}, u32[]{:S(2)}, u32[]{:S(2)}) async-start(bf16[4,8,192,128]{3,2,1,0:T(8,128)(2,1)} %broadcast_in_dim.22), calls=%async_computation.3 | async-start | bytes 3145728 | tf_op jit(solution)/shard_map/all_to_all | solution.py:111
  86.9 2.3 %copy-start.2 = (bf16[3072,768]{1,0:T(8,128)(2,1)S(1)}, bf16[3072,768]{1,0:T(8,128)(2,1)}, u32[]{:S(2)}) copy-start(bf16[3072,768]{1,0:T(8,128)(2,1)} %all-gather.3.cloned.1.call-done.weight_ref) | copy-start | bytes 14155780
  106.4 36.2 %all-to-all-start.2 = ((bf16[4,8,192,128]{3,2,1,0:T(8,128)(2,1)}), bf16[4,8,192,128]{3,2,1,0:T(8,128)(2,1)}, u32[]{:S(2)}, u32[]{:S(2)}) async-start(bf16[4,8,192,128]{3,2,1,0:T(8,128)(2,1)} %shard_map.59), calls=%async_computation.2 | async-start | bytes 3145728 | tf_op jit(solution)/shard_map/all_to_all | solution.py:115
  110.8 31.7 %collective-permute-start.1 = (bf16[128,768]{1,0:T(8,128)(2,1)S(1)}, bf16[128,768]{1,0:T(8,128)(2,1)S(1)}, u32[]{:S(2)}, u32[]{:S(2)}) collective-permute-start(bf16[128,768]{1,0:T(8,128)(2,1)S(1)} %constant_dynamic-slice_fusion.1), channel_id=1, source_target_pairs={{0,256},{256,0},{1,257},{257,1},{2,258},{258,2},{3,259},{259,3},{4... | collective-permute-start | bytes 589832 | tf_op jit(solution)/shard_map/ppermute | solution.py:106
  133.2 2.8 %copy-start.3 = (bf16[4096,768]{1,0:T(8,128)(2,1)S(1)}, bf16[4096,768]{1,0:T(8,128)(2,1)}, u32[]{:S(2)}) copy-start(bf16[4096,768]{1,0:T(8,128)(2,1)} %all-gather.5.cloned.1.call-done.grad_ref) | copy-start | bytes 18874372
  137.4 21.6 %collective-permute-start.3 = (bf16[192,768]{1,0:T(8,128)(2,1)S(1)}, bf16[192,768]{1,0:T(8,128)(2,1)S(1)}, u32[]{:S(2)}, u32[]{:S(2)}) collective-permute-start(bf16[192,768]{1,0:T(8,128)(2,1)S(1)} %shard_map.60), channel_id=1, source_target_pairs={{0,256},{256,0},{1,257},{257,1},{2,258},{258,2},{3,259},{259,3},{4... | collective-permute-start | bytes 884744 | tf_op jit(solution)/shard_map/ppermute | solution.py:106
  145.1 22.1 %all-to-all-start.4 = ((bf16[8,192,128]{2,1,0:T(8,128)(2,1)}), bf16[8,192,128]{2,1,0:T(8,128)(2,1)S(1)}, u32[]{:S(2)}, u32[]{:S(2)}) async-start(bf16[8,192,128]{2,1,0:T(8,128)(2,1)} %reduce_sum.24), calls=%async_computation.4 | async-start | bytes 786432 | tf_op jit(solution)/shard_map/all_to_all | solution.py:115
Sparse Core Ops, SparseCore 0:
  10.7 50.1 all-gather.2
  81.7 51.4 all-gather.4

commit v15 on v13

--- a/solution.py
+++ b/solution.py
@@ -20,12 +20,16 @@
     return lax.optimization_barrier((value,) + others)[0]
 
 
-def local_kernel(kernel, out_shape, flops, operands):
+def local_kernel(kernel, out_shape, flops, operands, place=None):
     moved = sum(x.size * x.dtype.itemsize for x in (*operands, out_shape))
+    in_specs = [pl.BlockSpec(memory_space=pltpu.VMEM)] * len(operands)
+    if place is not None:
+        in_specs = [pl.BlockSpec(memory_space=pltpu.SMEM)] + in_specs
+        operands = (place, *operands)
     return pl.pallas_call(
         kernel,
         out_shape=out_shape,
-        in_specs=[pl.BlockSpec(memory_space=pltpu.VMEM)] * len(operands),
+        in_specs=in_specs,
         out_specs=pl.BlockSpec(memory_space=pltpu.VMEM),
         compiler_params=pltpu.CompilerParams(vmem_limit_bytes=VMEM_BYTES),
         cost_estimate=pl.CostEstimate(flops=flops, bytes_accessed=moved, transcendentals=0),
@@ -80,9 +84,12 @@
     return local_kernel(input_grad_kernel, out_shape, 2 * weight.size * grad.shape[0], (weight, grad))
 
 
-def token_sum_kernel(block_ref, grad_ref, total_ref):
-    tokens = 2 * block_ref.shape[3]
-    blocks = [both_replicas(block_ref, row) for row in range(ROWS)]
+def token_sum_kernel(place_ref, block_ref, grad_ref, total_ref):
+    tokens = 2 * block_ref.shape[2]
+    blocks = []
+    for row in range(ROWS):
+        parts = [block_ref[place_ref[2 * row + d]] for d in range(2)]
+        blocks.append(jnp.concatenate(parts, axis=1))
     for start in range(0, total_ref.shape[1], LANES):
         units = pl.ds(start, LANES)
         total = None
@@ -96,10 +103,40 @@
         total_ref[:, units] = total.astype(total_ref.dtype)
 
 
-def token_sum(blocks, grads):
-    depth = blocks.shape[2]
+def token_sum(place, blocks, grads):
+    depth = blocks.shape[1]
     out_shape = jax.ShapeDtypeStruct((depth, grads.shape[1]), jnp.bfloat16)
-    return local_kernel(token_sum_kernel, out_shape, 2 * depth * grads.size, (blocks, grads))
+    return local_kernel(
+        token_sum_kernel, out_shape, 2 * depth * grads.size, (blocks, grads), place
+    )
+
+
+def places():
+    tables = []
+    for replica in range(2):
+        for col in range(COLS):
+            y, x = divmod(col, SIDE)
+            tables.append(
+                [
+                    ((x - c) % SIDE * SIDE + (y - c // SIDE) % SIDE) * 2 + (replica ^ d)
+                    for c in range(COLS)
+                    for d in range(2)
+                ]
+            )
+    return jnp.array(tables, jnp.int32)[lax.axis_index(("dp",) + COL)]
+
+
+def shifted(value, axis, steps):
+    return lax.ppermute(value, axis, [(i, (i + steps) % SIDE) for i in range(SIDE)])
+
+
+def from_line(block):
+    pair = jnp.stack([block, to_replica(block)])
+    return jnp.concatenate([pair] + [shifted(pair, "y", d) for d in range(1, SIDE)])
+
+
+def from_lines(line):
+    return jnp.concatenate([line] + [shifted(line, "x", e) for e in range(1, SIDE)])
 
 
 def to_replica(value):
@@ -130,15 +167,16 @@
         return jnp.concatenate(parts, axis=axis)
 
     weight = lax.all_gather(half_of(up_weight, replica), "row", axis=0, tiled=True)
-    line = to_all(features, ("dp", "y"), 2 * SIDE)
-    by_depth = to_all(line, "x", SIDE)
     turns = [(r * COLS + c, c * COLS + r) for r in range(ROWS) for c in range(COLS)]
     turned = lax.ppermute(features, ("row",) + COL, turns)
+    depth_line = to_all(features, ("dp", "y"), 2 * SIDE)
+    by_depth = to_all(depth_line, "x", SIDE)
+    token_line = from_line(after(turned, depth_line))
     out_grad = by_replica(
         half_of(out_grad, replica), to_replica(half_of(out_grad, 1 - replica)), 0
     )
 
-    hidden = hidden_sum(after(by_depth, turned), weight)
+    hidden = hidden_sum(after(by_depth, token_line), weight)
     normal_cdf = 0.5 * (1.0 + jax.scipy.special.erf(hidden / math.sqrt(2.0)))
     density = jnp.exp(-0.5 * hidden * hidden) / math.sqrt(2.0 * math.pi)
     gelu_half = (hidden * normal_cdf).astype(jnp.bfloat16)
@@ -147,10 +185,9 @@
     )
     grads = lax.all_gather(hidden_grad, "row", axis=0, tiled=True)
 
-    by_token = to_all(after(turned, hidden_grad), ("dp", "y"), 2 * SIDE)
-    by_token = to_all(by_token, "x", SIDE)
+    by_token = from_lines(after(token_line, hidden_grad))
     pieces = input_grad_pieces(weight, hidden_grad)
-    own = token_sum(by_token, grads)
+    own = token_sum(places(), by_token, grads)
     feature_grad = sum_along(sum_along(pieces, "x"), ("dp", "y")).T
 
     mine, other = (

time: 189 us -> 175 us (0.926)
  the two profiles are of different devices: /device:TPU:56 before, /device:TPU:17 now
where the time goes in v15:
time: 175 us; the launch traced here: 174 us
  starting transfers between devices  87.6 us (50%)
  waiting for transfers between devices  40.2 us (23%)
  local copies, waits for them, and re-layouts  17.3 us (10%)
  between operations  14.2 us (8%)
  other arithmetic  7.52 us (4%)
  Pallas kernels  7.13 us (4%)
    ppermute x4, starting transfers between devices, to_replica(): return lax.ppermute(value, 'dp', [(0, 1), (1, 0)])  27.9 us
    ppermute x6, starting transfers between devices, shifted(): lax.ppermute(value, axis, [(i, (i + steps) % SIDE) for i in range(SIDE)])  18.8 us
    ppermute x1, starting transfers between devices, per_device(): turned = lax.ppermute(features, ('row',) + COL, turns)  16.6 us
    ppermute x4, waiting for transfers between devices, to_replica(): return lax.ppermute(value, 'dp', [(0, 1), (1, 0)])  14.4 us
    all_to_all x2, starting transfers between devices, sum_along(): pieces = lax.all_to_all(pieces, axis, 0, 0, tiled=True)  12.6 us
    unnamed x18, local copies, waits for them, and re-layouts  12 us
    all_to_all x2, starting transfers between devices, to_all(): return lax.all_to_all(copies, axis, 0, 0, tiled=True)  11.7 us
    ppermute x6, waiting for transfers between devices, shifted(): lax.ppermute(value, axis, [(i, (i + steps) % SIDE) for i in range(SIDE)])  8.61 us
  transfers between devices with their start and end apart: 17, of which 8 were waited for; matrix products, arithmetic and copies ran while one was open for 7% of the time, Pallas kernels for 3%

profile of v15, /device:TPU:17, one launch (start us, length us, event | category | flops | bytes accessed | tf_op | source)
XLA Modules:
  0.0 173.9 jit_solution(17587478283213976337)
XLA Ops:
  9.0 1.6 broadcast_in_dim.4
  10.6 6.9 %all-to-all-start = ((bf16[8,192,128]{2,1,0:T(8,128)(2,1)}), bf16[8,192,128]{2,1,0:T(8,128)(2,1)S(1)}, u32[]{:S(2)}, u32[]{:S(2)}) async-start(bf16[8,192,128]{2,1,0:T(8,128)(2,1)} %broadcast_in_dim.4), calls=%async_computation | async-start | bytes 786432 | tf_op jit(solution)/shard_map/all_to_all | solution.py:148
  17.5 5.2 %collective-permute-start.6 = (bf16[128,768]{1,0:T(8,128)(2,1)S(1)}, bf16[128,768]{1,0:T(8,128)(2,1)S(1)}, u32[]{:S(2)}, u32[]{:S(2)}) collective-permute-start(bf16[128,768]{1,0:T(8,128)(2,1)S(1)} %constant_dynamic-slice_fusion.1), channel_id=1, source_target_pairs={{0,256},{256,0},{1,257},{257,1},{2,258},{258,2},{3,259},{259,3},{4... | collective-permute-start | bytes 589832 | tf_op jit(solution)/shard_map/ppermute | solution.py:143
  22.7 4.9 %all-to-all-done = bf16[8,192,128]{2,1,0:T(8,128)(2,1)S(1)} async-done(((bf16[8,192,128]{2,1,0:T(8,128)(2,1)}), bf16[8,192,128]{2,1,0:T(8,128)(2,1)S(1)}, u32[]{:S(2)}, u32[]{:S(2)}) %all-to-all-start) | async-done | bytes 393248 | tf_op jit(solution)/shard_map/all_to_all | solution.py:148
  27.7 1.6 broadcast_in_dim.5
  29.2 4.8 %all-to-all-start.1 = ((bf16[4,8,192,128]{3,2,1,0:T(8,128)(2,1)}), bf16[4,8,192,128]{3,2,1,0:T(8,128)(2,1)S(1)}, u32[]{:S(2)}, u32[]{:S(2)}) async-start(bf16[4,8,192,128]{3,2,1,0:T(8,128)(2,1)} %broadcast_in_dim.5), calls=%async_computation.1 | async-start | bytes 3145728 | tf_op jit(solution)/shard_map/all_to_all | solution.py:148
  34.0 16.6 %collective-permute-start = (bf16[192,128]{1,0:T(8,128)(2,1)S(1)}, bf16[192,128]{1,0:T(8,128)(2,1)S(1)}, u32[]{:S(2)}, u32[]{:S(2)}) collective-permute-start(bf16[192,128]{1,0:T(8,128)(2,1)S(1)} %bitcast.11), channel_id=1, source_target_pairs={{0,0},{1,16},{2,32},{3,48},{4,64},{5,80},{6,96},{7,112},{8,128},{9... | collective-permute-start | bytes 147464 | tf_op jit(solution)/shard_map/ppermute | solution.py:171
  50.7 2.4 %collective-permute-done = bf16[192,128]{1,0:T(8,128)(2,1)S(1)} collective-permute-done((bf16[192,128]{1,0:T(8,128)(2,1)S(1)}, bf16[192,128]{1,0:T(8,128)(2,1)S(1)}, u32[]{:S(2)}, u32[]{:S(2)}) %collective-permute-start) | collective-permute-done | bytes 49184 | tf_op jit(solution)/shard_map/ppermute | solution.py:171
  53.1 10.8 %collective-permute-start.1 = (bf16[192,128]{1,0:T(8,128)(2,1)S(1)}, bf16[192,128]{1,0:T(8,128)(2,1)S(1)}, u32[]{:S(2)}, u32[]{:S(2)}) collective-permute-start(bf16[192,128]{1,0:T(8,128)(2,1)S(1)} %collective-permute-done), channel_id=1, source_target_pairs={{0,256},{256,0},{1,257},{257,1},{2,258},{258,2},{3,259},{259,3},{4... | collective-permute-start | bytes 147464 | tf_op jit(solution)/shard_map/ppermute | solution.py:143
  64.5 1.2 collective-permute-done.1
  65.7 2.7 %collective-permute-start.2 = (bf16[2,192,128]{2,1,0:T(8,128)(2,1)S(1)}, bf16[2,192,128]{2,1,0:T(8,128)(2,1)S(1)}, u32[]{:S(2)}, u32[]{:S(2)}) collective-permute-start(bf16[2,192,128]{2,1,0:T(8,128)(2,1)S(1)} %pad_maximum_fusion.2), channel_id=1, source_target_pairs={{0,4},{4,8},{8,12},{12,0},{1,5},{5,9},{9,13},{13,1},{2,6},{6,10},{... | collective-permute-start | bytes 294920 | tf_op jit(solution)/shard_map/ppermute | solution.py:130
  68.4 2.3 %collective-permute-start.3 = (bf16[2,192,128]{2,1,0:T(8,128)(2,1)S(1)}, bf16[2,192,128]{2,1,0:T(8,128)(2,1)S(1)}, u32[]{:S(2)}, u32[]{:S(2)}) collective-permute-start(bf16[2,192,128]{2,1,0:T(8,128)(2,1)S(1)} %pad_maximum_fusion.2), channel_id=1, source_target_pairs={{0,8},{4,12},{8,0},{12,4},{1,9},{5,13},{9,1},{13,5},{2,10},{6,14},... | collective-permute-start | bytes 294920 | tf_op jit(solution)/shard_map/ppermute | solution.py:130
  70.7 4.3 %collective-permute-start.4 = (bf16[2,192,128]{2,1,0:T(8,128)(2,1)S(1)}, bf16[2,192,128]{2,1,0:T(8,128)(2,1)S(1)}, u32[]{:S(2)}, u32[]{:S(2)}) collective-permute-start(bf16[2,192,128]{2,1,0:T(8,128)(2,1)S(1)} %pad_maximum_fusion.2), channel_id=1, source_target_pairs={{0,12},{4,0},{8,4},{12,8},{1,13},{5,1},{9,5},{13,9},{2,14},{6,2},{... | collective-permute-start | bytes 294920 | tf_op jit(solution)/shard_map/ppermute | solution.py:130
  78.3 2.3 %copy-done.1 = bf16[3072,768]{1,0:T(8,128)(2,1)S(1)} copy-done((bf16[3072,768]{1,0:T(8,128)(2,1)S(1)}, bf16[3072,768]{1,0:T(8,128)(2,1)}, u32[]{:S(2)}) %copy-start.1) | copy-done | bytes 4718616
  80.6 1.8 %shard_map.67 = f32[256,768]{1,0:T(8,128)S(1)} custom-call(bf16[4,8,192,128]{3,2,1,0:T(8,128)(2,1)S(1)} %all-to-all-done.1.block_ref, bf16[3072,768]{1,0:T(8,128)(2,1)S(1)} %copy-done.1), custom_call_target="tpu_custom_call" | custom-call | flops 1207959552 | bytes 7077888 | tf_op jit(solution)/shard_map/pallas_call | solution.py:29
  83.6 2.3 %copy-done.2 = bf16[3072,768]{1,0:T(8,128)(2,1)S(1)} copy-done((bf16[3072,768]{1,0:T(8,128)(2,1)S(1)}, bf16[3072,768]{1,0:T(8,128)(2,1)}, u32[]{:S(2)}) %copy-start.2) | copy-done | bytes 4718616
  87.0 3.3 %shard_map.68 = bf16[4,8,192,128]{3,2,1,0:T(8,128)(2,1)} custom-call(bf16[3072,768]{1,0:T(8,128)(2,1)S(1)} %copy-done.2, bf16[256,768]{1,0:T(8,128)(2,1)S(1)} %copy-done.4), custom_call_target="tpu_custom_call" | custom-call | flops 1207959552 | bytes 6684672 | tf_op jit(solution)/shard_map/pallas_call | solution.py:29
  90.3 3.9 %all-to-all-start.2 = ((bf16[4,8,192,128]{3,2,1,0:T(8,128)(2,1)}), bf16[4,8,192,128]{3,2,1,0:T(8,128)(2,1)S(1)}, u32[]{:S(2)}, u32[]{:S(2)}) async-start(bf16[4,8,192,128]{3,2,1,0:T(8,128)(2,1)} %shard_map.68), calls=%async_computation.2 | async-start | bytes 3145728 | tf_op jit(solution)/shard_map/all_to_all | solution.py:152
  94.2 4.6 %collective-permute-start.9 = (bf16[8,192,128]{2,1,0:T(8,128)(2,1)}, bf16[8,192,128]{2,1,0:T(8,128)(2,1)}, u32[]{:S(2)}, u32[]{:S(2)}) collective-permute-start(bf16[8,192,128]{2,1,0:T(8,128)(2,1)} %constant_dynamic-update-slice_fusion), channel_id=1, source_target_pairs={{0,3},{1,0},{2,1},{3,2},{4,7},{5,4},{6,5},{7,6},{8,11},{9,8},{10,9... | collective-permute-start | bytes 1179656 | tf_op jit(solution)/shard_map/ppermute | solution.py:130
  98.8 2.5 %collective-permute-start.8 = (bf16[8,192,128]{2,1,0:T(8,128)(2,1)}, bf16[8,192,128]{2,1,0:T(8,128)(2,1)}, u32[]{:S(2)}, u32[]{:S(2)}) collective-permute-start(bf16[8,192,128]{2,1,0:T(8,128)(2,1)} %constant_dynamic-update-slice_fusion), channel_id=1, source_target_pairs={{0,2},{1,3},{2,0},{3,1},{4,6},{5,7},{6,4},{7,5},{8,10},{9,11},{10,... | collective-permute-start | bytes 1179656 | tf_op jit(solution)/shard_map/ppermute | solution.py:130
  101.3 2.5 %collective-permute-start.7 = (bf16[8,192,128]{2,1,0:T(8,128)(2,1)}, bf16[8,192,128]{2,1,0:T(8,128)(2,1)}, u32[]{:S(2)}, u32[]{:S(2)}) collective-permute-start(bf16[8,192,128]{2,1,0:T(8,128)(2,1)} %constant_dynamic-update-slice_fusion), channel_id=1, source_target_pairs={{0,1},{1,2},{2,3},{3,0},{4,5},{5,6},{6,7},{7,4},{8,9},{9,10},{10,1... | collective-permute-start | bytes 1179656 | tf_op jit(solution)/shard_map/ppermute | solution.py:130
  104.5 6.6 %collective-permute-start.5 = (bf16[128,768]{1,0:T(8,128)(2,1)S(1)}, bf16[128,768]{1,0:T(8,128)(2,1)}, u32[]{:S(2)}, u32[]{:S(2)}) collective-permute-start(bf16[128,768]{1,0:T(8,128)(2,1)S(1)} %constant_dynamic-slice_fusion.2), channel_id=1, source_target_pairs={{0,256},{256,0},{1,257},{257,1},{2,258},{258,2},{3,259},{259,3},{4... | collective-permute-start | bytes 589832 | tf_op jit(solution)/shard_map/ppermute | solution.py:143
  111.1 2.9 %all-to-all-done.2 = bf16[4,8,192,128]{3,2,1,0:T(8,128)(2,1)S(1)} async-done(((bf16[4,8,192,128]{3,2,1,0:T(8,128)(2,1)}), bf16[4,8,192,128]{3,2,1,0:T(8,128)(2,1)S(1)}, u32[]{:S(2)}, u32[]{:S(2)}) %all-to-all-start.2) | async-done | bytes 1572896 | tf_op jit(solution)/shard_map/all_to_all | solution.py:152
  115.1 8.7 %all-to-all-start.3 = ((bf16[8,192,128]{2,1,0:T(8,128)(2,1)}), bf16[8,192,128]{2,1,0:T(8,128)(2,1)S(1)}, u32[]{:S(2)}, u32[]{:S(2)}) async-start(bf16[8,192,128]{2,1,0:T(8,128)(2,1)} %reduce_sum.24), calls=%async_computation.3 | async-start | bytes 786432 | tf_op jit(solution)/shard_map/all_to_all | solution.py:152
  123.8 7.9 %collective-permute-done.7 = bf16[8,192,128]{2,1,0:T(8,128)(2,1)} collective-permute-done((bf16[8,192,128]{2,1,0:T(8,128)(2,1)}, bf16[8,192,128]{2,1,0:T(8,128)(2,1)}, u32[]{:S(2)}, u32[]{:S(2)}) %collective-permute-start.7) | collective-permute-done | bytes 393248 | tf_op jit(solution)/shard_map/ppermute | solution.py:130
  131.7 1.6 pad_maximum_fusion.block_ref
  133.2 6.9 %all-gather.5.cloned.1.call-done.grad_ref = bf16[4096,768]{1,0:T(8,128)(2,1)} async-done(((bf16[256,768]{1,0:T(8,128)(2,1)}), bf16[4096,768]{1,0:T(8,128)(2,1)}) %all-gather.5.cloned.1.call-update) | async-done | bytes 6291472 | tf_op jit(solution)/shard_map/all_gather | solution.py:186
  140.1 2.8 %copy-done.3 = bf16[4096,768]{1,0:T(8,128)(2,1)S(1)} copy-done((bf16[4096,768]{1,0:T(8,128)(2,1)S(1)}, bf16[4096,768]{1,0:T(8,128)(2,1)}, u32[]{:S(2)}) %copy-start.3) | copy-done | bytes 6291480
  142.9 2.0 %shard_map.69 = bf16[192,768]{1,0:T(8,128)(2,1)S(1)} custom-call(s32[32]{0:T(128)S(1)} %fusion.6.place_ref, bf16[32,192,128]{2,1,0:T(8,128)(2,1)S(1)} %pad_maximum_fusion.block_ref, bf16[4096,768]{1,0:T(8,128)(2,1)S(1)} %copy-done.3), custom_call_target="tpu_custom_call" | custom-call | flops 1207959552 | bytes 8159232 | tf_op jit(solution)/shard_map/pallas_call | solution.py:29
  144.9 5.3 %collective-permute-start.10 = (bf16[192,768]{1,0:T(8,128)(2,1)S(1)}, bf16[192,768]{1,0:T(8,128)(2,1)S(1)}, u32[]{:S(2)}, u32[]{:S(2)}) collective-permute-start(bf16[192,768]{1,0:T(8,128)(2,1)S(1)} %shard_map.69), channel_id=1, source_target_pairs={{0,256},{256,0},{1,257},{257,1},{2,258},{258,2},{3,259},{259,3},{4... | collective-permute-start | bytes 884744 | tf_op jit(solution)/shard_map/ppermute | solution.py:143
  152.6 13.3 %collective-permute-done.10 = bf16[192,768]{1,0:T(8,128)(2,1)S(1)} collective-permute-done((bf16[192,768]{1,0:T(8,128)(2,1)S(1)}, bf16[192,768]{1,0:T(8,128)(2,1)S(1)}, u32[]{:S(2)}, u32[]{:S(2)}) %collective-permute-start.10) | collective-permute-done | bytes 294944 | tf_op jit(solution)/shard_map/ppermute | solution.py:143
  166.0 1.1 maximum_convert_fusion
  (42 shorter events, 12.3 us)
Async XLA Ops:
  7.2 1.1 copy-start
  7.2 10.3 %copy-start.5 = (bf16[128,1536]{1,0:T(8,128)(2,1)S(1)}, bf16[128,1536]{1,0:T(8,128)(2,1)}, u32[]{:S(2)}) copy-start(bf16[128,1536]{1,0:T(8,128)(2,1)} %param.6) | copy-start | bytes 1179652
  7.2 71.1 %all-gather.3.cloned.1.call-start = ((), (), s32[]{:S(2)}) async-start(), calls=%async_computation.4 | async-start | bytes 5013504 | tf_op jit(solution)/shard_map/all_gather | solution.py:169
  10.6 17.1 %all-to-all-start = ((bf16[8,192,128]{2,1,0:T(8,128)(2,1)}), bf16[8,192,128]{2,1,0:T(8,128)(2,1)S(1)}, u32[]{:S(2)}, u32[]{:S(2)}) async-start(bf16[8,192,128]{2,1,0:T(8,128)(2,1)} %broadcast_in_dim.4), calls=%async_computation | async-start | bytes 786432 | tf_op jit(solution)/shard_map/all_to_all | solution.py:148
  17.5 33.1 %collective-permute-start.6 = (bf16[128,768]{1,0:T(8,128)(2,1)S(1)}, bf16[128,768]{1,0:T(8,128)(2,1)S(1)}, u32[]{:S(2)}, u32[]{:S(2)}) collective-permute-start(bf16[128,768]{1,0:T(8,128)(2,1)S(1)} %constant_dynamic-slice_fusion.1), channel_id=1, source_target_pairs={{0,256},{256,0},{1,257},{257,1},{2,258},{258,2},{3,259},{259,3},{4... | collective-permute-start | bytes 589832 | tf_op jit(solution)/shard_map/ppermute | solution.py:143
  29.2 4.8 %copy-start.6 = (bf16[128,192]{0,1:T(8,128)(2,1)S(1)}, bf16[128,192]{0,1:T(8,128)(2,1)}, u32[]{:S(2)}) copy-start(bf16[128,192]{0,1:T(8,128)(2,1)} %param.4) | copy-start | bytes 147460
  29.2 49.0 %all-to-all-start.1 = ((bf16[4,8,192,128]{3,2,1,0:T(8,128)(2,1)}), bf16[4,8,192,128]{3,2,1,0:T(8,128)(2,1)S(1)}, u32[]{:S(2)}, u32[]{:S(2)}) async-start(bf16[4,8,192,128]{3,2,1,0:T(8,128)(2,1)} %broadcast_in_dim.5), calls=%async_computation.1 | async-start | bytes 3145728 | tf_op jit(solution)/shard_map/all_to_all | solution.py:148
  34.0 106.1 %all-gather.5.cloned.1.call-start = ((), (), s32[]{:S(2)}) async-start(), calls=%async_computation.5 | async-start | bytes 6684672 | tf_op jit(solution)/shard_map/all_gather | solution.py:186
  34.0 19.1 %collective-permute-start = (bf16[192,128]{1,0:T(8,128)(2,1)S(1)}, bf16[192,128]{1,0:T(8,128)(2,1)S(1)}, u32[]{:S(2)}, u32[]{:S(2)}) collective-permute-start(bf16[192,128]{1,0:T(8,128)(2,1)S(1)} %bitcast.11), channel_id=1, source_target_pairs={{0,0},{1,16},{2,32},{3,48},{4,64},{5,80},{6,96},{7,112},{8,128},{9... | collective-permute-start | bytes 147464 | tf_op jit(solution)/shard_map/ppermute | solution.py:171
  53.1 12.6 %collective-permute-start.1 = (bf16[192,128]{1,0:T(8,128)(2,1)S(1)}, bf16[192,128]{1,0:T(8,128)(2,1)S(1)}, u32[]{:S(2)}, u32[]{:S(2)}) collective-permute-start(bf16[192,128]{1,0:T(8,128)(2,1)S(1)} %collective-permute-done), channel_id=1, source_target_pairs={{0,256},{256,0},{1,257},{257,1},{2,258},{258,2},{3,259},{259,3},{4... | collective-permute-start | bytes 147464 | tf_op jit(solution)/shard_map/ppermute | solution.py:143
  65.7 9.9 %collective-permute-start.2 = (bf16[2,192,128]{2,1,0:T(8,128)(2,1)S(1)}, bf16[2,192,128]{2,1,0:T(8,128)(2,1)S(1)}, u32[]{:S(2)}, u32[]{:S(2)}) collective-permute-start(bf16[2,192,128]{2,1,0:T(8,128)(2,1)S(1)} %pad_maximum_fusion.2), channel_id=1, source_target_pairs={{0,4},{4,8},{8,12},{12,0},{1,5},{5,9},{9,13},{13,1},{2,6},{6,10},{... | collective-permute-start | bytes 294920 | tf_op jit(solution)/shard_map/ppermute | solution.py:130
  68.4 7.8 %collective-permute-start.3 = (bf16[2,192,128]{2,1,0:T(8,128)(2,1)S(1)}, bf16[2,192,128]{2,1,0:T(8,128)(2,1)S(1)}, u32[]{:S(2)}, u32[]{:S(2)}) collective-permute-start(bf16[2,192,128]{2,1,0:T(8,128)(2,1)S(1)} %pad_maximum_fusion.2), channel_id=1, source_target_pairs={{0,8},{4,12},{8,0},{12,4},{1,9},{5,13},{9,1},{13,5},{2,10},{6,14},... | collective-permute-start | bytes 294920 | tf_op jit(solution)/shard_map/ppermute | solution.py:130
  70.7 6.9 %collective-permute-start.4 = (bf16[2,192,128]{2,1,0:T(8,128)(2,1)S(1)}, bf16[2,192,128]{2,1,0:T(8,128)(2,1)S(1)}, u32[]{:S(2)}, u32[]{:S(2)}) collective-permute-start(bf16[2,192,128]{2,1,0:T(8,128)(2,1)S(1)} %pad_maximum_fusion.2), channel_id=1, source_target_pairs={{0,12},{4,0},{8,4},{12,8},{1,13},{5,1},{9,5},{13,9},{2,14},{6,2},{... | collective-permute-start | bytes 294920 | tf_op jit(solution)/shard_map/ppermute | solution.py:130
  78.3 2.3 %copy-start.1 = (bf16[3072,768]{1,0:T(8,128)(2,1)S(1)}, bf16[3072,768]{1,0:T(8,128)(2,1)}, u32[]{:S(2)}) copy-start(bf16[3072,768]{1,0:T(8,128)(2,1)} %all-gather.3.cloned.1.call-done.weight_ref) | copy-start | bytes 14155780
  83.6 2.3 %copy-start.2 = (bf16[3072,768]{1,0:T(8,128)(2,1)S(1)}, bf16[3072,768]{1,0:T(8,128)(2,1)}, u32[]{:S(2)}) copy-start(bf16[3072,768]{1,0:T(8,128)(2,1)} %all-gather.3.cloned.1.call-done.weight_ref) | copy-start | bytes 14155780
  86.0 1.0 copy-start.4
  90.3 23.7 %all-to-all-start.2 = ((bf16[4,8,192,128]{3,2,1,0:T(8,128)(2,1)}), bf16[4,8,192,128]{3,2,1,0:T(8,128)(2,1)S(1)}, u32[]{:S(2)}, u32[]{:S(2)}) async-start(bf16[4,8,192,128]{3,2,1,0:T(8,128)(2,1)} %shard_map.68), calls=%async_computation.2 | async-start | bytes 3145728 | tf_op jit(solution)/shard_map/all_to_all | solution.py:152
  94.2 29.6 %collective-permute-start.9 = (bf16[8,192,128]{2,1,0:T(8,128)(2,1)}, bf16[8,192,128]{2,1,0:T(8,128)(2,1)}, u32[]{:S(2)}, u32[]{:S(2)}) collective-permute-start(bf16[8,192,128]{2,1,0:T(8,128)(2,1)} %constant_dynamic-update-slice_fusion), channel_id=1, source_target_pairs={{0,3},{1,0},{2,1},{3,2},{4,7},{5,4},{6,5},{7,6},{8,11},{9,8},{10,9... | collective-permute-start | bytes 1179656 | tf_op jit(solution)/shard_map/ppermute | solution.py:130
  98.8 25.0 %collective-permute-start.8 = (bf16[8,192,128]{2,1,0:T(8,128)(2,1)}, bf16[8,192,128]{2,1,0:T(8,128)(2,1)}, u32[]{:S(2)}, u32[]{:S(2)}) collective-permute-start(bf16[8,192,128]{2,1,0:T(8,128)(2,1)} %constant_dynamic-update-slice_fusion), channel_id=1, source_target_pairs={{0,2},{1,3},{2,0},{3,1},{4,6},{5,7},{6,4},{7,5},{8,10},{9,11},{10,... | collective-permute-start | bytes 1179656 | tf_op jit(solution)/shard_map/ppermute | solution.py:130
  101.3 30.4 %collective-permute-start.7 = (bf16[8,192,128]{2,1,0:T(8,128)(2,1)}, bf16[8,192,128]{2,1,0:T(8,128)(2,1)}, u32[]{:S(2)}, u32[]{:S(2)}) collective-permute-start(bf16[8,192,128]{2,1,0:T(8,128)(2,1)} %constant_dynamic-update-slice_fusion), channel_id=1, source_target_pairs={{0,1},{1,2},{2,3},{3,0},{4,5},{5,6},{6,7},{7,4},{8,9},{9,10},{10,1... | collective-permute-start | bytes 1179656 | tf_op jit(solution)/shard_map/ppermute | solution.py:130
  104.5 45.7 %collective-permute-start.5 = (bf16[128,768]{1,0:T(8,128)(2,1)S(1)}, bf16[128,768]{1,0:T(8,128)(2,1)}, u32[]{:S(2)}, u32[]{:S(2)}) collective-permute-start(bf16[128,768]{1,0:T(8,128)(2,1)S(1)} %constant_dynamic-slice_fusion.2), channel_id=1, source_target_pairs={{0,256},{256,0},{1,257},{257,1},{2,258},{258,2},{3,259},{259,3},{4... | collective-permute-start | bytes 589832 | tf_op jit(solution)/shard_map/ppermute | solution.py:143
  115.1 36.9 %all-to-all-start.3 = ((bf16[8,192,128]{2,1,0:T(8,128)(2,1)}), bf16[8,192,128]{2,1,0:T(8,128)(2,1)S(1)}, u32[]{:S(2)}, u32[]{:S(2)}) async-start(bf16[8,192,128]{2,1,0:T(8,128)(2,1)} %reduce_sum.24), calls=%async_computation.3 | async-start | bytes 786432 | tf_op jit(solution)/shard_map/all_to_all | solution.py:152
  140.1 2.8 %copy-start.3 = (bf16[4096,768]{1,0:T(8,128)(2,1)S(1)}, bf16[4096,768]{1,0:T(8,128)(2,1)}, u32[]{:S(2)}) copy-start(bf16[4096,768]{1,0:T(8,128)(2,1)} %all-gather.5.cloned.1.call-done.grad_ref) | copy-start | bytes 18874372
  144.9 21.0 %collective-permute-start.10 = (bf16[192,768]{1,0:T(8,128)(2,1)S(1)}, bf16[192,768]{1,0:T(8,128)(2,1)S(1)}, u32[]{:S(2)}, u32[]{:S(2)}) collective-permute-start(bf16[192,768]{1,0:T(8,128)(2,1)S(1)} %shard_map.69), channel_id=1, source_target_pairs={{0,256},{256,0},{1,257},{257,1},{2,258},{258,2},{3,259},{259,3},{4... | collective-permute-start | bytes 884744 | tf_op jit(solution)/shard_map/ppermute | solution.py:143
Sparse Core Ops, SparseCore 0:
  10.7 54.3 all-gather.2
  83.8 56.3 all-gather.4

commit v16 on v15

--- a/solution.py
+++ b/solution.py
@@ -171,12 +171,11 @@
     turned = lax.ppermute(features, ("row",) + COL, turns)
     depth_line = to_all(features, ("dp", "y"), 2 * SIDE)
     by_depth = to_all(depth_line, "x", SIDE)
-    token_line = from_line(after(turned, depth_line))
     out_grad = by_replica(
         half_of(out_grad, replica), to_replica(half_of(out_grad, 1 - replica)), 0
     )
 
-    hidden = hidden_sum(after(by_depth, token_line), weight)
+    hidden = hidden_sum(after(by_depth, turned), weight)
     normal_cdf = 0.5 * (1.0 + jax.scipy.special.erf(hidden / math.sqrt(2.0)))
     density = jnp.exp(-0.5 * hidden * hidden) / math.sqrt(2.0 * math.pi)
     gelu_half = (hidden * normal_cdf).astype(jnp.bfloat16)
@@ -185,7 +184,7 @@
     )
     grads = lax.all_gather(hidden_grad, "row", axis=0, tiled=True)
 
-    by_token = from_lines(after(token_line, hidden_grad))
+    by_token = from_lines(from_line(after(turned, hidden_grad)))
     pieces = input_grad_pieces(weight, hidden_grad)
     own = token_sum(places(), by_token, grads)
     feature_grad = sum_along(sum_along(pieces, "x"), ("dp", "y")).T

time: 175 us -> 169 us (0.966)
  the two profiles are of different devices: /device:TPU:17 before, /device:TPU:56 now
where the time goes in v16:
time: 169 us; the launch traced here: 168 us
  starting transfers between devices  74.4 us (44%)
  waiting for transfers between devices  28.4 us (17%)
  local copies, waits for them, and re-layouts  18.7 us (11%)
  blocking collectives  17.1 us (10%)
  between operations  14.3 us (8%)
  other arithmetic  7.39 us (4%)
  Pallas kernels  7.18 us (4%)
    ppermute x4, starting transfers between devices, to_replica(): return lax.ppermute(value, 'dp', [(0, 1), (1, 0)])  22.8 us
    ppermute x6, starting transfers between devices, shifted(): lax.ppermute(value, axis, [(i, (i + steps) % SIDE) for i in range(SIDE)])  21 us
    all_to_all x1, blocking collectives, to_all(): return lax.all_to_all(copies, axis, 0, 0, tiled=True)  17.1 us
    ppermute x1, starting transfers between devices, per_device(): turned = lax.ppermute(features, ('row',) + COL, turns)  13.8 us
    unnamed x20, local copies, waits for them, and re-layouts  13.1 us
    all_to_all x2, starting transfers between devices, sum_along(): pieces = lax.all_to_all(pieces, axis, 0, 0, tiled=True)  12.3 us
    ppermute x4, waiting for transfers between devices, to_replica(): return lax.ppermute(value, 'dp', [(0, 1), (1, 0)])  12.1 us
    pallas_call x3, Pallas kernels, local_kernel(): pl.pallas_call(kernel, out_shape=out_shape, in_specs=in_specs, out_specs=...  7.18 us
  transfers between devices with their start and end apart: 16, of which 6 were waited for; matrix products, arithmetic and copies ran while one was open for 8% of the time, Pallas kernels for 3%

profile of v16, /device:TPU:56, one launch (start us, length us, event | category | flops | bytes accessed | tf_op | source)
XLA Modules:
  0.0 167.5 jit_solution(14804862011504729154)
XLA Ops:
  9.8 17.1 %all_to_all.20 = bf16[8,192,128]{2,1,0:T(8,128)(2,1)S(1)} all-to-all(bf16[8,192,128]{2,1,0:T(8,128)(2,1)S(1)} %broadcast_in_dim.4), channel_id=1, replica_groups=mesh['dp'=2,'row'=16,'y'=4,'x'=4] {'dp','y'}, dimensions={0} | all-to-all | bytes 786432 | tf_op jit(solution)/shard_map/all_to_all | solution.py:148
  27.0 1.5 broadcast_in_dim.5
  28.5 4.6 %all-to-all-start.1 = ((bf16[4,8,192,128]{3,2,1,0:T(8,128)(2,1)}), bf16[4,8,192,128]{3,2,1,0:T(8,128)(2,1)S(1)}, u32[]{:S(2)}, u32[]{:S(2)}) async-start(bf16[4,8,192,128]{3,2,1,0:T(8,128)(2,1)} %broadcast_in_dim.5), calls=%async_computation.1 | async-start | bytes 3145728 | tf_op jit(solution)/shard_map/all_to_all | solution.py:148
  33.1 5.8 %collective-permute-start.2 = (bf16[128,768]{1,0:T(8,128)(2,1)S(1)}, bf16[128,768]{1,0:T(8,128)(2,1)S(1)}, u32[]{:S(2)}, u32[]{:S(2)}) collective-permute-start(bf16[128,768]{1,0:T(8,128)(2,1)S(1)} %constant_dynamic-slice_fusion.1), channel_id=1, source_target_pairs={{0,256},{256,0},{1,257},{257,1},{2,258},{258,2},{3,259},{259,3},{4... | collective-permute-start | bytes 589832 | tf_op jit(solution)/shard_map/ppermute | solution.py:143
  39.0 13.8 %collective-permute-start = (bf16[192,128]{1,0:T(8,128)(2,1)S(1)}, bf16[192,128]{1,0:T(8,128)(2,1)S(1)}, u32[]{:S(2)}, u32[]{:S(2)}) collective-permute-start(bf16[192,128]{1,0:T(8,128)(2,1)S(1)} %bitcast.13), channel_id=1, source_target_pairs={{0,0},{1,16},{2,32},{3,48},{4,64},{5,80},{6,96},{7,112},{8,128},{9... | collective-permute-start | bytes 147464 | tf_op jit(solution)/shard_map/ppermute | solution.py:171
  52.9 6.6 %collective-permute-done = bf16[192,128]{1,0:T(8,128)(2,1)S(1)} collective-permute-done((bf16[192,128]{1,0:T(8,128)(2,1)S(1)}, bf16[192,128]{1,0:T(8,128)(2,1)S(1)}, u32[]{:S(2)}, u32[]{:S(2)}) %collective-permute-start) | collective-permute-done | bytes 49184 | tf_op jit(solution)/shard_map/ppermute | solution.py:171
  59.5 4.2 %all-gather.3.cloned.1.call-done.weight_ref = bf16[3072,768]{1,0:T(8,128)(2,1)} async-done(((bf16[192,768]{1,0:T(8,128)(2,1)}), bf16[3072,768]{1,0:T(8,128)(2,1)}) %all-gather.3.cloned.1.call-update) | async-done | bytes 4718608 | tf_op jit(solution)/shard_map/all_gather | solution.py:169
  63.7 2.3 %copy-done.1 = bf16[3072,768]{1,0:T(8,128)(2,1)S(1)} copy-done((bf16[3072,768]{1,0:T(8,128)(2,1)S(1)}, bf16[3072,768]{1,0:T(8,128)(2,1)}, u32[]{:S(2)}) %copy-start.1) | copy-done | bytes 4718616
  66.0 1.8 %shard_map.67 = f32[256,768]{1,0:T(8,128)S(1)} custom-call(bf16[4,8,192,128]{3,2,1,0:T(8,128)(2,1)S(1)} %all-to-all-done.1.block_ref, bf16[3072,768]{1,0:T(8,128)(2,1)S(1)} %copy-done.1), custom_call_target="tpu_custom_call" | custom-call | flops 1207959552 | bytes 7077888 | tf_op jit(solution)/shard_map/pallas_call | solution.py:29
  67.9 1.1 fusion.5
  69.0 4.4 %collective-permute-start.3 = (bf16[192,128]{1,0:T(8,128)(2,1)S(1)}, bf16[192,128]{1,0:T(8,128)(2,1)S(1)}, u32[]{:S(2)}, u32[]{:S(2)}) collective-permute-start(bf16[192,128]{1,0:T(8,128)(2,1)S(1)} %collective-permute-done), channel_id=1, source_target_pairs={{0,256},{256,0},{1,257},{257,1},{2,258},{258,2},{3,259},{259,3},{4... | collective-permute-start | bytes 147464 | tf_op jit(solution)/shard_map/ppermute | solution.py:143
  74.1 2.3 %copy-done.2 = bf16[3072,768]{1,0:T(8,128)(2,1)S(1)} copy-done((bf16[3072,768]{1,0:T(8,128)(2,1)S(1)}, bf16[3072,768]{1,0:T(8,128)(2,1)}, u32[]{:S(2)}) %copy-start.2) | copy-done | bytes 4718616
  77.4 3.4 %shard_map.68 = bf16[4,8,192,128]{3,2,1,0:T(8,128)(2,1)} custom-call(bf16[3072,768]{1,0:T(8,128)(2,1)S(1)} %copy-done.2, bf16[256,768]{1,0:T(8,128)(2,1)S(1)} %copy-done.4), custom_call_target="tpu_custom_call" | custom-call | flops 1207959552 | bytes 6684672 | tf_op jit(solution)/shard_map/pallas_call | solution.py:29
  80.8 4.4 %all-to-all-start.2 = ((bf16[4,8,192,128]{3,2,1,0:T(8,128)(2,1)}), bf16[4,8,192,128]{3,2,1,0:T(8,128)(2,1)}, u32[]{:S(2)}, u32[]{:S(2)}) async-start(bf16[4,8,192,128]{3,2,1,0:T(8,128)(2,1)} %shard_map.68), calls=%async_computation.2 | async-start | bytes 3145728 | tf_op jit(solution)/shard_map/all_to_all | solution.py:152
  85.2 4.7 %collective-permute-start.4 = (bf16[2,192,128]{2,1,0:T(8,128)(2,1)S(1)}, bf16[2,192,128]{2,1,0:T(8,128)(2,1)S(1)}, u32[]{:S(2)}, u32[]{:S(2)}) collective-permute-start(bf16[2,192,128]{2,1,0:T(8,128)(2,1)S(1)} %pad_maximum_fusion.1), channel_id=1, source_target_pairs={{0,4},{4,8},{8,12},{12,0},{1,5},{5,9},{9,13},{13,1},{2,6},{6,10},{... | collective-permute-start | bytes 294920 | tf_op jit(solution)/shard_map/ppermute | solution.py:130
  89.9 1.9 %collective-permute-start.5 = (bf16[2,192,128]{2,1,0:T(8,128)(2,1)S(1)}, bf16[2,192,128]{2,1,0:T(8,128)(2,1)S(1)}, u32[]{:S(2)}, u32[]{:S(2)}) collective-permute-start(bf16[2,192,128]{2,1,0:T(8,128)(2,1)S(1)} %pad_maximum_fusion.1), channel_id=1, source_target_pairs={{0,8},{4,12},{8,0},{12,4},{1,9},{5,13},{9,1},{13,5},{2,10},{6,14},... | collective-permute-start | bytes 294920 | tf_op jit(solution)/shard_map/ppermute | solution.py:130
  91.9 2.5 %collective-permute-start.6 = (bf16[2,192,128]{2,1,0:T(8,128)(2,1)S(1)}, bf16[2,192,128]{2,1,0:T(8,128)(2,1)S(1)}, u32[]{:S(2)}, u32[]{:S(2)}) collective-permute-start(bf16[2,192,128]{2,1,0:T(8,128)(2,1)S(1)} %pad_maximum_fusion.1), channel_id=1, source_target_pairs={{0,12},{4,0},{8,4},{12,8},{1,13},{5,1},{9,5},{13,9},{2,14},{6,2},{... | collective-permute-start | bytes 294920 | tf_op jit(solution)/shard_map/ppermute | solution.py:130
  95.6 3.3 %collective-permute-done.5 = bf16[2,192,128]{2,1,0:T(8,128)(2,1)S(1)} collective-permute-done((bf16[2,192,128]{2,1,0:T(8,128)(2,1)S(1)}, bf16[2,192,128]{2,1,0:T(8,128)(2,1)S(1)}, u32[]{:S(2)}, u32[]{:S(2)}) %collective-permute-start.5) | collective-permute-done | bytes 98336 | tf_op jit(solution)/shard_map/ppermute | solution.py:130
  100.8 3.9 %collective-permute-start.7 = (bf16[8,192,128]{2,1,0:T(8,128)(2,1)}, bf16[8,192,128]{2,1,0:T(8,128)(2,1)}, u32[]{:S(2)}, u32[]{:S(2)}) collective-permute-start(bf16[8,192,128]{2,1,0:T(8,128)(2,1)} %get-tuple-element.15), channel_id=1, source_target_pairs={{0,1},{1,2},{2,3},{3,0},{4,5},{5,6},{6,7},{7,4},{8,9},{9,10},{10,1... | collective-permute-start | bytes 1179656 | tf_op jit(solution)/shard_map/ppermute | solution.py:130
  104.8 4.6 %collective-permute-start.8 = (bf16[8,192,128]{2,1,0:T(8,128)(2,1)}, bf16[8,192,128]{2,1,0:T(8,128)(2,1)S(1)}, u32[]{:S(2)}, u32[]{:S(2)}) collective-permute-start(bf16[8,192,128]{2,1,0:T(8,128)(2,1)} %get-tuple-element.15), channel_id=1, source_target_pairs={{0,2},{1,3},{2,0},{3,1},{4,6},{5,7},{6,4},{7,5},{8,10},{9,11},{10,... | collective-permute-start | bytes 1179656 | tf_op jit(solution)/shard_map/ppermute | solution.py:130
  109.4 3.4 %collective-permute-start.9 = (bf16[8,192,128]{2,1,0:T(8,128)(2,1)}, bf16[8,192,128]{2,1,0:T(8,128)(2,1)}, u32[]{:S(2)}, u32[]{:S(2)}) collective-permute-start(bf16[8,192,128]{2,1,0:T(8,128)(2,1)} %get-tuple-element.15), channel_id=1, source_target_pairs={{0,3},{1,0},{2,1},{3,2},{4,7},{5,4},{6,5},{7,6},{8,11},{9,8},{10,9... | collective-permute-start | bytes 1179656 | tf_op jit(solution)/shard_map/ppermute | solution.py:130
  113.5 7.4 %collective-permute-start.1 = (bf16[128,768]{1,0:T(8,128)(2,1)S(1)}, bf16[128,768]{1,0:T(8,128)(2,1)}, u32[]{:S(2)}, u32[]{:S(2)}) collective-permute-start(bf16[128,768]{1,0:T(8,128)(2,1)S(1)} %constant_dynamic-slice_fusion.2), channel_id=1, source_target_pairs={{0,256},{256,0},{1,257},{257,1},{2,258},{258,2},{3,259},{259,3},{4... | collective-permute-start | bytes 589832 | tf_op jit(solution)/shard_map/ppermute | solution.py:143
  120.9 1.0 constant_dynamic-update-slice_fusion.7
  121.9 1.6 collective-permute-done.8
  123.5 2.5 %reduce_sum.24 = bf16[8,192,128]{2,1,0:T(8,128)(2,1)} reduce(bf16[4,8,192,128]{3,2,1,0:T(8,128)(2,1)} %all-to-all-done.2, bf16[]{:T(256)} %constant.43.clone.1), dimensions={0}, to_apply=%region_0.1 | reduce | flops 589824 | bytes 1966082 | tf_op jit(solution)/shard_map/reduce_sum | solution.py:153
  126.1 7.9 %all-to-all-start.3 = ((bf16[8,192,128]{2,1,0:T(8,128)(2,1)}), bf16[8,192,128]{2,1,0:T(8,128)(2,1)S(1)}, u32[]{:S(2)}, u32[]{:S(2)}) async-start(bf16[8,192,128]{2,1,0:T(8,128)(2,1)} %reduce_sum.24), calls=%async_computation.3 | async-start | bytes 786432 | tf_op jit(solution)/shard_map/all_to_all | solution.py:152
  134.0 1.0 constant_dynamic-update-slice_fusion.5.block_ref
  135.0 2.8 %copy-done.3 = bf16[4096,768]{1,0:T(8,128)(2,1)S(1)} copy-done((bf16[4096,768]{1,0:T(8,128)(2,1)S(1)}, bf16[4096,768]{1,0:T(8,128)(2,1)}, u32[]{:S(2)}) %copy-start.3) | copy-done | bytes 6291480
  137.8 1.9 %shard_map.69 = bf16[192,768]{1,0:T(8,128)(2,1)S(1)} custom-call(s32[32]{0:T(128)S(1)} %fusion.6.place_ref, bf16[32,192,128]{2,1,0:T(8,128)(2,1)S(1)} %constant_dynamic-update-slice_fusion.5.block_ref, bf16[4096,768]{1,0:T(8,128)(2,1)S(1)} %copy-done.3), custom_call_target="tpu_custom_call" | custom-call | flops 1207959552 | bytes 8159232 | tf_op jit(solution)/shard_map/pallas_call | solution.py:29
  139.8 5.1 %collective-permute-start.10 = (bf16[192,768]{1,0:T(8,128)(2,1)S(1)}, bf16[192,768]{1,0:T(8,128)(2,1)S(1)}, u32[]{:S(2)}, u32[]{:S(2)}) collective-permute-start(bf16[192,768]{1,0:T(8,128)(2,1)S(1)} %shard_map.69), channel_id=1, source_target_pairs={{0,256},{256,0},{1,257},{257,1},{2,258},{258,2},{3,259},{259,3},{4... | collective-permute-start | bytes 884744 | tf_op jit(solution)/shard_map/ppermute | solution.py:143
  147.4 12.1 %collective-permute-done.10 = bf16[192,768]{1,0:T(8,128)(2,1)S(1)} collective-permute-done((bf16[192,768]{1,0:T(8,128)(2,1)S(1)}, bf16[192,768]{1,0:T(8,128)(2,1)S(1)}, u32[]{:S(2)}, u32[]{:S(2)}) %collective-permute-start.10) | collective-permute-done | bytes 294944 | tf_op jit(solution)/shard_map/ppermute | solution.py:143
  159.5 1.1 maximum_convert_fusion
  (43 shorter events, 10.9 us)
Async XLA Ops:
  7.2 1.1 copy-start
  7.2 56.5 %all-gather.3.cloned.1.call-start = ((), (), s32[]{:S(2)}) async-start(), calls=%async_computation.4 | async-start | bytes 5013504 | tf_op jit(solution)/shard_map/all_gather | solution.py:169
  28.5 4.6 %copy-start.5 = (bf16[128,1536]{1,0:T(8,128)(2,1)S(1)}, bf16[128,1536]{1,0:T(8,128)(2,1)}, u32[]{:S(2)}) copy-start(bf16[128,1536]{1,0:T(8,128)(2,1)} %param.6) | copy-start | bytes 1179652
  28.5 10.4 %copy-start.6 = (bf16[128,192]{0,1:T(8,128)(2,1)S(1)}, bf16[128,192]{0,1:T(8,128)(2,1)}, u32[]{:S(2)}) copy-start(bf16[128,192]{0,1:T(8,128)(2,1)} %param.4) | copy-start | bytes 147460
  28.5 31.0 %all-to-all-start.1 = ((bf16[4,8,192,128]{3,2,1,0:T(8,128)(2,1)}), bf16[4,8,192,128]{3,2,1,0:T(8,128)(2,1)S(1)}, u32[]{:S(2)}, u32[]{:S(2)}) async-start(bf16[4,8,192,128]{3,2,1,0:T(8,128)(2,1)} %broadcast_in_dim.5), calls=%async_computation.1 | async-start | bytes 3145728 | tf_op jit(solution)/shard_map/all_to_all | solution.py:148
  33.1 102.0 %all-gather.5.cloned.1.call-start = ((), (), s32[]{:S(2)}) async-start(), calls=%async_computation.5 | async-start | bytes 6684672 | tf_op jit(solution)/shard_map/all_gather | solution.py:185
  33.1 19.7 %collective-permute-start.2 = (bf16[128,768]{1,0:T(8,128)(2,1)S(1)}, bf16[128,768]{1,0:T(8,128)(2,1)S(1)}, u32[]{:S(2)}, u32[]{:S(2)}) collective-permute-start(bf16[128,768]{1,0:T(8,128)(2,1)S(1)} %constant_dynamic-slice_fusion.1), channel_id=1, source_target_pairs={{0,256},{256,0},{1,257},{257,1},{2,258},{258,2},{3,259},{259,3},{4... | collective-permute-start | bytes 589832 | tf_op jit(solution)/shard_map/ppermute | solution.py:143
  39.0 20.5 %collective-permute-start = (bf16[192,128]{1,0:T(8,128)(2,1)S(1)}, bf16[192,128]{1,0:T(8,128)(2,1)S(1)}, u32[]{:S(2)}, u32[]{:S(2)}) collective-permute-start(bf16[192,128]{1,0:T(8,128)(2,1)S(1)} %bitcast.13), channel_id=1, source_target_pairs={{0,0},{1,16},{2,32},{3,48},{4,64},{5,80},{6,96},{7,112},{8,128},{9... | collective-permute-start | bytes 147464 | tf_op jit(solution)/shard_map/ppermute | solution.py:171
  63.7 2.3 %copy-start.1 = (bf16[3072,768]{1,0:T(8,128)(2,1)S(1)}, bf16[3072,768]{1,0:T(8,128)(2,1)}, u32[]{:S(2)}) copy-start(bf16[3072,768]{1,0:T(8,128)(2,1)} %all-gather.3.cloned.1.call-done.weight_ref) | copy-start | bytes 14155780
  69.0 16.2 %collective-permute-start.3 = (bf16[192,128]{1,0:T(8,128)(2,1)S(1)}, bf16[192,128]{1,0:T(8,128)(2,1)S(1)}, u32[]{:S(2)}, u32[]{:S(2)}) collective-permute-start(bf16[192,128]{1,0:T(8,128)(2,1)S(1)} %collective-permute-done), channel_id=1, source_target_pairs={{0,256},{256,0},{1,257},{257,1},{2,258},{258,2},{3,259},{259,3},{4... | collective-permute-start | bytes 147464 | tf_op jit(solution)/shard_map/ppermute | solution.py:143
  74.1 2.3 %copy-start.2 = (bf16[3072,768]{1,0:T(8,128)(2,1)S(1)}, bf16[3072,768]{1,0:T(8,128)(2,1)}, u32[]{:S(2)}) copy-start(bf16[3072,768]{1,0:T(8,128)(2,1)} %all-gather.3.cloned.1.call-done.weight_ref) | copy-start | bytes 14155780
  76.4 1.0 copy-start.4
  80.8 42.7 %all-to-all-start.2 = ((bf16[4,8,192,128]{3,2,1,0:T(8,128)(2,1)}), bf16[4,8,192,128]{3,2,1,0:T(8,128)(2,1)}, u32[]{:S(2)}, u32[]{:S(2)}) async-start(bf16[4,8,192,128]{3,2,1,0:T(8,128)(2,1)} %shard_map.68), calls=%async_computation.2 | async-start | bytes 3145728 | tf_op jit(solution)/shard_map/all_to_all | solution.py:152
  85.2 9.8 %collective-permute-start.4 = (bf16[2,192,128]{2,1,0:T(8,128)(2,1)S(1)}, bf16[2,192,128]{2,1,0:T(8,128)(2,1)S(1)}, u32[]{:S(2)}, u32[]{:S(2)}) collective-permute-start(bf16[2,192,128]{2,1,0:T(8,128)(2,1)S(1)} %pad_maximum_fusion.1), channel_id=1, source_target_pairs={{0,4},{4,8},{8,12},{12,0},{1,5},{5,9},{9,13},{13,1},{2,6},{6,10},{... | collective-permute-start | bytes 294920 | tf_op jit(solution)/shard_map/ppermute | solution.py:130
  89.9 9.0 %collective-permute-start.5 = (bf16[2,192,128]{2,1,0:T(8,128)(2,1)S(1)}, bf16[2,192,128]{2,1,0:T(8,128)(2,1)S(1)}, u32[]{:S(2)}, u32[]{:S(2)}) collective-permute-start(bf16[2,192,128]{2,1,0:T(8,128)(2,1)S(1)} %pad_maximum_fusion.1), channel_id=1, source_target_pairs={{0,8},{4,12},{8,0},{12,4},{1,9},{5,13},{9,1},{13,5},{2,10},{6,14},... | collective-permute-start | bytes 294920 | tf_op jit(solution)/shard_map/ppermute | solution.py:130
  91.9 8.3 %collective-permute-start.6 = (bf16[2,192,128]{2,1,0:T(8,128)(2,1)S(1)}, bf16[2,192,128]{2,1,0:T(8,128)(2,1)S(1)}, u32[]{:S(2)}, u32[]{:S(2)}) collective-permute-start(bf16[2,192,128]{2,1,0:T(8,128)(2,1)S(1)} %pad_maximum_fusion.1), channel_id=1, source_target_pairs={{0,12},{4,0},{8,4},{12,8},{1,13},{5,1},{9,5},{13,9},{2,14},{6,2},{... | collective-permute-start | bytes 294920 | tf_op jit(solution)/shard_map/ppermute | solution.py:130
  100.8 20.0 %collective-permute-start.7 = (bf16[8,192,128]{2,1,0:T(8,128)(2,1)}, bf16[8,192,128]{2,1,0:T(8,128)(2,1)}, u32[]{:S(2)}, u32[]{:S(2)}) collective-permute-start(bf16[8,192,128]{2,1,0:T(8,128)(2,1)} %get-tuple-element.15), channel_id=1, source_target_pairs={{0,1},{1,2},{2,3},{3,0},{4,5},{5,6},{6,7},{7,4},{8,9},{9,10},{10,1... | collective-permute-start | bytes 1179656 | tf_op jit(solution)/shard_map/ppermute | solution.py:130
  104.8 18.7 %collective-permute-start.8 = (bf16[8,192,128]{2,1,0:T(8,128)(2,1)}, bf16[8,192,128]{2,1,0:T(8,128)(2,1)S(1)}, u32[]{:S(2)}, u32[]{:S(2)}) collective-permute-start(bf16[8,192,128]{2,1,0:T(8,128)(2,1)} %get-tuple-element.15), channel_id=1, source_target_pairs={{0,2},{1,3},{2,0},{3,1},{4,6},{5,7},{6,4},{7,5},{8,10},{9,11},{10,... | collective-permute-start | bytes 1179656 | tf_op jit(solution)/shard_map/ppermute | solution.py:130
  109.4 24.6 %collective-permute-start.9 = (bf16[8,192,128]{2,1,0:T(8,128)(2,1)}, bf16[8,192,128]{2,1,0:T(8,128)(2,1)}, u32[]{:S(2)}, u32[]{:S(2)}) collective-permute-start(bf16[8,192,128]{2,1,0:T(8,128)(2,1)} %get-tuple-element.15), channel_id=1, source_target_pairs={{0,3},{1,0},{2,1},{3,2},{4,7},{5,4},{6,5},{7,6},{8,11},{9,8},{10,9... | collective-permute-start | bytes 1179656 | tf_op jit(solution)/shard_map/ppermute | solution.py:130
  113.5 31.4 %collective-permute-start.1 = (bf16[128,768]{1,0:T(8,128)(2,1)S(1)}, bf16[128,768]{1,0:T(8,128)(2,1)}, u32[]{:S(2)}, u32[]{:S(2)}) collective-permute-start(bf16[128,768]{1,0:T(8,128)(2,1)S(1)} %constant_dynamic-slice_fusion.2), channel_id=1, source_target_pairs={{0,256},{256,0},{1,257},{257,1},{2,258},{258,2},{3,259},{259,3},{4... | collective-permute-start | bytes 589832 | tf_op jit(solution)/shard_map/ppermute | solution.py:143
  126.1 20.6 %all-to-all-start.3 = ((bf16[8,192,128]{2,1,0:T(8,128)(2,1)}), bf16[8,192,128]{2,1,0:T(8,128)(2,1)S(1)}, u32[]{:S(2)}, u32[]{:S(2)}) async-start(bf16[8,192,128]{2,1,0:T(8,128)(2,1)} %reduce_sum.24), calls=%async_computation.3 | async-start | bytes 786432 | tf_op jit(solution)/shard_map/all_to_all | solution.py:152
  135.0 2.8 %copy-start.3 = (bf16[4096,768]{1,0:T(8,128)(2,1)S(1)}, bf16[4096,768]{1,0:T(8,128)(2,1)}, u32[]{:S(2)}) copy-start(bf16[4096,768]{1,0:T(8,128)(2,1)} %all-gather.5.cloned.1.call-done.grad_ref) | copy-start | bytes 18874372
  139.8 19.7 %collective-permute-start.10 = (bf16[192,768]{1,0:T(8,128)(2,1)S(1)}, bf16[192,768]{1,0:T(8,128)(2,1)S(1)}, u32[]{:S(2)}, u32[]{:S(2)}) collective-permute-start(bf16[192,768]{1,0:T(8,128)(2,1)S(1)} %shard_map.69), channel_id=1, source_target_pairs={{0,256},{256,0},{1,257},{257,1},{2,258},{258,2},{3,259},{259,3},{4... | collective-permute-start | bytes 884744 | tf_op jit(solution)/shard_map/ppermute | solution.py:143
Sparse Core Ops, SparseCore 0:
  10.7 52.9 all-gather.2
  69.2 48.6 all-gather.4

commit v17 on v16

--- a/solution.py
+++ b/solution.py
@@ -130,9 +130,18 @@
     return lax.ppermute(value, axis, [(i, (i + steps) % SIDE) for i in range(SIDE)])
 
 
-def from_line(block):
-    pair = jnp.stack([block, to_replica(block)])
+def from_line(pair):
     return jnp.concatenate([pair] + [shifted(pair, "y", d) for d in range(1, SIDE)])
+
+
+def turn_moves(other):
+    moves = []
+    for d in range(2):
+        for r in range(ROWS):
+            for c in range(COLS):
+                source, target = ((d * ROWS + r) * COLS + c, ((d ^ other) * ROWS + c) * COLS + r)
+                moves.append((source, target))
+    return moves
 
 
 def from_lines(line):
@@ -167,8 +176,8 @@
         return jnp.concatenate(parts, axis=axis)
 
     weight = lax.all_gather(half_of(up_weight, replica), "row", axis=0, tiled=True)
-    turns = [(r * COLS + c, c * COLS + r) for r in range(ROWS) for c in range(COLS)]
-    turned = lax.ppermute(features, ("row",) + COL, turns)
+    turned = [lax.ppermute(features, ("dp", "row") + COL, turn_moves(other)) for other in (0, 1)]
+    turned = jnp.stack(turned)
     depth_line = to_all(features, ("dp", "y"), 2 * SIDE)
     by_depth = to_all(depth_line, "x", SIDE)
     out_grad = by_replica(

time: 169 us -> 170 us (level)
  waiting for transfers between devices: 28.4 us -> 35.2 us
  starting transfers between devices: 74.4 us -> 68.8 us
    ppermute x4 -> x3, starting transfers between devices: 22.8 us -> 13.7 us  [to_replica(): return lax.ppermute(value, 'dp', [(0, 1), (1, 0)])]
    ppermute x6, waiting for transfers between devices: 5.47 us -> 10.6 us  [shifted(): lax.ppermute(value, axis, [(i, (i + steps) % SIDE) for i in range(SIDE)])]
    ppermute x6, starting transfers between devices: 21 us -> 23.2 us  [shifted(): lax.ppermute(value, axis, [(i, (i + steps) % SIDE) for i in range(SIDE)])]
    ppermute x1 -> x2, starting transfers between devices: 13.8 us -> 15.7 us  [per_device(): lax.ppermute(features, ('dp', 'row') + COL, turn_moves(other))]
    ppermute x1 -> x2, waiting for transfers between devices: 6.62 us -> 7.66 us  [per_device(): lax.ppermute(features, ('dp', 'row') + COL, turn_moves(other))]
    unnamed x20 -> x19, local copies, waits for them, and re-layouts: 13.1 us -> 12.6 us
    ppermute x4 -> x3, waiting for transfers between devices: 12.1 us -> 12.3 us  [to_replica(): return lax.ppermute(value, 'dp', [(0, 1), (1, 0)])]
  transfers between devices with their start and end apart: 16 -> 16, of which waited for: 6 -> 7; matrix products, arithmetic and copies ran while one was open for 8% -> 8% of each run, Pallas kernels for 3% -> 3%
where the time goes in v17:
time: 170 us; the launch traced here: 168 us
  starting transfers between devices  68.8 us (40%)
  waiting for transfers between devices  35.2 us (21%)
  local copies, waits for them, and re-layouts  18.2 us (11%)
  blocking collectives  17.1 us (10%)
  between operations  14.3 us (8%)
  other arithmetic  7.39 us (4%)
  Pallas kernels  7.17 us (4%)
    ppermute x6, starting transfers between devices, shifted(): lax.ppermute(value, axis, [(i, (i + steps) % SIDE) for i in range(SIDE)])  23.2 us
    all_to_all x1, blocking collectives, to_all(): return lax.all_to_all(copies, axis, 0, 0, tiled=True)  17.1 us
    ppermute x2, starting transfers between devices, per_device(): lax.ppermute(features, ('dp', 'row') + COL, turn_moves(other))  15.7 us
    ppermute x3, starting transfers between devices, to_replica(): return lax.ppermute(value, 'dp', [(0, 1), (1, 0)])  13.7 us
    unnamed x19, local copies, waits for them, and re-layouts  12.6 us
    ppermute x3, waiting for transfers between devices, to_replica(): return lax.ppermute(value, 'dp', [(0, 1), (1, 0)])  12.3 us
    all_to_all x2, starting transfers between devices, sum_along(): pieces = lax.all_to_all(pieces, axis, 0, 0, tiled=True)  11.6 us
    ppermute x6, waiting for transfers between devices, shifted(): lax.ppermute(value, axis, [(i, (i + steps) % SIDE) for i in range(SIDE)])  10.6 us
  transfers between devices with their start and end apart: 16, of which 7 were waited for; matrix products, arithmetic and copies ran while one was open for 8% of the time, Pallas kernels for 3%

profile of v17, /device:TPU:56, one launch (start us, length us, event | category | flops | bytes accessed | tf_op | source)
XLA Modules:
  0.0 168.1 jit_solution(8528308917140528483)
XLA Ops:
  9.8 17.1 %all_to_all.20 = bf16[8,192,128]{2,1,0:T(8,128)(2,1)S(1)} all-to-all(bf16[8,192,128]{2,1,0:T(8,128)(2,1)S(1)} %broadcast_in_dim.4), channel_id=1, replica_groups=mesh['dp'=2,'row'=16,'y'=4,'x'=4] {'dp','y'}, dimensions={0} | all-to-all | bytes 786432 | tf_op jit(solution)/shard_map/all_to_all | solution.py:157
  27.0 1.5 broadcast_in_dim.5
  28.5 4.6 %all-to-all-start.1 = ((bf16[4,8,192,128]{3,2,1,0:T(8,128)(2,1)}), bf16[4,8,192,128]{3,2,1,0:T(8,128)(2,1)S(1)}, u32[]{:S(2)}, u32[]{:S(2)}) async-start(bf16[4,8,192,128]{3,2,1,0:T(8,128)(2,1)} %broadcast_in_dim.5), calls=%async_computation.1 | async-start | bytes 3145728 | tf_op jit(solution)/shard_map/all_to_all | solution.py:157
  33.1 5.8 %collective-permute-start.3 = (bf16[128,768]{1,0:T(8,128)(2,1)S(1)}, bf16[128,768]{1,0:T(8,128)(2,1)S(1)}, u32[]{:S(2)}, u32[]{:S(2)}) collective-permute-start(bf16[128,768]{1,0:T(8,128)(2,1)S(1)} %constant_dynamic-slice_fusion.1), channel_id=1, source_target_pairs={{0,256},{256,0},{1,257},{257,1},{2,258},{258,2},{3,259},{259,3},{4... | collective-permute-start | bytes 589832 | tf_op jit(solution)/shard_map/ppermute | solution.py:152
  39.0 11.1 %collective-permute-start.1 = (bf16[192,128]{1,0:T(8,128)(2,1)S(1)}, bf16[192,128]{1,0:T(8,128)(2,1)S(1)}, u32[]{:S(2)}, u32[]{:S(2)}) collective-permute-start(bf16[192,128]{1,0:T(8,128)(2,1)S(1)} %bitcast.7), channel_id=1, source_target_pairs={{0,256},{1,272},{2,288},{3,304},{4,320},{5,336},{6,352},{7,368},{8... | collective-permute-start | bytes 147464 | tf_op jit(solution)/shard_map/ppermute | solution.py:179
  50.1 4.6 %collective-permute-start = (bf16[192,128]{1,0:T(8,128)(2,1)S(1)}, bf16[192,128]{1,0:T(8,128)(2,1)S(1)}, u32[]{:S(2)}, u32[]{:S(2)}) collective-permute-start(bf16[192,128]{1,0:T(8,128)(2,1)S(1)} %bitcast.8), channel_id=1, source_target_pairs={{0,0},{1,16},{2,32},{3,48},{4,64},{5,80},{6,96},{7,112},{8,128},{9... | collective-permute-start | bytes 147464 | tf_op jit(solution)/shard_map/ppermute | solution.py:179
  54.7 6.2 %collective-permute-done.1 = bf16[192,128]{1,0:T(8,128)(2,1)S(1)} collective-permute-done((bf16[192,128]{1,0:T(8,128)(2,1)S(1)}, bf16[192,128]{1,0:T(8,128)(2,1)S(1)}, u32[]{:S(2)}, u32[]{:S(2)}) %collective-permute-start.1) | collective-permute-done | bytes 49184 | tf_op jit(solution)/shard_map/ppermute | solution.py:179
  60.9 1.5 collective-permute-done
  62.5 4.5 %all-gather.3.cloned.1.call-done.weight_ref = bf16[3072,768]{1,0:T(8,128)(2,1)} async-done(((bf16[192,768]{1,0:T(8,128)(2,1)}), bf16[3072,768]{1,0:T(8,128)(2,1)}) %all-gather.3.cloned.1.call-update) | async-done | bytes 4718608 | tf_op jit(solution)/shard_map/all_gather | solution.py:178
  67.0 2.3 %copy-done.1 = bf16[3072,768]{1,0:T(8,128)(2,1)S(1)} copy-done((bf16[3072,768]{1,0:T(8,128)(2,1)S(1)}, bf16[3072,768]{1,0:T(8,128)(2,1)}, u32[]{:S(2)}) %copy-start.1) | copy-done | bytes 4718616
  69.4 1.8 %shard_map.67 = f32[256,768]{1,0:T(8,128)S(1)} custom-call(bf16[4,8,192,128]{3,2,1,0:T(8,128)(2,1)S(1)} %all-to-all-done.1.block_ref, bf16[3072,768]{1,0:T(8,128)(2,1)S(1)} %copy-done.1), custom_call_target="tpu_custom_call" | custom-call | flops 1207959552 | bytes 7077888 | tf_op jit(solution)/shard_map/pallas_call | solution.py:29
  71.2 1.1 fusion.5
  72.4 2.3 %copy-done.2 = bf16[3072,768]{1,0:T(8,128)(2,1)S(1)} copy-done((bf16[3072,768]{1,0:T(8,128)(2,1)S(1)}, bf16[3072,768]{1,0:T(8,128)(2,1)}, u32[]{:S(2)}) %copy-start.2) | copy-done | bytes 4718616
  75.7 3.4 %shard_map.68 = bf16[4,8,192,128]{3,2,1,0:T(8,128)(2,1)} custom-call(bf16[3072,768]{1,0:T(8,128)(2,1)S(1)} %copy-done.2, bf16[256,768]{1,0:T(8,128)(2,1)S(1)} %copy-done.4), custom_call_target="tpu_custom_call" | custom-call | flops 1207959552 | bytes 6684672 | tf_op jit(solution)/shard_map/pallas_call | solution.py:29
  79.1 4.4 %all-to-all-start.2 = ((bf16[4,8,192,128]{3,2,1,0:T(8,128)(2,1)}), bf16[4,8,192,128]{3,2,1,0:T(8,128)(2,1)}, u32[]{:S(2)}, u32[]{:S(2)}) async-start(bf16[4,8,192,128]{3,2,1,0:T(8,128)(2,1)} %shard_map.68), calls=%async_computation.2 | async-start | bytes 3145728 | tf_op jit(solution)/shard_map/all_to_all | solution.py:161
  83.5 6.7 %collective-permute-start.4 = (bf16[2,192,128]{2,1,0:T(8,128)(2,1)S(1)}, bf16[2,192,128]{2,1,0:T(8,128)(2,1)S(1)}, u32[]{:S(2)}, u32[]{:S(2)}) collective-permute-start(bf16[2,192,128]{2,1,0:T(8,128)(2,1)S(1)} %pad_maximum_fusion.1), channel_id=1, source_target_pairs={{0,4},{4,8},{8,12},{12,0},{1,5},{5,9},{9,13},{13,1},{2,6},{6,10},{... | collective-permute-start | bytes 294920 | tf_op jit(solution)/shard_map/ppermute | solution.py:130
  90.2 1.9 %collective-permute-start.5 = (bf16[2,192,128]{2,1,0:T(8,128)(2,1)S(1)}, bf16[2,192,128]{2,1,0:T(8,128)(2,1)S(1)}, u32[]{:S(2)}, u32[]{:S(2)}) collective-permute-start(bf16[2,192,128]{2,1,0:T(8,128)(2,1)S(1)} %pad_maximum_fusion.1), channel_id=1, source_target_pairs={{0,8},{4,12},{8,0},{12,4},{1,9},{5,13},{9,1},{13,5},{2,10},{6,14},... | collective-permute-start | bytes 294920 | tf_op jit(solution)/shard_map/ppermute | solution.py:130
  92.2 2.6 %collective-permute-start.6 = (bf16[2,192,128]{2,1,0:T(8,128)(2,1)S(1)}, bf16[2,192,128]{2,1,0:T(8,128)(2,1)S(1)}, u32[]{:S(2)}, u32[]{:S(2)}) collective-permute-start(bf16[2,192,128]{2,1,0:T(8,128)(2,1)S(1)} %pad_maximum_fusion.1), channel_id=1, source_target_pairs={{0,12},{4,0},{8,4},{12,8},{1,13},{5,1},{9,5},{13,9},{2,14},{6,2},{... | collective-permute-start | bytes 294920 | tf_op jit(solution)/shard_map/ppermute | solution.py:130
  96.1 1.5 collective-permute-done.5
  98.3 2.2 %collective-permute-done.6 = bf16[2,192,128]{2,1,0:T(8,128)(2,1)S(1)} collective-permute-done((bf16[2,192,128]{2,1,0:T(8,128)(2,1)S(1)}, bf16[2,192,128]{2,1,0:T(8,128)(2,1)S(1)}, u32[]{:S(2)}, u32[]{:S(2)}) %collective-permute-start.6) | collective-permute-done | bytes 98336 | tf_op jit(solution)/shard_map/ppermute | solution.py:130
  101.1 3.9 %collective-permute-start.7 = (bf16[8,192,128]{2,1,0:T(8,128)(2,1)}, bf16[8,192,128]{2,1,0:T(8,128)(2,1)}, u32[]{:S(2)}, u32[]{:S(2)}) collective-permute-start(bf16[8,192,128]{2,1,0:T(8,128)(2,1)} %get-tuple-element.15), channel_id=1, source_target_pairs={{0,1},{1,2},{2,3},{3,0},{4,5},{5,6},{6,7},{7,4},{8,9},{9,10},{10,1... | collective-permute-start | bytes 1179656 | tf_op jit(solution)/shard_map/ppermute | solution.py:130
  105.1 4.6 %collective-permute-start.8 = (bf16[8,192,128]{2,1,0:T(8,128)(2,1)}, bf16[8,192,128]{2,1,0:T(8,128)(2,1)S(1)}, u32[]{:S(2)}, u32[]{:S(2)}) collective-permute-start(bf16[8,192,128]{2,1,0:T(8,128)(2,1)} %get-tuple-element.15), channel_id=1, source_target_pairs={{0,2},{1,3},{2,0},{3,1},{4,6},{5,7},{6,4},{7,5},{8,10},{9,11},{10,... | collective-permute-start | bytes 1179656 | tf_op jit(solution)/shard_map/ppermute | solution.py:130
  109.7 3.4 %collective-permute-start.9 = (bf16[8,192,128]{2,1,0:T(8,128)(2,1)}, bf16[8,192,128]{2,1,0:T(8,128)(2,1)}, u32[]{:S(2)}, u32[]{:S(2)}) collective-permute-start(bf16[8,192,128]{2,1,0:T(8,128)(2,1)} %get-tuple-element.15), channel_id=1, source_target_pairs={{0,3},{1,0},{2,1},{3,2},{4,7},{5,4},{6,5},{7,6},{8,11},{9,8},{10,9... | collective-permute-start | bytes 1179656 | tf_op jit(solution)/shard_map/ppermute | solution.py:130
  113.8 2.7 %collective-permute-start.2 = (bf16[128,768]{1,0:T(8,128)(2,1)S(1)}, bf16[128,768]{1,0:T(8,128)(2,1)}, u32[]{:S(2)}, u32[]{:S(2)}) collective-permute-start(bf16[128,768]{1,0:T(8,128)(2,1)S(1)} %constant_dynamic-slice_fusion.2), channel_id=1, source_target_pairs={{0,256},{256,0},{1,257},{257,1},{2,258},{258,2},{3,259},{259,3},{4... | collective-permute-start | bytes 589832 | tf_op jit(solution)/shard_map/ppermute | solution.py:152
  117.5 6.9 %collective-permute-done.8 = bf16[8,192,128]{2,1,0:T(8,128)(2,1)S(1)} collective-permute-done((bf16[8,192,128]{2,1,0:T(8,128)(2,1)}, bf16[8,192,128]{2,1,0:T(8,128)(2,1)S(1)}, u32[]{:S(2)}, u32[]{:S(2)}) %collective-permute-start.8) | collective-permute-done | bytes 393248 | tf_op jit(solution)/shard_map/ppermute | solution.py:130
  124.5 2.5 %reduce_sum.24 = bf16[8,192,128]{2,1,0:T(8,128)(2,1)} reduce(bf16[4,8,192,128]{3,2,1,0:T(8,128)(2,1)} %all-to-all-done.2, bf16[]{:T(256)} %constant.43.clone.1), dimensions={0}, to_apply=%region_0.1 | reduce | flops 589824 | bytes 1966082 | tf_op jit(solution)/shard_map/reduce_sum | solution.py:162
  127.0 7.3 %all-to-all-start.3 = ((bf16[8,192,128]{2,1,0:T(8,128)(2,1)}), bf16[8,192,128]{2,1,0:T(8,128)(2,1)S(1)}, u32[]{:S(2)}, u32[]{:S(2)}) async-start(bf16[8,192,128]{2,1,0:T(8,128)(2,1)} %reduce_sum.24), calls=%async_computation.3 | async-start | bytes 786432 | tf_op jit(solution)/shard_map/all_to_all | solution.py:161
  135.4 2.8 %copy-done.3 = bf16[4096,768]{1,0:T(8,128)(2,1)S(1)} copy-done((bf16[4096,768]{1,0:T(8,128)(2,1)S(1)}, bf16[4096,768]{1,0:T(8,128)(2,1)}, u32[]{:S(2)}) %copy-start.3) | copy-done | bytes 6291480
  138.2 1.9 %shard_map.69 = bf16[192,768]{1,0:T(8,128)(2,1)S(1)} custom-call(s32[32]{0:T(128)S(1)} %fusion.6.place_ref, bf16[32,192,128]{2,1,0:T(8,128)(2,1)S(1)} %constant_dynamic-update-slice_fusion.4.block_ref, bf16[4096,768]{1,0:T(8,128)(2,1)S(1)} %copy-done.3), custom_call_target="tpu_custom_call" | custom-call | flops 1207959552 | bytes 8159232 | tf_op jit(solution)/shard_map/pallas_call | solution.py:29
  140.1 5.2 %collective-permute-start.10 = (bf16[192,768]{1,0:T(8,128)(2,1)S(1)}, bf16[192,768]{1,0:T(8,128)(2,1)S(1)}, u32[]{:S(2)}, u32[]{:S(2)}) collective-permute-start(bf16[192,768]{1,0:T(8,128)(2,1)S(1)} %shard_map.69), channel_id=1, source_target_pairs={{0,256},{256,0},{1,257},{257,1},{2,258},{258,2},{3,259},{259,3},{4... | collective-permute-start | bytes 884744 | tf_op jit(solution)/shard_map/ppermute | solution.py:152
  147.8 12.3 %collective-permute-done.10 = bf16[192,768]{1,0:T(8,128)(2,1)S(1)} collective-permute-done((bf16[192,768]{1,0:T(8,128)(2,1)S(1)}, bf16[192,768]{1,0:T(8,128)(2,1)S(1)}, u32[]{:S(2)}, u32[]{:S(2)}) %collective-permute-start.10) | collective-permute-done | bytes 294944 | tf_op jit(solution)/shard_map/ppermute | solution.py:152
  160.1 1.1 maximum_convert_fusion
  (42 shorter events, 11.9 us)
Async XLA Ops:
  7.2 1.1 copy-start
  7.2 59.9 %all-gather.3.cloned.1.call-start = ((), (), s32[]{:S(2)}) async-start(), calls=%async_computation.4 | async-start | bytes 5013504 | tf_op jit(solution)/shard_map/all_gather | solution.py:178
  28.5 4.6 %copy-start.5 = (bf16[128,1536]{1,0:T(8,128)(2,1)S(1)}, bf16[128,1536]{1,0:T(8,128)(2,1)}, u32[]{:S(2)}) copy-start(bf16[128,1536]{1,0:T(8,128)(2,1)} %param.6) | copy-start | bytes 1179652
  28.5 10.4 %copy-start.6 = (bf16[128,192]{0,1:T(8,128)(2,1)S(1)}, bf16[128,192]{0,1:T(8,128)(2,1)}, u32[]{:S(2)}) copy-start(bf16[128,192]{0,1:T(8,128)(2,1)} %param.4) | copy-start | bytes 147460
  28.5 34.0 %all-to-all-start.1 = ((bf16[4,8,192,128]{3,2,1,0:T(8,128)(2,1)}), bf16[4,8,192,128]{3,2,1,0:T(8,128)(2,1)S(1)}, u32[]{:S(2)}, u32[]{:S(2)}) async-start(bf16[4,8,192,128]{3,2,1,0:T(8,128)(2,1)} %broadcast_in_dim.5), calls=%async_computation.1 | async-start | bytes 3145728 | tf_op jit(solution)/shard_map/all_to_all | solution.py:157
  33.1 102.3 %all-gather.5.cloned.1.call-start = ((), (), s32[]{:S(2)}) async-start(), calls=%async_computation.5 | async-start | bytes 6684672 | tf_op jit(solution)/shard_map/all_gather | solution.py:194
  33.1 29.3 %collective-permute-start.3 = (bf16[128,768]{1,0:T(8,128)(2,1)S(1)}, bf16[128,768]{1,0:T(8,128)(2,1)S(1)}, u32[]{:S(2)}, u32[]{:S(2)}) collective-permute-start(bf16[128,768]{1,0:T(8,128)(2,1)S(1)} %constant_dynamic-slice_fusion.1), channel_id=1, source_target_pairs={{0,256},{256,0},{1,257},{257,1},{2,258},{258,2},{3,259},{259,3},{4... | collective-permute-start | bytes 589832 | tf_op jit(solution)/shard_map/ppermute | solution.py:152
  39.0 21.9 %collective-permute-start.1 = (bf16[192,128]{1,0:T(8,128)(2,1)S(1)}, bf16[192,128]{1,0:T(8,128)(2,1)S(1)}, u32[]{:S(2)}, u32[]{:S(2)}) collective-permute-start(bf16[192,128]{1,0:T(8,128)(2,1)S(1)} %bitcast.7), channel_id=1, source_target_pairs={{0,256},{1,272},{2,288},{3,304},{4,320},{5,336},{6,352},{7,368},{8... | collective-permute-start | bytes 147464 | tf_op jit(solution)/shard_map/ppermute | solution.py:179
  50.1 12.3 %collective-permute-start = (bf16[192,128]{1,0:T(8,128)(2,1)S(1)}, bf16[192,128]{1,0:T(8,128)(2,1)S(1)}, u32[]{:S(2)}, u32[]{:S(2)}) collective-permute-start(bf16[192,128]{1,0:T(8,128)(2,1)S(1)} %bitcast.8), channel_id=1, source_target_pairs={{0,0},{1,16},{2,32},{3,48},{4,64},{5,80},{6,96},{7,112},{8,128},{9... | collective-permute-start | bytes 147464 | tf_op jit(solution)/shard_map/ppermute | solution.py:179
  67.0 2.3 %copy-start.1 = (bf16[3072,768]{1,0:T(8,128)(2,1)S(1)}, bf16[3072,768]{1,0:T(8,128)(2,1)}, u32[]{:S(2)}) copy-start(bf16[3072,768]{1,0:T(8,128)(2,1)} %all-gather.3.cloned.1.call-done.weight_ref) | copy-start | bytes 14155780
  72.4 2.3 %copy-start.2 = (bf16[3072,768]{1,0:T(8,128)(2,1)S(1)}, bf16[3072,768]{1,0:T(8,128)(2,1)}, u32[]{:S(2)}) copy-start(bf16[3072,768]{1,0:T(8,128)(2,1)} %all-gather.3.cloned.1.call-done.weight_ref) | copy-start | bytes 14155780
  74.7 1.0 copy-start.4
  79.1 45.4 %all-to-all-start.2 = ((bf16[4,8,192,128]{3,2,1,0:T(8,128)(2,1)}), bf16[4,8,192,128]{3,2,1,0:T(8,128)(2,1)}, u32[]{:S(2)}, u32[]{:S(2)}) async-start(bf16[4,8,192,128]{3,2,1,0:T(8,128)(2,1)} %shard_map.68), calls=%async_computation.2 | async-start | bytes 3145728 | tf_op jit(solution)/shard_map/all_to_all | solution.py:161
  83.5 12.0 %collective-permute-start.4 = (bf16[2,192,128]{2,1,0:T(8,128)(2,1)S(1)}, bf16[2,192,128]{2,1,0:T(8,128)(2,1)S(1)}, u32[]{:S(2)}, u32[]{:S(2)}) collective-permute-start(bf16[2,192,128]{2,1,0:T(8,128)(2,1)S(1)} %pad_maximum_fusion.1), channel_id=1, source_target_pairs={{0,4},{4,8},{8,12},{12,0},{1,5},{5,9},{9,13},{13,1},{2,6},{6,10},{... | collective-permute-start | bytes 294920 | tf_op jit(solution)/shard_map/ppermute | solution.py:130
  90.2 7.4 %collective-permute-start.5 = (bf16[2,192,128]{2,1,0:T(8,128)(2,1)S(1)}, bf16[2,192,128]{2,1,0:T(8,128)(2,1)S(1)}, u32[]{:S(2)}, u32[]{:S(2)}) collective-permute-start(bf16[2,192,128]{2,1,0:T(8,128)(2,1)S(1)} %pad_maximum_fusion.1), channel_id=1, source_target_pairs={{0,8},{4,12},{8,0},{12,4},{1,9},{5,13},{9,1},{13,5},{2,10},{6,14},... | collective-permute-start | bytes 294920 | tf_op jit(solution)/shard_map/ppermute | solution.py:130
  92.2 8.3 %collective-permute-start.6 = (bf16[2,192,128]{2,1,0:T(8,128)(2,1)S(1)}, bf16[2,192,128]{2,1,0:T(8,128)(2,1)S(1)}, u32[]{:S(2)}, u32[]{:S(2)}) collective-permute-start(bf16[2,192,128]{2,1,0:T(8,128)(2,1)S(1)} %pad_maximum_fusion.1), channel_id=1, source_target_pairs={{0,12},{4,0},{8,4},{12,8},{1,13},{5,1},{9,5},{13,9},{2,14},{6,2},{... | collective-permute-start | bytes 294920 | tf_op jit(solution)/shard_map/ppermute | solution.py:130
  101.1 15.3 %collective-permute-start.7 = (bf16[8,192,128]{2,1,0:T(8,128)(2,1)}, bf16[8,192,128]{2,1,0:T(8,128)(2,1)}, u32[]{:S(2)}, u32[]{:S(2)}) collective-permute-start(bf16[8,192,128]{2,1,0:T(8,128)(2,1)} %get-tuple-element.15), channel_id=1, source_target_pairs={{0,1},{1,2},{2,3},{3,0},{4,5},{5,6},{6,7},{7,4},{8,9},{9,10},{10,1... | collective-permute-start | bytes 1179656 | tf_op jit(solution)/shard_map/ppermute | solution.py:130
  105.1 19.4 %collective-permute-start.8 = (bf16[8,192,128]{2,1,0:T(8,128)(2,1)}, bf16[8,192,128]{2,1,0:T(8,128)(2,1)S(1)}, u32[]{:S(2)}, u32[]{:S(2)}) collective-permute-start(bf16[8,192,128]{2,1,0:T(8,128)(2,1)} %get-tuple-element.15), channel_id=1, source_target_pairs={{0,2},{1,3},{2,0},{3,1},{4,6},{5,7},{6,4},{7,5},{8,10},{9,11},{10,... | collective-permute-start | bytes 1179656 | tf_op jit(solution)/shard_map/ppermute | solution.py:130
  109.7 24.7 %collective-permute-start.9 = (bf16[8,192,128]{2,1,0:T(8,128)(2,1)}, bf16[8,192,128]{2,1,0:T(8,128)(2,1)}, u32[]{:S(2)}, u32[]{:S(2)}) collective-permute-start(bf16[8,192,128]{2,1,0:T(8,128)(2,1)} %get-tuple-element.15), channel_id=1, source_target_pairs={{0,3},{1,0},{2,1},{3,2},{4,7},{5,4},{6,5},{7,6},{8,11},{9,8},{10,9... | collective-permute-start | bytes 1179656 | tf_op jit(solution)/shard_map/ppermute | solution.py:130
  113.8 31.5 %collective-permute-start.2 = (bf16[128,768]{1,0:T(8,128)(2,1)S(1)}, bf16[128,768]{1,0:T(8,128)(2,1)}, u32[]{:S(2)}, u32[]{:S(2)}) collective-permute-start(bf16[128,768]{1,0:T(8,128)(2,1)S(1)} %constant_dynamic-slice_fusion.2), channel_id=1, source_target_pairs={{0,256},{256,0},{1,257},{257,1},{2,258},{258,2},{3,259},{259,3},{4... | collective-permute-start | bytes 589832 | tf_op jit(solution)/shard_map/ppermute | solution.py:152
  127.0 20.1 %all-to-all-start.3 = ((bf16[8,192,128]{2,1,0:T(8,128)(2,1)}), bf16[8,192,128]{2,1,0:T(8,128)(2,1)S(1)}, u32[]{:S(2)}, u32[]{:S(2)}) async-start(bf16[8,192,128]{2,1,0:T(8,128)(2,1)} %reduce_sum.24), calls=%async_computation.3 | async-start | bytes 786432 | tf_op jit(solution)/shard_map/all_to_all | solution.py:161
  135.4 2.8 %copy-start.3 = (bf16[4096,768]{1,0:T(8,128)(2,1)S(1)}, bf16[4096,768]{1,0:T(8,128)(2,1)}, u32[]{:S(2)}) copy-start(bf16[4096,768]{1,0:T(8,128)(2,1)} %all-gather.5.cloned.1.call-done.grad_ref) | copy-start | bytes 18874372
  140.1 20.0 %collective-permute-start.10 = (bf16[192,768]{1,0:T(8,128)(2,1)S(1)}, bf16[192,768]{1,0:T(8,128)(2,1)S(1)}, u32[]{:S(2)}, u32[]{:S(2)}) collective-permute-start(bf16[192,768]{1,0:T(8,128)(2,1)S(1)} %shard_map.69), channel_id=1, source_target_pairs={{0,256},{256,0},{1,257},{257,1},{2,258},{258,2},{3,259},{259,3},{4... | collective-permute-start | bytes 884744 | tf_op jit(solution)/shard_map/ppermute | solution.py:152
Sparse Core Ops, SparseCore 0:
  10.7 56.2 all-gather.2
  72.5 49.1 all-gather.4

commit v18 on v17

--- a/solution.py
+++ b/solution.py
@@ -178,13 +178,13 @@
     weight = lax.all_gather(half_of(up_weight, replica), "row", axis=0, tiled=True)
     turned = [lax.ppermute(features, ("dp", "row") + COL, turn_moves(other)) for other in (0, 1)]
     turned = jnp.stack(turned)
-    depth_line = to_all(features, ("dp", "y"), 2 * SIDE)
+    depth_line = to_all(after(features, turned), ("dp", "y"), 2 * SIDE)
     by_depth = to_all(depth_line, "x", SIDE)
     out_grad = by_replica(
         half_of(out_grad, replica), to_replica(half_of(out_grad, 1 - replica)), 0
     )
 
-    hidden = hidden_sum(after(by_depth, turned), weight)
+    hidden = hidden_sum(by_depth, weight)
     normal_cdf = 0.5 * (1.0 + jax.scipy.special.erf(hidden / math.sqrt(2.0)))
     density = jnp.exp(-0.5 * hidden * hidden) / math.sqrt(2.0 * math.pi)
     gelu_half = (hidden * normal_cdf).astype(jnp.bfloat16)
@@ -196,7 +196,7 @@
     by_token = from_lines(from_line(after(turned, hidden_grad)))
     pieces = input_grad_pieces(weight, hidden_grad)
     own = token_sum(places(), by_token, grads)
-    feature_grad = sum_along(sum_along(pieces, "x"), ("dp", "y")).T
+    feature_grad = sum_along(after(sum_along(pieces, "x"), own), ("dp", "y")).T
 
     mine, other = (
         lax.dynamic_slice_in_dim(gelu_half, which * tokens, tokens, axis=0)

time: 170 us -> 187 us (1.10)
  waiting for transfers between devices: 35.2 us -> 46.3 us
  starting transfers between devices: 68.8 us -> 71.7 us
  blocking collectives: 17.1 us -> 19.5 us
    all_to_all x2, waiting for transfers between devices: 0.01 us -> 11.7 us  [sum_along(): pieces = lax.all_to_all(pieces, axis, 0, 0, tiled=True)]
    all_to_all x1, waiting for transfers between devices: 0.01 us -> 8.21 us  [to_all(): return lax.all_to_all(copies, axis, 0, 0, tiled=True)]
    ppermute x3, waiting for transfers between devices: 12.3 us -> 6 us  [to_replica(): return lax.ppermute(value, 'dp', [(0, 1), (1, 0)])]
    ppermute x3, starting transfers between devices: 13.7 us -> 19.4 us  [to_replica(): return lax.ppermute(value, 'dp', [(0, 1), (1, 0)])]
    all_gather x1, waiting for transfers between devices: 4.54 us -> 0.01 us  [per_device(): lax.all_gather(half_of(up_weight, replica), 'row', axis=0, tiled=True)]
    ppermute x6, waiting for transfers between devices: 10.6 us -> 13.5 us  [shifted(): lax.ppermute(value, axis, [(i, (i + steps) % SIDE) for i in range(SIDE)])]
    all_to_all x1, blocking collectives: 17.1 us -> 19.5 us  [to_all(): return lax.all_to_all(copies, axis, 0, 0, tiled=True)]
    unnamed x19 -> x17, local copies, waits for them, and re-layouts: 12.6 us -> 12.8 us
  transfers between devices with their start and end apart: 16 -> 16, of which waited for: 7 -> 6; matrix products, arithmetic and copies ran while one was open for 8% -> 7% of each run, Pallas kernels for 3% -> 3%
where the time goes in v18:
time: 187 us; the launch traced here: 185 us
  starting transfers between devices  71.7 us (38%)
  waiting for transfers between devices  46.3 us (25%)
  blocking collectives  19.5 us (10%)
  local copies, waits for them, and re-layouts  18.4 us (10%)
  between operations  14.3 us (8%)
  other arithmetic  7.39 us (4%)
  Pallas kernels  7.18 us (4%)
    ppermute x6, starting transfers between devices, shifted(): lax.ppermute(value, axis, [(i, (i + steps) % SIDE) for i in range(SIDE)])  21.8 us
    all_to_all x1, blocking collectives, to_all(): return lax.all_to_all(copies, axis, 0, 0, tiled=True)  19.5 us
    ppermute x3, starting transfers between devices, to_replica(): return lax.ppermute(value, 'dp', [(0, 1), (1, 0)])  19.4 us
    ppermute x2, starting transfers between devices, per_device(): lax.ppermute(features, ('dp', 'row') + COL, turn_moves(other))  15.2 us
    ppermute x6, waiting for transfers between devices, shifted(): lax.ppermute(value, axis, [(i, (i + steps) % SIDE) for i in range(SIDE)])  13.5 us
    unnamed x17, local copies, waits for them, and re-layouts  12.8 us
    all_to_all x2, waiting for transfers between devices, sum_along(): pieces = lax.all_to_all(pieces, axis, 0, 0, tiled=True)  11.7 us
    all_to_all x2, starting transfers between devices, sum_along(): pieces = lax.all_to_all(pieces, axis, 0, 0, tiled=True)  11.3 us
  transfers between devices with their start and end apart: 16, of which 6 were waited for; matrix products, arithmetic and copies ran while one was open for 7% of the time, Pallas kernels for 3%

profile of v18, /device:TPU:56, one launch (start us, length us, event | category | flops | bytes accessed | tf_op | source)
XLA Modules:
  0.0 184.7 jit_solution(14102832553233672579)
XLA Ops:
  9.0 10.1 %collective-permute-start.1 = (bf16[192,128]{1,0:T(8,128)(2,1)}, bf16[192,128]{1,0:T(8,128)(2,1)S(1)}, u32[]{:S(2)}, u32[]{:S(2)}) collective-permute-start(bf16[192,128]{1,0:T(8,128)(2,1)} %bitcast.6), channel_id=1, source_target_pairs={{0,256},{1,272},{2,288},{3,304},{4,320},{5,336},{6,352},{7,368},{8... | collective-permute-start | bytes 147464 | tf_op jit(solution)/shard_map/ppermute | solution.py:179
  19.1 5.1 %collective-permute-start = (bf16[192,128]{1,0:T(8,128)(2,1)}, bf16[192,128]{1,0:T(8,128)(2,1)S(1)}, u32[]{:S(2)}, u32[]{:S(2)}) collective-permute-start(bf16[192,128]{1,0:T(8,128)(2,1)} %bitcast.7), channel_id=1, source_target_pairs={{0,0},{1,16},{2,32},{3,48},{4,64},{5,80},{6,96},{7,112},{8,128},{9... | collective-permute-start | bytes 147464 | tf_op jit(solution)/shard_map/ppermute | solution.py:179
  24.2 6.8 %collective-permute-done = bf16[192,128]{1,0:T(8,128)(2,1)S(1)} collective-permute-done((bf16[192,128]{1,0:T(8,128)(2,1)}, bf16[192,128]{1,0:T(8,128)(2,1)S(1)}, u32[]{:S(2)}, u32[]{:S(2)}) %collective-permute-start) | collective-permute-done | bytes 49184 | tf_op jit(solution)/shard_map/ppermute | solution.py:179
  31.9 19.5 %all_to_all.20 = bf16[8,192,128]{2,1,0:T(8,128)(2,1)S(1)} all-to-all(bf16[8,192,128]{2,1,0:T(8,128)(2,1)S(1)} %broadcast_in_dim.4), channel_id=1, replica_groups=mesh['dp'=2,'row'=16,'y'=4,'x'=4] {'dp','y'}, dimensions={0} | all-to-all | bytes 786432 | tf_op jit(solution)/shard_map/all_to_all | solution.py:157
  51.4 1.6 broadcast_in_dim.5
  53.0 3.9 %all-to-all-start.1 = ((bf16[4,8,192,128]{3,2,1,0:T(8,128)(2,1)}), bf16[4,8,192,128]{3,2,1,0:T(8,128)(2,1)S(1)}, u32[]{:S(2)}, u32[]{:S(2)}) async-start(bf16[4,8,192,128]{3,2,1,0:T(8,128)(2,1)} %broadcast_in_dim.5), calls=%async_computation.1 | async-start | bytes 3145728 | tf_op jit(solution)/shard_map/all_to_all | solution.py:157
  56.9 6.1 %collective-permute-start.3 = (bf16[128,768]{1,0:T(8,128)(2,1)S(1)}, bf16[128,768]{1,0:T(8,128)(2,1)S(1)}, u32[]{:S(2)}, u32[]{:S(2)}) collective-permute-start(bf16[128,768]{1,0:T(8,128)(2,1)S(1)} %constant_dynamic-slice_fusion.1), channel_id=1, source_target_pairs={{0,256},{256,0},{1,257},{257,1},{2,258},{258,2},{3,259},{259,3},{4... | collective-permute-start | bytes 589832 | tf_op jit(solution)/shard_map/ppermute | solution.py:152
  63.0 6.0 %collective-permute-done.3 = bf16[128,768]{1,0:T(8,128)(2,1)S(1)} collective-permute-done((bf16[128,768]{1,0:T(8,128)(2,1)S(1)}, bf16[128,768]{1,0:T(8,128)(2,1)S(1)}, u32[]{:S(2)}, u32[]{:S(2)}) %collective-permute-start.3) | collective-permute-done | bytes 196640 | tf_op jit(solution)/shard_map/ppermute | solution.py:152
  69.1 8.2 %all-to-all-done.1.block_ref = bf16[4,8,192,128]{3,2,1,0:T(8,128)(2,1)S(1)} async-done(((bf16[4,8,192,128]{3,2,1,0:T(8,128)(2,1)}), bf16[4,8,192,128]{3,2,1,0:T(8,128)(2,1)S(1)}, u32[]{:S(2)}, u32[]{:S(2)}) %all-to-all-start.1) | async-done | bytes 1572896 | tf_op jit(solution)/shard_map/all_to_all | solution.py:157
  77.3 2.3 %copy-done.1 = bf16[3072,768]{1,0:T(8,128)(2,1)S(1)} copy-done((bf16[3072,768]{1,0:T(8,128)(2,1)S(1)}, bf16[3072,768]{1,0:T(8,128)(2,1)}, u32[]{:S(2)}) %copy-start.1) | copy-done | bytes 4718616
  79.6 1.8 shard_map.67
  81.5 1.1 fusion.5
  82.6 4.5 %collective-permute-start.4 = (bf16[2,192,128]{2,1,0:T(8,128)(2,1)S(1)}, bf16[2,192,128]{2,1,0:T(8,128)(2,1)S(1)}, u32[]{:S(2)}, u32[]{:S(2)}) collective-permute-start(bf16[2,192,128]{2,1,0:T(8,128)(2,1)S(1)} %pad_maximum_fusion.1), channel_id=1, source_target_pairs={{0,4},{4,8},{8,12},{12,0},{1,5},{5,9},{9,13},{13,1},{2,6},{6,10},{... | collective-permute-start | bytes 294920 | tf_op jit(solution)/shard_map/ppermute | solution.py:130
  87.1 3.5 %collective-permute-start.5 = (bf16[2,192,128]{2,1,0:T(8,128)(2,1)S(1)}, bf16[2,192,128]{2,1,0:T(8,128)(2,1)S(1)}, u32[]{:S(2)}, u32[]{:S(2)}) collective-permute-start(bf16[2,192,128]{2,1,0:T(8,128)(2,1)S(1)} %pad_maximum_fusion.1), channel_id=1, source_target_pairs={{0,8},{4,12},{8,0},{12,4},{1,9},{5,13},{9,1},{13,5},{2,10},{6,14},... | collective-permute-start | bytes 294920 | tf_op jit(solution)/shard_map/ppermute | solution.py:130
  90.7 1.9 %collective-permute-start.6 = (bf16[2,192,128]{2,1,0:T(8,128)(2,1)S(1)}, bf16[2,192,128]{2,1,0:T(8,128)(2,1)S(1)}, u32[]{:S(2)}, u32[]{:S(2)}) collective-permute-start(bf16[2,192,128]{2,1,0:T(8,128)(2,1)S(1)} %pad_maximum_fusion.1), channel_id=1, source_target_pairs={{0,12},{4,0},{8,4},{12,8},{1,13},{5,1},{9,5},{13,9},{2,14},{6,2},{... | collective-permute-start | bytes 294920 | tf_op jit(solution)/shard_map/ppermute | solution.py:130
  92.6 2.6 %copy-done.2 = bf16[3072,768]{1,0:T(8,128)(2,1)S(1)} copy-done((bf16[3072,768]{1,0:T(8,128)(2,1)S(1)}, bf16[3072,768]{1,0:T(8,128)(2,1)}, u32[]{:S(2)}) %copy-start.2) | copy-done | bytes 4718616
  96.2 3.4 %shard_map.68 = bf16[4,8,192,128]{3,2,1,0:T(8,128)(2,1)} custom-call(bf16[3072,768]{1,0:T(8,128)(2,1)S(1)} %copy-done.2, bf16[256,768]{1,0:T(8,128)(2,1)S(1)} %copy-done.4), custom_call_target="tpu_custom_call" | custom-call | flops 1207959552 | bytes 6684672 | tf_op jit(solution)/shard_map/pallas_call | solution.py:29
  99.6 4.4 %all-to-all-start.2 = ((bf16[4,8,192,128]{3,2,1,0:T(8,128)(2,1)}), bf16[4,8,192,128]{3,2,1,0:T(8,128)(2,1)}, u32[]{:S(2)}, u32[]{:S(2)}) async-start(bf16[4,8,192,128]{3,2,1,0:T(8,128)(2,1)} %shard_map.68), calls=%async_computation.2 | async-start | bytes 3145728 | tf_op jit(solution)/shard_map/all_to_all | solution.py:161
  106.7 3.9 %collective-permute-start.7 = (bf16[8,192,128]{2,1,0:T(8,128)(2,1)}, bf16[8,192,128]{2,1,0:T(8,128)(2,1)}, u32[]{:S(2)}, u32[]{:S(2)}) collective-permute-start(bf16[8,192,128]{2,1,0:T(8,128)(2,1)} %get-tuple-element.17), channel_id=1, source_target_pairs={{0,1},{1,2},{2,3},{3,0},{4,5},{5,6},{6,7},{7,4},{8,9},{9,10},{10,1... | collective-permute-start | bytes 1179656 | tf_op jit(solution)/shard_map/ppermute | solution.py:130
  110.5 4.6 %collective-permute-start.8 = (bf16[8,192,128]{2,1,0:T(8,128)(2,1)}, bf16[8,192,128]{2,1,0:T(8,128)(2,1)S(1)}, u32[]{:S(2)}, u32[]{:S(2)}) collective-permute-start(bf16[8,192,128]{2,1,0:T(8,128)(2,1)} %get-tuple-element.17), channel_id=1, source_target_pairs={{0,2},{1,3},{2,0},{3,1},{4,6},{5,7},{6,4},{7,5},{8,10},{9,11},{10,... | collective-permute-start | bytes 1179656 | tf_op jit(solution)/shard_map/ppermute | solution.py:130
  115.1 3.4 %collective-permute-start.9 = (bf16[8,192,128]{2,1,0:T(8,128)(2,1)}, bf16[8,192,128]{2,1,0:T(8,128)(2,1)}, u32[]{:S(2)}, u32[]{:S(2)}) collective-permute-start(bf16[8,192,128]{2,1,0:T(8,128)(2,1)} %get-tuple-element.17), channel_id=1, source_target_pairs={{0,3},{1,0},{2,1},{3,2},{4,7},{5,4},{6,5},{7,6},{8,11},{9,8},{10,9... | collective-permute-start | bytes 1179656 | tf_op jit(solution)/shard_map/ppermute | solution.py:130
  119.2 6.4 %collective-permute-start.2 = (bf16[128,768]{1,0:T(8,128)(2,1)S(1)}, bf16[128,768]{1,0:T(8,128)(2,1)}, u32[]{:S(2)}, u32[]{:S(2)}) collective-permute-start(bf16[128,768]{1,0:T(8,128)(2,1)S(1)} %constant_dynamic-slice_fusion.2), channel_id=1, source_target_pairs={{0,256},{256,0},{1,257},{257,1},{2,258},{258,2},{3,259},{259,3},{4... | collective-permute-start | bytes 589832 | tf_op jit(solution)/shard_map/ppermute | solution.py:152
  125.7 8.3 %collective-permute-done.7 = bf16[8,192,128]{2,1,0:T(8,128)(2,1)} collective-permute-done((bf16[8,192,128]{2,1,0:T(8,128)(2,1)}, bf16[8,192,128]{2,1,0:T(8,128)(2,1)}, u32[]{:S(2)}, u32[]{:S(2)}) %collective-permute-start.7) | collective-permute-done | bytes 393248 | tf_op jit(solution)/shard_map/ppermute | solution.py:130
  135.1 5.2 %collective-permute-done.8 = bf16[8,192,128]{2,1,0:T(8,128)(2,1)S(1)} collective-permute-done((bf16[8,192,128]{2,1,0:T(8,128)(2,1)}, bf16[8,192,128]{2,1,0:T(8,128)(2,1)S(1)}, u32[]{:S(2)}, u32[]{:S(2)}) %collective-permute-start.8) | collective-permute-done | bytes 393248 | tf_op jit(solution)/shard_map/ppermute | solution.py:130
  140.3 1.0 constant_dynamic-update-slice_fusion.4.block_ref
  141.4 2.8 %copy-done.3 = bf16[4096,768]{1,0:T(8,128)(2,1)S(1)} copy-done((bf16[4096,768]{1,0:T(8,128)(2,1)S(1)}, bf16[4096,768]{1,0:T(8,128)(2,1)}, u32[]{:S(2)}) %copy-start.3) | copy-done | bytes 6291480
  144.2 1.9 %shard_map.69 = bf16[192,768]{1,0:T(8,128)(2,1)S(1)} custom-call(s32[32]{0:T(128)S(1)} %fusion.6.place_ref, bf16[32,192,128]{2,1,0:T(8,128)(2,1)S(1)} %constant_dynamic-update-slice_fusion.4.block_ref, bf16[4096,768]{1,0:T(8,128)(2,1)S(1)} %copy-done.3), custom_call_target="tpu_custom_call" | custom-call | flops 1207959552 | bytes 8159232 | tf_op jit(solution)/shard_map/pallas_call | solution.py:29
  146.1 7.0 %collective-permute-start.10 = (bf16[192,768]{1,0:T(8,128)(2,1)S(1)}, bf16[192,768]{1,0:T(8,128)(2,1)S(1)}, u32[]{:S(2)}, u32[]{:S(2)}) collective-permute-start(bf16[192,768]{1,0:T(8,128)(2,1)S(1)} %shard_map.69), channel_id=1, source_target_pairs={{0,256},{256,0},{1,257},{257,1},{2,258},{258,2},{3,259},{259,3},{4... | collective-permute-start | bytes 884744 | tf_op jit(solution)/shard_map/ppermute | solution.py:152
  154.1 2.5 %reduce_sum.24 = bf16[8,192,128]{2,1,0:T(8,128)(2,1)} reduce(bf16[4,8,192,128]{3,2,1,0:T(8,128)(2,1)} %all-to-all-done.2, bf16[]{:T(256)} %constant.43.clone.1), dimensions={0}, to_apply=%region_0.1 | reduce | flops 589824 | bytes 1966082 | tf_op jit(solution)/shard_map/reduce_sum | solution.py:162
  156.7 7.0 %all-to-all-start.3 = ((bf16[8,192,128]{2,1,0:T(8,128)(2,1)}), bf16[8,192,128]{2,1,0:T(8,128)(2,1)S(1)}, u32[]{:S(2)}, u32[]{:S(2)}) async-start(bf16[8,192,128]{2,1,0:T(8,128)(2,1)} %reduce_sum.24), calls=%async_computation.3 | async-start | bytes 786432 | tf_op jit(solution)/shard_map/all_to_all | solution.py:161
  164.4 1.1 maximum_convert_fusion
  165.6 11.7 %all-to-all-done.3 = bf16[8,192,128]{2,1,0:T(8,128)(2,1)S(1)} async-done(((bf16[8,192,128]{2,1,0:T(8,128)(2,1)}), bf16[8,192,128]{2,1,0:T(8,128)(2,1)S(1)}, u32[]{:S(2)}, u32[]{:S(2)}) %all-to-all-start.3) | async-done | bytes 393248 | tf_op jit(solution)/shard_map/all_to_all | solution.py:161
  (40 shorter events, 10.8 us)
Async XLA Ops:
  7.2 1.1 copy-start
  7.2 70.1 %all-gather.3.cloned.1.call-start = ((), (), s32[]{:S(2)}) async-start(), calls=%async_computation.4 | async-start | bytes 5013504 | tf_op jit(solution)/shard_map/all_gather | solution.py:178
  9.0 15.2 %collective-permute-start.1 = (bf16[192,128]{1,0:T(8,128)(2,1)}, bf16[192,128]{1,0:T(8,128)(2,1)S(1)}, u32[]{:S(2)}, u32[]{:S(2)}) collective-permute-start(bf16[192,128]{1,0:T(8,128)(2,1)} %bitcast.6), channel_id=1, source_target_pairs={{0,256},{1,272},{2,288},{3,304},{4,320},{5,336},{6,352},{7,368},{8... | collective-permute-start | bytes 147464 | tf_op jit(solution)/shard_map/ppermute | solution.py:179
  19.1 11.9 %collective-permute-start = (bf16[192,128]{1,0:T(8,128)(2,1)}, bf16[192,128]{1,0:T(8,128)(2,1)S(1)}, u32[]{:S(2)}, u32[]{:S(2)}) collective-permute-start(bf16[192,128]{1,0:T(8,128)(2,1)} %bitcast.7), channel_id=1, source_target_pairs={{0,0},{1,16},{2,32},{3,48},{4,64},{5,80},{6,96},{7,112},{8,128},{9... | collective-permute-start | bytes 147464 | tf_op jit(solution)/shard_map/ppermute | solution.py:179
  53.0 3.9 %copy-start.5 = (bf16[128,1536]{1,0:T(8,128)(2,1)S(1)}, bf16[128,1536]{1,0:T(8,128)(2,1)}, u32[]{:S(2)}) copy-start(bf16[128,1536]{1,0:T(8,128)(2,1)} %param.6) | copy-start | bytes 1179652
  53.0 24.3 %all-to-all-start.1 = ((bf16[4,8,192,128]{3,2,1,0:T(8,128)(2,1)}), bf16[4,8,192,128]{3,2,1,0:T(8,128)(2,1)S(1)}, u32[]{:S(2)}, u32[]{:S(2)}) async-start(bf16[4,8,192,128]{3,2,1,0:T(8,128)(2,1)} %broadcast_in_dim.5), calls=%async_computation.1 | async-start | bytes 3145728 | tf_op jit(solution)/shard_map/all_to_all | solution.py:157
  56.9 84.5 %all-gather.5.cloned.1.call-start = ((), (), s32[]{:S(2)}) async-start(), calls=%async_computation.5 | async-start | bytes 6684672 | tf_op jit(solution)/shard_map/all_gather | solution.py:194
  56.9 12.1 %collective-permute-start.3 = (bf16[128,768]{1,0:T(8,128)(2,1)S(1)}, bf16[128,768]{1,0:T(8,128)(2,1)S(1)}, u32[]{:S(2)}, u32[]{:S(2)}) collective-permute-start(bf16[128,768]{1,0:T(8,128)(2,1)S(1)} %constant_dynamic-slice_fusion.1), channel_id=1, source_target_pairs={{0,256},{256,0},{1,257},{257,1},{2,258},{258,2},{3,259},{259,3},{4... | collective-permute-start | bytes 589832 | tf_op jit(solution)/shard_map/ppermute | solution.py:152
  77.3 2.3 %copy-start.1 = (bf16[3072,768]{1,0:T(8,128)(2,1)S(1)}, bf16[3072,768]{1,0:T(8,128)(2,1)}, u32[]{:S(2)}) copy-start(bf16[3072,768]{1,0:T(8,128)(2,1)} %all-gather.3.cloned.1.call-done.weight_ref) | copy-start | bytes 14155780
  82.6 22.0 %collective-permute-start.4 = (bf16[2,192,128]{2,1,0:T(8,128)(2,1)S(1)}, bf16[2,192,128]{2,1,0:T(8,128)(2,1)S(1)}, u32[]{:S(2)}, u32[]{:S(2)}) collective-permute-start(bf16[2,192,128]{2,1,0:T(8,128)(2,1)S(1)} %pad_maximum_fusion.1), channel_id=1, source_target_pairs={{0,4},{4,8},{8,12},{12,0},{1,5},{5,9},{9,13},{13,1},{2,6},{6,10},{... | collective-permute-start | bytes 294920 | tf_op jit(solution)/shard_map/ppermute | solution.py:130
  87.1 18.2 %collective-permute-start.5 = (bf16[2,192,128]{2,1,0:T(8,128)(2,1)S(1)}, bf16[2,192,128]{2,1,0:T(8,128)(2,1)S(1)}, u32[]{:S(2)}, u32[]{:S(2)}) collective-permute-start(bf16[2,192,128]{2,1,0:T(8,128)(2,1)S(1)} %pad_maximum_fusion.1), channel_id=1, source_target_pairs={{0,8},{4,12},{8,0},{12,4},{1,9},{5,13},{9,1},{13,5},{2,10},{6,14},... | collective-permute-start | bytes 294920 | tf_op jit(solution)/shard_map/ppermute | solution.py:130
  90.7 15.3 %collective-permute-start.6 = (bf16[2,192,128]{2,1,0:T(8,128)(2,1)S(1)}, bf16[2,192,128]{2,1,0:T(8,128)(2,1)S(1)}, u32[]{:S(2)}, u32[]{:S(2)}) collective-permute-start(bf16[2,192,128]{2,1,0:T(8,128)(2,1)S(1)} %pad_maximum_fusion.1), channel_id=1, source_target_pairs={{0,12},{4,0},{8,4},{12,8},{1,13},{5,1},{9,5},{13,9},{2,14},{6,2},{... | collective-permute-start | bytes 294920 | tf_op jit(solution)/shard_map/ppermute | solution.py:130
  92.6 2.6 %copy-start.2 = (bf16[3072,768]{1,0:T(8,128)(2,1)S(1)}, bf16[3072,768]{1,0:T(8,128)(2,1)}, u32[]{:S(2)}) copy-start(bf16[3072,768]{1,0:T(8,128)(2,1)} %all-gather.3.cloned.1.call-done.weight_ref) | copy-start | bytes 14155780
  95.2 1.0 copy-start.4
  99.6 54.5 %all-to-all-start.2 = ((bf16[4,8,192,128]{3,2,1,0:T(8,128)(2,1)}), bf16[4,8,192,128]{3,2,1,0:T(8,128)(2,1)}, u32[]{:S(2)}, u32[]{:S(2)}) async-start(bf16[4,8,192,128]{3,2,1,0:T(8,128)(2,1)} %shard_map.68), calls=%async_computation.2 | async-start | bytes 3145728 | tf_op jit(solution)/shard_map/all_to_all | solution.py:161
  106.7 27.4 %collective-permute-start.7 = (bf16[8,192,128]{2,1,0:T(8,128)(2,1)}, bf16[8,192,128]{2,1,0:T(8,128)(2,1)}, u32[]{:S(2)}, u32[]{:S(2)}) collective-permute-start(bf16[8,192,128]{2,1,0:T(8,128)(2,1)} %get-tuple-element.17), channel_id=1, source_target_pairs={{0,1},{1,2},{2,3},{3,0},{4,5},{5,6},{6,7},{7,4},{8,9},{9,10},{10,1... | collective-permute-start | bytes 1179656 | tf_op jit(solution)/shard_map/ppermute | solution.py:130
  110.5 29.7 %collective-permute-start.8 = (bf16[8,192,128]{2,1,0:T(8,128)(2,1)}, bf16[8,192,128]{2,1,0:T(8,128)(2,1)S(1)}, u32[]{:S(2)}, u32[]{:S(2)}) collective-permute-start(bf16[8,192,128]{2,1,0:T(8,128)(2,1)} %get-tuple-element.17), channel_id=1, source_target_pairs={{0,2},{1,3},{2,0},{3,1},{4,6},{5,7},{6,4},{7,5},{8,10},{9,11},{10,... | collective-permute-start | bytes 1179656 | tf_op jit(solution)/shard_map/ppermute | solution.py:130
  115.1 25.2 %collective-permute-start.9 = (bf16[8,192,128]{2,1,0:T(8,128)(2,1)}, bf16[8,192,128]{2,1,0:T(8,128)(2,1)}, u32[]{:S(2)}, u32[]{:S(2)}) collective-permute-start(bf16[8,192,128]{2,1,0:T(8,128)(2,1)} %get-tuple-element.17), channel_id=1, source_target_pairs={{0,3},{1,0},{2,1},{3,2},{4,7},{5,4},{6,5},{7,6},{8,11},{9,8},{10,9... | collective-permute-start | bytes 1179656 | tf_op jit(solution)/shard_map/ppermute | solution.py:130
  119.2 33.9 %collective-permute-start.2 = (bf16[128,768]{1,0:T(8,128)(2,1)S(1)}, bf16[128,768]{1,0:T(8,128)(2,1)}, u32[]{:S(2)}, u32[]{:S(2)}) collective-permute-start(bf16[128,768]{1,0:T(8,128)(2,1)S(1)} %constant_dynamic-slice_fusion.2), channel_id=1, source_target_pairs={{0,256},{256,0},{1,257},{257,1},{2,258},{258,2},{3,259},{259,3},{4... | collective-permute-start | bytes 589832 | tf_op jit(solution)/shard_map/ppermute | solution.py:152
  141.4 2.8 %copy-start.3 = (bf16[4096,768]{1,0:T(8,128)(2,1)S(1)}, bf16[4096,768]{1,0:T(8,128)(2,1)}, u32[]{:S(2)}) copy-start(bf16[4096,768]{1,0:T(8,128)(2,1)} %all-gather.5.cloned.1.call-done.grad_ref) | copy-start | bytes 18874372
  146.1 18.3 %collective-permute-start.10 = (bf16[192,768]{1,0:T(8,128)(2,1)S(1)}, bf16[192,768]{1,0:T(8,128)(2,1)S(1)}, u32[]{:S(2)}, u32[]{:S(2)}) collective-permute-start(bf16[192,768]{1,0:T(8,128)(2,1)S(1)} %shard_map.69), channel_id=1, source_target_pairs={{0,256},{256,0},{1,257},{257,1},{2,258},{258,2},{3,259},{259,3},{4... | collective-permute-start | bytes 884744 | tf_op jit(solution)/shard_map/ppermute | solution.py:152
  156.7 20.6 %all-to-all-start.3 = ((bf16[8,192,128]{2,1,0:T(8,128)(2,1)}), bf16[8,192,128]{2,1,0:T(8,128)(2,1)S(1)}, u32[]{:S(2)}, u32[]{:S(2)}) async-start(bf16[8,192,128]{2,1,0:T(8,128)(2,1)} %reduce_sum.24), calls=%async_computation.3 | async-start | bytes 786432 | tf_op jit(solution)/shard_map/all_to_all | solution.py:161
Sparse Core Ops, SparseCore 0:
  10.7 50.0 all-gather.2
  82.8 46.8 all-gather.4

commit v19 on v17

--- a/solution.py
+++ b/solution.py
@@ -196,7 +196,7 @@
     by_token = from_lines(from_line(after(turned, hidden_grad)))
     pieces = input_grad_pieces(weight, hidden_grad)
     own = token_sum(places(), by_token, grads)
-    feature_grad = sum_along(sum_along(pieces, "x"), ("dp", "y")).T
+    feature_grad = sum_along(after(sum_along(pieces, "x"), grads), ("dp", "y")).T
 
     mine, other = (
         lax.dynamic_slice_in_dim(gelu_half, which * tokens, tokens, axis=0)

time: 170 us -> 181 us (1.065)
  the two profiles are of different devices: /device:TPU:56 before, /device:TPU:3 now
where the time goes in v19:
time: 181 us; the launch traced here: 180 us
  starting transfers between devices  60.4 us (33%)
  waiting for transfers between devices  52.2 us (29%)
  blocking collectives  20.1 us (11%)
  local copies, waits for them, and re-layouts  18.1 us (10%)
  between operations  14.3 us (8%)
  other arithmetic  7.4 us (4%)
  Pallas kernels  7.17 us (4%)
    ppermute x6, starting transfers between devices, shifted(): lax.ppermute(value, axis, [(i, (i + steps) % SIDE) for i in range(SIDE)])  23.5 us
    all_to_all x1, blocking collectives, to_all(): return lax.all_to_all(copies, axis, 0, 0, tiled=True)  20.1 us
    all_to_all x2, waiting for transfers between devices, sum_along(): pieces = lax.all_to_all(pieces, axis, 0, 0, tiled=True)  17.7 us
    ppermute x3, starting transfers between devices, to_replica(): return lax.ppermute(value, 'dp', [(0, 1), (1, 0)])  17.1 us
    ppermute x6, waiting for transfers between devices, shifted(): lax.ppermute(value, axis, [(i, (i + steps) % SIDE) for i in range(SIDE)])  15.9 us
    unnamed x19, local copies, waits for them, and re-layouts  12.6 us
    all_gather x1, waiting for transfers between devices, per_device(): lax.all_gather(half_of(up_weight, replica), 'row', axis=0, tiled=True)  11.3 us
    all_to_all x2, starting transfers between devices, sum_along(): pieces = lax.all_to_all(pieces, axis, 0, 0, tiled=True)  8.77 us
  transfers between devices with their start and end apart: 16, of which 7 were waited for; matrix products, arithmetic and copies ran while one was open for 8% of the time, Pallas kernels for 3%

profile of v19, /device:TPU:3, one launch (start us, length us, event | category | flops | bytes accessed | tf_op | source)
XLA Modules:
  0.0 179.7 jit_solution(13914087836005800343)
XLA Ops:
  9.8 20.1 %all_to_all.20 = bf16[8,192,128]{2,1,0:T(8,128)(2,1)S(1)} all-to-all(bf16[8,192,128]{2,1,0:T(8,128)(2,1)S(1)} %broadcast_in_dim.4), channel_id=1, replica_groups=mesh['dp'=2,'row'=16,'y'=4,'x'=4] {'dp','y'}, dimensions={0} | all-to-all | bytes 786432 | tf_op jit(solution)/shard_map/all_to_all | solution.py:157
  30.0 1.5 broadcast_in_dim.5
  31.5 4.4 %all-to-all-start.1 = ((bf16[4,8,192,128]{3,2,1,0:T(8,128)(2,1)}), bf16[4,8,192,128]{3,2,1,0:T(8,128)(2,1)S(1)}, u32[]{:S(2)}, u32[]{:S(2)}) async-start(bf16[4,8,192,128]{3,2,1,0:T(8,128)(2,1)} %broadcast_in_dim.5), calls=%async_computation.1 | async-start | bytes 3145728 | tf_op jit(solution)/shard_map/all_to_all | solution.py:157
  36.0 3.3 %collective-permute-start.3 = (bf16[128,768]{1,0:T(8,128)(2,1)S(1)}, bf16[128,768]{1,0:T(8,128)(2,1)S(1)}, u32[]{:S(2)}, u32[]{:S(2)}) collective-permute-start(bf16[128,768]{1,0:T(8,128)(2,1)S(1)} %constant_dynamic-slice_fusion.1), channel_id=1, source_target_pairs={{0,256},{256,0},{1,257},{257,1},{2,258},{258,2},{3,259},{259,3},{4... | collective-permute-start | bytes 589832 | tf_op jit(solution)/shard_map/ppermute | solution.py:152
  39.3 5.9 %collective-permute-start.1 = (bf16[192,128]{1,0:T(8,128)(2,1)S(1)}, bf16[192,128]{1,0:T(8,128)(2,1)S(1)}, u32[]{:S(2)}, u32[]{:S(2)}) collective-permute-start(bf16[192,128]{1,0:T(8,128)(2,1)S(1)} %bitcast.7), channel_id=1, source_target_pairs={{0,256},{1,272},{2,288},{3,304},{4,320},{5,336},{6,352},{7,368},{8... | collective-permute-start | bytes 147464 | tf_op jit(solution)/shard_map/ppermute | solution.py:179
  45.8 4.4 %collective-permute-done.1 = bf16[192,128]{1,0:T(8,128)(2,1)S(1)} collective-permute-done((bf16[192,128]{1,0:T(8,128)(2,1)S(1)}, bf16[192,128]{1,0:T(8,128)(2,1)S(1)}, u32[]{:S(2)}, u32[]{:S(2)}) %collective-permute-start.1) | collective-permute-done | bytes 49184 | tf_op jit(solution)/shard_map/ppermute | solution.py:179
  50.4 2.8 %all-to-all-done.1.block_ref = bf16[4,8,192,128]{3,2,1,0:T(8,128)(2,1)S(1)} async-done(((bf16[4,8,192,128]{3,2,1,0:T(8,128)(2,1)}), bf16[4,8,192,128]{3,2,1,0:T(8,128)(2,1)S(1)}, u32[]{:S(2)}, u32[]{:S(2)}) %all-to-all-start.1) | async-done | bytes 1572896 | tf_op jit(solution)/shard_map/all_to_all | solution.py:157
  53.2 11.3 %all-gather.3.cloned.1.call-done.weight_ref = bf16[3072,768]{1,0:T(8,128)(2,1)} async-done(((bf16[192,768]{1,0:T(8,128)(2,1)}), bf16[3072,768]{1,0:T(8,128)(2,1)}) %all-gather.3.cloned.1.call-update) | async-done | bytes 4718608 | tf_op jit(solution)/shard_map/all_gather | solution.py:178
  64.5 2.3 %copy-done.1 = bf16[3072,768]{1,0:T(8,128)(2,1)S(1)} copy-done((bf16[3072,768]{1,0:T(8,128)(2,1)S(1)}, bf16[3072,768]{1,0:T(8,128)(2,1)}, u32[]{:S(2)}) %copy-start.1) | copy-done | bytes 4718616
  66.8 1.8 %shard_map.67 = f32[256,768]{1,0:T(8,128)S(1)} custom-call(bf16[4,8,192,128]{3,2,1,0:T(8,128)(2,1)S(1)} %all-to-all-done.1.block_ref, bf16[3072,768]{1,0:T(8,128)(2,1)S(1)} %copy-done.1), custom_call_target="tpu_custom_call" | custom-call | flops 1207959552 | bytes 7077888 | tf_op jit(solution)/shard_map/pallas_call | solution.py:29
  68.7 1.1 fusion.5
  69.8 3.5 %collective-permute-start.4 = (bf16[2,192,128]{2,1,0:T(8,128)(2,1)S(1)}, bf16[2,192,128]{2,1,0:T(8,128)(2,1)S(1)}, u32[]{:S(2)}, u32[]{:S(2)}) collective-permute-start(bf16[2,192,128]{2,1,0:T(8,128)(2,1)S(1)} %pad_maximum_fusion.1), channel_id=1, source_target_pairs={{0,4},{4,8},{8,12},{12,0},{1,5},{5,9},{9,13},{13,1},{2,6},{6,10},{... | collective-permute-start | bytes 294920 | tf_op jit(solution)/shard_map/ppermute | solution.py:130
  73.3 8.1 %collective-permute-start.5 = (bf16[2,192,128]{2,1,0:T(8,128)(2,1)S(1)}, bf16[2,192,128]{2,1,0:T(8,128)(2,1)S(1)}, u32[]{:S(2)}, u32[]{:S(2)}) collective-permute-start(bf16[2,192,128]{2,1,0:T(8,128)(2,1)S(1)} %pad_maximum_fusion.1), channel_id=1, source_target_pairs={{0,8},{4,12},{8,0},{12,4},{1,9},{5,13},{9,1},{13,5},{2,10},{6,14},... | collective-permute-start | bytes 294920 | tf_op jit(solution)/shard_map/ppermute | solution.py:130
  81.4 1.9 %collective-permute-start.6 = (bf16[2,192,128]{2,1,0:T(8,128)(2,1)S(1)}, bf16[2,192,128]{2,1,0:T(8,128)(2,1)S(1)}, u32[]{:S(2)}, u32[]{:S(2)}) collective-permute-start(bf16[2,192,128]{2,1,0:T(8,128)(2,1)S(1)} %pad_maximum_fusion.1), channel_id=1, source_target_pairs={{0,12},{4,0},{8,4},{12,8},{1,13},{5,1},{9,5},{13,9},{2,14},{6,2},{... | collective-permute-start | bytes 294920 | tf_op jit(solution)/shard_map/ppermute | solution.py:130
  83.4 2.3 %copy-done.2 = bf16[3072,768]{1,0:T(8,128)(2,1)S(1)} copy-done((bf16[3072,768]{1,0:T(8,128)(2,1)S(1)}, bf16[3072,768]{1,0:T(8,128)(2,1)}, u32[]{:S(2)}) %copy-start.2) | copy-done | bytes 4718616
  86.7 3.4 %shard_map.68 = bf16[4,8,192,128]{3,2,1,0:T(8,128)(2,1)} custom-call(bf16[3072,768]{1,0:T(8,128)(2,1)S(1)} %copy-done.2, bf16[256,768]{1,0:T(8,128)(2,1)S(1)} %copy-done.4), custom_call_target="tpu_custom_call" | custom-call | flops 1207959552 | bytes 6684672 | tf_op jit(solution)/shard_map/pallas_call | solution.py:29
  90.1 5.3 %all-to-all-start.2 = ((bf16[4,8,192,128]{3,2,1,0:T(8,128)(2,1)}), bf16[4,8,192,128]{3,2,1,0:T(8,128)(2,1)}, u32[]{:S(2)}, u32[]{:S(2)}) async-start(bf16[4,8,192,128]{3,2,1,0:T(8,128)(2,1)} %shard_map.68), calls=%async_computation.2 | async-start | bytes 3145728 | tf_op jit(solution)/shard_map/all_to_all | solution.py:161
  98.1 3.1 %collective-permute-start.7 = (bf16[8,192,128]{2,1,0:T(8,128)(2,1)}, bf16[8,192,128]{2,1,0:T(8,128)(2,1)}, u32[]{:S(2)}, u32[]{:S(2)}) collective-permute-start(bf16[8,192,128]{2,1,0:T(8,128)(2,1)} %get-tuple-element.17), channel_id=1, source_target_pairs={{0,1},{1,2},{2,3},{3,0},{4,5},{5,6},{6,7},{7,4},{8,9},{9,10},{10,1... | collective-permute-start | bytes 1179656 | tf_op jit(solution)/shard_map/ppermute | solution.py:130
  101.2 3.0 %collective-permute-start.8 = (bf16[8,192,128]{2,1,0:T(8,128)(2,1)}, bf16[8,192,128]{2,1,0:T(8,128)(2,1)S(1)}, u32[]{:S(2)}, u32[]{:S(2)}) collective-permute-start(bf16[8,192,128]{2,1,0:T(8,128)(2,1)} %get-tuple-element.17), channel_id=1, source_target_pairs={{0,2},{1,3},{2,0},{3,1},{4,6},{5,7},{6,4},{7,5},{8,10},{9,11},{10,... | collective-permute-start | bytes 1179656 | tf_op jit(solution)/shard_map/ppermute | solution.py:130
  104.2 4.0 %collective-permute-start.9 = (bf16[8,192,128]{2,1,0:T(8,128)(2,1)}, bf16[8,192,128]{2,1,0:T(8,128)(2,1)}, u32[]{:S(2)}, u32[]{:S(2)}) collective-permute-start(bf16[8,192,128]{2,1,0:T(8,128)(2,1)} %get-tuple-element.17), channel_id=1, source_target_pairs={{0,3},{1,0},{2,1},{3,2},{4,7},{5,4},{6,5},{7,6},{8,11},{9,8},{10,9... | collective-permute-start | bytes 1179656 | tf_op jit(solution)/shard_map/ppermute | solution.py:130
  108.9 6.9 %collective-permute-start.2 = (bf16[128,768]{1,0:T(8,128)(2,1)S(1)}, bf16[128,768]{1,0:T(8,128)(2,1)}, u32[]{:S(2)}, u32[]{:S(2)}) collective-permute-start(bf16[128,768]{1,0:T(8,128)(2,1)S(1)} %constant_dynamic-slice_fusion.2), channel_id=1, source_target_pairs={{0,256},{256,0},{1,257},{257,1},{2,258},{258,2},{3,259},{259,3},{4... | collective-permute-start | bytes 589832 | tf_op jit(solution)/shard_map/ppermute | solution.py:152
  115.8 5.1 %collective-permute-done.7 = bf16[8,192,128]{2,1,0:T(8,128)(2,1)} collective-permute-done((bf16[8,192,128]{2,1,0:T(8,128)(2,1)}, bf16[8,192,128]{2,1,0:T(8,128)(2,1)}, u32[]{:S(2)}, u32[]{:S(2)}) %collective-permute-start.7) | collective-permute-done | bytes 393248 | tf_op jit(solution)/shard_map/ppermute | solution.py:130
  120.9 1.0 constant_dynamic-update-slice_fusion.6
  121.9 1.2 collective-permute-done.8
  123.2 9.6 %collective-permute-done.9 = bf16[8,192,128]{2,1,0:T(8,128)(2,1)} collective-permute-done((bf16[8,192,128]{2,1,0:T(8,128)(2,1)}, bf16[8,192,128]{2,1,0:T(8,128)(2,1)}, u32[]{:S(2)}, u32[]{:S(2)}) %collective-permute-start.9) | collective-permute-done | bytes 393248 | tf_op jit(solution)/shard_map/ppermute | solution.py:130
  133.9 2.8 %copy-done.3 = bf16[4096,768]{1,0:T(8,128)(2,1)S(1)} copy-done((bf16[4096,768]{1,0:T(8,128)(2,1)S(1)}, bf16[4096,768]{1,0:T(8,128)(2,1)}, u32[]{:S(2)}) %copy-start.3) | copy-done | bytes 6291480
  136.7 1.9 %shard_map.69 = bf16[192,768]{1,0:T(8,128)(2,1)S(1)} custom-call(s32[32]{0:T(128)S(1)} %fusion.6.place_ref, bf16[32,192,128]{2,1,0:T(8,128)(2,1)S(1)} %constant_dynamic-update-slice_fusion.4.block_ref, bf16[4096,768]{1,0:T(8,128)(2,1)S(1)} %copy-done.3), custom_call_target="tpu_custom_call" | custom-call | flops 1207959552 | bytes 8159232 | tf_op jit(solution)/shard_map/pallas_call | solution.py:29
  138.6 6.9 %collective-permute-start.10 = (bf16[192,768]{1,0:T(8,128)(2,1)S(1)}, bf16[192,768]{1,0:T(8,128)(2,1)S(1)}, u32[]{:S(2)}, u32[]{:S(2)}) collective-permute-start(bf16[192,768]{1,0:T(8,128)(2,1)S(1)} %shard_map.69), channel_id=1, source_target_pairs={{0,256},{256,0},{1,257},{257,1},{2,258},{258,2},{3,259},{259,3},{4... | collective-permute-start | bytes 884744 | tf_op jit(solution)/shard_map/ppermute | solution.py:152
  146.5 2.5 %reduce_sum.24 = bf16[8,192,128]{2,1,0:T(8,128)(2,1)} reduce(bf16[4,8,192,128]{3,2,1,0:T(8,128)(2,1)} %all-to-all-done.2, bf16[]{:T(256)} %constant.43.clone.1), dimensions={0}, to_apply=%region_0.1 | reduce | flops 589824 | bytes 1966082 | tf_op jit(solution)/shard_map/reduce_sum | solution.py:162
  149.0 3.5 %all-to-all-start.3 = ((bf16[8,192,128]{2,1,0:T(8,128)(2,1)}), bf16[8,192,128]{2,1,0:T(8,128)(2,1)S(1)}, u32[]{:S(2)}, u32[]{:S(2)}) async-start(bf16[8,192,128]{2,1,0:T(8,128)(2,1)} %reduce_sum.24), calls=%async_computation.3 | async-start | bytes 786432 | tf_op jit(solution)/shard_map/all_to_all | solution.py:161
  153.3 1.1 maximum_convert_fusion
  154.5 17.7 %all-to-all-done.3 = bf16[8,192,128]{2,1,0:T(8,128)(2,1)S(1)} async-done(((bf16[8,192,128]{2,1,0:T(8,128)(2,1)}), bf16[8,192,128]{2,1,0:T(8,128)(2,1)S(1)}, u32[]{:S(2)}, u32[]{:S(2)}) %all-to-all-start.3) | async-done | bytes 393248 | tf_op jit(solution)/shard_map/all_to_all | solution.py:161
  (42 shorter events, 11.5 us)
Async XLA Ops:
  7.2 1.1 copy-start
  7.2 57.3 %all-gather.3.cloned.1.call-start = ((), (), s32[]{:S(2)}) async-start(), calls=%async_computation.4 | async-start | bytes 5013504 | tf_op jit(solution)/shard_map/all_gather | solution.py:178
  31.5 4.4 %copy-start.5 = (bf16[128,1536]{1,0:T(8,128)(2,1)S(1)}, bf16[128,1536]{1,0:T(8,128)(2,1)}, u32[]{:S(2)}) copy-start(bf16[128,1536]{1,0:T(8,128)(2,1)} %param.6) | copy-start | bytes 1179652
  31.5 7.7 %copy-start.6 = (bf16[128,192]{0,1:T(8,128)(2,1)S(1)}, bf16[128,192]{0,1:T(8,128)(2,1)}, u32[]{:S(2)}) copy-start(bf16[128,192]{0,1:T(8,128)(2,1)} %param.4) | copy-start | bytes 147460
  31.5 21.7 %all-to-all-start.1 = ((bf16[4,8,192,128]{3,2,1,0:T(8,128)(2,1)}), bf16[4,8,192,128]{3,2,1,0:T(8,128)(2,1)S(1)}, u32[]{:S(2)}, u32[]{:S(2)}) async-start(bf16[4,8,192,128]{3,2,1,0:T(8,128)(2,1)} %broadcast_in_dim.5), calls=%async_computation.1 | async-start | bytes 3145728 | tf_op jit(solution)/shard_map/all_to_all | solution.py:157
  35.9 97.9 %all-gather.5.cloned.1.call-start = ((), (), s32[]{:S(2)}) async-start(), calls=%async_computation.5 | async-start | bytes 6684672 | tf_op jit(solution)/shard_map/all_gather | solution.py:194
  36.0 14.3 %collective-permute-start.3 = (bf16[128,768]{1,0:T(8,128)(2,1)S(1)}, bf16[128,768]{1,0:T(8,128)(2,1)S(1)}, u32[]{:S(2)}, u32[]{:S(2)}) collective-permute-start(bf16[128,768]{1,0:T(8,128)(2,1)S(1)} %constant_dynamic-slice_fusion.1), channel_id=1, source_target_pairs={{0,256},{256,0},{1,257},{257,1},{2,258},{258,2},{3,259},{259,3},{4... | collective-permute-start | bytes 589832 | tf_op jit(solution)/shard_map/ppermute | solution.py:152
  39.3 11.0 %collective-permute-start.1 = (bf16[192,128]{1,0:T(8,128)(2,1)S(1)}, bf16[192,128]{1,0:T(8,128)(2,1)S(1)}, u32[]{:S(2)}, u32[]{:S(2)}) collective-permute-start(bf16[192,128]{1,0:T(8,128)(2,1)S(1)} %bitcast.7), channel_id=1, source_target_pairs={{0,256},{1,272},{2,288},{3,304},{4,320},{5,336},{6,352},{7,368},{8... | collective-permute-start | bytes 147464 | tf_op jit(solution)/shard_map/ppermute | solution.py:179
  45.2 5.1 %collective-permute-start = (bf16[192,128]{1,0:T(8,128)(2,1)S(1)}, bf16[192,128]{1,0:T(8,128)(2,1)S(1)}, u32[]{:S(2)}, u32[]{:S(2)}) collective-permute-start(bf16[192,128]{1,0:T(8,128)(2,1)S(1)} %bitcast.8), channel_id=1, source_target_pairs={{0,0},{1,16},{2,32},{3,48},{4,64},{5,80},{6,96},{7,112},{8,128},{9... | collective-permute-start | bytes 147464 | tf_op jit(solution)/shard_map/ppermute | solution.py:179
  64.5 2.3 %copy-start.1 = (bf16[3072,768]{1,0:T(8,128)(2,1)S(1)}, bf16[3072,768]{1,0:T(8,128)(2,1)}, u32[]{:S(2)}) copy-start(bf16[3072,768]{1,0:T(8,128)(2,1)} %all-gather.3.cloned.1.call-done.weight_ref) | copy-start | bytes 14155780
  69.8 26.3 %collective-permute-start.4 = (bf16[2,192,128]{2,1,0:T(8,128)(2,1)S(1)}, bf16[2,192,128]{2,1,0:T(8,128)(2,1)S(1)}, u32[]{:S(2)}, u32[]{:S(2)}) collective-permute-start(bf16[2,192,128]{2,1,0:T(8,128)(2,1)S(1)} %pad_maximum_fusion.1), channel_id=1, source_target_pairs={{0,4},{4,8},{8,12},{12,0},{1,5},{5,9},{9,13},{13,1},{2,6},{6,10},{... | collective-permute-start | bytes 294920 | tf_op jit(solution)/shard_map/ppermute | solution.py:130
  73.3 23.4 %collective-permute-start.5 = (bf16[2,192,128]{2,1,0:T(8,128)(2,1)S(1)}, bf16[2,192,128]{2,1,0:T(8,128)(2,1)S(1)}, u32[]{:S(2)}, u32[]{:S(2)}) collective-permute-start(bf16[2,192,128]{2,1,0:T(8,128)(2,1)S(1)} %pad_maximum_fusion.1), channel_id=1, source_target_pairs={{0,8},{4,12},{8,0},{12,4},{1,9},{5,13},{9,1},{13,5},{2,10},{6,14},... | collective-permute-start | bytes 294920 | tf_op jit(solution)/shard_map/ppermute | solution.py:130
  81.4 16.0 %collective-permute-start.6 = (bf16[2,192,128]{2,1,0:T(8,128)(2,1)S(1)}, bf16[2,192,128]{2,1,0:T(8,128)(2,1)S(1)}, u32[]{:S(2)}, u32[]{:S(2)}) collective-permute-start(bf16[2,192,128]{2,1,0:T(8,128)(2,1)S(1)} %pad_maximum_fusion.1), channel_id=1, source_target_pairs={{0,12},{4,0},{8,4},{12,8},{1,13},{5,1},{9,5},{13,9},{2,14},{6,2},{... | collective-permute-start | bytes 294920 | tf_op jit(solution)/shard_map/ppermute | solution.py:130
  83.4 2.3 %copy-start.2 = (bf16[3072,768]{1,0:T(8,128)(2,1)S(1)}, bf16[3072,768]{1,0:T(8,128)(2,1)}, u32[]{:S(2)}) copy-start(bf16[3072,768]{1,0:T(8,128)(2,1)} %all-gather.3.cloned.1.call-done.weight_ref) | copy-start | bytes 14155780
  85.7 1.0 copy-start.4
  90.1 56.4 %all-to-all-start.2 = ((bf16[4,8,192,128]{3,2,1,0:T(8,128)(2,1)}), bf16[4,8,192,128]{3,2,1,0:T(8,128)(2,1)}, u32[]{:S(2)}, u32[]{:S(2)}) async-start(bf16[4,8,192,128]{3,2,1,0:T(8,128)(2,1)} %shard_map.68), calls=%async_computation.2 | async-start | bytes 3145728 | tf_op jit(solution)/shard_map/all_to_all | solution.py:161
  98.1 22.7 %collective-permute-start.7 = (bf16[8,192,128]{2,1,0:T(8,128)(2,1)}, bf16[8,192,128]{2,1,0:T(8,128)(2,1)}, u32[]{:S(2)}, u32[]{:S(2)}) collective-permute-start(bf16[8,192,128]{2,1,0:T(8,128)(2,1)} %get-tuple-element.17), channel_id=1, source_target_pairs={{0,1},{1,2},{2,3},{3,0},{4,5},{5,6},{6,7},{7,4},{8,9},{9,10},{10,1... | collective-permute-start | bytes 1179656 | tf_op jit(solution)/shard_map/ppermute | solution.py:130
  101.2 21.9 %collective-permute-start.8 = (bf16[8,192,128]{2,1,0:T(8,128)(2,1)}, bf16[8,192,128]{2,1,0:T(8,128)(2,1)S(1)}, u32[]{:S(2)}, u32[]{:S(2)}) collective-permute-start(bf16[8,192,128]{2,1,0:T(8,128)(2,1)} %get-tuple-element.17), channel_id=1, source_target_pairs={{0,2},{1,3},{2,0},{3,1},{4,6},{5,7},{6,4},{7,5},{8,10},{9,11},{10,... | collective-permute-start | bytes 1179656 | tf_op jit(solution)/shard_map/ppermute | solution.py:130
  104.2 28.6 %collective-permute-start.9 = (bf16[8,192,128]{2,1,0:T(8,128)(2,1)}, bf16[8,192,128]{2,1,0:T(8,128)(2,1)}, u32[]{:S(2)}, u32[]{:S(2)}) collective-permute-start(bf16[8,192,128]{2,1,0:T(8,128)(2,1)} %get-tuple-element.17), channel_id=1, source_target_pairs={{0,3},{1,0},{2,1},{3,2},{4,7},{5,4},{6,5},{7,6},{8,11},{9,8},{10,9... | collective-permute-start | bytes 1179656 | tf_op jit(solution)/shard_map/ppermute | solution.py:130
  108.9 36.6 %collective-permute-start.2 = (bf16[128,768]{1,0:T(8,128)(2,1)S(1)}, bf16[128,768]{1,0:T(8,128)(2,1)}, u32[]{:S(2)}, u32[]{:S(2)}) collective-permute-start(bf16[128,768]{1,0:T(8,128)(2,1)S(1)} %constant_dynamic-slice_fusion.2), channel_id=1, source_target_pairs={{0,256},{256,0},{1,257},{257,1},{2,258},{258,2},{3,259},{259,3},{4... | collective-permute-start | bytes 589832 | tf_op jit(solution)/shard_map/ppermute | solution.py:152
  133.9 2.8 %copy-start.3 = (bf16[4096,768]{1,0:T(8,128)(2,1)S(1)}, bf16[4096,768]{1,0:T(8,128)(2,1)}, u32[]{:S(2)}) copy-start(bf16[4096,768]{1,0:T(8,128)(2,1)} %all-gather.5.cloned.1.call-done.grad_ref) | copy-start | bytes 18874372
  138.6 14.7 %collective-permute-start.10 = (bf16[192,768]{1,0:T(8,128)(2,1)S(1)}, bf16[192,768]{1,0:T(8,128)(2,1)S(1)}, u32[]{:S(2)}, u32[]{:S(2)}) collective-permute-start(bf16[192,768]{1,0:T(8,128)(2,1)S(1)} %shard_map.69), channel_id=1, source_target_pairs={{0,256},{256,0},{1,257},{257,1},{2,258},{258,2},{3,259},{259,3},{4... | collective-permute-start | bytes 884744 | tf_op jit(solution)/shard_map/ppermute | solution.py:152
  149.0 23.2 %all-to-all-start.3 = ((bf16[8,192,128]{2,1,0:T(8,128)(2,1)}), bf16[8,192,128]{2,1,0:T(8,128)(2,1)S(1)}, u32[]{:S(2)}, u32[]{:S(2)}) async-start(bf16[8,192,128]{2,1,0:T(8,128)(2,1)} %reduce_sum.24), calls=%async_computation.3 | async-start | bytes 786432 | tf_op jit(solution)/shard_map/all_to_all | solution.py:161
Sparse Core Ops, SparseCore 0:
  10.7 53.7 all-gather.2
  69.9 52.7 all-gather.4

commit v20 on v19

--- a/solution.py
+++ b/solution.py
@@ -145,7 +145,7 @@
 
 
 def from_lines(line):
-    return jnp.concatenate([line] + [shifted(line, "x", e) for e in range(1, SIDE)])
+    return [line] + [shifted(line, "x", e) for e in range(1, SIDE)]
 
 
 def to_replica(value):
@@ -193,10 +193,11 @@
     )
     grads = lax.all_gather(hidden_grad, "row", axis=0, tiled=True)
 
-    by_token = from_lines(from_line(after(turned, hidden_grad)))
-    pieces = input_grad_pieces(weight, hidden_grad)
-    own = token_sum(places(), by_token, grads)
-    feature_grad = sum_along(after(sum_along(pieces, "x"), grads), ("dp", "y")).T
+    token_lines = from_lines(from_line(after(turned, hidden_grad)))
+    pieces = sum_along(input_grad_pieces(weight, hidden_grad), "x")
+    feature_grad = sum_along(after(pieces, token_lines[1]), ("dp", "y"))
+    own = token_sum(places(), after(jnp.concatenate(token_lines), feature_grad), grads)
+    feature_grad = feature_grad.T
 
     mine, other = (
         lax.dynamic_slice_in_dim(gelu_half, which * tokens, tokens, axis=0)

time: 181 us -> 180 us (level)
  the two profiles are of different devices: /device:TPU:3 before, /device:TPU:14 now
where the time goes in v20:
time: 180 us; the launch traced here: 179 us
  starting transfers between devices  64.1 us (36%)
  waiting for transfers between devices  47.3 us (26%)
  blocking collectives  20.6 us (11%)
  local copies, waits for them, and re-layouts  18.1 us (10%)
  between operations  14.3 us (8%)
  other arithmetic  7.49 us (4%)
  Pallas kernels  7.18 us (4%)
    all_to_all x1, blocking collectives, to_all(): return lax.all_to_all(copies, axis, 0, 0, tiled=True)  20.6 us
    ppermute x6, starting transfers between devices, shifted(): lax.ppermute(value, axis, [(i, (i + steps) % SIDE) for i in range(SIDE)])  17 us
    ppermute x6, waiting for transfers between devices, shifted(): lax.ppermute(value, axis, [(i, (i + steps) % SIDE) for i in range(SIDE)])  16.8 us
    ppermute x3, starting transfers between devices, to_replica(): return lax.ppermute(value, 'dp', [(0, 1), (1, 0)])  16.1 us
    ppermute x2, starting transfers between devices, per_device(): lax.ppermute(features, ('dp', 'row') + COL, turn_moves(other))  13.4 us
    unnamed x20, local copies, waits for them, and re-layouts  13.2 us
    ppermute x3, waiting for transfers between devices, to_replica(): return lax.ppermute(value, 'dp', [(0, 1), (1, 0)])  12.9 us
    all_to_all x2, starting transfers between devices, sum_along(): pieces = lax.all_to_all(pieces, axis, 0, 0, tiled=True)  12.7 us
  transfers between devices with their start and end apart: 16, of which 9 were waited for; matrix products, arithmetic and copies ran while one was open for 7% of the time, Pallas kernels for 3%

profile of v20, /device:TPU:14, one launch (start us, length us, event | category | flops | bytes accessed | tf_op | source)
XLA Modules:
  0.0 179.1 jit_solution(6897904108145438291)
XLA Ops:
  9.8 20.6 %all_to_all.20 = bf16[8,192,128]{2,1,0:T(8,128)(2,1)S(1)} all-to-all(bf16[8,192,128]{2,1,0:T(8,128)(2,1)S(1)} %broadcast_in_dim.4), channel_id=1, replica_groups=mesh['dp'=2,'row'=16,'y'=4,'x'=4] {'dp','y'}, dimensions={0} | all-to-all | bytes 786432 | tf_op jit(solution)/shard_map/all_to_all | solution.py:157
  30.4 1.5 broadcast_in_dim.5
  32.0 4.9 %all-to-all-start.1 = ((bf16[4,8,192,128]{3,2,1,0:T(8,128)(2,1)}), bf16[4,8,192,128]{3,2,1,0:T(8,128)(2,1)S(1)}, u32[]{:S(2)}, u32[]{:S(2)}) async-start(bf16[4,8,192,128]{3,2,1,0:T(8,128)(2,1)} %broadcast_in_dim.5), calls=%async_computation.1 | async-start | bytes 3145728 | tf_op jit(solution)/shard_map/all_to_all | solution.py:157
  36.9 3.4 %collective-permute-start.3 = (bf16[128,768]{1,0:T(8,128)(2,1)S(1)}, bf16[128,768]{1,0:T(8,128)(2,1)S(1)}, u32[]{:S(2)}, u32[]{:S(2)}) collective-permute-start(bf16[128,768]{1,0:T(8,128)(2,1)S(1)} %constant_dynamic-slice_fusion.1), channel_id=1, source_target_pairs={{0,256},{256,0},{1,257},{257,1},{2,258},{258,2},{3,259},{259,3},{4... | collective-permute-start | bytes 589832 | tf_op jit(solution)/shard_map/ppermute | solution.py:152
  40.3 8.7 %collective-permute-start.1 = (bf16[192,128]{1,0:T(8,128)(2,1)S(1)}, bf16[192,128]{1,0:T(8,128)(2,1)S(1)}, u32[]{:S(2)}, u32[]{:S(2)}) collective-permute-start(bf16[192,128]{1,0:T(8,128)(2,1)S(1)} %bitcast.7), channel_id=1, source_target_pairs={{0,256},{1,272},{2,288},{3,304},{4,320},{5,336},{6,352},{7,368},{8... | collective-permute-start | bytes 147464 | tf_op jit(solution)/shard_map/ppermute | solution.py:179
  49.0 4.7 %collective-permute-start = (bf16[192,128]{1,0:T(8,128)(2,1)S(1)}, bf16[192,128]{1,0:T(8,128)(2,1)S(1)}, u32[]{:S(2)}, u32[]{:S(2)}) collective-permute-start(bf16[192,128]{1,0:T(8,128)(2,1)S(1)} %bitcast.8), channel_id=1, source_target_pairs={{0,0},{1,16},{2,32},{3,48},{4,64},{5,80},{6,96},{7,112},{8,128},{9... | collective-permute-start | bytes 147464 | tf_op jit(solution)/shard_map/ppermute | solution.py:179
  53.7 4.9 %collective-permute-done.1 = bf16[192,128]{1,0:T(8,128)(2,1)S(1)} collective-permute-done((bf16[192,128]{1,0:T(8,128)(2,1)S(1)}, bf16[192,128]{1,0:T(8,128)(2,1)S(1)}, u32[]{:S(2)}, u32[]{:S(2)}) %collective-permute-start.1) | collective-permute-done | bytes 49184 | tf_op jit(solution)/shard_map/ppermute | solution.py:179
  58.5 2.2 %collective-permute-done = bf16[192,128]{1,0:T(8,128)(2,1)S(1)} collective-permute-done((bf16[192,128]{1,0:T(8,128)(2,1)S(1)}, bf16[192,128]{1,0:T(8,128)(2,1)S(1)}, u32[]{:S(2)}, u32[]{:S(2)}) %collective-permute-start) | collective-permute-done | bytes 49184 | tf_op jit(solution)/shard_map/ppermute | solution.py:179
  60.9 8.3 %all-gather.3.cloned.1.call-done.weight_ref = bf16[3072,768]{1,0:T(8,128)(2,1)} async-done(((bf16[192,768]{1,0:T(8,128)(2,1)}), bf16[3072,768]{1,0:T(8,128)(2,1)}) %all-gather.3.cloned.1.call-update) | async-done | bytes 4718608 | tf_op jit(solution)/shard_map/all_gather | solution.py:178
  69.2 2.3 %copy-done.1 = bf16[3072,768]{1,0:T(8,128)(2,1)S(1)} copy-done((bf16[3072,768]{1,0:T(8,128)(2,1)S(1)}, bf16[3072,768]{1,0:T(8,128)(2,1)}, u32[]{:S(2)}) %copy-start.1) | copy-done | bytes 4718616
  71.5 1.8 %shard_map.67 = f32[256,768]{1,0:T(8,128)S(1)} custom-call(bf16[4,8,192,128]{3,2,1,0:T(8,128)(2,1)S(1)} %all-to-all-done.1.block_ref, bf16[3072,768]{1,0:T(8,128)(2,1)S(1)} %copy-done.1), custom_call_target="tpu_custom_call" | custom-call | flops 1207959552 | bytes 7077888 | tf_op jit(solution)/shard_map/pallas_call | solution.py:29
  74.5 2.3 %copy-done.2 = bf16[3072,768]{1,0:T(8,128)(2,1)S(1)} copy-done((bf16[3072,768]{1,0:T(8,128)(2,1)S(1)}, bf16[3072,768]{1,0:T(8,128)(2,1)}, u32[]{:S(2)}) %copy-start.2) | copy-done | bytes 4718616
  77.8 3.4 %shard_map.68 = bf16[4,8,192,128]{3,2,1,0:T(8,128)(2,1)} custom-call(bf16[3072,768]{1,0:T(8,128)(2,1)S(1)} %copy-done.2, bf16[256,768]{1,0:T(8,128)(2,1)S(1)} %copy-done.4), custom_call_target="tpu_custom_call" | custom-call | flops 1207959552 | bytes 6684672 | tf_op jit(solution)/shard_map/pallas_call | solution.py:29
  81.2 4.9 %all-to-all-start.2 = ((bf16[4,8,192,128]{3,2,1,0:T(8,128)(2,1)}), bf16[4,8,192,128]{3,2,1,0:T(8,128)(2,1)}, u32[]{:S(2)}, u32[]{:S(2)}) async-start(bf16[4,8,192,128]{3,2,1,0:T(8,128)(2,1)} %shard_map.68), calls=%async_computation.2 | async-start | bytes 3145728 | tf_op jit(solution)/shard_map/all_to_all | solution.py:161
  86.1 1.9 %collective-permute-start.4 = (bf16[2,192,128]{2,1,0:T(8,128)(2,1)S(1)}, bf16[2,192,128]{2,1,0:T(8,128)(2,1)S(1)}, u32[]{:S(2)}, u32[]{:S(2)}) collective-permute-start(bf16[2,192,128]{2,1,0:T(8,128)(2,1)S(1)} %pad_maximum_fusion.1), channel_id=1, source_target_pairs={{0,4},{4,8},{8,12},{12,0},{1,5},{5,9},{9,13},{13,1},{2,6},{6,10},{... | collective-permute-start | bytes 294920 | tf_op jit(solution)/shard_map/ppermute | solution.py:130
  88.0 5.1 %collective-permute-start.5 = (bf16[2,192,128]{2,1,0:T(8,128)(2,1)S(1)}, bf16[2,192,128]{2,1,0:T(8,128)(2,1)S(1)}, u32[]{:S(2)}, u32[]{:S(2)}) collective-permute-start(bf16[2,192,128]{2,1,0:T(8,128)(2,1)S(1)} %pad_maximum_fusion.1), channel_id=1, source_target_pairs={{0,8},{4,12},{8,0},{12,4},{1,9},{5,13},{9,1},{13,5},{2,10},{6,14},... | collective-permute-start | bytes 294920 | tf_op jit(solution)/shard_map/ppermute | solution.py:130
  93.1 1.9 %collective-permute-start.6 = (bf16[2,192,128]{2,1,0:T(8,128)(2,1)S(1)}, bf16[2,192,128]{2,1,0:T(8,128)(2,1)S(1)}, u32[]{:S(2)}, u32[]{:S(2)}) collective-permute-start(bf16[2,192,128]{2,1,0:T(8,128)(2,1)S(1)} %pad_maximum_fusion.1), channel_id=1, source_target_pairs={{0,12},{4,0},{8,4},{12,8},{1,13},{5,1},{9,5},{13,9},{2,14},{6,2},{... | collective-permute-start | bytes 294920 | tf_op jit(solution)/shard_map/ppermute | solution.py:130
  97.1 3.3 %collective-permute-done.6 = bf16[2,192,128]{2,1,0:T(8,128)(2,1)S(1)} collective-permute-done((bf16[2,192,128]{2,1,0:T(8,128)(2,1)S(1)}, bf16[2,192,128]{2,1,0:T(8,128)(2,1)S(1)}, u32[]{:S(2)}, u32[]{:S(2)}) %collective-permute-start.6) | collective-permute-done | bytes 98336 | tf_op jit(solution)/shard_map/ppermute | solution.py:130
  101.0 1.9 %collective-permute-start.7 = (bf16[8,192,128]{2,1,0:T(8,128)(2,1)}, bf16[8,192,128]{2,1,0:T(8,128)(2,1)S(1)}, u32[]{:S(2)}, u32[]{:S(2)}) collective-permute-start(bf16[8,192,128]{2,1,0:T(8,128)(2,1)} %get-tuple-element.20), channel_id=1, source_target_pairs={{0,1},{1,2},{2,3},{3,0},{4,5},{5,6},{6,7},{7,4},{8,9},{9,10},{10,1... | collective-permute-start | bytes 1179656 | tf_op jit(solution)/shard_map/ppermute | solution.py:130
  102.9 2.3 %all-to-all-done.2 = bf16[4,8,192,128]{3,2,1,0:T(8,128)(2,1)} async-done(((bf16[4,8,192,128]{3,2,1,0:T(8,128)(2,1)}), bf16[4,8,192,128]{3,2,1,0:T(8,128)(2,1)}, u32[]{:S(2)}, u32[]{:S(2)}) %all-to-all-start.2) | async-done | bytes 1572896 | tf_op jit(solution)/shard_map/all_to_all | solution.py:161
  105.3 2.6 %reduce_sum.24 = bf16[8,192,128]{2,1,0:T(8,128)(2,1)} reduce(bf16[4,8,192,128]{3,2,1,0:T(8,128)(2,1)} %all-to-all-done.2, bf16[]{:T(256)} %constant.43.clone.1), dimensions={0}, to_apply=%region_0.1 | reduce | flops 589824 | bytes 1966082 | tf_op jit(solution)/shard_map/reduce_sum | solution.py:162
  107.8 6.1 %collective-permute-done.7 = bf16[8,192,128]{2,1,0:T(8,128)(2,1)S(1)} collective-permute-done((bf16[8,192,128]{2,1,0:T(8,128)(2,1)}, bf16[8,192,128]{2,1,0:T(8,128)(2,1)S(1)}, u32[]{:S(2)}, u32[]{:S(2)}) %collective-permute-start.7) | collective-permute-done | bytes 393248 | tf_op jit(solution)/shard_map/ppermute | solution.py:130
  113.9 7.8 %all-to-all-start.3 = ((bf16[8,192,128]{2,1,0:T(8,128)(2,1)}), bf16[8,192,128]{2,1,0:T(8,128)(2,1)S(1)}, u32[]{:S(2)}, u32[]{:S(2)}) async-start(bf16[8,192,128]{2,1,0:T(8,128)(2,1)} %reduce_sum.24), calls=%async_computation.3 | async-start | bytes 786432 | tf_op jit(solution)/shard_map/all_to_all | solution.py:161
  121.8 2.6 %collective-permute-start.8 = (bf16[8,192,128]{2,1,0:T(8,128)(2,1)}, bf16[8,192,128]{2,1,0:T(8,128)(2,1)}, u32[]{:S(2)}, u32[]{:S(2)}) collective-permute-start(bf16[8,192,128]{2,1,0:T(8,128)(2,1)} %get-tuple-element.20), channel_id=1, source_target_pairs={{0,2},{1,3},{2,0},{3,1},{4,6},{5,7},{6,4},{7,5},{8,10},{9,11},{10,... | collective-permute-start | bytes 1179656 | tf_op jit(solution)/shard_map/ppermute | solution.py:130
  124.5 3.5 %collective-permute-start.9 = (bf16[8,192,128]{2,1,0:T(8,128)(2,1)}, bf16[8,192,128]{2,1,0:T(8,128)(2,1)}, u32[]{:S(2)}, u32[]{:S(2)}) collective-permute-start(bf16[8,192,128]{2,1,0:T(8,128)(2,1)} %get-tuple-element.20), channel_id=1, source_target_pairs={{0,3},{1,0},{2,1},{3,2},{4,7},{5,4},{6,5},{7,6},{8,11},{9,8},{10,9... | collective-permute-start | bytes 1179656 | tf_op jit(solution)/shard_map/ppermute | solution.py:130
  128.7 6.4 %collective-permute-start.2 = (bf16[128,768]{1,0:T(8,128)(2,1)S(1)}, bf16[128,768]{1,0:T(8,128)(2,1)}, u32[]{:S(2)}, u32[]{:S(2)}) collective-permute-start(bf16[128,768]{1,0:T(8,128)(2,1)S(1)} %constant_dynamic-slice_fusion.2), channel_id=1, source_target_pairs={{0,256},{256,0},{1,257},{257,1},{2,258},{258,2},{3,259},{259,3},{4... | collective-permute-start | bytes 589832 | tf_op jit(solution)/shard_map/ppermute | solution.py:152
  135.2 2.4 %collective-permute-done.8 = bf16[8,192,128]{2,1,0:T(8,128)(2,1)} collective-permute-done((bf16[8,192,128]{2,1,0:T(8,128)(2,1)}, bf16[8,192,128]{2,1,0:T(8,128)(2,1)}, u32[]{:S(2)}, u32[]{:S(2)}) %collective-permute-start.8) | collective-permute-done | bytes 393248 | tf_op jit(solution)/shard_map/ppermute | solution.py:130
  138.6 4.9 %collective-permute-done.9 = bf16[8,192,128]{2,1,0:T(8,128)(2,1)} collective-permute-done((bf16[8,192,128]{2,1,0:T(8,128)(2,1)}, bf16[8,192,128]{2,1,0:T(8,128)(2,1)}, u32[]{:S(2)}, u32[]{:S(2)}) %collective-permute-start.9) | collective-permute-done | bytes 393248 | tf_op jit(solution)/shard_map/ppermute | solution.py:130
  145.3 2.8 %copy-done.3 = bf16[4096,768]{1,0:T(8,128)(2,1)S(1)} copy-done((bf16[4096,768]{1,0:T(8,128)(2,1)S(1)}, bf16[4096,768]{1,0:T(8,128)(2,1)}, u32[]{:S(2)}) %copy-start.3) | copy-done | bytes 6291480
  148.1 1.9 %shard_map.69 = bf16[192,768]{1,0:T(8,128)(2,1)S(1)} custom-call(s32[32]{0:T(128)S(1)} %fusion.6.place_ref, bf16[32,192,128]{2,1,0:T(8,128)(2,1)S(1)} %constant_dynamic-update-slice_fusion.4.block_ref, bf16[4096,768]{1,0:T(8,128)(2,1)S(1)} %copy-done.3), custom_call_target="tpu_custom_call" | custom-call | flops 1207959552 | bytes 8159232 | tf_op jit(solution)/shard_map/pallas_call | solution.py:29
  150.0 6.4 %collective-permute-start.10 = (bf16[192,768]{1,0:T(8,128)(2,1)S(1)}, bf16[192,768]{1,0:T(8,128)(2,1)S(1)}, u32[]{:S(2)}, u32[]{:S(2)}) collective-permute-start(bf16[192,768]{1,0:T(8,128)(2,1)S(1)} %shard_map.69), channel_id=1, source_target_pairs={{0,256},{256,0},{1,257},{257,1},{2,258},{258,2},{3,259},{259,3},{4... | collective-permute-start | bytes 884744 | tf_op jit(solution)/shard_map/ppermute | solution.py:152
  158.2 12.9 %collective-permute-done.10 = bf16[192,768]{1,0:T(8,128)(2,1)S(1)} collective-permute-done((bf16[192,768]{1,0:T(8,128)(2,1)S(1)}, bf16[192,768]{1,0:T(8,128)(2,1)S(1)}, u32[]{:S(2)}, u32[]{:S(2)}) %collective-permute-start.10) | collective-permute-done | bytes 294944 | tf_op jit(solution)/shard_map/ppermute | solution.py:152
  (42 shorter events, 14.2 us)
Async XLA Ops:
  7.2 1.1 copy-start
  7.2 62.0 %all-gather.3.cloned.1.call-start = ((), (), s32[]{:S(2)}) async-start(), calls=%async_computation.4 | async-start | bytes 5013504 | tf_op jit(solution)/shard_map/all_gather | solution.py:178
  32.0 4.9 %copy-start.5 = (bf16[128,1536]{1,0:T(8,128)(2,1)S(1)}, bf16[128,1536]{1,0:T(8,128)(2,1)}, u32[]{:S(2)}) copy-start(bf16[128,1536]{1,0:T(8,128)(2,1)} %param.6) | copy-start | bytes 1179652
  32.0 8.3 %copy-start.6 = (bf16[128,192]{0,1:T(8,128)(2,1)S(1)}, bf16[128,192]{0,1:T(8,128)(2,1)}, u32[]{:S(2)}) copy-start(bf16[128,192]{0,1:T(8,128)(2,1)} %param.4) | copy-start | bytes 147460
  32.0 28.9 %all-to-all-start.1 = ((bf16[4,8,192,128]{3,2,1,0:T(8,128)(2,1)}), bf16[4,8,192,128]{3,2,1,0:T(8,128)(2,1)S(1)}, u32[]{:S(2)}, u32[]{:S(2)}) async-start(bf16[4,8,192,128]{3,2,1,0:T(8,128)(2,1)} %broadcast_in_dim.5), calls=%async_computation.1 | async-start | bytes 3145728 | tf_op jit(solution)/shard_map/all_to_all | solution.py:157
  36.9 108.4 %all-gather.5.cloned.1.call-start = ((), (), s32[]{:S(2)}) async-start(), calls=%async_computation.5 | async-start | bytes 6684672 | tf_op jit(solution)/shard_map/all_gather | solution.py:194
  36.9 23.9 %collective-permute-start.3 = (bf16[128,768]{1,0:T(8,128)(2,1)S(1)}, bf16[128,768]{1,0:T(8,128)(2,1)S(1)}, u32[]{:S(2)}, u32[]{:S(2)}) collective-permute-start(bf16[128,768]{1,0:T(8,128)(2,1)S(1)} %constant_dynamic-slice_fusion.1), channel_id=1, source_target_pairs={{0,256},{256,0},{1,257},{257,1},{2,258},{258,2},{3,259},{259,3},{4... | collective-permute-start | bytes 589832 | tf_op jit(solution)/shard_map/ppermute | solution.py:152
  40.3 18.3 %collective-permute-start.1 = (bf16[192,128]{1,0:T(8,128)(2,1)S(1)}, bf16[192,128]{1,0:T(8,128)(2,1)S(1)}, u32[]{:S(2)}, u32[]{:S(2)}) collective-permute-start(bf16[192,128]{1,0:T(8,128)(2,1)S(1)} %bitcast.7), channel_id=1, source_target_pairs={{0,256},{1,272},{2,288},{3,304},{4,320},{5,336},{6,352},{7,368},{8... | collective-permute-start | bytes 147464 | tf_op jit(solution)/shard_map/ppermute | solution.py:179
  49.0 11.8 %collective-permute-start = (bf16[192,128]{1,0:T(8,128)(2,1)S(1)}, bf16[192,128]{1,0:T(8,128)(2,1)S(1)}, u32[]{:S(2)}, u32[]{:S(2)}) collective-permute-start(bf16[192,128]{1,0:T(8,128)(2,1)S(1)} %bitcast.8), channel_id=1, source_target_pairs={{0,0},{1,16},{2,32},{3,48},{4,64},{5,80},{6,96},{7,112},{8,128},{9... | collective-permute-start | bytes 147464 | tf_op jit(solution)/shard_map/ppermute | solution.py:179
  69.2 2.3 %copy-start.1 = (bf16[3072,768]{1,0:T(8,128)(2,1)S(1)}, bf16[3072,768]{1,0:T(8,128)(2,1)}, u32[]{:S(2)}) copy-start(bf16[3072,768]{1,0:T(8,128)(2,1)} %all-gather.3.cloned.1.call-done.weight_ref) | copy-start | bytes 14155780
  74.5 2.3 %copy-start.2 = (bf16[3072,768]{1,0:T(8,128)(2,1)S(1)}, bf16[3072,768]{1,0:T(8,128)(2,1)}, u32[]{:S(2)}) copy-start(bf16[3072,768]{1,0:T(8,128)(2,1)} %all-gather.3.cloned.1.call-done.weight_ref) | copy-start | bytes 14155780
  76.8 1.0 copy-start.4
  81.2 24.0 %all-to-all-start.2 = ((bf16[4,8,192,128]{3,2,1,0:T(8,128)(2,1)}), bf16[4,8,192,128]{3,2,1,0:T(8,128)(2,1)}, u32[]{:S(2)}, u32[]{:S(2)}) async-start(bf16[4,8,192,128]{3,2,1,0:T(8,128)(2,1)} %shard_map.68), calls=%async_computation.2 | async-start | bytes 3145728 | tf_op jit(solution)/shard_map/all_to_all | solution.py:161
  86.1 9.6 %collective-permute-start.4 = (bf16[2,192,128]{2,1,0:T(8,128)(2,1)S(1)}, bf16[2,192,128]{2,1,0:T(8,128)(2,1)S(1)}, u32[]{:S(2)}, u32[]{:S(2)}) collective-permute-start(bf16[2,192,128]{2,1,0:T(8,128)(2,1)S(1)} %pad_maximum_fusion.1), channel_id=1, source_target_pairs={{0,4},{4,8},{8,12},{12,0},{1,5},{5,9},{9,13},{13,1},{2,6},{6,10},{... | collective-permute-start | bytes 294920 | tf_op jit(solution)/shard_map/ppermute | solution.py:130
  88.0 8.3 %collective-permute-start.5 = (bf16[2,192,128]{2,1,0:T(8,128)(2,1)S(1)}, bf16[2,192,128]{2,1,0:T(8,128)(2,1)S(1)}, u32[]{:S(2)}, u32[]{:S(2)}) collective-permute-start(bf16[2,192,128]{2,1,0:T(8,128)(2,1)S(1)} %pad_maximum_fusion.1), channel_id=1, source_target_pairs={{0,8},{4,12},{8,0},{12,4},{1,9},{5,13},{9,1},{13,5},{2,10},{6,14},... | collective-permute-start | bytes 294920 | tf_op jit(solution)/shard_map/ppermute | solution.py:130
  93.1 7.2 %collective-permute-start.6 = (bf16[2,192,128]{2,1,0:T(8,128)(2,1)S(1)}, bf16[2,192,128]{2,1,0:T(8,128)(2,1)S(1)}, u32[]{:S(2)}, u32[]{:S(2)}) collective-permute-start(bf16[2,192,128]{2,1,0:T(8,128)(2,1)S(1)} %pad_maximum_fusion.1), channel_id=1, source_target_pairs={{0,12},{4,0},{8,4},{12,8},{1,13},{5,1},{9,5},{13,9},{2,14},{6,2},{... | collective-permute-start | bytes 294920 | tf_op jit(solution)/shard_map/ppermute | solution.py:130
  101.0 12.9 %collective-permute-start.7 = (bf16[8,192,128]{2,1,0:T(8,128)(2,1)}, bf16[8,192,128]{2,1,0:T(8,128)(2,1)S(1)}, u32[]{:S(2)}, u32[]{:S(2)}) collective-permute-start(bf16[8,192,128]{2,1,0:T(8,128)(2,1)} %get-tuple-element.20), channel_id=1, source_target_pairs={{0,1},{1,2},{2,3},{3,0},{4,5},{5,6},{6,7},{7,4},{8,9},{9,10},{10,1... | collective-permute-start | bytes 1179656 | tf_op jit(solution)/shard_map/ppermute | solution.py:130
  113.9 30.7 %all-to-all-start.3 = ((bf16[8,192,128]{2,1,0:T(8,128)(2,1)}), bf16[8,192,128]{2,1,0:T(8,128)(2,1)S(1)}, u32[]{:S(2)}, u32[]{:S(2)}) async-start(bf16[8,192,128]{2,1,0:T(8,128)(2,1)} %reduce_sum.24), calls=%async_computation.3 | async-start | bytes 786432 | tf_op jit(solution)/shard_map/all_to_all | solution.py:161
  121.8 15.8 %collective-permute-start.8 = (bf16[8,192,128]{2,1,0:T(8,128)(2,1)}, bf16[8,192,128]{2,1,0:T(8,128)(2,1)}, u32[]{:S(2)}, u32[]{:S(2)}) collective-permute-start(bf16[8,192,128]{2,1,0:T(8,128)(2,1)} %get-tuple-element.20), channel_id=1, source_target_pairs={{0,2},{1,3},{2,0},{3,1},{4,6},{5,7},{6,4},{7,5},{8,10},{9,11},{10,... | collective-permute-start | bytes 1179656 | tf_op jit(solution)/shard_map/ppermute | solution.py:130
  124.5 19.1 %collective-permute-start.9 = (bf16[8,192,128]{2,1,0:T(8,128)(2,1)}, bf16[8,192,128]{2,1,0:T(8,128)(2,1)}, u32[]{:S(2)}, u32[]{:S(2)}) collective-permute-start(bf16[8,192,128]{2,1,0:T(8,128)(2,1)} %get-tuple-element.20), channel_id=1, source_target_pairs={{0,3},{1,0},{2,1},{3,2},{4,7},{5,4},{6,5},{7,6},{8,11},{9,8},{10,9... | collective-permute-start | bytes 1179656 | tf_op jit(solution)/shard_map/ppermute | solution.py:130
  128.7 27.7 %collective-permute-start.2 = (bf16[128,768]{1,0:T(8,128)(2,1)S(1)}, bf16[128,768]{1,0:T(8,128)(2,1)}, u32[]{:S(2)}, u32[]{:S(2)}) collective-permute-start(bf16[128,768]{1,0:T(8,128)(2,1)S(1)} %constant_dynamic-slice_fusion.2), channel_id=1, source_target_pairs={{0,256},{256,0},{1,257},{257,1},{2,258},{258,2},{3,259},{259,3},{4... | collective-permute-start | bytes 589832 | tf_op jit(solution)/shard_map/ppermute | solution.py:152
  145.3 2.8 %copy-start.3 = (bf16[4096,768]{1,0:T(8,128)(2,1)S(1)}, bf16[4096,768]{1,0:T(8,128)(2,1)}, u32[]{:S(2)}) copy-start(bf16[4096,768]{1,0:T(8,128)(2,1)} %all-gather.5.cloned.1.call-done.grad_ref) | copy-start | bytes 18874372
  150.0 21.1 %collective-permute-start.10 = (bf16[192,768]{1,0:T(8,128)(2,1)S(1)}, bf16[192,768]{1,0:T(8,128)(2,1)S(1)}, u32[]{:S(2)}, u32[]{:S(2)}) collective-permute-start(bf16[192,768]{1,0:T(8,128)(2,1)S(1)} %shard_map.69), channel_id=1, source_target_pairs={{0,256},{256,0},{1,257},{257,1},{2,258},{258,2},{3,259},{259,3},{4... | collective-permute-start | bytes 884744 | tf_op jit(solution)/shard_map/ppermute | solution.py:152
Sparse Core Ops, SparseCore 0:
  10.7 58.3 all-gather.2
  74.6 47.4 all-gather.4

commit v21 on v16

--- a/solution.py
+++ b/solution.py
@@ -12,7 +12,9 @@
 COLS = 16
 SIDE = 4
 LANES = 256
+CHUNKS = 4
 VMEM_BYTES = 32 * 2**20
+CHUNKED_VMEM_BYTES = 48 * 2**20
 COL = ("y", "x")
 
 
@@ -41,27 +43,72 @@
     return jnp.concatenate([block_ref[x, y], block_ref[x, SIDE + y]], axis=1)
 
 
-def hidden_kernel(block_ref, weight_ref, hidden_ref):
+def chunk_copies(source_ref, held_ref, sems):
+    rows = source_ref.shape[0] // CHUNKS
+    copies = []
+    for chunk in range(CHUNKS):
+        span = pl.ds(chunk * rows, rows)
+        copies.append(pltpu.make_async_copy(source_ref.at[span], held_ref.at[span], sems.at[chunk]))
+    for copy in copies:
+        copy.start()
+    return copies
+
+
+def chunked_sum(copies, count, term_of, total_ref):
+    per_chunk = count // CHUNKS
+    for chunk, copy in enumerate(copies):
+        copy.wait()
+        for start in range(0, total_ref.shape[1], LANES):
+            units = pl.ds(start, LANES)
+            total = total_ref[:, units] if chunk else None
+            for index in range(chunk * per_chunk, (chunk + 1) * per_chunk):
+                term = term_of(index, units)
+                total = term if total is None else total + term
+            total_ref[:, units] = total
+
+
+def chunked_kernel(kernel, out_shape, flops, place, blocks, value, scratch=()):
+    operands = ([] if place is None else [place]) + [blocks, value]
+    vmem = pl.BlockSpec(memory_space=pltpu.VMEM)
+    in_specs = [vmem, pl.BlockSpec(memory_space=pl.ANY)]
+    if place is not None:
+        in_specs = [pl.BlockSpec(memory_space=pltpu.SMEM)] + in_specs
+    moved = sum(x.size * x.dtype.itemsize for x in (blocks, value, out_shape))
+    return pl.pallas_call(
+        kernel,
+        out_shape=out_shape,
+        in_specs=in_specs,
+        out_specs=vmem,
+        scratch_shapes=[
+            pltpu.VMEM(value.shape, value.dtype),
+            pltpu.SemaphoreType.DMA((CHUNKS,)),
+            *scratch,
+        ],
+        compiler_params=pltpu.CompilerParams(vmem_limit_bytes=CHUNKED_VMEM_BYTES),
+        cost_estimate=pl.CostEstimate(flops=flops, bytes_accessed=moved, transcendentals=0),
+    )(*operands)
+
+
+def hidden_kernel(block_ref, weight_ref, hidden_ref, held_ref, sems):
     depth = block_ref.shape[2]
+    copies = chunk_copies(weight_ref, held_ref, sems)
     blocks = [both_replicas(block_ref, col) for col in range(COLS)]
-    for start in range(0, hidden_ref.shape[1], LANES):
-        units = pl.ds(start, LANES)
-        total = None
-        for col, block in enumerate(blocks):
-            term = lax.dot_general(
-                block,
-                weight_ref[pl.ds(col * depth, depth), units],
-                (((0,), (0,)), ((), ())),
-                preferred_element_type=jnp.float32,
-            )
-            total = term if total is None else total + term
-        hidden_ref[:, units] = total
+
+    def term_of(col, units):
+        return lax.dot_general(
+            blocks[col],
+            held_ref[pl.ds(col * depth, depth), units],
+            (((0,), (0,)), ((), ())),
+            preferred_element_type=jnp.float32,
+        )
+
+    chunked_sum(copies, COLS, term_of, hidden_ref)
 
 
 def hidden_sum(blocks, weight):
     tokens = 2 * blocks.shape[3]
     out_shape = jax.ShapeDtypeStruct((tokens, weight.shape[1]), jnp.float32)
-    return local_kernel(hidden_kernel, out_shape, 2 * tokens * weight.size, (blocks, weight))
+    return chunked_kernel(hidden_kernel, out_shape, 2 * tokens * weight.size, None, blocks, weight)
 
 
 def input_grad_kernel(weight_ref, grad_ref, pieces_ref):
@@ -84,31 +131,28 @@
     return local_kernel(input_grad_kernel, out_shape, 2 * weight.size * grad.shape[0], (weight, grad))
 
 
-def token_sum_kernel(place_ref, block_ref, grad_ref, total_ref):
+def token_sum_kernel(place_ref, block_ref, grad_ref, out_ref, held_ref, sems, total_ref):
     tokens = 2 * block_ref.shape[2]
+    copies = chunk_copies(grad_ref, held_ref, sems)
     blocks = []
     for row in range(ROWS):
         parts = [block_ref[place_ref[2 * row + d]] for d in range(2)]
         blocks.append(jnp.concatenate(parts, axis=1))
-    for start in range(0, total_ref.shape[1], LANES):
-        units = pl.ds(start, LANES)
-        total = None
-        for row, block in enumerate(blocks):
-            term = jnp.dot(
-                block,
-                grad_ref[pl.ds(row * tokens, tokens), units],
-                preferred_element_type=jnp.float32,
-            )
-            total = term if total is None else total + term
-        total_ref[:, units] = total.astype(total_ref.dtype)
+
+    def term_of(row, units):
+        grad = held_ref[pl.ds(row * tokens, tokens), units]
+        return jnp.dot(blocks[row], grad, preferred_element_type=jnp.float32)
+
+    chunked_sum(copies, ROWS, term_of, total_ref)
+    out_ref[...] = total_ref[...].astype(out_ref.dtype)
 
 
 def token_sum(place, blocks, grads):
-    depth = blocks.shape[1]
-    out_shape = jax.ShapeDtypeStruct((depth, grads.shape[1]), jnp.bfloat16)
-    return local_kernel(
-        token_sum_kernel, out_shape, 2 * depth * grads.size, (blocks, grads), place
-    )
+    shape = (blocks.shape[1], grads.shape[1])
+    out_shape = jax.ShapeDtypeStruct(shape, jnp.bfloat16)
+    total = pltpu.VMEM(shape, jnp.float32)
+    flops = 2 * shape[0] * grads.size
+    return chunked_kernel(token_sum_kernel, out_shape, flops, place, blocks, grads, (total,))
 
 
 def places():

time: 169 us -> 169 us (level)
  the two profiles are of different devices: /device:TPU:56 before, /device:TPU:16 now
where the time goes in v21:
time: 169 us; the launch traced here: 168 us
  starting transfers between devices  71 us (42%)
  waiting for transfers between devices  30.4 us (18%)
  blocking collectives  19.1 us (11%)
  between operations  14.3 us (8%)
  local copies, waits for them, and re-layouts  13.6 us (8%)
  Pallas kernels  11.9 us (7%)
  other arithmetic  7.39 us (4%)
    ppermute x6, starting transfers between devices, shifted(): lax.ppermute(value, axis, [(i, (i + steps) % SIDE) for i in range(SIDE)])  25.6 us
    all_to_all x1, blocking collectives, to_all(): return lax.all_to_all(copies, axis, 0, 0, tiled=True)  19.1 us
    ppermute x4, starting transfers between devices, to_replica(): return lax.ppermute(value, 'dp', [(0, 1), (1, 0)])  18.1 us
    ppermute x4, waiting for transfers between devices, to_replica(): return lax.ppermute(value, 'dp', [(0, 1), (1, 0)])  11.8 us
    all_to_all x2, starting transfers between devices, sum_along(): pieces = lax.all_to_all(pieces, axis, 0, 0, tiled=True)  11.7 us
    ppermute x1, starting transfers between devices, per_device(): turned = lax.ppermute(features, ('row',) + COL, turns)  11.2 us
    pallas_call x2, Pallas kernels, chunked_kernel(): pl.pallas_call(kernel, out_shape=out_shape, in_specs=in_specs, out_specs=...  8.48 us
    ppermute x1, waiting for transfers between devices, per_device(): turned = lax.ppermute(features, ('row',) + COL, turns)  8.41 us
  transfers between devices with their start and end apart: 16, of which 5 were waited for; matrix products, arithmetic and copies ran while one was open for 8% of the time, Pallas kernels for 5%

profile of v21, /device:TPU:16, one launch (start us, length us, event | category | flops | bytes accessed | tf_op | source)
XLA Modules:
  0.0 167.7 jit_solution(5727189031721325613)
XLA Ops:
  7.2 1.0 copy-done
  9.8 19.1 %all_to_all.20 = bf16[8,192,128]{2,1,0:T(8,128)(2,1)S(1)} all-to-all(bf16[8,192,128]{2,1,0:T(8,128)(2,1)S(1)} %broadcast_in_dim.4), channel_id=1, replica_groups=mesh['dp'=2,'row'=16,'y'=4,'x'=4] {'dp','y'}, dimensions={0} | all-to-all | bytes 786432 | tf_op jit(solution)/shard_map/all_to_all | solution.py:192
  28.9 1.6 broadcast_in_dim.5
  30.5 4.4 %all-to-all-start.1 = ((bf16[4,8,192,128]{3,2,1,0:T(8,128)(2,1)}), bf16[4,8,192,128]{3,2,1,0:T(8,128)(2,1)S(1)}, u32[]{:S(2)}, u32[]{:S(2)}) async-start(bf16[4,8,192,128]{3,2,1,0:T(8,128)(2,1)} %broadcast_in_dim.5), calls=%async_computation.1 | async-start | bytes 3145728 | tf_op jit(solution)/shard_map/all_to_all | solution.py:192
  34.9 4.5 %collective-permute-start.2 = (bf16[128,768]{1,0:T(8,128)(2,1)S(1)}, bf16[128,768]{1,0:T(8,128)(2,1)S(1)}, u32[]{:S(2)}, u32[]{:S(2)}) collective-permute-start(bf16[128,768]{1,0:T(8,128)(2,1)S(1)} %constant_dynamic-slice_fusion.1), channel_id=1, source_target_pairs={{0,256},{256,0},{1,257},{257,1},{2,258},{258,2},{3,259},{259,3},{4... | collective-permute-start | bytes 589832 | tf_op jit(solution)/shard_map/ppermute | solution.py:187
  39.4 11.2 %collective-permute-start = (bf16[192,128]{1,0:T(8,128)(2,1)S(1)}, bf16[192,128]{1,0:T(8,128)(2,1)S(1)}, u32[]{:S(2)}, u32[]{:S(2)}) collective-permute-start(bf16[192,128]{1,0:T(8,128)(2,1)S(1)} %bitcast.13), channel_id=1, source_target_pairs={{0,0},{1,16},{2,32},{3,48},{4,64},{5,80},{6,96},{7,112},{8,128},{9... | collective-permute-start | bytes 147464 | tf_op jit(solution)/shard_map/ppermute | solution.py:215
  50.7 8.4 %collective-permute-done = bf16[192,128]{1,0:T(8,128)(2,1)S(1)} collective-permute-done((bf16[192,128]{1,0:T(8,128)(2,1)S(1)}, bf16[192,128]{1,0:T(8,128)(2,1)S(1)}, u32[]{:S(2)}, u32[]{:S(2)}) %collective-permute-start) | collective-permute-done | bytes 49184 | tf_op jit(solution)/shard_map/ppermute | solution.py:215
  59.1 2.7 %all-gather.3.cloned.1.call-done.weight_ref = bf16[3072,768]{1,0:T(8,128)(2,1)} async-done(((bf16[192,768]{1,0:T(8,128)(2,1)}), bf16[3072,768]{1,0:T(8,128)(2,1)}) %all-gather.3.cloned.1.call-update) | async-done | bytes 4718608 | tf_op jit(solution)/shard_map/all_gather | solution.py:213
  61.9 4.3 %shard_map.67 = f32[256,768]{1,0:T(8,128)S(1)} custom-call(bf16[4,8,192,128]{3,2,1,0:T(8,128)(2,1)S(1)} %all-to-all-done.1.block_ref, bf16[3072,768]{1,0:T(8,128)(2,1)} %all-gather.3.cloned.1.call-done.weight_ref), custom_call_target="tpu_custom_call" | custom-call | flops 1207959552 | bytes 7077888 | tf_op jit(solution)/shard_map/pallas_call | solution.py:77
  66.1 1.1 fusion.5
  67.3 5.7 %collective-permute-start.3 = (bf16[192,128]{1,0:T(8,128)(2,1)S(1)}, bf16[192,128]{1,0:T(8,128)(2,1)S(1)}, u32[]{:S(2)}, u32[]{:S(2)}) collective-permute-start(bf16[192,128]{1,0:T(8,128)(2,1)S(1)} %collective-permute-done), channel_id=1, source_target_pairs={{0,256},{256,0},{1,257},{257,1},{2,258},{258,2},{3,259},{259,3},{4... | collective-permute-start | bytes 147464 | tf_op jit(solution)/shard_map/ppermute | solution.py:187
  73.7 2.3 %copy-done.1 = bf16[3072,768]{1,0:T(8,128)(2,1)S(1)} copy-done((bf16[3072,768]{1,0:T(8,128)(2,1)S(1)}, bf16[3072,768]{1,0:T(8,128)(2,1)}, u32[]{:S(2)}) %copy-start.1) | copy-done | bytes 4718616
  76.0 1.0 copy-done.2
  77.0 3.4 %shard_map.68 = bf16[4,8,192,128]{3,2,1,0:T(8,128)(2,1)} custom-call(bf16[3072,768]{1,0:T(8,128)(2,1)S(1)} %copy-done.1, bf16[256,768]{1,0:T(8,128)(2,1)S(1)} %copy-done.2), custom_call_target="tpu_custom_call" | custom-call | flops 1207959552 | bytes 6684672 | tf_op jit(solution)/shard_map/pallas_call | solution.py:31
  80.4 5.2 %all-to-all-start.2 = ((bf16[4,8,192,128]{3,2,1,0:T(8,128)(2,1)}), bf16[4,8,192,128]{3,2,1,0:T(8,128)(2,1)}, u32[]{:S(2)}, u32[]{:S(2)}) async-start(bf16[4,8,192,128]{3,2,1,0:T(8,128)(2,1)} %shard_map.68), calls=%async_computation.2 | async-start | bytes 3145728 | tf_op jit(solution)/shard_map/all_to_all | solution.py:196
  85.6 3.8 %collective-permute-start.4 = (bf16[2,192,128]{2,1,0:T(8,128)(2,1)S(1)}, bf16[2,192,128]{2,1,0:T(8,128)(2,1)S(1)}, u32[]{:S(2)}, u32[]{:S(2)}) collective-permute-start(bf16[2,192,128]{2,1,0:T(8,128)(2,1)S(1)} %pad_maximum_fusion.1), channel_id=1, source_target_pairs={{0,4},{4,8},{8,12},{12,0},{1,5},{5,9},{9,13},{13,1},{2,6},{6,10},{... | collective-permute-start | bytes 294920 | tf_op jit(solution)/shard_map/ppermute | solution.py:174
  89.4 5.3 %collective-permute-start.5 = (bf16[2,192,128]{2,1,0:T(8,128)(2,1)S(1)}, bf16[2,192,128]{2,1,0:T(8,128)(2,1)S(1)}, u32[]{:S(2)}, u32[]{:S(2)}) collective-permute-start(bf16[2,192,128]{2,1,0:T(8,128)(2,1)S(1)} %pad_maximum_fusion.1), channel_id=1, source_target_pairs={{0,8},{4,12},{8,0},{12,4},{1,9},{5,13},{9,1},{13,5},{2,10},{6,14},... | collective-permute-start | bytes 294920 | tf_op jit(solution)/shard_map/ppermute | solution.py:174
  94.7 4.8 %collective-permute-start.6 = (bf16[2,192,128]{2,1,0:T(8,128)(2,1)S(1)}, bf16[2,192,128]{2,1,0:T(8,128)(2,1)S(1)}, u32[]{:S(2)}, u32[]{:S(2)}) collective-permute-start(bf16[2,192,128]{2,1,0:T(8,128)(2,1)S(1)} %pad_maximum_fusion.1), channel_id=1, source_target_pairs={{0,12},{4,0},{8,4},{12,8},{1,13},{5,1},{9,5},{13,9},{2,14},{6,2},{... | collective-permute-start | bytes 294920 | tf_op jit(solution)/shard_map/ppermute | solution.py:174
  102.6 3.8 %collective-permute-start.7 = (bf16[8,192,128]{2,1,0:T(8,128)(2,1)}, bf16[8,192,128]{2,1,0:T(8,128)(2,1)}, u32[]{:S(2)}, u32[]{:S(2)}) collective-permute-start(bf16[8,192,128]{2,1,0:T(8,128)(2,1)} %get-tuple-element.15), channel_id=1, source_target_pairs={{0,1},{1,2},{2,3},{3,0},{4,5},{5,6},{6,7},{7,4},{8,9},{9,10},{10,1... | collective-permute-start | bytes 1179656 | tf_op jit(solution)/shard_map/ppermute | solution.py:174
  106.3 4.6 %collective-permute-start.8 = (bf16[8,192,128]{2,1,0:T(8,128)(2,1)}, bf16[8,192,128]{2,1,0:T(8,128)(2,1)S(1)}, u32[]{:S(2)}, u32[]{:S(2)}) collective-permute-start(bf16[8,192,128]{2,1,0:T(8,128)(2,1)} %get-tuple-element.15), channel_id=1, source_target_pairs={{0,2},{1,3},{2,0},{3,1},{4,6},{5,7},{6,4},{7,5},{8,10},{9,11},{10,... | collective-permute-start | bytes 1179656 | tf_op jit(solution)/shard_map/ppermute | solution.py:174
  110.9 3.4 %collective-permute-start.9 = (bf16[8,192,128]{2,1,0:T(8,128)(2,1)}, bf16[8,192,128]{2,1,0:T(8,128)(2,1)}, u32[]{:S(2)}, u32[]{:S(2)}) collective-permute-start(bf16[8,192,128]{2,1,0:T(8,128)(2,1)} %get-tuple-element.15), channel_id=1, source_target_pairs={{0,3},{1,0},{2,1},{3,2},{4,7},{5,4},{6,5},{7,6},{8,11},{9,8},{10,9... | collective-permute-start | bytes 1179656 | tf_op jit(solution)/shard_map/ppermute | solution.py:174
  115.0 2.4 %collective-permute-start.1 = (bf16[128,768]{1,0:T(8,128)(2,1)S(1)}, bf16[128,768]{1,0:T(8,128)(2,1)}, u32[]{:S(2)}, u32[]{:S(2)}) collective-permute-start(bf16[128,768]{1,0:T(8,128)(2,1)S(1)} %constant_dynamic-slice_fusion.2), channel_id=1, source_target_pairs={{0,256},{256,0},{1,257},{257,1},{2,258},{258,2},{3,259},{259,3},{4... | collective-permute-start | bytes 589832 | tf_op jit(solution)/shard_map/ppermute | solution.py:187
  117.4 1.0 constant_dynamic-update-slice_fusion.7
  118.5 7.1 %collective-permute-done.8 = bf16[8,192,128]{2,1,0:T(8,128)(2,1)S(1)} collective-permute-done((bf16[8,192,128]{2,1,0:T(8,128)(2,1)}, bf16[8,192,128]{2,1,0:T(8,128)(2,1)S(1)}, u32[]{:S(2)}, u32[]{:S(2)}) %collective-permute-start.8) | collective-permute-done | bytes 393248 | tf_op jit(solution)/shard_map/ppermute | solution.py:174
  125.6 2.5 %reduce_sum.24 = bf16[8,192,128]{2,1,0:T(8,128)(2,1)} reduce(bf16[4,8,192,128]{3,2,1,0:T(8,128)(2,1)} %all-to-all-done.2, bf16[]{:T(256)} %constant.43.clone.1), dimensions={0}, to_apply=%region_0.1 | reduce | flops 589824 | bytes 1966082 | tf_op jit(solution)/shard_map/reduce_sum | solution.py:197
  128.1 6.4 %all-to-all-start.3 = ((bf16[8,192,128]{2,1,0:T(8,128)(2,1)}), bf16[8,192,128]{2,1,0:T(8,128)(2,1)S(1)}, u32[]{:S(2)}, u32[]{:S(2)}) async-start(bf16[8,192,128]{2,1,0:T(8,128)(2,1)} %reduce_sum.24), calls=%async_computation.3 | async-start | bytes 786432 | tf_op jit(solution)/shard_map/all_to_all | solution.py:196
  134.6 1.0 constant_dynamic-update-slice_fusion.5.block_ref
  135.7 4.2 %shard_map.69 = bf16[192,768]{1,0:T(8,128)(2,1)S(1)} custom-call(s32[32]{0:T(128)S(1)} %fusion.6.place_ref, bf16[32,192,128]{2,1,0:T(8,128)(2,1)S(1)} %constant_dynamic-update-slice_fusion.5.block_ref, bf16[4096,768]{1,0:T(8,128)(2,1)} %all-gather.5.cloned.1.call-done.grad_ref), custom_call_target="tpu_custom_call" | custom-call | flops 1207959552 | bytes 8159232 | tf_op jit(solution)/shard_map/pallas_call | solution.py:77
  139.9 5.5 %collective-permute-start.10 = (bf16[192,768]{1,0:T(8,128)(2,1)S(1)}, bf16[192,768]{1,0:T(8,128)(2,1)S(1)}, u32[]{:S(2)}, u32[]{:S(2)}) collective-permute-start(bf16[192,768]{1,0:T(8,128)(2,1)S(1)} %shard_map.69), channel_id=1, source_target_pairs={{0,256},{256,0},{1,257},{257,1},{2,258},{258,2},{3,259},{259,3},{4... | collective-permute-start | bytes 884744 | tf_op jit(solution)/shard_map/ppermute | solution.py:187
  145.4 1.0 broadcast_select_fusion.5
  147.9 11.8 %collective-permute-done.10 = bf16[192,768]{1,0:T(8,128)(2,1)S(1)} collective-permute-done((bf16[192,768]{1,0:T(8,128)(2,1)S(1)}, bf16[192,768]{1,0:T(8,128)(2,1)S(1)}, u32[]{:S(2)}, u32[]{:S(2)}) %collective-permute-start.10) | collective-permute-done | bytes 294944 | tf_op jit(solution)/shard_map/ppermute | solution.py:187
  159.7 1.1 maximum_convert_fusion
  (39 shorter events, 7.7 us)
Async XLA Ops:
  7.2 1.1 copy-start
  7.2 54.7 %all-gather.3.cloned.1.call-start = ((), (), s32[]{:S(2)}) async-start(), calls=%async_computation.4 | async-start | bytes 5013504 | tf_op jit(solution)/shard_map/all_gather | solution.py:213
  30.5 4.4 %copy-start.3 = (bf16[128,1536]{1,0:T(8,128)(2,1)S(1)}, bf16[128,1536]{1,0:T(8,128)(2,1)}, u32[]{:S(2)}) copy-start(bf16[128,1536]{1,0:T(8,128)(2,1)} %param.6) | copy-start | bytes 1179652
  30.5 9.0 %copy-start.4 = (bf16[128,192]{0,1:T(8,128)(2,1)S(1)}, bf16[128,192]{0,1:T(8,128)(2,1)}, u32[]{:S(2)}) copy-start(bf16[128,192]{0,1:T(8,128)(2,1)} %param.4) | copy-start | bytes 147460
  30.5 28.7 %all-to-all-start.1 = ((bf16[4,8,192,128]{3,2,1,0:T(8,128)(2,1)}), bf16[4,8,192,128]{3,2,1,0:T(8,128)(2,1)S(1)}, u32[]{:S(2)}, u32[]{:S(2)}) async-start(bf16[4,8,192,128]{3,2,1,0:T(8,128)(2,1)} %broadcast_in_dim.5), calls=%async_computation.1 | async-start | bytes 3145728 | tf_op jit(solution)/shard_map/all_to_all | solution.py:192
  34.9 100.8 %all-gather.5.cloned.1.call-start = ((), (), s32[]{:S(2)}) async-start(), calls=%async_computation.5 | async-start | bytes 6684672 | tf_op jit(solution)/shard_map/all_gather | solution.py:229
  34.9 15.7 %collective-permute-start.2 = (bf16[128,768]{1,0:T(8,128)(2,1)S(1)}, bf16[128,768]{1,0:T(8,128)(2,1)S(1)}, u32[]{:S(2)}, u32[]{:S(2)}) collective-permute-start(bf16[128,768]{1,0:T(8,128)(2,1)S(1)} %constant_dynamic-slice_fusion.1), channel_id=1, source_target_pairs={{0,256},{256,0},{1,257},{257,1},{2,258},{258,2},{3,259},{259,3},{4... | collective-permute-start | bytes 589832 | tf_op jit(solution)/shard_map/ppermute | solution.py:187
  39.4 19.7 %collective-permute-start = (bf16[192,128]{1,0:T(8,128)(2,1)S(1)}, bf16[192,128]{1,0:T(8,128)(2,1)S(1)}, u32[]{:S(2)}, u32[]{:S(2)}) collective-permute-start(bf16[192,128]{1,0:T(8,128)(2,1)S(1)} %bitcast.13), channel_id=1, source_target_pairs={{0,0},{1,16},{2,32},{3,48},{4,64},{5,80},{6,96},{7,112},{8,128},{9... | collective-permute-start | bytes 147464 | tf_op jit(solution)/shard_map/ppermute | solution.py:215
  67.3 18.3 %collective-permute-start.3 = (bf16[192,128]{1,0:T(8,128)(2,1)S(1)}, bf16[192,128]{1,0:T(8,128)(2,1)S(1)}, u32[]{:S(2)}, u32[]{:S(2)}) collective-permute-start(bf16[192,128]{1,0:T(8,128)(2,1)S(1)} %collective-permute-done), channel_id=1, source_target_pairs={{0,256},{256,0},{1,257},{257,1},{2,258},{258,2},{3,259},{259,3},{4... | collective-permute-start | bytes 147464 | tf_op jit(solution)/shard_map/ppermute | solution.py:187
  73.7 2.3 %copy-start.1 = (bf16[3072,768]{1,0:T(8,128)(2,1)S(1)}, bf16[3072,768]{1,0:T(8,128)(2,1)}, u32[]{:S(2)}) copy-start(bf16[3072,768]{1,0:T(8,128)(2,1)} %all-gather.3.cloned.1.call-done.weight_ref) | copy-start | bytes 14155780
  76.0 1.0 copy-start.2
  80.4 45.2 %all-to-all-start.2 = ((bf16[4,8,192,128]{3,2,1,0:T(8,128)(2,1)}), bf16[4,8,192,128]{3,2,1,0:T(8,128)(2,1)}, u32[]{:S(2)}, u32[]{:S(2)}) async-start(bf16[4,8,192,128]{3,2,1,0:T(8,128)(2,1)} %shard_map.68), calls=%async_computation.2 | async-start | bytes 3145728 | tf_op jit(solution)/shard_map/all_to_all | solution.py:196
  85.6 14.5 %collective-permute-start.4 = (bf16[2,192,128]{2,1,0:T(8,128)(2,1)S(1)}, bf16[2,192,128]{2,1,0:T(8,128)(2,1)S(1)}, u32[]{:S(2)}, u32[]{:S(2)}) collective-permute-start(bf16[2,192,128]{2,1,0:T(8,128)(2,1)S(1)} %pad_maximum_fusion.1), channel_id=1, source_target_pairs={{0,4},{4,8},{8,12},{12,0},{1,5},{5,9},{9,13},{13,1},{2,6},{6,10},{... | collective-permute-start | bytes 294920 | tf_op jit(solution)/shard_map/ppermute | solution.py:174
  89.4 11.4 %collective-permute-start.5 = (bf16[2,192,128]{2,1,0:T(8,128)(2,1)S(1)}, bf16[2,192,128]{2,1,0:T(8,128)(2,1)S(1)}, u32[]{:S(2)}, u32[]{:S(2)}) collective-permute-start(bf16[2,192,128]{2,1,0:T(8,128)(2,1)S(1)} %pad_maximum_fusion.1), channel_id=1, source_target_pairs={{0,8},{4,12},{8,0},{12,4},{1,9},{5,13},{9,1},{13,5},{2,10},{6,14},... | collective-permute-start | bytes 294920 | tf_op jit(solution)/shard_map/ppermute | solution.py:174
  94.7 7.2 %collective-permute-start.6 = (bf16[2,192,128]{2,1,0:T(8,128)(2,1)S(1)}, bf16[2,192,128]{2,1,0:T(8,128)(2,1)S(1)}, u32[]{:S(2)}, u32[]{:S(2)}) collective-permute-start(bf16[2,192,128]{2,1,0:T(8,128)(2,1)S(1)} %pad_maximum_fusion.1), channel_id=1, source_target_pairs={{0,12},{4,0},{8,4},{12,8},{1,13},{5,1},{9,5},{13,9},{2,14},{6,2},{... | collective-permute-start | bytes 294920 | tf_op jit(solution)/shard_map/ppermute | solution.py:174
  102.6 14.9 %collective-permute-start.7 = (bf16[8,192,128]{2,1,0:T(8,128)(2,1)}, bf16[8,192,128]{2,1,0:T(8,128)(2,1)}, u32[]{:S(2)}, u32[]{:S(2)}) collective-permute-start(bf16[8,192,128]{2,1,0:T(8,128)(2,1)} %get-tuple-element.15), channel_id=1, source_target_pairs={{0,1},{1,2},{2,3},{3,0},{4,5},{5,6},{6,7},{7,4},{8,9},{9,10},{10,1... | collective-permute-start | bytes 1179656 | tf_op jit(solution)/shard_map/ppermute | solution.py:174
  106.3 19.2 %collective-permute-start.8 = (bf16[8,192,128]{2,1,0:T(8,128)(2,1)}, bf16[8,192,128]{2,1,0:T(8,128)(2,1)S(1)}, u32[]{:S(2)}, u32[]{:S(2)}) collective-permute-start(bf16[8,192,128]{2,1,0:T(8,128)(2,1)} %get-tuple-element.15), channel_id=1, source_target_pairs={{0,2},{1,3},{2,0},{3,1},{4,6},{5,7},{6,4},{7,5},{8,10},{9,11},{10,... | collective-permute-start | bytes 1179656 | tf_op jit(solution)/shard_map/ppermute | solution.py:174
  110.9 23.6 %collective-permute-start.9 = (bf16[8,192,128]{2,1,0:T(8,128)(2,1)}, bf16[8,192,128]{2,1,0:T(8,128)(2,1)}, u32[]{:S(2)}, u32[]{:S(2)}) collective-permute-start(bf16[8,192,128]{2,1,0:T(8,128)(2,1)} %get-tuple-element.15), channel_id=1, source_target_pairs={{0,3},{1,0},{2,1},{3,2},{4,7},{5,4},{6,5},{7,6},{8,11},{9,8},{10,9... | collective-permute-start | bytes 1179656 | tf_op jit(solution)/shard_map/ppermute | solution.py:174
  115.0 30.3 %collective-permute-start.1 = (bf16[128,768]{1,0:T(8,128)(2,1)S(1)}, bf16[128,768]{1,0:T(8,128)(2,1)}, u32[]{:S(2)}, u32[]{:S(2)}) collective-permute-start(bf16[128,768]{1,0:T(8,128)(2,1)S(1)} %constant_dynamic-slice_fusion.2), channel_id=1, source_target_pairs={{0,256},{256,0},{1,257},{257,1},{2,258},{258,2},{3,259},{259,3},{4... | collective-permute-start | bytes 589832 | tf_op jit(solution)/shard_map/ppermute | solution.py:187
  128.1 19.0 %all-to-all-start.3 = ((bf16[8,192,128]{2,1,0:T(8,128)(2,1)}), bf16[8,192,128]{2,1,0:T(8,128)(2,1)S(1)}, u32[]{:S(2)}, u32[]{:S(2)}) async-start(bf16[8,192,128]{2,1,0:T(8,128)(2,1)} %reduce_sum.24), calls=%async_computation.3 | async-start | bytes 786432 | tf_op jit(solution)/shard_map/all_to_all | solution.py:196
  139.9 19.8 %collective-permute-start.10 = (bf16[192,768]{1,0:T(8,128)(2,1)S(1)}, bf16[192,768]{1,0:T(8,128)(2,1)S(1)}, u32[]{:S(2)}, u32[]{:S(2)}) collective-permute-start(bf16[192,768]{1,0:T(8,128)(2,1)S(1)} %shard_map.69), channel_id=1, source_target_pairs={{0,256},{256,0},{1,257},{257,1},{2,258},{258,2},{3,259},{259,3},{4... | collective-permute-start | bytes 884744 | tf_op jit(solution)/shard_map/ppermute | solution.py:187
Sparse Core Ops, SparseCore 0:
  10.7 51.1 all-gather.2
  67.4 50.8 all-gather.4
